TPU v7x, 32 devices: a whole 2x2x4 slice. The times are simulated.
32 devices in a mesh: cuts: 2 (over y), row: 16 (over z, x, core).
Axes of the slice: x: 2, y: 2, z: 4, core: 2. Of those that a mesh axis runs over, the one named last changes fastest.
Arguments:
- block_tiles: float32 [48, 24, 128, 128], P('row'), may hold values from -0.109375 to 0.109375
- tile_pattern: int32 [48, 24], P('row'), may hold values from 0 to 47, as said below
- start_vectors: float32 [2, 32, 6144], P('cuts', None, 'row'), may hold values from -8 to 8
- centers: float32 [2], P('cuts'), may hold values from -0.3 to 0.3
- halfwidths: float32 [2], P('cuts'), may hold values from 0.9 to 1.3
- dup_pairs: int32 [2, 8, 2], P('cuts'), may hold values from 0 to 31, as said below
Outputs:
- filtered_basis: float32 [2, 32, 6144], P('cuts', None, 'row')
- projected: float32 [2, 32, 32], P('cuts')
Inputs may be any that keep to these rules, and one draw needn't show every extreme that they name: tile_pattern[r, 0] = r; the other entries of block row r are distinct block rows, each within 12 of r cyclically and different from r. `dup_pairs`: within one slice the first entries of the pairs are distinct, and so are the second entries; the pairs of slice 0 are not used.
All inputs are finite; a program needn't handle non-finite values.
Results may differ from a plain program's by a relative error of at most 0.00015.
Values sent between devices are 32-bit elements; how exact they have to be, the bound alone decides.
No kernel may reach another device: no remote copies, remote signals or barrier semaphores. Data moves between devices by JAX's collectives and lax.ppermute only.
A program may use at most 64 MiB of HBM per device.

v0:
```python
import math

import jax
import jax.numpy as jnp
from jax import lax
from jax.sharding import PartitionSpec as P

DEG = 8
REACH = 12


def from_behind(shard, axis, by):
    size = lax.axis_size(axis)
    return lax.ppermute(shard, axis, [(i, (i + by) % size) for i in range(size)])


def from_behind_2(value, axis, steps):
    count = lax.axis_size(axis)
    leading, last = (max(0, -steps), min(count, count - steps))
    return lax.ppermute(value, axis, [(source, source + steps) for source in range(leading, last)])


def apply_local(vectors, block_tiles, tile_pattern):
    vec_count = vectors.shape[0]
    local_rows = block_tiles.shape[0]
    tile_width = block_tiles.shape[2]
    device_reach = (REACH + local_rows - 1) // local_rows
    pieces = []
    for offset in range(-device_reach, device_reach + 1):
        if offset == 0:
            pieces.append(vectors)
        else:
            pieces.append(from_behind(vectors, "row", -offset))
    extended = jnp.concatenate(pieces, axis=1).reshape(
        vec_count, len(pieces) * local_rows, tile_width
    )
    total_rows = local_rows * lax.axis_size("row")
    lowest = (lax.axis_index("row") - device_reach) * local_rows
    positions = (tile_pattern - lowest) % total_rows
    picked = jnp.take(extended, positions, axis=1)
    product = jnp.einsum("vrkc,rkdc->vrd", picked, block_tiles, precision=lax.Precision.HIGHEST)
    return product.reshape(vec_count, local_rows * tile_width)


def lower_solve(factor, right_side):
    return lax.linalg.triangular_solve(factor, right_side, left_side=True, lower=True)


def local(block_tiles, tile_pattern, start_vectors, centers, halfwidths, dup_pairs):
    initial = start_vectors[0]
    center = centers[0]
    halfwidth = halfwidths[0]
    order_total = initial.shape[1] * lax.axis_size("row")
    previous = initial
    current = (apply_local(initial, block_tiles, tile_pattern) - center * initial) / halfwidth
    for degree in range(DEG - 1):
        following = (
            2.0 * (apply_local(current, block_tiles, tile_pattern) - center * current) / halfwidth
            - previous
        )
        previous, current = (current, following)
    imaged = apply_local(current, block_tiles, tile_pattern)
    gram_matrix, cross_sum = lax.psum(
        (
            jnp.dot(current, current.T, precision=lax.Precision.HIGHEST),
            jnp.dot(current, imaged.T, precision=lax.Precision.HIGHEST),
        ),
        "row",
    )
    factor = jnp.linalg.cholesky(gram_matrix)
    basis_raw = math.sqrt(order_total) * lower_solve(factor, current)
    halfway = lower_solve(factor, cross_sum)
    projected = lower_solve(factor, halfway.T).T
    vec_count = basis_raw.shape[0]
    columns = jnp.arange(vec_count, dtype=jnp.int32)
    own_index = dup_pairs[0, :, 0]
    their_index = dup_pairs[0, :, 1]
    target_mask = (own_index[:, None] == columns[None, :]).astype(jnp.float32)
    lower_basis = from_behind_2(basis_raw, "cuts", 1)
    selector = (their_index[:, None] == columns[None, :]).astype(jnp.float32)
    lower_rows = jnp.dot(selector, lower_basis, precision=lax.Precision.HIGHEST)
    correlation = (
        lax.psum(jnp.dot(lower_rows, basis_raw.T, precision=lax.Precision.HIGHEST), "row")
        / order_total
    )
    filtered_basis = basis_raw - jnp.dot(
        (target_mask * correlation).T, lower_rows, precision=lax.Precision.HIGHEST
    )
    return (filtered_basis[None], projected[None])


def solution(mesh):
    in_specs = (
        P("row", None, None, None),
        P("row", None),
        P("cuts", None, "row"),
        P("cuts"),
        P("cuts"),
        P("cuts", None, None),
    )
    out_specs = (P("cuts", None, "row"), P("cuts", None, None))
    return jax.shard_map(local, mesh=mesh, in_specs=in_specs, out_specs=out_specs, check_vma=False)
```

profile of v0, /device:TPU:0, one launch (start us, length us, event | category | flops | bytes accessed | tf_op | source)
XLA Modules:
  0.0 315.9 jit_solution(13397705707559684629)
XLA Ops:
  0.6 3.1 collective-permute-start
  4.4 1.5 collective-permute-start.2
  6.6 3.7 %collective-permute-start.4 = (f32[32,384]{1,0:T(8,128)}, f32[32,384]{1,0:T(8,128)S(1)}, u32[]{:S(2)}, u32[]{:S(2)}) collective-permute-start(f32[32,384]{1,0:T(8,128)} %bitcast.404), channel_id=1, source_target_pairs={{0,15},{1,0},{2,1},{3,2},{4,3},{5,4},{6,5},{7,6},{8,7},{9,8},{10,9... | collective-permute-start | bytes 147464 | tf_op jit(solution)/shard_map/ppermute | solution.py:14
  11.1 0.8 concatenate.50
  13.9 0.8 collective-permute-start.7
  14.8 3.3 %collective-permute-done.5 = f32[32,384]{1,0:T(8,128)S(1)} collective-permute-done((f32[32,384]{1,0:T(8,128)}, f32[32,384]{1,0:T(8,128)S(1)}, u32[]{:S(2)}, u32[]{:S(2)}) %collective-permute-start.5) | collective-permute-done | bytes 49184 | tf_op jit(solution)/shard_map/ppermute | solution.py:14
  19.1 6.7 %fusion.16 = f32[3,32,128,1]{2,1,3,0:T(8,128)S(1)} fusion(f32[3,24,128,128]{3,2,1,0:T(8,128)} %param.10, f32[3,24,32,128]{3,2,1,0:T(8,128)S(1)} %bitcast.393, pred[3,24]{1,0:T(4,128)(4,1)S(1)} %get-tuple-element.12), kind=kOutput, calls=%fused_computation.25 | convolution fusion | flops 453279744 | bytes 5947464 | tf_op jit(solution)/shard_map/vrkc,rkdc->vrd/dot_general | solution.py:41
  25.9 1.1 collective-permute-start.8
  27.0 1.8 collective-permute-start.10
  28.8 4.4 %collective-permute-start.12 = (f32[32,384]{1,0:T(8,128)S(1)}, f32[32,384]{1,0:T(8,128)S(1)}, u32[]{:S(2)}, u32[]{:S(2)}) collective-permute-start(f32[32,384]{1,0:T(8,128)S(1)} %fusion.72), channel_id=1, source_target_pairs={{0,15},{1,0},{2,1},{3,2},{4,3},{5,4},{6,5},{7,6},{8,7},{9,8},{10,9... | collective-permute-start | bytes 147464 | tf_op jit(solution)/shard_map/ppermute | solution.py:14
  33.8 0.9 collective-permute-start.14
  34.9 1.3 collective-permute-start.15
  36.2 1.6 collective-permute-done.13
  37.9 1.1 collective-permute-done.15
  39.7 6.7 %fusion.14 = f32[3,32,128,1]{2,1,3,0:T(8,128)S(1)} fusion(f32[3,24,128,128]{3,2,1,0:T(8,128)} %param.10, f32[3,24,32,128]{3,2,1,0:T(8,128)S(1)} %bitcast.394, pred[3,24]{1,0:T(4,128)(4,1)S(1)} %get-tuple-element.12), kind=kOutput, calls=%fused_computation.23 | convolution fusion | flops 453279744 | bytes 5947464 | tf_op jit(solution)/shard_map/vrkc,rkdc->vrd/dot_general | solution.py:41
  46.5 1.2 collective-permute-start.16
  47.6 1.6 collective-permute-start.18
  49.4 4.3 %collective-permute-start.20 = (f32[32,384]{1,0:T(8,128)S(1)}, f32[32,384]{1,0:T(8,128)S(1)}, u32[]{:S(2)}, u32[]{:S(2)}) collective-permute-start(f32[32,384]{1,0:T(8,128)S(1)} %fusion.71), channel_id=1, source_target_pairs={{0,15},{1,0},{2,1},{3,2},{4,3},{5,4},{6,5},{7,6},{8,7},{9,8},{10,9... | collective-permute-start | bytes 147464 | tf_op jit(solution)/shard_map/ppermute | solution.py:14
  53.7 1.2 collective-permute-start.21
  55.2 1.5 collective-permute-start.23
  56.8 1.0 collective-permute-done.21
  58.5 1.0 collective-permute-done.23
  60.2 6.7 %fusion.12 = f32[3,32,128,1]{2,1,3,0:T(8,128)S(1)} fusion(f32[3,24,128,128]{3,2,1,0:T(8,128)} %param.10, f32[3,24,32,128]{3,2,1,0:T(8,128)S(1)} %bitcast.395, pred[3,24]{1,0:T(4,128)(4,1)S(1)} %get-tuple-element.12), kind=kOutput, calls=%fused_computation.21 | convolution fusion | flops 453279744 | bytes 5947464 | tf_op jit(solution)/shard_map/vrkc,rkdc->vrd/dot_general | solution.py:41
  66.9 0.9 collective-permute-start.24
  67.9 1.9 collective-permute-start.26
  69.8 4.4 %collective-permute-start.28 = (f32[32,384]{1,0:T(8,128)S(1)}, f32[32,384]{1,0:T(8,128)S(1)}, u32[]{:S(2)}, u32[]{:S(2)}) collective-permute-start(f32[32,384]{1,0:T(8,128)S(1)} %fusion.68), channel_id=1, source_target_pairs={{0,15},{1,0},{2,1},{3,2},{4,3},{5,4},{6,5},{7,6},{8,7},{9,8},{10,9... | collective-permute-start | bytes 147464 | tf_op jit(solution)/shard_map/ppermute | solution.py:14
  76.7 2.0 collective-permute-done.29
  78.8 1.3 collective-permute-done.31
  80.9 6.7 %fusion.10 = f32[3,32,128,1]{2,1,3,0:T(8,128)S(1)} fusion(f32[3,24,128,128]{3,2,1,0:T(8,128)} %param.10, f32[3,24,32,128]{3,2,1,0:T(8,128)S(1)} %bitcast.396, pred[3,24]{1,0:T(4,128)(4,1)S(1)} %get-tuple-element.12), kind=kOutput, calls=%fused_computation.19 | convolution fusion | flops 453279744 | bytes 5947464 | tf_op jit(solution)/shard_map/vrkc,rkdc->vrd/dot_general | solution.py:41
  88.3 1.7 collective-permute-start.34
  90.0 4.4 %collective-permute-start.36 = (f32[32,384]{1,0:T(8,128)S(1)}, f32[32,384]{1,0:T(8,128)S(1)}, u32[]{:S(2)}, u32[]{:S(2)}) collective-permute-start(f32[32,384]{1,0:T(8,128)S(1)} %fusion.65), channel_id=1, source_target_pairs={{0,15},{1,0},{2,1},{3,2},{4,3},{5,4},{6,5},{7,6},{8,7},{9,8},{10,9... | collective-permute-start | bytes 147464 | tf_op jit(solution)/shard_map/ppermute | solution.py:14
  94.5 1.1 collective-permute-start.37
  95.9 1.4 collective-permute-start.39
  97.4 1.2 collective-permute-done.37
  99.1 0.9 collective-permute-done.39
  100.8 6.7 %fusion.8 = f32[3,32,128,1]{2,1,3,0:T(8,128)S(1)} fusion(f32[3,24,128,128]{3,2,1,0:T(8,128)} %param.10, f32[3,24,32,128]{3,2,1,0:T(8,128)S(1)} %bitcast.397, pred[3,24]{1,0:T(4,128)(4,1)S(1)} %get-tuple-element.12), kind=kOutput, calls=%fused_computation.17 | convolution fusion | flops 453279744 | bytes 5947464 | tf_op jit(solution)/shard_map/vrkc,rkdc->vrd/dot_general | solution.py:41
  107.5 0.9 collective-permute-start.40
  108.4 2.0 collective-permute-start.42
  110.5 4.4 %collective-permute-start.44 = (f32[32,384]{1,0:T(8,128)S(1)}, f32[32,384]{1,0:T(8,128)S(1)}, u32[]{:S(2)}, u32[]{:S(2)}) collective-permute-start(f32[32,384]{1,0:T(8,128)S(1)} %fusion.62), channel_id=1, source_target_pairs={{0,15},{1,0},{2,1},{3,2},{4,3},{5,4},{6,5},{7,6},{8,7},{9,8},{10,9... | collective-permute-start | bytes 147464 | tf_op jit(solution)/shard_map/ppermute | solution.py:14
  116.1 1.1 collective-permute-start.47
  117.4 2.1 collective-permute-done.45
  119.5 1.2 collective-permute-done.47
  121.3 6.7 %fusion.6 = f32[3,32,128,1]{2,1,3,0:T(8,128)S(1)} fusion(f32[3,24,128,128]{3,2,1,0:T(8,128)} %param.10, f32[3,24,32,128]{3,2,1,0:T(8,128)S(1)} %bitcast.398, pred[3,24]{1,0:T(4,128)(4,1)S(1)} %get-tuple-element.12), kind=kOutput, calls=%fused_computation.15 | convolution fusion | flops 453279744 | bytes 5947464 | tf_op jit(solution)/shard_map/vrkc,rkdc->vrd/dot_general | solution.py:41
  128.8 1.8 collective-permute-start.50
  130.6 4.4 %collective-permute-start.52 = (f32[32,384]{1,0:T(8,128)S(1)}, f32[32,384]{1,0:T(8,128)S(1)}, u32[]{:S(2)}, u32[]{:S(2)}) collective-permute-start(f32[32,384]{1,0:T(8,128)S(1)} %fusion.59), channel_id=1, source_target_pairs={{0,15},{1,0},{2,1},{3,2},{4,3},{5,4},{6,5},{7,6},{8,7},{9,8},{10,9... | collective-permute-start | bytes 147464 | tf_op jit(solution)/shard_map/ppermute | solution.py:14
  136.8 0.9 collective-permute-start.55
  137.8 1.7 collective-permute-done.53
  139.7 1.5 collective-permute-done.55
  141.9 6.7 %fusion.4 = f32[3,32,128,1]{2,1,3,0:T(8,128)S(1)} fusion(f32[3,24,128,128]{3,2,1,0:T(8,128)} %param.10, f32[3,24,32,128]{3,2,1,0:T(8,128)S(1)} %bitcast.399, pred[3,24]{1,0:T(4,128)(4,1)S(1)} %get-tuple-element.12), kind=kOutput, calls=%fused_computation.13 | convolution fusion | flops 453279744 | bytes 5947464 | tf_op jit(solution)/shard_map/vrkc,rkdc->vrd/dot_general | solution.py:41
  149.4 1.5 collective-permute-start.58
  151.0 4.4 %collective-permute-start.60 = (f32[32,384]{1,0:T(8,128)S(1)}, f32[32,384]{1,0:T(8,128)S(1)}, u32[]{:S(2)}, u32[]{:S(2)}) collective-permute-start(f32[32,384]{1,0:T(8,128)S(1)} %fusion.56), channel_id=1, source_target_pairs={{0,15},{1,0},{2,1},{3,2},{4,3},{5,4},{6,5},{7,6},{8,7},{9,8},{10,9... | collective-permute-start | bytes 147464 | tf_op jit(solution)/shard_map/ppermute | solution.py:14
  156.8 1.4 collective-permute-start.63
  158.3 1.4 collective-permute-done.61
  160.0 1.4 collective-permute-done.63
  162.1 7.2 %fusion.75 = (f32[32,3,128]{2,0,1:T(8,128)S(1)}, f32[3,32,128,1]{2,1,3,0:T(8,128)S(1)}) fusion(f32[3,32,128,1]{2,1,3,0:T(8,128)S(1)} %fusion.4, f32[3,32,128,1]{2,1,3,0:T(8,128)S(1)} %fusion.6, f32[3,32,128,1]{2,1,3,0:T(8,128)S(1)} %fusion.8, f32[3,32,128,1]{2,1,3,0:T(8,128)S(1)} %fusion.10, f32[3,32,128,1]{2,1,3,0:T(8,128)S(1)} %fusion.12, ...), kind=kOutput, calls=%fused_computation.186 | convolution fusion | flops 453746688 | bytes 6389840 | tf_op jit(solution)/shard_map/vrkc,rkdc->vrd/dot_general | solution.py:41
  170.1 1.8 collective-permute-start.67
  172.1 4.3 %collective-permute-start.69 = (f32[32,384]{1,0:T(8,128)S(1)}, f32[32,384]{1,0:T(8,128)S(1)}, u32[]{:S(2)}, u32[]{:S(2)}) collective-permute-start(f32[32,384]{1,0:T(8,128)S(1)} %fusion.51), channel_id=1, source_target_pairs={{0,15},{1,0},{2,1},{3,2},{4,3},{5,4},{6,5},{7,6},{8,7},{9,8},{10,9... | collective-permute-start | bytes 147464 | tf_op jit(solution)/shard_map/ppermute | solution.py:14
  176.5 57.6 %psum.21 = f32[32,32]{0,1:T(8,128)S(1)} all-reduce(f32[32,32]{0,1:T(8,128)S(1)} %convolution_bitcast_fusion.3), channel_id=1, replica_groups=mesh['cuts'=2,'row'=16] {'row'}, use_global_device_ids=true, to_apply=%region_0.2 | all-reduce | flops 1024 | bytes 8192 | tf_op jit(solution)/shard_map/psum | solution.py:63
  234.2 2.9 cholesky.16
  238.5 2.4 custom-call.9
  241.5 3.4 %collective-permute-start.64 = (f32[32,384]{1,0:T(8,128)S(1)}, f32[32,384]{1,0:T(8,128)S(1)}, u32[]{:S(2)}, u32[]{:S(2)}) collective-permute-start(f32[32,384]{1,0:T(8,128)S(1)} %convolution_multiply_fusion), channel_id=1, source_target_pairs={{0,16},{1,17},{2,18},{3,19},{4,20},{5,21},{6,22},{7,23},{8,24},{9,... | collective-permute-start | bytes 147464 | tf_op jit(solution)/shard_map/ppermute | solution.py:20
  246.3 6.7 %fusion.27 = f32[32,3,128]{2,0,1:T(8,128)S(1)} fusion(f32[3,24,128,128]{3,2,1,0:T(8,128)} %param.10, f32[3,24,32,128]{3,2,1,0:T(8,128)S(1)} %bitcast.392, pred[3,24]{1,0:T(4,128)(4,1)S(1)} %get-tuple-element.12), kind=kOutput, calls=%fused_computation.36 | convolution fusion | flops 453279744 | bytes 5947464 | tf_op jit(solution)/shard_map/vrkc,rkdc->vrd/dot_general | solution.py:41
  253.5 60.3 %all-reduce = (f32[8,32]{1,0:T(8,128)S(1)}, f32[32,32]{1,0:T(8,128)S(1)}) all-reduce(f32[8,32]{1,0:T(8,128)S(1)} %fusion.119, f32[32,32]{1,0:T(8,128)S(1)} %convolution_bitcast_fusion.2), channel_id=1, replica_groups=mesh['cuts'=2,'row'=16] {'row'}, use_global_device_ids=true, to_apply=%region_3.5 | all-reduce | flops 1280 | bytes 10240 | tf_op jit(solution)/shard_map/psum | solution.py:83
  314.9 0.9 fusion.30
  (224 shorter events, 27.5 us)
Async XLA Ops:
  0.6 12.6 %collective-permute-start = (f32[32,384]{1,0:T(8,128)}, f32[32,384]{1,0:T(8,128)S(1)}, u32[]{:S(2)}, u32[]{:S(2)}) collective-permute-start(f32[32,384]{1,0:T(8,128)} %bitcast.400), channel_id=1, source_target_pairs={{0,4},{1,5},{2,6},{3,7},{4,8},{5,9},{6,10},{7,11},{8,12},{9,13},{1... | collective-permute-start | bytes 147464 | tf_op jit(solution)/shard_map/ppermute | solution.py:14
  3.7 10.1 %collective-permute-start.1 = (f32[32,384]{1,0:T(8,128)}, f32[32,384]{1,0:T(8,128)S(1)}, u32[]{:S(2)}, u32[]{:S(2)}) collective-permute-start(f32[32,384]{1,0:T(8,128)} %bitcast.401), channel_id=1, source_target_pairs={{0,3},{1,4},{2,5},{3,6},{4,7},{5,8},{6,9},{7,10},{8,11},{9,12},{10... | collective-permute-start | bytes 147464 | tf_op jit(solution)/shard_map/ppermute | solution.py:14
  4.4 9.5 %collective-permute-start.2 = (f32[32,384]{1,0:T(8,128)}, f32[32,384]{1,0:T(8,128)S(1)}, u32[]{:S(2)}, u32[]{:S(2)}) collective-permute-start(f32[32,384]{1,0:T(8,128)} %bitcast.402), channel_id=1, source_target_pairs={{0,2},{1,3},{2,4},{3,5},{4,6},{5,7},{6,8},{7,9},{8,10},{9,11},{10,... | collective-permute-start | bytes 147464 | tf_op jit(solution)/shard_map/ppermute | solution.py:14
  5.9 8.8 %collective-permute-start.3 = (f32[32,384]{1,0:T(8,128)}, f32[32,384]{1,0:T(8,128)S(1)}, u32[]{:S(2)}, u32[]{:S(2)}) collective-permute-start(f32[32,384]{1,0:T(8,128)} %bitcast.403), channel_id=1, source_target_pairs={{0,1},{1,2},{2,3},{3,4},{4,5},{5,6},{6,7},{7,8},{8,9},{9,10},{10,1... | collective-permute-start | bytes 147464 | tf_op jit(solution)/shard_map/ppermute | solution.py:14
  6.6 8.1 %collective-permute-start.4 = (f32[32,384]{1,0:T(8,128)}, f32[32,384]{1,0:T(8,128)S(1)}, u32[]{:S(2)}, u32[]{:S(2)}) collective-permute-start(f32[32,384]{1,0:T(8,128)} %bitcast.404), channel_id=1, source_target_pairs={{0,15},{1,0},{2,1},{3,2},{4,3},{5,4},{6,5},{7,6},{8,7},{9,8},{10,9... | collective-permute-start | bytes 147464 | tf_op jit(solution)/shard_map/ppermute | solution.py:14
  13.3 4.8 %collective-permute-start.5 = (f32[32,384]{1,0:T(8,128)}, f32[32,384]{1,0:T(8,128)S(1)}, u32[]{:S(2)}, u32[]{:S(2)}) collective-permute-start(f32[32,384]{1,0:T(8,128)} %bitcast.405), channel_id=1, source_target_pairs={{0,14},{1,15},{2,0},{3,1},{4,2},{5,3},{6,4},{7,5},{8,6},{9,7},{10,... | collective-permute-start | bytes 147464 | tf_op jit(solution)/shard_map/ppermute | solution.py:14
  13.8 4.3 %collective-permute-start.6 = (f32[32,384]{1,0:T(8,128)}, f32[32,384]{1,0:T(8,128)S(1)}, u32[]{:S(2)}, u32[]{:S(2)}) collective-permute-start(f32[32,384]{1,0:T(8,128)} %bitcast.406), channel_id=1, source_target_pairs={{0,13},{1,14},{2,15},{3,0},{4,1},{5,2},{6,3},{7,4},{8,5},{9,6},{10... | collective-permute-start | bytes 147464 | tf_op jit(solution)/shard_map/ppermute | solution.py:14
  13.9 4.6 %collective-permute-start.7 = (f32[32,384]{1,0:T(8,128)}, f32[32,384]{1,0:T(8,128)S(1)}, u32[]{:S(2)}, u32[]{:S(2)}) collective-permute-start(f32[32,384]{1,0:T(8,128)} %bitcast.407), channel_id=1, source_target_pairs={{0,12},{1,13},{2,14},{3,15},{4,0},{5,1},{6,2},{7,3},{8,4},{9,5},{1... | collective-permute-start | bytes 147464 | tf_op jit(solution)/shard_map/ppermute | solution.py:14
  25.9 7.4 %collective-permute-start.8 = (f32[32,384]{1,0:T(8,128)S(1)}, f32[32,384]{1,0:T(8,128)S(1)}, u32[]{:S(2)}, u32[]{:S(2)}) collective-permute-start(f32[32,384]{1,0:T(8,128)S(1)} %fusion.72), channel_id=1, source_target_pairs={{0,4},{1,5},{2,6},{3,7},{4,8},{5,9},{6,10},{7,11},{8,12},{9,13},{1... | collective-permute-start | bytes 147464 | tf_op jit(solution)/shard_map/ppermute | solution.py:14
  27.0 6.8 %collective-permute-start.9 = (f32[32,384]{1,0:T(8,128)S(1)}, f32[32,384]{1,0:T(8,128)S(1)}, u32[]{:S(2)}, u32[]{:S(2)}) collective-permute-start(f32[32,384]{1,0:T(8,128)S(1)} %fusion.72), channel_id=1, source_target_pairs={{0,3},{1,4},{2,5},{3,6},{4,7},{5,8},{6,9},{7,10},{8,11},{9,12},{10... | collective-permute-start | bytes 147464 | tf_op jit(solution)/shard_map/ppermute | solution.py:14
  27.0 7.9 %collective-permute-start.10 = (f32[32,384]{1,0:T(8,128)S(1)}, f32[32,384]{1,0:T(8,128)S(1)}, u32[]{:S(2)}, u32[]{:S(2)}) collective-permute-start(f32[32,384]{1,0:T(8,128)S(1)} %fusion.72), channel_id=1, source_target_pairs={{0,2},{1,3},{2,4},{3,5},{4,6},{5,7},{6,8},{7,9},{8,10},{9,11},{10,... | collective-permute-start | bytes 147464 | tf_op jit(solution)/shard_map/ppermute | solution.py:14
  28.8 7.4 %collective-permute-start.11 = (f32[32,384]{1,0:T(8,128)S(1)}, f32[32,384]{1,0:T(8,128)S(1)}, u32[]{:S(2)}, u32[]{:S(2)}) collective-permute-start(f32[32,384]{1,0:T(8,128)S(1)} %fusion.72), channel_id=1, source_target_pairs={{0,1},{1,2},{2,3},{3,4},{4,5},{5,6},{6,7},{7,8},{8,9},{9,10},{10,1... | collective-permute-start | bytes 147464 | tf_op jit(solution)/shard_map/ppermute | solution.py:14
  28.8 7.4 %collective-permute-start.12 = (f32[32,384]{1,0:T(8,128)S(1)}, f32[32,384]{1,0:T(8,128)S(1)}, u32[]{:S(2)}, u32[]{:S(2)}) collective-permute-start(f32[32,384]{1,0:T(8,128)S(1)} %fusion.72), channel_id=1, source_target_pairs={{0,15},{1,0},{2,1},{3,2},{4,3},{5,4},{6,5},{7,6},{8,7},{9,8},{10,9... | collective-permute-start | bytes 147464 | tf_op jit(solution)/shard_map/ppermute | solution.py:14
  33.3 4.6 %collective-permute-start.13 = (f32[32,384]{1,0:T(8,128)S(1)}, f32[32,384]{1,0:T(8,128)S(1)}, u32[]{:S(2)}, u32[]{:S(2)}) collective-permute-start(f32[32,384]{1,0:T(8,128)S(1)} %fusion.72), channel_id=1, source_target_pairs={{0,14},{1,15},{2,0},{3,1},{4,2},{5,3},{6,4},{7,5},{8,6},{9,7},{10,... | collective-permute-start | bytes 147464 | tf_op jit(solution)/shard_map/ppermute | solution.py:14
  34.9 4.1 %collective-permute-start.15 = (f32[32,384]{1,0:T(8,128)S(1)}, f32[32,384]{1,0:T(8,128)S(1)}, u32[]{:S(2)}, u32[]{:S(2)}) collective-permute-start(f32[32,384]{1,0:T(8,128)S(1)} %fusion.72), channel_id=1, source_target_pairs={{0,12},{1,13},{2,14},{3,15},{4,0},{5,1},{6,2},{7,3},{8,4},{9,5},{1... | collective-permute-start | bytes 147464 | tf_op jit(solution)/shard_map/ppermute | solution.py:14
  46.5 7.2 %collective-permute-start.16 = (f32[32,384]{1,0:T(8,128)S(1)}, f32[32,384]{1,0:T(8,128)S(1)}, u32[]{:S(2)}, u32[]{:S(2)}) collective-permute-start(f32[32,384]{1,0:T(8,128)S(1)} %fusion.71), channel_id=1, source_target_pairs={{0,4},{1,5},{2,6},{3,7},{4,8},{5,9},{6,10},{7,11},{8,12},{9,13},{1... | collective-permute-start | bytes 147464 | tf_op jit(solution)/shard_map/ppermute | solution.py:14
  47.6 7.3 %collective-permute-start.17 = (f32[32,384]{1,0:T(8,128)S(1)}, f32[32,384]{1,0:T(8,128)S(1)}, u32[]{:S(2)}, u32[]{:S(2)}) collective-permute-start(f32[32,384]{1,0:T(8,128)S(1)} %fusion.71), channel_id=1, source_target_pairs={{0,3},{1,4},{2,5},{3,6},{4,7},{5,8},{6,9},{7,10},{8,11},{9,12},{10... | collective-permute-start | bytes 147464 | tf_op jit(solution)/shard_map/ppermute | solution.py:14
  47.6 7.6 %collective-permute-start.18 = (f32[32,384]{1,0:T(8,128)S(1)}, f32[32,384]{1,0:T(8,128)S(1)}, u32[]{:S(2)}, u32[]{:S(2)}) collective-permute-start(f32[32,384]{1,0:T(8,128)S(1)} %fusion.71), channel_id=1, source_target_pairs={{0,2},{1,3},{2,4},{3,5},{4,6},{5,7},{6,8},{7,9},{8,10},{9,11},{10,... | collective-permute-start | bytes 147464 | tf_op jit(solution)/shard_map/ppermute | solution.py:14
  49.2 7.5 %collective-permute-start.19 = (f32[32,384]{1,0:T(8,128)S(1)}, f32[32,384]{1,0:T(8,128)S(1)}, u32[]{:S(2)}, u32[]{:S(2)}) collective-permute-start(f32[32,384]{1,0:T(8,128)S(1)} %fusion.71), channel_id=1, source_target_pairs={{0,1},{1,2},{2,3},{3,4},{4,5},{5,6},{6,7},{7,8},{8,9},{9,10},{10,1... | collective-permute-start | bytes 147464 | tf_op jit(solution)/shard_map/ppermute | solution.py:14
  49.4 7.4 %collective-permute-start.20 = (f32[32,384]{1,0:T(8,128)S(1)}, f32[32,384]{1,0:T(8,128)S(1)}, u32[]{:S(2)}, u32[]{:S(2)}) collective-permute-start(f32[32,384]{1,0:T(8,128)S(1)} %fusion.71), channel_id=1, source_target_pairs={{0,15},{1,0},{2,1},{3,2},{4,3},{5,4},{6,5},{7,6},{8,7},{9,8},{10,9... | collective-permute-start | bytes 147464 | tf_op jit(solution)/shard_map/ppermute | solution.py:14
  55.2 4.3 %collective-permute-start.23 = (f32[32,384]{1,0:T(8,128)S(1)}, f32[32,384]{1,0:T(8,128)S(1)}, u32[]{:S(2)}, u32[]{:S(2)}) collective-permute-start(f32[32,384]{1,0:T(8,128)S(1)} %fusion.71), channel_id=1, source_target_pairs={{0,12},{1,13},{2,14},{3,15},{4,0},{5,1},{6,2},{7,3},{8,4},{9,5},{1... | collective-permute-start | bytes 147464 | tf_op jit(solution)/shard_map/ppermute | solution.py:14
  66.9 7.3 %collective-permute-start.24 = (f32[32,384]{1,0:T(8,128)S(1)}, f32[32,384]{1,0:T(8,128)S(1)}, u32[]{:S(2)}, u32[]{:S(2)}) collective-permute-start(f32[32,384]{1,0:T(8,128)S(1)} %fusion.68), channel_id=1, source_target_pairs={{0,4},{1,5},{2,6},{3,7},{4,8},{5,9},{6,10},{7,11},{8,12},{9,13},{1... | collective-permute-start | bytes 147464 | tf_op jit(solution)/shard_map/ppermute | solution.py:14
  67.9 6.9 %collective-permute-start.25 = (f32[32,384]{1,0:T(8,128)S(1)}, f32[32,384]{1,0:T(8,128)S(1)}, u32[]{:S(2)}, u32[]{:S(2)}) collective-permute-start(f32[32,384]{1,0:T(8,128)S(1)} %fusion.68), channel_id=1, source_target_pairs={{0,3},{1,4},{2,5},{3,6},{4,7},{5,8},{6,9},{7,10},{8,11},{9,12},{10... | collective-permute-start | bytes 147464 | tf_op jit(solution)/shard_map/ppermute | solution.py:14
  67.9 8.0 %collective-permute-start.26 = (f32[32,384]{1,0:T(8,128)S(1)}, f32[32,384]{1,0:T(8,128)S(1)}, u32[]{:S(2)}, u32[]{:S(2)}) collective-permute-start(f32[32,384]{1,0:T(8,128)S(1)} %fusion.68), channel_id=1, source_target_pairs={{0,2},{1,3},{2,4},{3,5},{4,6},{5,7},{6,8},{7,9},{8,10},{9,11},{10,... | collective-permute-start | bytes 147464 | tf_op jit(solution)/shard_map/ppermute | solution.py:14
  69.8 6.9 %collective-permute-start.27 = (f32[32,384]{1,0:T(8,128)S(1)}, f32[32,384]{1,0:T(8,128)S(1)}, u32[]{:S(2)}, u32[]{:S(2)}) collective-permute-start(f32[32,384]{1,0:T(8,128)S(1)} %fusion.68), channel_id=1, source_target_pairs={{0,1},{1,2},{2,3},{3,4},{4,5},{5,6},{6,7},{7,8},{8,9},{9,10},{10,1... | collective-permute-start | bytes 147464 | tf_op jit(solution)/shard_map/ppermute | solution.py:14
  69.8 7.0 %collective-permute-start.28 = (f32[32,384]{1,0:T(8,128)S(1)}, f32[32,384]{1,0:T(8,128)S(1)}, u32[]{:S(2)}, u32[]{:S(2)}) collective-permute-start(f32[32,384]{1,0:T(8,128)S(1)} %fusion.68), channel_id=1, source_target_pairs={{0,15},{1,0},{2,1},{3,2},{4,3},{5,4},{6,5},{7,6},{8,7},{9,8},{10,9... | collective-permute-start | bytes 147464 | tf_op jit(solution)/shard_map/ppermute | solution.py:14
  74.2 4.5 %collective-permute-start.29 = (f32[32,384]{1,0:T(8,128)S(1)}, f32[32,384]{1,0:T(8,128)S(1)}, u32[]{:S(2)}, u32[]{:S(2)}) collective-permute-start(f32[32,384]{1,0:T(8,128)S(1)} %fusion.68), channel_id=1, source_target_pairs={{0,14},{1,15},{2,0},{3,1},{4,2},{5,3},{6,4},{7,5},{8,6},{9,7},{10,... | collective-permute-start | bytes 147464 | tf_op jit(solution)/shard_map/ppermute | solution.py:14
  75.9 4.3 %collective-permute-start.31 = (f32[32,384]{1,0:T(8,128)S(1)}, f32[32,384]{1,0:T(8,128)S(1)}, u32[]{:S(2)}, u32[]{:S(2)}) collective-permute-start(f32[32,384]{1,0:T(8,128)S(1)} %fusion.68), channel_id=1, source_target_pairs={{0,12},{1,13},{2,14},{3,15},{4,0},{5,1},{6,2},{7,3},{8,4},{9,5},{1... | collective-permute-start | bytes 147464 | tf_op jit(solution)/shard_map/ppermute | solution.py:14
  87.6 6.9 %collective-permute-start.32 = (f32[32,384]{1,0:T(8,128)S(1)}, f32[32,384]{1,0:T(8,128)S(1)}, u32[]{:S(2)}, u32[]{:S(2)}) collective-permute-start(f32[32,384]{1,0:T(8,128)S(1)} %fusion.65), channel_id=1, source_target_pairs={{0,4},{1,5},{2,6},{3,7},{4,8},{5,9},{6,10},{7,11},{8,12},{9,13},{1... | collective-permute-start | bytes 147464 | tf_op jit(solution)/shard_map/ppermute | solution.py:14
  88.3 7.3 %collective-permute-start.33 = (f32[32,384]{1,0:T(8,128)S(1)}, f32[32,384]{1,0:T(8,128)S(1)}, u32[]{:S(2)}, u32[]{:S(2)}) collective-permute-start(f32[32,384]{1,0:T(8,128)S(1)} %fusion.65), channel_id=1, source_target_pairs={{0,3},{1,4},{2,5},{3,6},{4,7},{5,8},{6,9},{7,10},{8,11},{9,12},{10... | collective-permute-start | bytes 147464 | tf_op jit(solution)/shard_map/ppermute | solution.py:14
  88.3 7.6 %collective-permute-start.34 = (f32[32,384]{1,0:T(8,128)S(1)}, f32[32,384]{1,0:T(8,128)S(1)}, u32[]{:S(2)}, u32[]{:S(2)}) collective-permute-start(f32[32,384]{1,0:T(8,128)S(1)} %fusion.65), channel_id=1, source_target_pairs={{0,2},{1,3},{2,4},{3,5},{4,6},{5,7},{6,8},{7,9},{8,10},{9,11},{10,... | collective-permute-start | bytes 147464 | tf_op jit(solution)/shard_map/ppermute | solution.py:14
  90.0 7.3 %collective-permute-start.35 = (f32[32,384]{1,0:T(8,128)S(1)}, f32[32,384]{1,0:T(8,128)S(1)}, u32[]{:S(2)}, u32[]{:S(2)}) collective-permute-start(f32[32,384]{1,0:T(8,128)S(1)} %fusion.65), channel_id=1, source_target_pairs={{0,1},{1,2},{2,3},{3,4},{4,5},{5,6},{6,7},{7,8},{8,9},{9,10},{10,1... | collective-permute-start | bytes 147464 | tf_op jit(solution)/shard_map/ppermute | solution.py:14
  90.0 7.3 %collective-permute-start.36 = (f32[32,384]{1,0:T(8,128)S(1)}, f32[32,384]{1,0:T(8,128)S(1)}, u32[]{:S(2)}, u32[]{:S(2)}) collective-permute-start(f32[32,384]{1,0:T(8,128)S(1)} %fusion.65), channel_id=1, source_target_pairs={{0,15},{1,0},{2,1},{3,2},{4,3},{5,4},{6,5},{7,6},{8,7},{9,8},{10,9... | collective-permute-start | bytes 147464 | tf_op jit(solution)/shard_map/ppermute | solution.py:14
  95.9 4.2 %collective-permute-start.39 = (f32[32,384]{1,0:T(8,128)S(1)}, f32[32,384]{1,0:T(8,128)S(1)}, u32[]{:S(2)}, u32[]{:S(2)}) collective-permute-start(f32[32,384]{1,0:T(8,128)S(1)} %fusion.65), channel_id=1, source_target_pairs={{0,12},{1,13},{2,14},{3,15},{4,0},{5,1},{6,2},{7,3},{8,4},{9,5},{1... | collective-permute-start | bytes 147464 | tf_op jit(solution)/shard_map/ppermute | solution.py:14
  107.5 7.4 %collective-permute-start.40 = (f32[32,384]{1,0:T(8,128)S(1)}, f32[32,384]{1,0:T(8,128)S(1)}, u32[]{:S(2)}, u32[]{:S(2)}) collective-permute-start(f32[32,384]{1,0:T(8,128)S(1)} %fusion.62), channel_id=1, source_target_pairs={{0,4},{1,5},{2,6},{3,7},{4,8},{5,9},{6,10},{7,11},{8,12},{9,13},{1... | collective-permute-start | bytes 147464 | tf_op jit(solution)/shard_map/ppermute | solution.py:14
  108.4 6.9 %collective-permute-start.41 = (f32[32,384]{1,0:T(8,128)S(1)}, f32[32,384]{1,0:T(8,128)S(1)}, u32[]{:S(2)}, u32[]{:S(2)}) collective-permute-start(f32[32,384]{1,0:T(8,128)S(1)} %fusion.62), channel_id=1, source_target_pairs={{0,3},{1,4},{2,5},{3,6},{4,7},{5,8},{6,9},{7,10},{8,11},{9,12},{10... | collective-permute-start | bytes 147464 | tf_op jit(solution)/shard_map/ppermute | solution.py:14
  108.4 7.7 %collective-permute-start.42 = (f32[32,384]{1,0:T(8,128)S(1)}, f32[32,384]{1,0:T(8,128)S(1)}, u32[]{:S(2)}, u32[]{:S(2)}) collective-permute-start(f32[32,384]{1,0:T(8,128)S(1)} %fusion.62), channel_id=1, source_target_pairs={{0,2},{1,3},{2,4},{3,5},{4,6},{5,7},{6,8},{7,9},{8,10},{9,11},{10,... | collective-permute-start | bytes 147464 | tf_op jit(solution)/shard_map/ppermute | solution.py:14
  110.4 6.9 %collective-permute-start.43 = (f32[32,384]{1,0:T(8,128)S(1)}, f32[32,384]{1,0:T(8,128)S(1)}, u32[]{:S(2)}, u32[]{:S(2)}) collective-permute-start(f32[32,384]{1,0:T(8,128)S(1)} %fusion.62), channel_id=1, source_target_pairs={{0,1},{1,2},{2,3},{3,4},{4,5},{5,6},{6,7},{7,8},{8,9},{9,10},{10,1... | collective-permute-start | bytes 147464 | tf_op jit(solution)/shard_map/ppermute | solution.py:14
  110.5 6.9 %collective-permute-start.44 = (f32[32,384]{1,0:T(8,128)S(1)}, f32[32,384]{1,0:T(8,128)S(1)}, u32[]{:S(2)}, u32[]{:S(2)}) collective-permute-start(f32[32,384]{1,0:T(8,128)S(1)} %fusion.62), channel_id=1, source_target_pairs={{0,15},{1,0},{2,1},{3,2},{4,3},{5,4},{6,5},{7,6},{8,7},{9,8},{10,9... | collective-permute-start | bytes 147464 | tf_op jit(solution)/shard_map/ppermute | solution.py:14
  114.9 4.6 %collective-permute-start.45 = (f32[32,384]{1,0:T(8,128)S(1)}, f32[32,384]{1,0:T(8,128)S(1)}, u32[]{:S(2)}, u32[]{:S(2)}) collective-permute-start(f32[32,384]{1,0:T(8,128)S(1)} %fusion.62), channel_id=1, source_target_pairs={{0,14},{1,15},{2,0},{3,1},{4,2},{5,3},{6,4},{7,5},{8,6},{9,7},{10,... | collective-permute-start | bytes 147464 | tf_op jit(solution)/shard_map/ppermute | solution.py:14
  116.1 4.5 %collective-permute-start.47 = (f32[32,384]{1,0:T(8,128)S(1)}, f32[32,384]{1,0:T(8,128)S(1)}, u32[]{:S(2)}, u32[]{:S(2)}) collective-permute-start(f32[32,384]{1,0:T(8,128)S(1)} %fusion.62), channel_id=1, source_target_pairs={{0,12},{1,13},{2,14},{3,15},{4,0},{5,1},{6,2},{7,3},{8,4},{9,5},{1... | collective-permute-start | bytes 147464 | tf_op jit(solution)/shard_map/ppermute | solution.py:14
  128.1 7.0 %collective-permute-start.48 = (f32[32,384]{1,0:T(8,128)S(1)}, f32[32,384]{1,0:T(8,128)S(1)}, u32[]{:S(2)}, u32[]{:S(2)}) collective-permute-start(f32[32,384]{1,0:T(8,128)S(1)} %fusion.59), channel_id=1, source_target_pairs={{0,4},{1,5},{2,6},{3,7},{4,8},{5,9},{6,10},{7,11},{8,12},{9,13},{1... | collective-permute-start | bytes 147464 | tf_op jit(solution)/shard_map/ppermute | solution.py:14
  128.7 7.0 %collective-permute-start.49 = (f32[32,384]{1,0:T(8,128)S(1)}, f32[32,384]{1,0:T(8,128)S(1)}, u32[]{:S(2)}, u32[]{:S(2)}) collective-permute-start(f32[32,384]{1,0:T(8,128)S(1)} %fusion.59), channel_id=1, source_target_pairs={{0,3},{1,4},{2,5},{3,6},{4,7},{5,8},{6,9},{7,10},{8,11},{9,12},{10... | collective-permute-start | bytes 147464 | tf_op jit(solution)/shard_map/ppermute | solution.py:14
  128.8 8.0 %collective-permute-start.50 = (f32[32,384]{1,0:T(8,128)S(1)}, f32[32,384]{1,0:T(8,128)S(1)}, u32[]{:S(2)}, u32[]{:S(2)}) collective-permute-start(f32[32,384]{1,0:T(8,128)S(1)} %fusion.59), channel_id=1, source_target_pairs={{0,2},{1,3},{2,4},{3,5},{4,6},{5,7},{6,8},{7,9},{8,10},{9,11},{10,... | collective-permute-start | bytes 147464 | tf_op jit(solution)/shard_map/ppermute | solution.py:14
  130.6 7.1 %collective-permute-start.51 = (f32[32,384]{1,0:T(8,128)S(1)}, f32[32,384]{1,0:T(8,128)S(1)}, u32[]{:S(2)}, u32[]{:S(2)}) collective-permute-start(f32[32,384]{1,0:T(8,128)S(1)} %fusion.59), channel_id=1, source_target_pairs={{0,1},{1,2},{2,3},{3,4},{4,5},{5,6},{6,7},{7,8},{8,9},{9,10},{10,1... | collective-permute-start | bytes 147464 | tf_op jit(solution)/shard_map/ppermute | solution.py:14
  130.6 7.2 %collective-permute-start.52 = (f32[32,384]{1,0:T(8,128)S(1)}, f32[32,384]{1,0:T(8,128)S(1)}, u32[]{:S(2)}, u32[]{:S(2)}) collective-permute-start(f32[32,384]{1,0:T(8,128)S(1)} %fusion.59), channel_id=1, source_target_pairs={{0,15},{1,0},{2,1},{3,2},{4,3},{5,4},{6,5},{7,6},{8,7},{9,8},{10,9... | collective-permute-start | bytes 147464 | tf_op jit(solution)/shard_map/ppermute | solution.py:14
  135.1 4.5 %collective-permute-start.53 = (f32[32,384]{1,0:T(8,128)S(1)}, f32[32,384]{1,0:T(8,128)S(1)}, u32[]{:S(2)}, u32[]{:S(2)}) collective-permute-start(f32[32,384]{1,0:T(8,128)S(1)} %fusion.59), channel_id=1, source_target_pairs={{0,14},{1,15},{2,0},{3,1},{4,2},{5,3},{6,4},{7,5},{8,6},{9,7},{10,... | collective-permute-start | bytes 147464 | tf_op jit(solution)/shard_map/ppermute | solution.py:14
  136.8 4.4 %collective-permute-start.55 = (f32[32,384]{1,0:T(8,128)S(1)}, f32[32,384]{1,0:T(8,128)S(1)}, u32[]{:S(2)}, u32[]{:S(2)}) collective-permute-start(f32[32,384]{1,0:T(8,128)S(1)} %fusion.59), channel_id=1, source_target_pairs={{0,12},{1,13},{2,14},{3,15},{4,0},{5,1},{6,2},{7,3},{8,4},{9,5},{1... | collective-permute-start | bytes 147464 | tf_op jit(solution)/shard_map/ppermute | solution.py:14
  148.7 6.7 %collective-permute-start.56 = (f32[32,384]{1,0:T(8,128)S(1)}, f32[32,384]{1,0:T(8,128)S(1)}, u32[]{:S(2)}, u32[]{:S(2)}) collective-permute-start(f32[32,384]{1,0:T(8,128)S(1)} %fusion.56), channel_id=1, source_target_pairs={{0,4},{1,5},{2,6},{3,7},{4,8},{5,9},{6,10},{7,11},{8,12},{9,13},{1... | collective-permute-start | bytes 147464 | tf_op jit(solution)/shard_map/ppermute | solution.py:14
  149.1 7.1 %collective-permute-start.57 = (f32[32,384]{1,0:T(8,128)S(1)}, f32[32,384]{1,0:T(8,128)S(1)}, u32[]{:S(2)}, u32[]{:S(2)}) collective-permute-start(f32[32,384]{1,0:T(8,128)S(1)} %fusion.56), channel_id=1, source_target_pairs={{0,3},{1,4},{2,5},{3,6},{4,7},{5,8},{6,9},{7,10},{8,11},{9,12},{10... | collective-permute-start | bytes 147464 | tf_op jit(solution)/shard_map/ppermute | solution.py:14
  149.4 7.4 %collective-permute-start.58 = (f32[32,384]{1,0:T(8,128)S(1)}, f32[32,384]{1,0:T(8,128)S(1)}, u32[]{:S(2)}, u32[]{:S(2)}) collective-permute-start(f32[32,384]{1,0:T(8,128)S(1)} %fusion.56), channel_id=1, source_target_pairs={{0,2},{1,3},{2,4},{3,5},{4,6},{5,7},{6,8},{7,9},{8,10},{9,11},{10,... | collective-permute-start | bytes 147464 | tf_op jit(solution)/shard_map/ppermute | solution.py:14
  151.0 7.3 %collective-permute-start.59 = (f32[32,384]{1,0:T(8,128)S(1)}, f32[32,384]{1,0:T(8,128)S(1)}, u32[]{:S(2)}, u32[]{:S(2)}) collective-permute-start(f32[32,384]{1,0:T(8,128)S(1)} %fusion.56), channel_id=1, source_target_pairs={{0,1},{1,2},{2,3},{3,4},{4,5},{5,6},{6,7},{7,8},{8,9},{9,10},{10,1... | collective-permute-start | bytes 147464 | tf_op jit(solution)/shard_map/ppermute | solution.py:14
  151.0 7.3 %collective-permute-start.60 = (f32[32,384]{1,0:T(8,128)S(1)}, f32[32,384]{1,0:T(8,128)S(1)}, u32[]{:S(2)}, u32[]{:S(2)}) collective-permute-start(f32[32,384]{1,0:T(8,128)S(1)} %fusion.56), channel_id=1, source_target_pairs={{0,15},{1,0},{2,1},{3,2},{4,3},{5,4},{6,5},{7,6},{8,7},{9,8},{10,9... | collective-permute-start | bytes 147464 | tf_op jit(solution)/shard_map/ppermute | solution.py:14
  155.4 4.3 %collective-permute-start.61 = (f32[32,384]{1,0:T(8,128)S(1)}, f32[32,384]{1,0:T(8,128)S(1)}, u32[]{:S(2)}, u32[]{:S(2)}) collective-permute-start(f32[32,384]{1,0:T(8,128)S(1)} %fusion.56), channel_id=1, source_target_pairs={{0,14},{1,15},{2,0},{3,1},{4,2},{5,3},{6,4},{7,5},{8,6},{9,7},{10,... | collective-permute-start | bytes 147464 | tf_op jit(solution)/shard_map/ppermute | solution.py:14
  156.8 4.5 %collective-permute-start.63 = (f32[32,384]{1,0:T(8,128)S(1)}, f32[32,384]{1,0:T(8,128)S(1)}, u32[]{:S(2)}, u32[]{:S(2)}) collective-permute-start(f32[32,384]{1,0:T(8,128)S(1)} %fusion.56), channel_id=1, source_target_pairs={{0,12},{1,13},{2,14},{3,15},{4,0},{5,1},{6,2},{7,3},{8,4},{9,5},{1... | collective-permute-start | bytes 147464 | tf_op jit(solution)/shard_map/ppermute | solution.py:14
  169.3 71.9 %collective-permute-start.65 = (f32[32,384]{1,0:T(8,128)S(1)}, f32[32,384]{1,0:T(8,128)S(1)}, u32[]{:S(2)}, u32[]{:S(2)}) collective-permute-start(f32[32,384]{1,0:T(8,128)S(1)} %fusion.51), channel_id=1, source_target_pairs={{0,4},{1,5},{2,6},{3,7},{4,8},{5,9},{6,10},{7,11},{8,12},{9,13},{1... | collective-permute-start | bytes 147464 | tf_op jit(solution)/shard_map/ppermute | solution.py:14
  169.7 71.6 %collective-permute-start.66 = (f32[32,384]{1,0:T(8,128)S(1)}, f32[32,384]{1,0:T(8,128)S(1)}, u32[]{:S(2)}, u32[]{:S(2)}) collective-permute-start(f32[32,384]{1,0:T(8,128)S(1)} %fusion.51), channel_id=1, source_target_pairs={{0,3},{1,4},{2,5},{3,6},{4,7},{5,8},{6,9},{7,10},{8,11},{9,12},{10... | collective-permute-start | bytes 147464 | tf_op jit(solution)/shard_map/ppermute | solution.py:14
  170.1 71.3 %collective-permute-start.67 = (f32[32,384]{1,0:T(8,128)S(1)}, f32[32,384]{1,0:T(8,128)S(1)}, u32[]{:S(2)}, u32[]{:S(2)}) collective-permute-start(f32[32,384]{1,0:T(8,128)S(1)} %fusion.51), channel_id=1, source_target_pairs={{0,2},{1,3},{2,4},{3,5},{4,6},{5,7},{6,8},{7,9},{8,10},{9,11},{10,... | collective-permute-start | bytes 147464 | tf_op jit(solution)/shard_map/ppermute | solution.py:14
  171.9 69.6 %collective-permute-start.68 = (f32[32,384]{1,0:T(8,128)S(1)}, f32[32,384]{1,0:T(8,128)S(1)}, u32[]{:S(2)}, u32[]{:S(2)}) collective-permute-start(f32[32,384]{1,0:T(8,128)S(1)} %fusion.51), channel_id=1, source_target_pairs={{0,1},{1,2},{2,3},{3,4},{4,5},{5,6},{6,7},{7,8},{8,9},{9,10},{10,1... | collective-permute-start | bytes 147464 | tf_op jit(solution)/shard_map/ppermute | solution.py:14
  172.1 72.9 %collective-permute-start.69 = (f32[32,384]{1,0:T(8,128)S(1)}, f32[32,384]{1,0:T(8,128)S(1)}, u32[]{:S(2)}, u32[]{:S(2)}) collective-permute-start(f32[32,384]{1,0:T(8,128)S(1)} %fusion.51), channel_id=1, source_target_pairs={{0,15},{1,0},{2,1},{3,2},{4,3},{5,4},{6,5},{7,6},{8,7},{9,8},{10,9... | collective-permute-start | bytes 147464 | tf_op jit(solution)/shard_map/ppermute | solution.py:14
  241.2 4.2 %collective-permute-start.70 = (f32[32,384]{1,0:T(8,128)S(1)}, f32[32,384]{1,0:T(8,128)S(1)}, u32[]{:S(2)}, u32[]{:S(2)}) collective-permute-start(f32[32,384]{1,0:T(8,128)S(1)} %fusion.51), channel_id=1, source_target_pairs={{0,14},{1,15},{2,0},{3,1},{4,2},{5,3},{6,4},{7,5},{8,6},{9,7},{10,... | collective-permute-start | bytes 147464 | tf_op jit(solution)/shard_map/ppermute | solution.py:14
  241.3 4.1 %collective-permute-start.71 = (f32[32,384]{1,0:T(8,128)S(1)}, f32[32,384]{1,0:T(8,128)S(1)}, u32[]{:S(2)}, u32[]{:S(2)}) collective-permute-start(f32[32,384]{1,0:T(8,128)S(1)} %fusion.51), channel_id=1, source_target_pairs={{0,13},{1,14},{2,15},{3,0},{4,1},{5,2},{6,3},{7,4},{8,5},{9,6},{10... | collective-permute-start | bytes 147464 | tf_op jit(solution)/shard_map/ppermute | solution.py:14
  241.4 4.1 %collective-permute-start.72 = (f32[32,384]{1,0:T(8,128)S(1)}, f32[32,384]{1,0:T(8,128)S(1)}, u32[]{:S(2)}, u32[]{:S(2)}) collective-permute-start(f32[32,384]{1,0:T(8,128)S(1)} %fusion.51), channel_id=1, source_target_pairs={{0,12},{1,13},{2,14},{3,15},{4,0},{5,1},{6,2},{7,3},{8,4},{9,5},{1... | collective-permute-start | bytes 147464 | tf_op jit(solution)/shard_map/ppermute | solution.py:14
  241.5 11.7 %collective-permute-start.64 = (f32[32,384]{1,0:T(8,128)S(1)}, f32[32,384]{1,0:T(8,128)S(1)}, u32[]{:S(2)}, u32[]{:S(2)}) collective-permute-start(f32[32,384]{1,0:T(8,128)S(1)} %convolution_multiply_fusion), channel_id=1, source_target_pairs={{0,16},{1,17},{2,18},{3,19},{4,20},{5,21},{6,22},{7,23},{8,24},{9,... | collective-permute-start | bytes 147464 | tf_op jit(solution)/shard_map/ppermute | solution.py:20
  (11 other events, 49.2 us)
where the time goes:
time: 316 us
  blocking collectives  118 us (37%)
  starting transfers between devices  89.1 us (28%)
  matrix products  63.2 us (20%)
  waiting for transfers between devices  26.9 us (9%)
  local copies, waits for them, and re-layouts  8.41 us (3%)
  other arithmetic  7.52 us (2%)
    ppermute x72, starting transfers between devices, from_behind(): lax.ppermute(shard, axis, [(i, (i + by) % size) for i in range(size)])  85.7 us
    dot_general x9, matrix products, apply_local(): jnp.einsum('vrkc,rkdc->vrd', picked, block_tiles, precision=lax.Precision...  60.9 us
    psum x1, blocking collectives, local(): lax.psum(jnp.dot(lower_rows, basis_raw.T, precision=lax.Precision.HIGHEST...  60.3 us
    psum x1, blocking collectives, local(): lax.psum((jnp.dot(current, current.T, precision=lax.Precision.HIGHEST), j...  57.6 us
    ppermute x72, waiting for transfers between devices, from_behind(): lax.ppermute(shard, axis, [(i, (i + by) % size) for i in range(size)])  26.9 us
  transfers between devices with their start and end apart: 73, of which 27 were waited for; matrix products, arithmetic and copies ran while one was open for 5% of the time, Pallas kernels for 0%

commit v1 on v0

v1 whole, which is shorter than its diff:
```python
import functools
import math

import jax
import jax.numpy as jnp
from jax import lax
from jax.experimental import pallas as pl
from jax.experimental.pallas import tpu as pltpu
from jax.sharding import PartitionSpec as P

DEG = 8
REACH = 12
F32 = jnp.float32
BF16 = jnp.bfloat16
NN = (((1,), (0,)), ((), ()))
NT = (((1,), (1,)), ((), ()))
TN = (((0,), (0,)), ((), ()))
VMEM = pl.BlockSpec(memory_space=pltpu.VMEM)
SMEM = pl.BlockSpec(memory_space=pltpu.SMEM)
ANY = pl.BlockSpec(memory_space=pl.ANY)
PARAMS = pltpu.CompilerParams(vmem_limit_bytes=40 * 2**20)


def column_of(slot, core, rows):
    pair = 2 * rows
    if slot >= 2 * pair:
        return core * rows + slot - 2 * pair
    chip, block = divmod(slot, pair)
    natural = (block + core * rows) % pair
    return natural - (chip + 1) * pair if core == 0 else natural + (chip + 1) * pair


def sent_slots(rows):
    pair = 2 * rows
    return [s for s in range(5 * rows) if not pair <= s < pair + rows]


def gather_kernel(where, pattern, tiles, sent, table, zeros, sems, *, rows, stored, total):
    pair = 2 * rows
    span = 2 * REACH + pair
    core = where[0] % 2
    first = (where[0] // 2) * pair
    zeros[...] = jnp.zeros_like(zeros)
    for entry in range(rows * span):
        table[entry] = -1
    for row in range(rows):
        for k in range(stored):
            column = pattern[row, k] - first
            column = jnp.where(column >= total // 2, column - total, column)
            column = jnp.where(column < -(total // 2), column + total, column)
            table[row * span + column + REACH] = k
    copies = []
    for place, slot in enumerate(sent_slots(rows)):
        for row in range(rows):
            column = jnp.where(core == 0, column_of(slot, 1, rows), column_of(slot, 0, rows))
            k = table[row * span + column + REACH]
            copies.append((place, row, k))
    for number, (place, row, k) in enumerate(copies):
        target = sent.at[place, row]

        @pl.when(k >= 0)
        def _():
            pltpu.make_async_copy(tiles.at[row, k], target, sems.at[number]).start()

        @pl.when(k < 0)
        def _():
            pltpu.make_async_copy(zeros, target, sems.at[number]).start()

    for number, (place, row, k) in enumerate(copies):
        pltpu.make_async_copy(zeros, sent.at[place, row], sems.at[number]).wait()


def store_tile(tile, high, low, slot, lane):
    tile = tile.T
    top = tile.astype(BF16)
    rest = (tile - top.astype(F32)).astype(BF16)
    width = tile.shape[0]
    high[slot * width : (slot + 1) * width, lane * width : (lane + 1) * width] = top
    low[slot * width : (slot + 1) * width, lane * width : (lane + 1) * width] = rest


def own_weights_kernel(where, table, tiles, high, low, *, rows):
    span = 2 * REACH + 2 * rows
    core = where[0] % 2
    for slot in range(5 * rows):
        for row in range(rows):
            column = jnp.where(core == 0, column_of(slot, 0, rows), column_of(slot, 1, rows))
            k = table[row * span + column + REACH]
            tile = tiles[row, jnp.maximum(k, 0)]
            store_tile(jnp.where(k >= 0, tile, 0.0), high, low, slot, row)


def other_weights_kernel(received, _high, _low, high, low, *, rows):
    places = sent_slots(rows)
    width = received.shape[2]
    for slot in range(5 * rows):
        for row in range(rows):
            if slot in places:
                store_tile(received[places.index(slot), row], high, low, slot, rows + row)
            else:
                blank = jnp.zeros((width, width), BF16)
                lane = rows + row
                high[slot * width : (slot + 1) * width, lane * width : (lane + 1) * width] = blank
                low[slot * width : (slot + 1) * width, lane * width : (lane + 1) * width] = blank


def multiply(vectors, high, low, start, depth):
    count = vectors.shape[0]
    top = vectors.astype(BF16)
    rest = (vectors - top.astype(F32)).astype(BF16)
    both = jnp.concatenate([top, rest], axis=0)
    by_high = lax.dot_general(both, high[start : start + depth, :], NN, preferred_element_type=F32)
    by_low = lax.dot_general(top, low[start : start + depth, :], NN, preferred_element_type=F32)
    return by_high[:count] + (by_high[count:] + by_low)


def own_kernel(vectors, high, low, out, *, start, depth):
    out[...] = multiply(vectors[:, :depth], high, low, start, depth)


def add_kernel(vectors, before, high, low, out, *, start, depth):
    out[...] = before[...] + multiply(vectors[...], high, low, start, depth)


def step_kernel(scale, partial, other, current, previous, out, *, half, first):
    image = partial[:, :half] + other[:, half:], partial[:, half:] + other[:, :half]
    center = scale[0]
    halfwidth = scale[1]
    for number, part in enumerate(image):
        lanes = slice(number * half, (number + 1) * half)
        value = (part - center * current[:, lanes]) / halfwidth
        out[:, lanes] = value if first else 2.0 * value - previous[:, lanes]


def dot(a, b, dims):
    return lax.dot_general(a, b, dims, precision=lax.Precision.HIGHEST, preferred_element_type=F32)


def products_kernel(pair, lower, partial, out, *, half):
    own = pair[:, :half]
    below = lower[...]
    gram = dot(own, own, NT)
    gram_below = dot(below, below, NT)
    mixed = dot(below, own, NT)
    cross = dot(pair[...], partial[...], NT)
    out[...] = jnp.concatenate([gram, gram_below, mixed, cross], axis=1)


def finish_kernel(where, pairs, parts, vectors, lower, filtered, projected, *, order):
    count = vectors.shape[0]
    total = parts[0]
    for device in range(1, parts.shape[0]):
        total = total + parts[device]
    lane = lax.broadcasted_iota(jnp.int32, (count, 4 * count), 1)
    sub = lax.broadcasted_iota(jnp.int32, (count, 4 * count), 0)
    gram = total[:, :count]
    gram_below = total[:, count : 2 * count]
    mixed = total[:, 2 * count : 3 * count]
    cross = total[:, 3 * count :]
    column = lax.broadcasted_iota(jnp.int32, (count, count), 1)
    row = lax.broadcasted_iota(jnp.int32, (count, count), 0)
    eye = (column == row).astype(F32)
    gram_below = jnp.where(where[1] == 0, eye, gram_below)
    work = jnp.concatenate([gram, eye, gram_below, eye], axis=1)
    left = lane < 2 * count
    for k in range(count):
        pivot = jnp.where(left[:1], work[k : k + 1, k : k + 1], work[k : k + 1, 2 * count + k : 2 * count + k + 1])
        root = 1.0 / jnp.sqrt(pivot)
        scaled = work[k : k + 1, :] * root
        factor = jnp.where(left, work[:, k : k + 1], work[:, 2 * count + k : 2 * count + k + 1]) * root
        work = jnp.where(sub > k, work - factor * scaled, jnp.where(sub == k, scaled, work))
    inverse = work[:, count : 2 * count]
    inverse_below = work[:, 3 * count :]
    projected[...] = dot(dot(inverse, cross, NN), inverse, NT)
    correlation = dot(dot(inverse_below, mixed, NN), inverse, NT)
    chosen = jnp.zeros((count, count), F32)
    for p in range(pairs.shape[0]):
        chosen = chosen + ((row == pairs[p, 1]) & (column == pairs[p, 0])).astype(F32)
    removal = dot((chosen * correlation).T, inverse_below, NN)
    filtered[...] = math.sqrt(order) * (dot(inverse, vectors[...], NN) - dot(removal, lower[...], NN))


def call(kernel, out_shape, in_specs, out_specs, **options):
    options.setdefault("compiler_params", PARAMS)
    return pl.pallas_call(kernel, out_shape=out_shape, in_specs=in_specs, out_specs=out_specs, **options)


def local(block_tiles, tile_pattern, start_vectors, centers, halfwidths, dup_pairs):
    rows, stored, width, _ = block_tiles.shape
    devices = lax.axis_size("row")
    cuts = lax.axis_size("cuts")
    chips = devices // 2
    total = rows * devices
    pair = 2 * rows
    half = rows * width
    whole = 2 * half
    initial = start_vectors[0]
    count = initial.shape[0]
    me = lax.axis_index("row")
    where = jnp.stack([me, lax.axis_index("cuts")]).astype(jnp.int32)
    scale = jnp.concatenate([centers, halfwidths])

    swap = [(i, i ^ 1) for i in range(devices)]

    def toward(steps):
        return [(i, (i + (2 * steps if i % 2 == 0 else -2 * steps)) % devices) for i in range(devices)]

    nearer, farther = toward(1), toward(2)
    span = 2 * REACH + pair
    places = len(sent_slots(rows))
    slots = 5 * rows
    weight = jax.ShapeDtypeStruct((slots * width, whole), BF16)
    vec = jax.ShapeDtypeStruct((count, whole), F32)

    sent, table = call(
        functools.partial(gather_kernel, rows=rows, stored=stored, total=total),
        (
            jax.ShapeDtypeStruct((places, rows, width, width), F32),
            jax.ShapeDtypeStruct((rows * span,), jnp.int32),
        ),
        [SMEM, SMEM, ANY],
        (ANY, SMEM),
        scratch_shapes=[pltpu.VMEM((width, width), F32), pltpu.SemaphoreType.DMA((places * rows,))],
    )(where, tile_pattern, block_tiles)
    received = lax.ppermute(sent, "row", swap)
    high, low = call(
        functools.partial(own_weights_kernel, rows=rows), (weight, weight), [SMEM, SMEM, VMEM], (VMEM, VMEM)
    )(where, table, block_tiles)
    high, low = call(
        functools.partial(other_weights_kernel, rows=rows),
        (weight, weight),
        [VMEM, VMEM, VMEM],
        (VMEM, VMEM),
        input_output_aliases={1: 0, 2: 1},
    )(received, high, low)

    def cost(depth):
        return pl.CostEstimate(
            flops=6 * count * depth * whole, bytes_accessed=4 * depth * whole, transcendentals=0
        )

    def part(kernel, start, depth, *vectors):
        return call(
            functools.partial(kernel, start=start * width, depth=depth * width),
            vec,
            [VMEM] * (len(vectors) + 2),
            VMEM,
            cost_estimate=cost(depth * width),
        )(*vectors, high, low)

    def apply_part(vectors):
        near = lax.ppermute(vectors, "row", nearer)
        far = lax.ppermute(vectors, "row", farther)
        partial = part(own_kernel, 2 * pair, rows, vectors)
        partial = part(add_kernel, 0, pair, near, partial)
        return part(add_kernel, pair, pair, far, partial)

    current = jnp.concatenate([initial, lax.ppermute(initial, "row", swap)], axis=1)
    previous = current
    for degree in range(DEG):
        partial = apply_part(current)
        other = lax.ppermute(partial, "row", swap)
        following = call(
            functools.partial(step_kernel, half=half, first=degree == 0),
            vec,
            [SMEM, VMEM, VMEM, VMEM, VMEM],
            VMEM,
        )(scale, partial, other, current, previous)
        previous, current = current, following

    own = current[:, :half]
    lower = lax.ppermute(own, "cuts", [(s, s + 1) for s in range(cuts - 1)])
    partial = apply_part(current)
    products = call(
        functools.partial(products_kernel, half=half),
        jax.ShapeDtypeStruct((count, 4 * count), F32),
        [VMEM, VMEM, VMEM],
        VMEM,
    )(current, lower, partial)
    spread = jnp.broadcast_to(products[None], (devices, *products.shape))
    parts = lax.all_to_all(spread, "row", 0, 0, tiled=True)
    filtered, projected = call(
        functools.partial(finish_kernel, order=total * width),
        (jax.ShapeDtypeStruct((count, half), F32), jax.ShapeDtypeStruct((count, count), F32)),
        [SMEM, SMEM, VMEM, VMEM, VMEM],
        (VMEM, VMEM),
    )(where, dup_pairs[0], parts, own, lower)
    return (filtered[None], projected[None])


def solution(mesh):
    in_specs = (
        P("row", None, None, None),
        P("row", None),
        P("cuts", None, "row"),
        P("cuts"),
        P("cuts"),
        P("cuts", None, None),
    )
    out_specs = (P("cuts", None, "row"), P("cuts", None, None))
    return jax.shard_map(local, mesh=mesh, in_specs=in_specs, out_specs=out_specs, check_vma=False)
```

time: 316 us -> 128 us (0.41)
  blocking collectives: 118 us -> 0 us
  starting transfers between devices: 89.1 us -> 22.2 us
  matrix products: 63.2 us -> 0 us
  waiting for transfers between devices: 26.9 us -> 69 us
  Pallas kernels: 0 us -> 29.6 us
  other arithmetic: 7.52 us -> 0.96 us
  local copies, waits for them, and re-layouts: 8.41 us -> 3.85 us
    psum x2 -> x0, blocking collectives: 118 us -> none  [the longest x1 60.3 us: local(): lax.psum(jnp.dot(lower_rows, basis_raw.T, precision=lax.Precision.HIGHEST...]
    ppermute x73 -> x29, starting transfers between devices: 89.1 us -> 18.7 us  [the longest x9 11.9 us: apply_part(): near = lax.ppermute(vectors, 'row', nearer)]
    dot_general x14 -> x0, matrix products: 62.5 us -> none  [the longest x9 60.9 us: apply_local(): jnp.einsum('vrkc,rkdc->vrd', picked, block_tiles, precision=lax.Precision...]
    ppermute x73 -> x29, waiting for transfers between devices: 26.9 us -> 59.1 us  [the longest x9 44.1 us: apply_part(): near = lax.ppermute(vectors, 'row', nearer)]
    pallas_call x0 -> x40, Pallas kernels: none -> 29.6 us  [the longest x27 11.3 us: part(): call(functools.partial(kernel, start=start * width, depth=depth * width),...]
    all_to_all x0 -> x1, waiting for transfers between devices: none -> 9.91 us  [local(): parts = lax.all_to_all(spread, 'row', 0, 0, tiled=True)]
    another operation x5 -> x1, other arithmetic: 6.68 us -> 0.08 us  [local(): where = jnp.stack([me, lax.axis_index('cuts')]).astype(jnp.int32)]
    gather x9 -> x0, local copies, waits for them, and re-layouts: 5.96 us -> none  [apply_local(): picked = jnp.take(extended, positions, axis=1)]
  transfers between devices with their start and end apart: 73 -> 30, of which waited for: 27 -> 20; matrix products, arithmetic and copies ran while one was open for 5% -> 1% of each run, Pallas kernels for 0% -> 7%
where the time goes in v1:
time: 128 us
  waiting for transfers between devices  69 us (54%)
  Pallas kernels  29.6 us (23%)
  starting transfers between devices  22.2 us (17%)
  local copies, waits for them, and re-layouts  3.85 us (3%)
  between operations  2.19 us (2%)
    ppermute x9, waiting for transfers between devices, apply_part(): near = lax.ppermute(vectors, 'row', nearer)  44.1 us
    ppermute x9, starting transfers between devices, apply_part(): near = lax.ppermute(vectors, 'row', nearer)  11.9 us
    pallas_call x27, Pallas kernels, part(): call(functools.partial(kernel, start=start * width, depth=depth * width),...  11.3 us
    ppermute x8, waiting for transfers between devices, local(): other = lax.ppermute(partial, 'row', swap)  10.2 us
    all_to_all x1, waiting for transfers between devices, local(): parts = lax.all_to_all(spread, 'row', 0, 0, tiled=True)  9.91 us
    pallas_call x1, Pallas kernels, local(): call(functools.partial(gather_kernel, rows=rows, stored=stored, total=tot...  5.96 us
    pallas_call x1, Pallas kernels, local(): call(functools.partial(finish_kernel, order=total * width), (jax.ShapeDty...  5.24 us
    pallas_call x8, Pallas kernels, local(): call(functools.partial(step_kernel, half=half, first=degree == 0), vec, [...  4.58 us
  transfers between devices with their start and end apart: 30, of which 20 were waited for; matrix products, arithmetic and copies ran while one was open for 1% of the time, Pallas kernels for 7%

profile of v1, /device:TPU:0, one launch (start us, length us, event | category | flops | bytes accessed | tf_op | source)
XLA Modules:
  0.0 127.9 jit_solution(12830216721046871603)
XLA Ops:
  0.7 2.3 %copy-done = f32[3,24,128,128]{3,2,1,0:T(8,128)S(1)} copy-done((f32[3,24,128,128]{3,2,1,0:T(8,128)S(1)}, f32[3,24,128,128]{3,2,1,0:T(8,128)}, u32[]{:S(2)}) %copy-start) | copy-done | bytes 4718616
  3.0 0.7 copy-done.2
  3.7 6.0 %shard_map.77 = (f32[12,3,128,128]{3,2,1,0:T(8,128)S(1)}, s32[90]{0:T(128)S(1)}) custom-call(s32[2]{0:T(128)S(1)} %pad_add_fusion.where, s32[3,24]{1,0:T(4,128)S(1)} %copy-done.2, f32[3,24,128,128]{3,2,1,0:T(8,128)S(1)} %copy-done), custom_call_target="tpu_custom_call" | custom-call | tf_op jit(solution)/shard_map/pallas_call | solution.py:215
  9.7 0.5 collective-permute-start.3
  10.3 4.3 %collective-permute-done = f32[32,384]{1,0:T(8,128)S(1)} collective-permute-done((f32[32,384]{1,0:T(8,128)}, f32[32,384]{1,0:T(8,128)S(1)}, u32[]{:S(2)}, u32[]{:S(2)}) %collective-permute-start) | collective-permute-done | bytes 49184 | tf_op jit(solution)/shard_map/ppermute | solution.py:258
  14.6 0.8 pad_maximum_fusion.vectors.current.previous
  15.4 2.6 %collective-permute-start.2 = (f32[32,768]{1,0:T(8,128)S(1)}, f32[32,768]{1,0:T(8,128)S(1)}, u32[]{:S(2)}, u32[]{:S(2)}) collective-permute-start(f32[32,768]{1,0:T(8,128)S(1)} %pad_maximum_fusion.vectors.current.previous), channel_id=1, source_target_pairs={{0,2},{1,15},{2,4},{3,1},{4,6},{5,3},{6,8},{7,5},{8,10},{9,7},{10,... | collective-permute-start | bytes 294920 | tf_op jit(solution)/shard_map/ppermute | solution.py:252
  18.0 1.6 %collective-permute-start.1 = (f32[32,768]{1,0:T(8,128)S(1)}, f32[32,768]{1,0:T(8,128)S(1)}, u32[]{:S(2)}, u32[]{:S(2)}) collective-permute-start(f32[32,768]{1,0:T(8,128)S(1)} %pad_maximum_fusion.vectors.current.previous), channel_id=1, source_target_pairs={{0,4},{1,13},{2,6},{3,15},{4,8},{5,1},{6,10},{7,3},{8,12},{9,5},{1... | collective-permute-start | bytes 294920 | tf_op jit(solution)/shard_map/ppermute | solution.py:253
  19.5 1.4 %shard_map.78 = (bf16[1920,768]{1,0:T(8,128)(2,1)S(1)}, bf16[1920,768]{1,0:T(8,128)(2,1)S(1)}) custom-call(s32[2]{0:T(128)S(1)} %pad_add_fusion.where, s32[90]{0:T(128)S(1)} %get-tuple-element.11.table, f32[3,24,128,128]{3,2,1,0:T(8,128)S(1)} %copy-done.1), custom_call_target="tpu_custom_call" | custom-call | tf_op jit(solution)/shard_map/pallas_call | solution.py:226
  22.3 0.7 shard_map.79
  23.3 1.2 collective-permute-done.2.vectors
  24.5 0.5 shard_map.81.before
  25.4 0.5 shard_map.82.partial
  26.1 1.1 collective-permute-done.4.other
  27.2 0.6 shard_map.83.vectors.current.previous
  27.8 0.9 collective-permute-start.6
  28.7 0.7 collective-permute-start.5
  29.7 5.5 %collective-permute-done.6.vectors = f32[32,768]{1,0:T(8,128)S(1)} collective-permute-done((f32[32,768]{1,0:T(8,128)S(1)}, f32[32,768]{1,0:T(8,128)S(1)}, u32[]{:S(2)}, u32[]{:S(2)}) %collective-permute-start.6) | collective-permute-done | bytes 98336 | tf_op jit(solution)/shard_map/ppermute | solution.py:252
  35.2 0.5 shard_map.85.before
  35.7 0.5 shard_map.86.partial
  36.2 1.3 %collective-permute-done.7.other = f32[32,768]{1,0:T(8,128)S(1)} collective-permute-done((f32[32,768]{1,0:T(8,128)S(1)}, f32[32,768]{1,0:T(8,128)S(1)}, u32[]{:S(2)}, u32[]{:S(2)}) %collective-permute-start.7) | collective-permute-done | bytes 98336 | tf_op jit(solution)/shard_map/ppermute | solution.py:262
  37.5 0.6 shard_map.87.vectors.current.previous
  38.0 1.4 %collective-permute-start.9 = (f32[32,768]{1,0:T(8,128)S(1)}, f32[32,768]{1,0:T(8,128)S(1)}, u32[]{:S(2)}, u32[]{:S(2)}) collective-permute-start(f32[32,768]{1,0:T(8,128)S(1)} %shard_map.87.vectors.current.previous), channel_id=1, source_target_pairs={{0,2},{1,15},{2,4},{3,1},{4,6},{5,3},{6,8},{7,5},{8,10},{9,7},{10,... | collective-permute-start | bytes 294920 | tf_op jit(solution)/shard_map/ppermute | solution.py:252
  40.1 5.3 %collective-permute-done.9.vectors = f32[32,768]{1,0:T(8,128)S(1)} collective-permute-done((f32[32,768]{1,0:T(8,128)S(1)}, f32[32,768]{1,0:T(8,128)S(1)}, u32[]{:S(2)}, u32[]{:S(2)}) %collective-permute-start.9) | collective-permute-done | bytes 98336 | tf_op jit(solution)/shard_map/ppermute | solution.py:252
  45.9 0.5 shard_map.90.partial
  46.4 1.3 %collective-permute-done.10.other = f32[32,768]{1,0:T(8,128)S(1)} collective-permute-done((f32[32,768]{1,0:T(8,128)S(1)}, f32[32,768]{1,0:T(8,128)S(1)}, u32[]{:S(2)}, u32[]{:S(2)}) %collective-permute-start.10) | collective-permute-done | bytes 98336 | tf_op jit(solution)/shard_map/ppermute | solution.py:262
  47.7 0.6 shard_map.91.vectors.current.previous
  48.3 1.2 collective-permute-start.12
  49.8 5.9 %collective-permute-done.12.vectors = f32[32,768]{1,0:T(8,128)S(1)} collective-permute-done((f32[32,768]{1,0:T(8,128)S(1)}, f32[32,768]{1,0:T(8,128)S(1)}, u32[]{:S(2)}, u32[]{:S(2)}) %collective-permute-start.12) | collective-permute-done | bytes 98336 | tf_op jit(solution)/shard_map/ppermute | solution.py:252
  55.7 0.5 shard_map.93.before
  56.2 0.5 shard_map.94.partial
  56.7 1.3 %collective-permute-done.13.other = f32[32,768]{1,0:T(8,128)S(1)} collective-permute-done((f32[32,768]{1,0:T(8,128)S(1)}, f32[32,768]{1,0:T(8,128)S(1)}, u32[]{:S(2)}, u32[]{:S(2)}) %collective-permute-start.13) | collective-permute-done | bytes 98336 | tf_op jit(solution)/shard_map/ppermute | solution.py:262
  58.0 0.6 shard_map.95.vectors.current.previous
  58.5 1.2 collective-permute-start.15
  60.0 5.9 %collective-permute-done.15.vectors = f32[32,768]{1,0:T(8,128)S(1)} collective-permute-done((f32[32,768]{1,0:T(8,128)S(1)}, f32[32,768]{1,0:T(8,128)S(1)}, u32[]{:S(2)}, u32[]{:S(2)}) %collective-permute-start.15) | collective-permute-done | bytes 98336 | tf_op jit(solution)/shard_map/ppermute | solution.py:252
  66.4 0.5 shard_map.98.partial
  66.9 1.3 %collective-permute-done.16.other = f32[32,768]{1,0:T(8,128)S(1)} collective-permute-done((f32[32,768]{1,0:T(8,128)S(1)}, f32[32,768]{1,0:T(8,128)S(1)}, u32[]{:S(2)}, u32[]{:S(2)}) %collective-permute-start.16) | collective-permute-done | bytes 98336 | tf_op jit(solution)/shard_map/ppermute | solution.py:262
  68.2 0.6 shard_map.99.vectors.current.previous
  68.8 1.2 collective-permute-start.18
  70.2 5.9 %collective-permute-done.18.vectors = f32[32,768]{1,0:T(8,128)S(1)} collective-permute-done((f32[32,768]{1,0:T(8,128)S(1)}, f32[32,768]{1,0:T(8,128)S(1)}, u32[]{:S(2)}, u32[]{:S(2)}) %collective-permute-start.18) | collective-permute-done | bytes 98336 | tf_op jit(solution)/shard_map/ppermute | solution.py:252
  76.7 0.5 shard_map.102.partial
  77.2 1.3 %collective-permute-done.19.other = f32[32,768]{1,0:T(8,128)S(1)} collective-permute-done((f32[32,768]{1,0:T(8,128)S(1)}, f32[32,768]{1,0:T(8,128)S(1)}, u32[]{:S(2)}, u32[]{:S(2)}) %collective-permute-start.19) | collective-permute-done | bytes 98336 | tf_op jit(solution)/shard_map/ppermute | solution.py:262
  78.5 0.6 shard_map.103.vectors.current.previous
  79.0 1.2 collective-permute-start.21
  80.5 5.9 %collective-permute-done.21.vectors = f32[32,768]{1,0:T(8,128)S(1)} collective-permute-done((f32[32,768]{1,0:T(8,128)S(1)}, f32[32,768]{1,0:T(8,128)S(1)}, u32[]{:S(2)}, u32[]{:S(2)}) %collective-permute-start.21) | collective-permute-done | bytes 98336 | tf_op jit(solution)/shard_map/ppermute | solution.py:252
  86.4 0.5 shard_map.105.before
  86.9 0.5 shard_map.106.partial
  87.4 1.3 %collective-permute-done.22.other = f32[32,768]{1,0:T(8,128)S(1)} collective-permute-done((f32[32,768]{1,0:T(8,128)S(1)}, f32[32,768]{1,0:T(8,128)S(1)}, u32[]{:S(2)}, u32[]{:S(2)}) %collective-permute-start.22) | collective-permute-done | bytes 98336 | tf_op jit(solution)/shard_map/ppermute | solution.py:262
  88.7 0.6 shard_map.107.vectors.current
  89.3 1.2 collective-permute-start.24
  90.8 5.9 %collective-permute-done.24.vectors = f32[32,768]{1,0:T(8,128)S(1)} collective-permute-done((f32[32,768]{1,0:T(8,128)S(1)}, f32[32,768]{1,0:T(8,128)S(1)}, u32[]{:S(2)}, u32[]{:S(2)}) %collective-permute-start.24) | collective-permute-done | bytes 98336 | tf_op jit(solution)/shard_map/ppermute | solution.py:252
  96.7 0.5 shard_map.109.before
  97.2 0.5 shard_map.110.partial
  97.7 1.3 %collective-permute-done.25.other = f32[32,768]{1,0:T(8,128)S(1)} collective-permute-done((f32[32,768]{1,0:T(8,128)S(1)}, f32[32,768]{1,0:T(8,128)S(1)}, u32[]{:S(2)}, u32[]{:S(2)}) %collective-permute-start.25) | collective-permute-done | bytes 98336 | tf_op jit(solution)/shard_map/ppermute | solution.py:262
  99.0 0.6 shard_map.111.vectors.pair
  99.6 1.2 collective-permute-start.28
  100.7 3.4 %collective-permute-start.26 = (f32[32,384]{1,0:T(8,128)S(1)}, f32[32,384]{1,0:T(8,128)S(1)}, u32[]{:S(2)}, u32[]{:S(2)}) collective-permute-start(f32[32,384]{1,0:T(8,128)S(1)} %slice.4.vectors), channel_id=1, source_target_pairs={{0,16},{1,17},{2,18},{3,19},{4,20},{5,21},{6,22},{7,23},{8,24},{9,... | collective-permute-start | bytes 147464 | tf_op jit(solution)/shard_map/ppermute | solution.py:272
  104.4 2.5 %collective-permute-done.28.vectors = f32[32,768]{1,0:T(8,128)S(1)} collective-permute-done((f32[32,768]{1,0:T(8,128)S(1)}, f32[32,768]{1,0:T(8,128)S(1)}, u32[]{:S(2)}, u32[]{:S(2)}) %collective-permute-start.28) | collective-permute-done | bytes 98336 | tf_op jit(solution)/shard_map/ppermute | solution.py:252
  106.9 0.5 shard_map.113.before
  107.4 0.5 shard_map.114.partial
  108.4 0.7 broadcast_in_dim.12
  109.1 3.5 %all-to-all-start = ((f32[16,32,128]{2,1,0:T(8,128)}), f32[16,32,128]{2,1,0:T(8,128)S(1)}, u32[]{:S(2)}, u32[]{:S(2)}) async-start(f32[16,32,128]{2,1,0:T(8,128)} %broadcast_in_dim.12), calls=%async_computation | async-start | bytes 524288 | tf_op jit(solution)/shard_map/all_to_all | solution.py:281
  112.7 9.9 %all-to-all-done.parts = f32[16,32,128]{2,1,0:T(8,128)S(1)} async-done(((f32[16,32,128]{2,1,0:T(8,128)}), f32[16,32,128]{2,1,0:T(8,128)S(1)}, u32[]{:S(2)}, u32[]{:S(2)}) %all-to-all-start) | async-done | bytes 262176 | tf_op jit(solution)/shard_map/all_to_all | solution.py:281
  122.6 5.2 %shard_map.116 = (f32[32,384]{1,0:T(8,128)}, f32[32,32]{1,0:T(8,128)}) custom-call(s32[2]{0:T(128)S(1)} %pad_add_fusion.where, s32[8,2]{1,0:T(8,128)S(1)} %copy.10.pairs, f32[16,32,128]{2,1,0:T(8,128)S(1)} %all-to-all-done.parts, f32[32,384]{1,0:T(8,128)S(1)} %slice.4.vectors, f32[32,384]{1,0:T(8,128)S(1)} %collective-permute-done.26.lower), custom_call_target="tpu_custom_call" | custom-call | tf_op jit(solution)/shard_map/pallas_call | solution.py:282
  (50 shorter events, 5.9 us)
Async XLA Ops:
  0.7 2.3 %copy-start = (f32[3,24,128,128]{3,2,1,0:T(8,128)S(1)}, f32[3,24,128,128]{3,2,1,0:T(8,128)}, u32[]{:S(2)}) copy-start(f32[3,24,128,128]{3,2,1,0:T(8,128)} %tiles.3) | copy-start | bytes 14155780
  3.0 0.7 copy-start.2
  3.7 15.8 %copy-start.1 = (f32[3,24,128,128]{3,2,1,0:T(8,128)S(1)}, f32[3,24,128,128]{3,2,1,0:T(8,128)}, u32[]{:S(2)}) copy-start(f32[3,24,128,128]{3,2,1,0:T(8,128)} %tiles.3) | copy-start | bytes 14155780
  9.7 12.5 %collective-permute-start.3 = (f32[12,3,128,128]{3,2,1,0:T(8,128)S(1)}, f32[12,3,128,128]{3,2,1,0:T(8,128)S(1)}, u32[]{:S(2)}, u32[]{:S(2)}) collective-permute-start(f32[12,3,128,128]{3,2,1,0:T(8,128)S(1)} %get-tuple-element.10), channel_id=1, source_target_pairs={{0,1},{1,0},{2,3},{3,2},{4,5},{5,4},{6,7},{7,6},{8,9},{9,8},{10,11... | collective-permute-start | bytes 7077896 | tf_op jit(solution)/shard_map/ppermute | solution.py:225
  10.2 4.4 %collective-permute-start = (f32[32,384]{1,0:T(8,128)}, f32[32,384]{1,0:T(8,128)S(1)}, u32[]{:S(2)}, u32[]{:S(2)}) collective-permute-start(f32[32,384]{1,0:T(8,128)} %bitcast.6), channel_id=1, source_target_pairs={{0,1},{1,0},{2,3},{3,2},{4,5},{5,4},{6,7},{7,6},{8,9},{9,8},{10,11... | collective-permute-start | bytes 147464 | tf_op jit(solution)/shard_map/ppermute | solution.py:258
  15.4 9.1 %collective-permute-start.2 = (f32[32,768]{1,0:T(8,128)S(1)}, f32[32,768]{1,0:T(8,128)S(1)}, u32[]{:S(2)}, u32[]{:S(2)}) collective-permute-start(f32[32,768]{1,0:T(8,128)S(1)} %pad_maximum_fusion.vectors.current.previous), channel_id=1, source_target_pairs={{0,2},{1,15},{2,4},{3,1},{4,6},{5,3},{6,8},{7,5},{8,10},{9,7},{10,... | collective-permute-start | bytes 294920 | tf_op jit(solution)/shard_map/ppermute | solution.py:252
  18.0 7.5 %collective-permute-start.1 = (f32[32,768]{1,0:T(8,128)S(1)}, f32[32,768]{1,0:T(8,128)S(1)}, u32[]{:S(2)}, u32[]{:S(2)}) collective-permute-start(f32[32,768]{1,0:T(8,128)S(1)} %pad_maximum_fusion.vectors.current.previous), channel_id=1, source_target_pairs={{0,4},{1,13},{2,6},{3,15},{4,8},{5,1},{6,10},{7,3},{8,12},{9,5},{1... | collective-permute-start | bytes 294920 | tf_op jit(solution)/shard_map/ppermute | solution.py:253
  25.9 1.3 %collective-permute-start.4 = (f32[32,768]{1,0:T(8,128)S(1)}, f32[32,768]{1,0:T(8,128)S(1)}, u32[]{:S(2)}, u32[]{:S(2)}) collective-permute-start(f32[32,768]{1,0:T(8,128)S(1)} %shard_map.82.partial), channel_id=1, source_target_pairs={{0,1},{1,0},{2,3},{3,2},{4,5},{5,4},{6,7},{7,6},{8,9},{9,8},{10,11... | collective-permute-start | bytes 294920 | tf_op jit(solution)/shard_map/ppermute | solution.py:262
  27.8 7.4 %collective-permute-start.6 = (f32[32,768]{1,0:T(8,128)S(1)}, f32[32,768]{1,0:T(8,128)S(1)}, u32[]{:S(2)}, u32[]{:S(2)}) collective-permute-start(f32[32,768]{1,0:T(8,128)S(1)} %shard_map.83.vectors.current.previous), channel_id=1, source_target_pairs={{0,2},{1,15},{2,4},{3,1},{4,6},{5,3},{6,8},{7,5},{8,10},{9,7},{10,... | collective-permute-start | bytes 294920 | tf_op jit(solution)/shard_map/ppermute | solution.py:252
  28.7 7.0 %collective-permute-start.5 = (f32[32,768]{1,0:T(8,128)S(1)}, f32[32,768]{1,0:T(8,128)S(1)}, u32[]{:S(2)}, u32[]{:S(2)}) collective-permute-start(f32[32,768]{1,0:T(8,128)S(1)} %shard_map.83.vectors.current.previous), channel_id=1, source_target_pairs={{0,4},{1,13},{2,6},{3,15},{4,8},{5,1},{6,10},{7,3},{8,12},{9,5},{1... | collective-permute-start | bytes 294920 | tf_op jit(solution)/shard_map/ppermute | solution.py:253
  36.1 1.3 %collective-permute-start.7 = (f32[32,768]{1,0:T(8,128)S(1)}, f32[32,768]{1,0:T(8,128)S(1)}, u32[]{:S(2)}, u32[]{:S(2)}) collective-permute-start(f32[32,768]{1,0:T(8,128)S(1)} %shard_map.86.partial), channel_id=1, source_target_pairs={{0,1},{1,0},{2,3},{3,2},{4,5},{5,4},{6,7},{7,6},{8,9},{9,8},{10,11... | collective-permute-start | bytes 294920 | tf_op jit(solution)/shard_map/ppermute | solution.py:262
  38.0 7.4 %collective-permute-start.9 = (f32[32,768]{1,0:T(8,128)S(1)}, f32[32,768]{1,0:T(8,128)S(1)}, u32[]{:S(2)}, u32[]{:S(2)}) collective-permute-start(f32[32,768]{1,0:T(8,128)S(1)} %shard_map.87.vectors.current.previous), channel_id=1, source_target_pairs={{0,2},{1,15},{2,4},{3,1},{4,6},{5,3},{6,8},{7,5},{8,10},{9,7},{10,... | collective-permute-start | bytes 294920 | tf_op jit(solution)/shard_map/ppermute | solution.py:252
  39.5 6.4 %collective-permute-start.8 = (f32[32,768]{1,0:T(8,128)S(1)}, f32[32,768]{1,0:T(8,128)S(1)}, u32[]{:S(2)}, u32[]{:S(2)}) collective-permute-start(f32[32,768]{1,0:T(8,128)S(1)} %shard_map.87.vectors.current.previous), channel_id=1, source_target_pairs={{0,4},{1,13},{2,6},{3,15},{4,8},{5,1},{6,10},{7,3},{8,12},{9,5},{1... | collective-permute-start | bytes 294920 | tf_op jit(solution)/shard_map/ppermute | solution.py:253
  46.4 1.3 %collective-permute-start.10 = (f32[32,768]{1,0:T(8,128)S(1)}, f32[32,768]{1,0:T(8,128)S(1)}, u32[]{:S(2)}, u32[]{:S(2)}) collective-permute-start(f32[32,768]{1,0:T(8,128)S(1)} %shard_map.90.partial), channel_id=1, source_target_pairs={{0,1},{1,0},{2,3},{3,2},{4,5},{5,4},{6,7},{7,6},{8,9},{9,8},{10,11... | collective-permute-start | bytes 294920 | tf_op jit(solution)/shard_map/ppermute | solution.py:262
  48.3 7.4 %collective-permute-start.12 = (f32[32,768]{1,0:T(8,128)S(1)}, f32[32,768]{1,0:T(8,128)S(1)}, u32[]{:S(2)}, u32[]{:S(2)}) collective-permute-start(f32[32,768]{1,0:T(8,128)S(1)} %shard_map.91.vectors.current.previous), channel_id=1, source_target_pairs={{0,2},{1,15},{2,4},{3,1},{4,6},{5,3},{6,8},{7,5},{8,10},{9,7},{10,... | collective-permute-start | bytes 294920 | tf_op jit(solution)/shard_map/ppermute | solution.py:252
  49.5 6.7 %collective-permute-start.11 = (f32[32,768]{1,0:T(8,128)S(1)}, f32[32,768]{1,0:T(8,128)S(1)}, u32[]{:S(2)}, u32[]{:S(2)}) collective-permute-start(f32[32,768]{1,0:T(8,128)S(1)} %shard_map.91.vectors.current.previous), channel_id=1, source_target_pairs={{0,4},{1,13},{2,6},{3,15},{4,8},{5,1},{6,10},{7,3},{8,12},{9,5},{1... | collective-permute-start | bytes 294920 | tf_op jit(solution)/shard_map/ppermute | solution.py:253
  56.6 1.3 %collective-permute-start.13 = (f32[32,768]{1,0:T(8,128)S(1)}, f32[32,768]{1,0:T(8,128)S(1)}, u32[]{:S(2)}, u32[]{:S(2)}) collective-permute-start(f32[32,768]{1,0:T(8,128)S(1)} %shard_map.94.partial), channel_id=1, source_target_pairs={{0,1},{1,0},{2,3},{3,2},{4,5},{5,4},{6,7},{7,6},{8,9},{9,8},{10,11... | collective-permute-start | bytes 294920 | tf_op jit(solution)/shard_map/ppermute | solution.py:262
  58.5 7.4 %collective-permute-start.15 = (f32[32,768]{1,0:T(8,128)S(1)}, f32[32,768]{1,0:T(8,128)S(1)}, u32[]{:S(2)}, u32[]{:S(2)}) collective-permute-start(f32[32,768]{1,0:T(8,128)S(1)} %shard_map.95.vectors.current.previous), channel_id=1, source_target_pairs={{0,2},{1,15},{2,4},{3,1},{4,6},{5,3},{6,8},{7,5},{8,10},{9,7},{10,... | collective-permute-start | bytes 294920 | tf_op jit(solution)/shard_map/ppermute | solution.py:252
  59.7 6.7 %collective-permute-start.14 = (f32[32,768]{1,0:T(8,128)S(1)}, f32[32,768]{1,0:T(8,128)S(1)}, u32[]{:S(2)}, u32[]{:S(2)}) collective-permute-start(f32[32,768]{1,0:T(8,128)S(1)} %shard_map.95.vectors.current.previous), channel_id=1, source_target_pairs={{0,4},{1,13},{2,6},{3,15},{4,8},{5,1},{6,10},{7,3},{8,12},{9,5},{1... | collective-permute-start | bytes 294920 | tf_op jit(solution)/shard_map/ppermute | solution.py:253
  66.9 1.3 %collective-permute-start.16 = (f32[32,768]{1,0:T(8,128)S(1)}, f32[32,768]{1,0:T(8,128)S(1)}, u32[]{:S(2)}, u32[]{:S(2)}) collective-permute-start(f32[32,768]{1,0:T(8,128)S(1)} %shard_map.98.partial), channel_id=1, source_target_pairs={{0,1},{1,0},{2,3},{3,2},{4,5},{5,4},{6,7},{7,6},{8,9},{9,8},{10,11... | collective-permute-start | bytes 294920 | tf_op jit(solution)/shard_map/ppermute | solution.py:262
  68.8 7.4 %collective-permute-start.18 = (f32[32,768]{1,0:T(8,128)S(1)}, f32[32,768]{1,0:T(8,128)S(1)}, u32[]{:S(2)}, u32[]{:S(2)}) collective-permute-start(f32[32,768]{1,0:T(8,128)S(1)} %shard_map.99.vectors.current.previous), channel_id=1, source_target_pairs={{0,2},{1,15},{2,4},{3,1},{4,6},{5,3},{6,8},{7,5},{8,10},{9,7},{10,... | collective-permute-start | bytes 294920 | tf_op jit(solution)/shard_map/ppermute | solution.py:252
  70.0 6.7 %collective-permute-start.17 = (f32[32,768]{1,0:T(8,128)S(1)}, f32[32,768]{1,0:T(8,128)S(1)}, u32[]{:S(2)}, u32[]{:S(2)}) collective-permute-start(f32[32,768]{1,0:T(8,128)S(1)} %shard_map.99.vectors.current.previous), channel_id=1, source_target_pairs={{0,4},{1,13},{2,6},{3,15},{4,8},{5,1},{6,10},{7,3},{8,12},{9,5},{1... | collective-permute-start | bytes 294920 | tf_op jit(solution)/shard_map/ppermute | solution.py:253
  77.1 1.3 %collective-permute-start.19 = (f32[32,768]{1,0:T(8,128)S(1)}, f32[32,768]{1,0:T(8,128)S(1)}, u32[]{:S(2)}, u32[]{:S(2)}) collective-permute-start(f32[32,768]{1,0:T(8,128)S(1)} %shard_map.102.partial), channel_id=1, source_target_pairs={{0,1},{1,0},{2,3},{3,2},{4,5},{5,4},{6,7},{7,6},{8,9},{9,8},{10,11... | collective-permute-start | bytes 294920 | tf_op jit(solution)/shard_map/ppermute | solution.py:262
  79.0 7.4 %collective-permute-start.21 = (f32[32,768]{1,0:T(8,128)S(1)}, f32[32,768]{1,0:T(8,128)S(1)}, u32[]{:S(2)}, u32[]{:S(2)}) collective-permute-start(f32[32,768]{1,0:T(8,128)S(1)} %shard_map.103.vectors.current.previous), channel_id=1, source_target_pairs={{0,2},{1,15},{2,4},{3,1},{4,6},{5,3},{6,8},{7,5},{8,10},{9,7},{10,... | collective-permute-start | bytes 294920 | tf_op jit(solution)/shard_map/ppermute | solution.py:252
  80.2 6.7 %collective-permute-start.20 = (f32[32,768]{1,0:T(8,128)S(1)}, f32[32,768]{1,0:T(8,128)S(1)}, u32[]{:S(2)}, u32[]{:S(2)}) collective-permute-start(f32[32,768]{1,0:T(8,128)S(1)} %shard_map.103.vectors.current.previous), channel_id=1, source_target_pairs={{0,4},{1,13},{2,6},{3,15},{4,8},{5,1},{6,10},{7,3},{8,12},{9,5},{1... | collective-permute-start | bytes 294920 | tf_op jit(solution)/shard_map/ppermute | solution.py:253
  87.4 1.3 %collective-permute-start.22 = (f32[32,768]{1,0:T(8,128)S(1)}, f32[32,768]{1,0:T(8,128)S(1)}, u32[]{:S(2)}, u32[]{:S(2)}) collective-permute-start(f32[32,768]{1,0:T(8,128)S(1)} %shard_map.106.partial), channel_id=1, source_target_pairs={{0,1},{1,0},{2,3},{3,2},{4,5},{5,4},{6,7},{7,6},{8,9},{9,8},{10,11... | collective-permute-start | bytes 294920 | tf_op jit(solution)/shard_map/ppermute | solution.py:262
  89.3 7.4 %collective-permute-start.24 = (f32[32,768]{1,0:T(8,128)S(1)}, f32[32,768]{1,0:T(8,128)S(1)}, u32[]{:S(2)}, u32[]{:S(2)}) collective-permute-start(f32[32,768]{1,0:T(8,128)S(1)} %shard_map.107.vectors.current), channel_id=1, source_target_pairs={{0,2},{1,15},{2,4},{3,1},{4,6},{5,3},{6,8},{7,5},{8,10},{9,7},{10,... | collective-permute-start | bytes 294920 | tf_op jit(solution)/shard_map/ppermute | solution.py:252
  90.5 6.7 %collective-permute-start.23 = (f32[32,768]{1,0:T(8,128)S(1)}, f32[32,768]{1,0:T(8,128)S(1)}, u32[]{:S(2)}, u32[]{:S(2)}) collective-permute-start(f32[32,768]{1,0:T(8,128)S(1)} %shard_map.107.vectors.current), channel_id=1, source_target_pairs={{0,4},{1,13},{2,6},{3,15},{4,8},{5,1},{6,10},{7,3},{8,12},{9,5},{1... | collective-permute-start | bytes 294920 | tf_op jit(solution)/shard_map/ppermute | solution.py:253
  97.7 1.3 %collective-permute-start.25 = (f32[32,768]{1,0:T(8,128)S(1)}, f32[32,768]{1,0:T(8,128)S(1)}, u32[]{:S(2)}, u32[]{:S(2)}) collective-permute-start(f32[32,768]{1,0:T(8,128)S(1)} %shard_map.110.partial), channel_id=1, source_target_pairs={{0,1},{1,0},{2,3},{3,2},{4,5},{5,4},{6,7},{7,6},{8,9},{9,8},{10,11... | collective-permute-start | bytes 294920 | tf_op jit(solution)/shard_map/ppermute | solution.py:262
  99.6 7.4 %collective-permute-start.28 = (f32[32,768]{1,0:T(8,128)S(1)}, f32[32,768]{1,0:T(8,128)S(1)}, u32[]{:S(2)}, u32[]{:S(2)}) collective-permute-start(f32[32,768]{1,0:T(8,128)S(1)} %shard_map.111.vectors.pair), channel_id=1, source_target_pairs={{0,2},{1,15},{2,4},{3,1},{4,6},{5,3},{6,8},{7,5},{8,10},{9,7},{10,... | collective-permute-start | bytes 294920 | tf_op jit(solution)/shard_map/ppermute | solution.py:252
  100.7 6.7 %collective-permute-start.27 = (f32[32,768]{1,0:T(8,128)S(1)}, f32[32,768]{1,0:T(8,128)S(1)}, u32[]{:S(2)}, u32[]{:S(2)}) collective-permute-start(f32[32,768]{1,0:T(8,128)S(1)} %shard_map.111.vectors.pair), channel_id=1, source_target_pairs={{0,4},{1,13},{2,6},{3,15},{4,8},{5,1},{6,10},{7,3},{8,12},{9,5},{1... | collective-permute-start | bytes 294920 | tf_op jit(solution)/shard_map/ppermute | solution.py:253
  100.7 7.2 %collective-permute-start.26 = (f32[32,384]{1,0:T(8,128)S(1)}, f32[32,384]{1,0:T(8,128)S(1)}, u32[]{:S(2)}, u32[]{:S(2)}) collective-permute-start(f32[32,384]{1,0:T(8,128)S(1)} %slice.4.vectors), channel_id=1, source_target_pairs={{0,16},{1,17},{2,18},{3,19},{4,20},{5,21},{6,22},{7,23},{8,24},{9,... | collective-permute-start | bytes 147464 | tf_op jit(solution)/shard_map/ppermute | solution.py:272
  107.4 5.2 %copy-start.3 = (s32[1,8,2]{1,2,0:T(2,128)S(1)}, s32[1,8,2]{1,2,0:T(2,128)}, u32[]{:S(2)}) copy-start(s32[1,8,2]{1,2,0:T(2,128)} %param.11) | copy-start | bytes 196
  109.1 13.5 %all-to-all-start = ((f32[16,32,128]{2,1,0:T(8,128)}), f32[16,32,128]{2,1,0:T(8,128)S(1)}, u32[]{:S(2)}, u32[]{:S(2)}) async-start(f32[16,32,128]{2,1,0:T(8,128)} %broadcast_in_dim.12), calls=%async_computation | async-start | bytes 524288 | tf_op jit(solution)/shard_map/all_to_all | solution.py:281

commit v2 on v1

v2 whole, which is shorter than its diff:
```python
import functools
import math

import jax
import jax.numpy as jnp
from jax import lax
from jax.experimental import pallas as pl
from jax.experimental.pallas import tpu as pltpu
from jax.sharding import PartitionSpec as P

DEG = 8
REACH = 12
F32 = jnp.float32
BF16 = jnp.bfloat16
NN = (((1,), (0,)), ((), ()))
NT = (((1,), (1,)), ((), ()))
VMEM = pl.BlockSpec(memory_space=pltpu.VMEM)
SMEM = pl.BlockSpec(memory_space=pltpu.SMEM)
HBM = pl.BlockSpec(memory_space=pltpu.HBM)
PARAMS = pltpu.CompilerParams(vmem_limit_bytes=24 * 2**20)


def column_of(slot, core, rows):
    pair = 2 * rows
    if slot >= 2 * pair:
        return core * rows + slot - 2 * pair
    chip, block = divmod(slot, pair)
    natural = (block + core * rows) % pair
    return natural - (chip + 1) * pair if core == 0 else natural + (chip + 1) * pair


def sent_slots(rows):
    pair = 2 * rows
    return [s for s in range(5 * rows) if not pair <= s < pair + rows]


def gather_kernel(where, pattern, tiles, sent, table, zeros, sems, *, rows, stored, total):
    pair = 2 * rows
    span = 2 * REACH + pair
    core = where[0] % 2
    first = (where[0] // 2) * pair
    zeros[...] = jnp.zeros_like(zeros)
    slots = sent_slots(rows)
    for row in range(rows):
        for entry in range(span):
            table[row * span + entry] = -1
        for k in range(stored):
            column = pattern[row, k] - first
            column = jnp.where(column >= total // 2, column - total, column)
            column = jnp.where(column < -(total // 2), column + total, column)
            table[row * span + column + REACH] = k
        for place, slot in enumerate(slots):
            column = jnp.where(core == 0, column_of(slot, 1, rows), column_of(slot, 0, rows))
            k = table[row * span + column + REACH]

            @pl.when(k >= 0)
            def _():
                pltpu.make_async_copy(tiles.at[row, k], sent.at[place, row], sems.at[place, row]).start()

            @pl.when(k < 0)
            def _():
                pltpu.make_async_copy(zeros, sent.at[place, row], sems.at[place, row]).start()

    for row in range(rows):
        for place in range(len(slots)):
            pltpu.make_async_copy(zeros, sent.at[place, row], sems.at[place, row]).wait()


def place_of(slot, rows):
    return divmod(slot, 2 * rows)


def store_tile(tile, high, low, place, lane):
    tile = tile.T
    top = tile.astype(BF16)
    rest = (tile - top.astype(F32)).astype(BF16)
    width = tile.shape[0]
    high[place * width : (place + 1) * width, lane * width : (lane + 1) * width] = top
    low[place * width : (place + 1) * width, lane * width : (lane + 1) * width] = rest


def own_weights_kernel(where, table, tiles, *weights, rows):
    span = 2 * REACH + 2 * rows
    core = where[0] % 2
    for slot in range(5 * rows):
        group, place = place_of(slot, rows)
        for row in range(rows):
            column = jnp.where(core == 0, column_of(slot, 0, rows), column_of(slot, 1, rows))
            k = table[row * span + column + REACH]
            tile = tiles[row, jnp.maximum(k, 0)]
            store_tile(jnp.where(k >= 0, tile, 0.0), *weights[2 * group : 2 * group + 2], place, row)


def other_weights_kernel(received, *refs, rows):
    weights = refs[len(refs) // 2 :]
    places = sent_slots(rows)
    width = received.shape[2]
    for slot in range(5 * rows):
        group, place = place_of(slot, rows)
        for row in range(rows):
            if slot in places:
                tile = received[places.index(slot), row]
            else:
                tile = jnp.zeros((width, width), F32)
            store_tile(tile, *weights[2 * group : 2 * group + 2], place, rows + row)


def multiply(vectors, high, low):
    count = vectors.shape[0]
    top = vectors.astype(BF16)
    rest = (vectors - top.astype(F32)).astype(BF16)
    both = jnp.concatenate([top, rest], axis=0)
    by_high = lax.dot_general(both, high[...], NN, preferred_element_type=F32)
    by_low = lax.dot_general(top, low[...], NN, preferred_element_type=F32)
    return by_high[:count] + (by_high[count:] + by_low)


def own_kernel(vectors, high, low, out):
    out[...] = multiply(vectors[:, : high.shape[0]], high, low)


def add_kernel(vectors, before, high, low, out):
    out[...] = before[...] + multiply(vectors[...], high, low)


def join_kernel(first, second, out, *, half):
    out[:, :half] = first[...]
    out[:, half:] = second[...]


def step_kernel(factors, partial, other, current, previous, out, *, half, first):
    image = partial[:, :half] + other[:, half:], partial[:, half:] + other[:, :half]
    scale = factors[0:1, 0:1]
    shift = factors[1:2, 0:1]
    for number, part in enumerate(image):
        lanes = slice(number * half, (number + 1) * half)
        value = scale * part - shift * current[:, lanes]
        out[:, lanes] = value if first else 2.0 * value - previous[:, lanes]


def dot(a, b, dims):
    return lax.dot_general(a, b, dims, precision=lax.Precision.HIGHEST, preferred_element_type=F32)


def pack(square):
    count = square.shape[0]
    strip = count * count // 128
    return jnp.concatenate([square[i * strip : (i + 1) * strip] for i in range(count // strip)], axis=1)


def unpack(rows, count):
    return jnp.concatenate([rows[:, i : i + count] for i in range(0, 128, count)], axis=0)


def gram_kernel(where, pairs, pair, lower, packed, chosen, *, half):
    own = pair[:, :half]
    below = lower[...]
    squares = [dot(own, own, NT), dot(below, below, NT), dot(below, own, NT)]
    packed[...] = jnp.concatenate([pack(square) for square in squares], axis=0)
    row = lax.broadcasted_iota(jnp.int32, chosen.shape, 0)
    column = lax.broadcasted_iota(jnp.int32, chosen.shape, 1)
    total = jnp.zeros(chosen.shape, F32)
    for p in range(pairs.shape[1]):
        total = total + ((row == pairs[1, p]) & (column == pairs[0, p])).astype(F32)
    chosen[...] = jnp.where(where[1] == 0, 0.0, total)


def cross_kernel(pair, partial, packed, out):
    every = jnp.concatenate([packed[...], pack(dot(pair[...], partial[...], NT))], axis=0)
    for device in range(out.shape[0]):
        out[device] = every


def summed(parts):
    total = parts[0]
    for device in range(1, parts.shape[0]):
        total = total + parts[device]
    return total


def inverses(gram, gram_below):
    count = gram.shape[0]
    block = 8
    row = lax.broadcasted_iota(jnp.int32, (count, count), 0)
    column = lax.broadcasted_iota(jnp.int32, (count, count), 1)
    eye = (row == column).astype(F32)
    work = jnp.concatenate([gram, eye, gram_below, eye], axis=1)
    sub = lax.broadcasted_iota(jnp.int32, work.shape, 0)
    left = lax.broadcasted_iota(jnp.int32, work.shape, 1) < 2 * count

    def spread(values, k):
        return jnp.where(left[: values.shape[0]], values[:, k : k + 1], values[:, 2 * count + k : 2 * count + k + 1])

    for k in range(0, count, block):
        rows = [work[k + i : k + i + 1, :] for i in range(block)]
        corner = [[spread(r, k + j) for j in range(block)] for r in rows]
        columns = [spread(work, k + j) for j in range(block)]
        for i in range(block):
            pivot = 1.0 / corner[i][i]
            factor = jnp.where(sub > k + i, columns[i] * pivot, 0.0)
            work = work - factor * rows[i]
            for j in range(i + 1, block):
                columns[j] = columns[j] - factor * corner[i][j]
                ratio = corner[j][i] * pivot
                rows[j] = rows[j] - ratio * rows[i]
                for m in range(i + 1, block):
                    corner[j][m] = corner[j][m] - ratio * corner[i][m]

    def scaled(start):
        pivots = jnp.sum(eye * work[:, start : start + count], axis=1, keepdims=True)
        return work[:, start + count : start + 2 * count] * (1.0 / jnp.sqrt(pivots))

    return scaled(0), scaled(2 * count)


def finish_kernel(parts, chosen, vectors, lower, filtered, projected, *, order):
    count = vectors.shape[0]
    total = summed(parts)
    strip = count * count // 128
    gram, gram_below, mixed, cross = (unpack(total[i * strip : (i + 1) * strip], count) for i in range(4))
    inverse, inverse_below = inverses(gram, gram_below)
    correlation = dot(dot(inverse_below, mixed, NN), inverse, NT)
    projected[...] = dot(dot(inverse, cross, NN), inverse, NT)
    some = jnp.max(chosen[...]) > 0.0
    removal = jnp.where(some, dot((chosen[...] * correlation).T, inverse_below, NN), 0.0)
    filtered[...] = math.sqrt(order) * (dot(inverse, vectors[...], NN) - dot(removal, lower[...], NN))


def call(kernel, out_shape, in_specs, out_specs, **options):
    options.setdefault("compiler_params", PARAMS)
    options.setdefault("cost_estimate", pl.CostEstimate(flops=10**6, bytes_accessed=10**5, transcendentals=0))
    return pl.pallas_call(kernel, out_shape=out_shape, in_specs=in_specs, out_specs=out_specs, **options)


def local(block_tiles, tile_pattern, start_vectors, centers, halfwidths, dup_pairs):
    rows, stored, width, _ = block_tiles.shape
    devices = lax.axis_size("row")
    cuts = lax.axis_size("cuts")
    chips = devices // 2
    total = rows * devices
    pair = 2 * rows
    half = rows * width
    whole = 2 * half
    initial = start_vectors[0]
    count = initial.shape[0]
    me = lax.axis_index("row")
    where = jnp.stack([me, lax.axis_index("cuts")]).astype(jnp.int32)
    factors = jnp.broadcast_to(jnp.concatenate([1.0 / halfwidths, centers / halfwidths])[:, None], (2, 128))

    swap = [(i, i ^ 1) for i in range(devices)]
    below = [(s, (s + 1) % cuts) for s in range(cuts)]

    def toward(steps):
        return [(i, (i + (2 * steps if i % 2 == 0 else -2 * steps)) % devices) for i in range(devices)]

    nearer, farther = toward(1), toward(2)
    span = 2 * REACH + pair
    places = len(sent_slots(rows))
    shapes = tuple(
        jax.ShapeDtypeStruct((depth * width, whole), BF16) for depth in (pair, pair, rows) for _ in range(2)
    )
    vec = jax.ShapeDtypeStruct((count, whole), F32)

    beside = lax.ppermute(initial, "row", swap)
    sent, table = call(
        functools.partial(gather_kernel, rows=rows, stored=stored, total=total),
        (
            jax.ShapeDtypeStruct((places, rows, width, width), F32),
            jax.ShapeDtypeStruct((rows * span,), jnp.int32),
        ),
        [SMEM, SMEM, HBM],
        (VMEM, SMEM),
        scratch_shapes=[pltpu.VMEM((width, width), F32), pltpu.SemaphoreType.DMA((places, rows))],
    )(where, tile_pattern, pltpu.with_memory_space_constraint(block_tiles, pltpu.HBM))
    sent, beside = lax.optimization_barrier((sent, beside))
    received = lax.ppermute(sent, "row", swap)
    weights = call(
        functools.partial(own_weights_kernel, rows=rows), shapes, [SMEM, SMEM, VMEM], (VMEM,) * 6
    )(where, table, block_tiles)
    weights = call(
        functools.partial(other_weights_kernel, rows=rows),
        shapes,
        [VMEM] * 7,
        (VMEM,) * 6,
        input_output_aliases={1 + i: i for i in range(6)},
    )(received, *weights)
    near_weights, far_weights, own_weights = weights[:2], weights[2:4], weights[4:]

    def part(kernel, group, *vectors):
        high, low = group
        depth = high.shape[0]
        return call(
            kernel,
            vec,
            [VMEM] * (len(vectors) + 2),
            VMEM,
            cost_estimate=pl.CostEstimate(
                flops=6 * count * depth * whole, bytes_accessed=4 * depth * whole, transcendentals=0
            ),
        )(*vectors, high, low)

    def apply_part(vectors):
        near = lax.ppermute(vectors, "row", nearer)
        far = lax.ppermute(vectors, "row", farther)
        partial = part(own_kernel, own_weights, vectors)
        partial = part(add_kernel, far_weights, far, partial)
        return part(add_kernel, near_weights, near, partial)

    current = call(functools.partial(join_kernel, half=half), vec, [VMEM, VMEM], VMEM)(initial, beside)
    previous = current
    for degree in range(DEG):
        partial = apply_part(current)
        other = lax.ppermute(partial, "row", swap)
        following = call(
            functools.partial(step_kernel, half=half, first=degree == 0),
            vec,
            [VMEM] * 5,
            VMEM,
        )(factors, partial, other, current, previous)
        previous, current = current, following

    own = current[:, :half]
    strip = count * count // 128
    lower = lax.ppermute(own, "cuts", below)
    partial = apply_part(current)
    small = jax.ShapeDtypeStruct((count, count), F32)
    lower, partial = lax.optimization_barrier((lower, partial))
    packed, chosen = call(
        functools.partial(gram_kernel, half=half),
        (jax.ShapeDtypeStruct((3 * strip, 128), F32), small),
        [SMEM, SMEM, VMEM, VMEM],
        (VMEM, VMEM),
    )(where, dup_pairs[0].T, current, lower)
    products = call(
        cross_kernel, jax.ShapeDtypeStruct((devices, 4 * strip, 128), F32), [VMEM, VMEM, VMEM], VMEM
    )(current, partial, packed)
    parts = lax.all_to_all(products, "row", 0, 0, tiled=True)
    filtered, projected = call(
        functools.partial(finish_kernel, order=total * width),
        (jax.ShapeDtypeStruct((count, half), F32), small),
        [VMEM] * 4,
        (VMEM, VMEM),
    )(parts, chosen, own, lower)
    return (filtered[None], projected[None])


def solution(mesh):
    in_specs = (
        P("row", None, None, None),
        P("row", None),
        P("cuts", None, "row"),
        P("cuts"),
        P("cuts"),
        P("cuts", None, None),
    )
    out_specs = (P("cuts", None, "row"), P("cuts", None, None))
    return jax.shard_map(local, mesh=mesh, in_specs=in_specs, out_specs=out_specs, check_vma=False)
```

time: 128 us -> 110 us (0.86)
  blocking collectives: 0 us -> 13.2 us
  starting transfers between devices: 22.2 us -> 9.4 us
  Pallas kernels: 29.6 us -> 21.2 us
  waiting for transfers between devices: 69 us -> 62 us
  local copies, waits for them, and re-layouts: 3.85 us -> 1.56 us
    ppermute x9, waiting for transfers between devices: 0.52 us -> 45.8 us  [apply_part(): far = lax.ppermute(vectors, 'row', farther)]
    ppermute x9, waiting for transfers between devices: 44.1 us -> 5.81 us  [apply_part(): near = lax.ppermute(vectors, 'row', nearer)]
    all_to_all x0 -> x1, blocking collectives: none -> 13.2 us  [local(): parts = lax.all_to_all(products, 'row', 0, 0, tiled=True)]
    all_to_all x1 -> x0, waiting for transfers between devices: 9.91 us -> none  [local(): parts = lax.all_to_all(spread, 'row', 0, 0, tiled=True)]
    ppermute x9, starting transfers between devices: 11.9 us -> 2.34 us  [apply_part(): near = lax.ppermute(vectors, 'row', nearer)]
    ppermute x2, waiting for transfers between devices: 4.3 us -> 0.02 us  [the longest x1 0.02 us: local(): lower = lax.ppermute(own, 'cuts', below)]
    pallas_call x8, Pallas kernels: 4.58 us -> 0.44 us  [local(): call(functools.partial(step_kernel, half=half, first=degree == 0), vec, [...]
    all_to_all x1 -> x0, starting transfers between devices: 3.53 us -> none  [local(): parts = lax.all_to_all(spread, 'row', 0, 0, tiled=True)]
  transfers between devices with their start and end apart: 30 -> 29, of which waited for: 20 -> 26; matrix products, arithmetic and copies ran while one was open for 1% -> 0% of each run, Pallas kernels for 7% -> 12%
where the time goes in v2:
time: 110 us
  waiting for transfers between devices  62 us (56%)
  Pallas kernels  21.2 us (19%)
  blocking collectives  13.2 us (12%)
  starting transfers between devices  9.4 us (9%)
  between operations  2.36 us (2%)
  local copies, waits for them, and re-layouts  1.56 us (1%)
    ppermute x9, waiting for transfers between devices, apply_part(): far = lax.ppermute(vectors, 'row', farther)  45.8 us
    all_to_all x1, blocking collectives, local(): parts = lax.all_to_all(products, 'row', 0, 0, tiled=True)  13.2 us
    pallas_call x27, Pallas kernels, part(): call(kernel, vec, [VMEM] * (len(vectors) + 2), VMEM, cost_estimate=pl.Cos...  11.3 us
    ppermute x8, waiting for transfers between devices, local(): other = lax.ppermute(partial, 'row', swap)  10.3 us
    ppermute x9, waiting for transfers between devices, apply_part(): near = lax.ppermute(vectors, 'row', nearer)  5.81 us
    ppermute x9, starting transfers between devices, apply_part(): far = lax.ppermute(vectors, 'row', farther)  4.7 us
    pallas_call x1, Pallas kernels, local(): call(functools.partial(gather_kernel, rows=rows, stored=stored, total=tot...  3.56 us
    pallas_call x1, Pallas kernels, local(): call(functools.partial(finish_kernel, order=total * width), (jax.ShapeDty...  2.52 us
  transfers between devices with their start and end apart: 29, of which 26 were waited for; matrix products, arithmetic and copies ran while one was open for 0% of the time, Pallas kernels for 12%

profile of v2, /device:TPU:0, one launch (start us, length us, event | category | flops | bytes accessed | tf_op | source)
XLA Modules:
  0.0 109.8 jit_solution(3333880184636189606)
XLA Ops:
  0.6 0.5 collective-permute-start
  1.2 0.7 copy-done.2
  1.9 3.6 %shard_map.77 = (f32[12,3,128,128]{3,2,1,0:T(8,128)S(1)}, s32[90]{0:T(128)S(1)}) custom-call(s32[2]{0:T(128)S(1)} %pad_add_fusion.where, s32[3,24]{1,0:T(4,128)S(1)} %copy-done.2, f32[3,24,128,128]{3,2,1,0:T(8,128)} %tiles.3), custom_call_target="tpu_custom_call" | custom-call | flops 1000000 | bytes 100000 | tf_op jit(solution)/shard_map/pallas_call | solution.py:265
  5.6 0.8 copy-done.1
  6.4 3.1 %collective-permute-start.2 = (f32[32,768]{1,0:T(8,128)S(1)}, f32[32,768]{1,0:T(8,128)S(1)}, u32[]{:S(2)}, u32[]{:S(2)}) collective-permute-start(f32[32,768]{1,0:T(8,128)S(1)} %shard_map.78.vectors.current.previous), channel_id=1, source_target_pairs={{0,4},{1,13},{2,6},{3,15},{4,8},{5,1},{6,10},{7,3},{8,12},{9,5},{1... | collective-permute-start | bytes 294920 | tf_op jit(solution)/shard_map/ppermute | solution.py:304
  9.6 1.4 %collective-permute-start.1 = (f32[32,768]{1,0:T(8,128)S(1)}, f32[32,768]{1,0:T(8,128)S(1)}, u32[]{:S(2)}, u32[]{:S(2)}) collective-permute-start(f32[32,768]{1,0:T(8,128)S(1)} %shard_map.78.vectors.current.previous), channel_id=1, source_target_pairs={{0,2},{1,15},{2,4},{3,1},{4,6},{5,3},{6,8},{7,5},{8,10},{9,7},{10,... | collective-permute-start | bytes 294920 | tf_op jit(solution)/shard_map/ppermute | solution.py:303
  12.4 1.4 %shard_map.79 = (bf16[768,768]{1,0:T(8,128)(2,1)S(1)}, bf16[768,768]{1,0:T(8,128)(2,1)S(1)}, bf16[768,768]{1,0:T(8,128)(2,1)S(1)}, bf16[768,768]{1,0:T(8,128)(2,...) custom-call(s32[2]{0:T(128)S(1)} %pad_add_fusion.where, s32[90]{0:T(128)S(1)} %get-tuple-element.27.table, ...), custom_call_target="tpu_custom_call" | custom-call | flops 1000000 | bytes 100000 | tf_op jit(solution)/shard_map/pallas_call | solution.py:277
  13.8 0.7 shard_map.80
  15.1 0.5 shard_map.82.before
  15.6 1.3 %collective-permute-done.1.vectors = f32[32,768]{1,0:T(8,128)S(1)} collective-permute-done((f32[32,768]{1,0:T(8,128)S(1)}, f32[32,768]{1,0:T(8,128)S(1)}, u32[]{:S(2)}, u32[]{:S(2)}) %collective-permute-start.1) | collective-permute-done | bytes 98336 | tf_op jit(solution)/shard_map/ppermute | solution.py:303
  16.9 0.5 shard_map.83.partial
  17.5 1.2 %collective-permute-done.4.other = f32[32,768]{1,0:T(8,128)S(1)} collective-permute-done((f32[32,768]{1,0:T(8,128)S(1)}, f32[32,768]{1,0:T(8,128)S(1)}, u32[]{:S(2)}, u32[]{:S(2)}) %collective-permute-start.4) | collective-permute-done | bytes 98336 | tf_op jit(solution)/shard_map/ppermute | solution.py:313
  18.8 1.2 %collective-permute-start.6 = (f32[32,768]{1,0:T(8,128)S(1)}, f32[32,768]{1,0:T(8,128)S(1)}, u32[]{:S(2)}, u32[]{:S(2)}) collective-permute-start(f32[32,768]{1,0:T(8,128)S(1)} %shard_map.84.vectors.current.previous), channel_id=1, source_target_pairs={{0,4},{1,13},{2,6},{3,15},{4,8},{5,1},{6,10},{7,3},{8,12},{9,5},{1... | collective-permute-start | bytes 294920 | tf_op jit(solution)/shard_map/ppermute | solution.py:304
  20.0 0.5 collective-permute-start.5
  20.8 4.7 %collective-permute-done.6.vectors = f32[32,768]{1,0:T(8,128)S(1)} collective-permute-done((f32[32,768]{1,0:T(8,128)S(1)}, f32[32,768]{1,0:T(8,128)S(1)}, u32[]{:S(2)}, u32[]{:S(2)}) %collective-permute-start.6) | collective-permute-done | bytes 98336 | tf_op jit(solution)/shard_map/ppermute | solution.py:304
  25.5 0.5 shard_map.86.before
  26.0 1.3 %collective-permute-done.5.vectors = f32[32,768]{1,0:T(8,128)S(1)} collective-permute-done((f32[32,768]{1,0:T(8,128)S(1)}, f32[32,768]{1,0:T(8,128)S(1)}, u32[]{:S(2)}, u32[]{:S(2)}) %collective-permute-start.5) | collective-permute-done | bytes 98336 | tf_op jit(solution)/shard_map/ppermute | solution.py:303
  27.3 0.5 shard_map.87.partial
  27.8 1.3 %collective-permute-done.7.other = f32[32,768]{1,0:T(8,128)S(1)} collective-permute-done((f32[32,768]{1,0:T(8,128)S(1)}, f32[32,768]{1,0:T(8,128)S(1)}, u32[]{:S(2)}, u32[]{:S(2)}) %collective-permute-start.7) | collective-permute-done | bytes 98336 | tf_op jit(solution)/shard_map/ppermute | solution.py:313
  29.3 0.3 shard_map.89.before
  29.6 6.0 %collective-permute-done.9.vectors = f32[32,768]{1,0:T(8,128)S(1)} collective-permute-done((f32[32,768]{1,0:T(8,128)S(1)}, f32[32,768]{1,0:T(8,128)S(1)}, u32[]{:S(2)}, u32[]{:S(2)}) %collective-permute-start.9) | collective-permute-done | bytes 98336 | tf_op jit(solution)/shard_map/ppermute | solution.py:304
  35.6 0.5 shard_map.90.before
  36.1 0.5 collective-permute-done.8.vectors
  36.6 0.5 shard_map.91.partial
  37.1 1.3 %collective-permute-done.10.other = f32[32,768]{1,0:T(8,128)S(1)} collective-permute-done((f32[32,768]{1,0:T(8,128)S(1)}, f32[32,768]{1,0:T(8,128)S(1)}, u32[]{:S(2)}, u32[]{:S(2)}) %collective-permute-start.10) | collective-permute-done | bytes 98336 | tf_op jit(solution)/shard_map/ppermute | solution.py:313
  38.6 0.3 shard_map.93.before
  38.9 6.0 %collective-permute-done.12.vectors = f32[32,768]{1,0:T(8,128)S(1)} collective-permute-done((f32[32,768]{1,0:T(8,128)S(1)}, f32[32,768]{1,0:T(8,128)S(1)}, u32[]{:S(2)}, u32[]{:S(2)}) %collective-permute-start.12) | collective-permute-done | bytes 98336 | tf_op jit(solution)/shard_map/ppermute | solution.py:304
  44.9 0.5 shard_map.94.before
  45.4 0.5 collective-permute-done.11.vectors
  45.9 0.5 shard_map.95.partial
  46.4 1.3 %collective-permute-done.13.other = f32[32,768]{1,0:T(8,128)S(1)} collective-permute-done((f32[32,768]{1,0:T(8,128)S(1)}, f32[32,768]{1,0:T(8,128)S(1)}, u32[]{:S(2)}, u32[]{:S(2)}) %collective-permute-start.13) | collective-permute-done | bytes 98336 | tf_op jit(solution)/shard_map/ppermute | solution.py:313
  47.9 0.3 shard_map.97.before
  48.2 6.1 %collective-permute-done.15.vectors = f32[32,768]{1,0:T(8,128)S(1)} collective-permute-done((f32[32,768]{1,0:T(8,128)S(1)}, f32[32,768]{1,0:T(8,128)S(1)}, u32[]{:S(2)}, u32[]{:S(2)}) %collective-permute-start.15) | collective-permute-done | bytes 98336 | tf_op jit(solution)/shard_map/ppermute | solution.py:304
  54.2 0.5 shard_map.98.before
  54.7 0.5 collective-permute-done.14.vectors
  55.2 0.5 shard_map.99.partial
  55.7 1.3 %collective-permute-done.16.other = f32[32,768]{1,0:T(8,128)S(1)} collective-permute-done((f32[32,768]{1,0:T(8,128)S(1)}, f32[32,768]{1,0:T(8,128)S(1)}, u32[]{:S(2)}, u32[]{:S(2)}) %collective-permute-start.16) | collective-permute-done | bytes 98336 | tf_op jit(solution)/shard_map/ppermute | solution.py:313
  57.2 0.3 shard_map.101.before
  57.5 6.1 %collective-permute-done.18.vectors = f32[32,768]{1,0:T(8,128)S(1)} collective-permute-done((f32[32,768]{1,0:T(8,128)S(1)}, f32[32,768]{1,0:T(8,128)S(1)}, u32[]{:S(2)}, u32[]{:S(2)}) %collective-permute-start.18) | collective-permute-done | bytes 98336 | tf_op jit(solution)/shard_map/ppermute | solution.py:304
  63.5 0.5 shard_map.102.before
  64.0 0.5 collective-permute-done.17.vectors
  64.5 0.5 shard_map.103.partial
  65.0 1.3 %collective-permute-done.19.other = f32[32,768]{1,0:T(8,128)S(1)} collective-permute-done((f32[32,768]{1,0:T(8,128)S(1)}, f32[32,768]{1,0:T(8,128)S(1)}, u32[]{:S(2)}, u32[]{:S(2)}) %collective-permute-start.19) | collective-permute-done | bytes 98336 | tf_op jit(solution)/shard_map/ppermute | solution.py:313
  66.5 0.3 shard_map.105.before
  66.8 6.1 %collective-permute-done.21.vectors = f32[32,768]{1,0:T(8,128)S(1)} collective-permute-done((f32[32,768]{1,0:T(8,128)S(1)}, f32[32,768]{1,0:T(8,128)S(1)}, u32[]{:S(2)}, u32[]{:S(2)}) %collective-permute-start.21) | collective-permute-done | bytes 98336 | tf_op jit(solution)/shard_map/ppermute | solution.py:304
  72.8 0.5 shard_map.106.before
  73.3 0.5 collective-permute-done.20.vectors
  73.8 0.5 shard_map.107.partial
  74.3 1.3 %collective-permute-done.22.other = f32[32,768]{1,0:T(8,128)S(1)} collective-permute-done((f32[32,768]{1,0:T(8,128)S(1)}, f32[32,768]{1,0:T(8,128)S(1)}, u32[]{:S(2)}, u32[]{:S(2)}) %collective-permute-start.22) | collective-permute-done | bytes 98336 | tf_op jit(solution)/shard_map/ppermute | solution.py:313
  75.8 0.3 shard_map.109.before
  76.1 6.1 %collective-permute-done.24.vectors = f32[32,768]{1,0:T(8,128)S(1)} collective-permute-done((f32[32,768]{1,0:T(8,128)S(1)}, f32[32,768]{1,0:T(8,128)S(1)}, u32[]{:S(2)}, u32[]{:S(2)}) %collective-permute-start.24) | collective-permute-done | bytes 98336 | tf_op jit(solution)/shard_map/ppermute | solution.py:304
  82.1 0.5 shard_map.110.before
  82.6 0.5 collective-permute-done.23.vectors
  83.1 0.5 shard_map.111.partial
  83.6 1.3 %collective-permute-done.25.other = f32[32,768]{1,0:T(8,128)S(1)} collective-permute-done((f32[32,768]{1,0:T(8,128)S(1)}, f32[32,768]{1,0:T(8,128)S(1)}, u32[]{:S(2)}, u32[]{:S(2)}) %collective-permute-start.25) | collective-permute-done | bytes 98336 | tf_op jit(solution)/shard_map/ppermute | solution.py:313
  85.1 1.6 %collective-permute-start.26 = (f32[32,384]{1,0:T(8,128)S(1)}, f32[32,384]{1,0:T(8,128)S(1)}, u32[]{:S(2)}, u32[]{:S(2)}) collective-permute-start(f32[32,384]{1,0:T(8,128)S(1)} %slice.4.vectors), channel_id=1, source_target_pairs={{0,16},{16,0},{1,17},{17,1},{2,18},{18,2},{3,19},{19,3},{4,20},{20... | collective-permute-start | bytes 147464 | tf_op jit(solution)/shard_map/ppermute | solution.py:324
  87.0 4.5 %collective-permute-done.28.vectors = f32[32,768]{1,0:T(8,128)S(1)} collective-permute-done((f32[32,768]{1,0:T(8,128)S(1)}, f32[32,768]{1,0:T(8,128)S(1)}, u32[]{:S(2)}, u32[]{:S(2)}) %collective-permute-start.28) | collective-permute-done | bytes 98336 | tf_op jit(solution)/shard_map/ppermute | solution.py:304
  91.4 0.5 shard_map.114.before
  91.9 0.4 collective-permute-done.27.vectors
  92.4 0.5 shard_map.115.partial
  92.9 0.9 shard_map.116
  93.8 0.3 shard_map.117
  94.1 13.2 %all_to_all.5.parts = f32[16,32,128]{2,1,0:T(8,128)S(1)} all-to-all(f32[16,32,128]{2,1,0:T(8,128)S(1)} %shard_map.117), channel_id=1, replica_groups=mesh['cuts'=2,'row'=16] {'row'}, dimensions={0} | all-to-all | bytes 524288 | tf_op jit(solution)/shard_map/all_to_all | solution.py:337
  107.3 2.5 %shard_map.118 = (f32[32,384]{1,0:T(8,128)}, f32[32,32]{1,0:T(8,128)}) custom-call(f32[16,32,128]{2,1,0:T(8,128)S(1)} %all_to_all.5.parts, f32[32,32]{1,0:T(8,128)S(1)} %get-tuple-element.43.chosen, f32[32,384]{1,0:T(8,128)S(1)} %slice.4.vectors, f32[32,384]{1,0:T(8,128)S(1)} %collective-permute-done.26.lower), custom_call_target="tpu_custom_call" | custom-call | flops 1000000 | bytes 100000 | tf_op jit(solution)/shard_map/pallas_call | solution.py:338
  (49 shorter events, 2.9 us)
Async XLA Ops:
  0.6 4.8 %collective-permute-start = (f32[32,384]{1,0:T(8,128)}, f32[32,384]{1,0:T(8,128)S(1)}, u32[]{:S(2)}, u32[]{:S(2)}) collective-permute-start(f32[32,384]{1,0:T(8,128)} %bitcast.8), channel_id=1, source_target_pairs={{0,1},{1,0},{2,3},{3,2},{4,5},{5,4},{6,7},{7,6},{8,9},{9,8},{10,11... | collective-permute-start | bytes 147464 | tf_op jit(solution)/shard_map/ppermute | solution.py:264
  1.2 0.7 copy-start.2
  1.9 10.4 %copy-start = (f32[3,24,128,128]{3,2,1,0:T(8,128)S(1)}, f32[3,24,128,128]{3,2,1,0:T(8,128)}, u32[]{:S(2)}) copy-start(f32[3,24,128,128]{3,2,1,0:T(8,128)} %tiles.3) | copy-start | bytes 14155780
  5.5 8.3 %collective-permute-start.3 = (f32[12,3,128,128]{3,2,1,0:T(8,128)S(1)}, f32[12,3,128,128]{3,2,1,0:T(8,128)S(1)}, u32[]{:S(2)}, u32[]{:S(2)}) collective-permute-start(f32[12,3,128,128]{3,2,1,0:T(8,128)S(1)} %get-tuple-element.26), channel_id=1, source_target_pairs={{0,1},{1,0},{2,3},{3,2},{4,5},{5,4},{6,7},{7,6},{8,9},{9,8},{10,11... | collective-permute-start | bytes 7077896 | tf_op jit(solution)/shard_map/ppermute | solution.py:276
  5.6 0.8 copy-start.1
  6.4 8.7 %collective-permute-start.2 = (f32[32,768]{1,0:T(8,128)S(1)}, f32[32,768]{1,0:T(8,128)S(1)}, u32[]{:S(2)}, u32[]{:S(2)}) collective-permute-start(f32[32,768]{1,0:T(8,128)S(1)} %shard_map.78.vectors.current.previous), channel_id=1, source_target_pairs={{0,4},{1,13},{2,6},{3,15},{4,8},{5,1},{6,10},{7,3},{8,12},{9,5},{1... | collective-permute-start | bytes 294920 | tf_op jit(solution)/shard_map/ppermute | solution.py:304
  9.6 7.3 %collective-permute-start.1 = (f32[32,768]{1,0:T(8,128)S(1)}, f32[32,768]{1,0:T(8,128)S(1)}, u32[]{:S(2)}, u32[]{:S(2)}) collective-permute-start(f32[32,768]{1,0:T(8,128)S(1)} %shard_map.78.vectors.current.previous), channel_id=1, source_target_pairs={{0,2},{1,15},{2,4},{3,1},{4,6},{5,3},{6,8},{7,5},{8,10},{9,7},{10,... | collective-permute-start | bytes 294920 | tf_op jit(solution)/shard_map/ppermute | solution.py:303
  17.4 1.3 %collective-permute-start.4 = (f32[32,768]{1,0:T(8,128)S(1)}, f32[32,768]{1,0:T(8,128)S(1)}, u32[]{:S(2)}, u32[]{:S(2)}) collective-permute-start(f32[32,768]{1,0:T(8,128)S(1)} %shard_map.83.partial), channel_id=1, source_target_pairs={{0,1},{1,0},{2,3},{3,2},{4,5},{5,4},{6,7},{7,6},{8,9},{9,8},{10,11... | collective-permute-start | bytes 294920 | tf_op jit(solution)/shard_map/ppermute | solution.py:313
  18.8 6.7 %collective-permute-start.6 = (f32[32,768]{1,0:T(8,128)S(1)}, f32[32,768]{1,0:T(8,128)S(1)}, u32[]{:S(2)}, u32[]{:S(2)}) collective-permute-start(f32[32,768]{1,0:T(8,128)S(1)} %shard_map.84.vectors.current.previous), channel_id=1, source_target_pairs={{0,4},{1,13},{2,6},{3,15},{4,8},{5,1},{6,10},{7,3},{8,12},{9,5},{1... | collective-permute-start | bytes 294920 | tf_op jit(solution)/shard_map/ppermute | solution.py:304
  20.0 7.3 %collective-permute-start.5 = (f32[32,768]{1,0:T(8,128)S(1)}, f32[32,768]{1,0:T(8,128)S(1)}, u32[]{:S(2)}, u32[]{:S(2)}) collective-permute-start(f32[32,768]{1,0:T(8,128)S(1)} %shard_map.84.vectors.current.previous), channel_id=1, source_target_pairs={{0,2},{1,15},{2,4},{3,1},{4,6},{5,3},{6,8},{7,5},{8,10},{9,7},{10,... | collective-permute-start | bytes 294920 | tf_op jit(solution)/shard_map/ppermute | solution.py:303
  27.8 1.3 %collective-permute-start.7 = (f32[32,768]{1,0:T(8,128)S(1)}, f32[32,768]{1,0:T(8,128)S(1)}, u32[]{:S(2)}, u32[]{:S(2)}) collective-permute-start(f32[32,768]{1,0:T(8,128)S(1)} %shard_map.87.partial), channel_id=1, source_target_pairs={{0,1},{1,0},{2,3},{3,2},{4,5},{5,4},{6,7},{7,6},{8,9},{9,8},{10,11... | collective-permute-start | bytes 294920 | tf_op jit(solution)/shard_map/ppermute | solution.py:313
  29.1 6.5 %collective-permute-start.9 = (f32[32,768]{1,0:T(8,128)S(1)}, f32[32,768]{1,0:T(8,128)S(1)}, u32[]{:S(2)}, u32[]{:S(2)}) collective-permute-start(f32[32,768]{1,0:T(8,128)S(1)} %shard_map.88.vectors.current.previous), channel_id=1, source_target_pairs={{0,4},{1,13},{2,6},{3,15},{4,8},{5,1},{6,10},{7,3},{8,12},{9,5},{1... | collective-permute-start | bytes 294920 | tf_op jit(solution)/shard_map/ppermute | solution.py:304
  29.2 7.4 %collective-permute-start.8 = (f32[32,768]{1,0:T(8,128)S(1)}, f32[32,768]{1,0:T(8,128)S(1)}, u32[]{:S(2)}, u32[]{:S(2)}) collective-permute-start(f32[32,768]{1,0:T(8,128)S(1)} %shard_map.88.vectors.current.previous), channel_id=1, source_target_pairs={{0,2},{1,15},{2,4},{3,1},{4,6},{5,3},{6,8},{7,5},{8,10},{9,7},{10,... | collective-permute-start | bytes 294920 | tf_op jit(solution)/shard_map/ppermute | solution.py:303
  37.1 1.3 %collective-permute-start.10 = (f32[32,768]{1,0:T(8,128)S(1)}, f32[32,768]{1,0:T(8,128)S(1)}, u32[]{:S(2)}, u32[]{:S(2)}) collective-permute-start(f32[32,768]{1,0:T(8,128)S(1)} %shard_map.91.partial), channel_id=1, source_target_pairs={{0,1},{1,0},{2,3},{3,2},{4,5},{5,4},{6,7},{7,6},{8,9},{9,8},{10,11... | collective-permute-start | bytes 294920 | tf_op jit(solution)/shard_map/ppermute | solution.py:313
  38.4 6.5 %collective-permute-start.12 = (f32[32,768]{1,0:T(8,128)S(1)}, f32[32,768]{1,0:T(8,128)S(1)}, u32[]{:S(2)}, u32[]{:S(2)}) collective-permute-start(f32[32,768]{1,0:T(8,128)S(1)} %shard_map.92.vectors.current.previous), channel_id=1, source_target_pairs={{0,4},{1,13},{2,6},{3,15},{4,8},{5,1},{6,10},{7,3},{8,12},{9,5},{1... | collective-permute-start | bytes 294920 | tf_op jit(solution)/shard_map/ppermute | solution.py:304
  38.5 7.4 %collective-permute-start.11 = (f32[32,768]{1,0:T(8,128)S(1)}, f32[32,768]{1,0:T(8,128)S(1)}, u32[]{:S(2)}, u32[]{:S(2)}) collective-permute-start(f32[32,768]{1,0:T(8,128)S(1)} %shard_map.92.vectors.current.previous), channel_id=1, source_target_pairs={{0,2},{1,15},{2,4},{3,1},{4,6},{5,3},{6,8},{7,5},{8,10},{9,7},{10,... | collective-permute-start | bytes 294920 | tf_op jit(solution)/shard_map/ppermute | solution.py:303
  46.4 1.3 %collective-permute-start.13 = (f32[32,768]{1,0:T(8,128)S(1)}, f32[32,768]{1,0:T(8,128)S(1)}, u32[]{:S(2)}, u32[]{:S(2)}) collective-permute-start(f32[32,768]{1,0:T(8,128)S(1)} %shard_map.95.partial), channel_id=1, source_target_pairs={{0,1},{1,0},{2,3},{3,2},{4,5},{5,4},{6,7},{7,6},{8,9},{9,8},{10,11... | collective-permute-start | bytes 294920 | tf_op jit(solution)/shard_map/ppermute | solution.py:313
  47.7 6.5 %collective-permute-start.15 = (f32[32,768]{1,0:T(8,128)S(1)}, f32[32,768]{1,0:T(8,128)S(1)}, u32[]{:S(2)}, u32[]{:S(2)}) collective-permute-start(f32[32,768]{1,0:T(8,128)S(1)} %shard_map.96.vectors.current.previous), channel_id=1, source_target_pairs={{0,4},{1,13},{2,6},{3,15},{4,8},{5,1},{6,10},{7,3},{8,12},{9,5},{1... | collective-permute-start | bytes 294920 | tf_op jit(solution)/shard_map/ppermute | solution.py:304
  47.8 7.4 %collective-permute-start.14 = (f32[32,768]{1,0:T(8,128)S(1)}, f32[32,768]{1,0:T(8,128)S(1)}, u32[]{:S(2)}, u32[]{:S(2)}) collective-permute-start(f32[32,768]{1,0:T(8,128)S(1)} %shard_map.96.vectors.current.previous), channel_id=1, source_target_pairs={{0,2},{1,15},{2,4},{3,1},{4,6},{5,3},{6,8},{7,5},{8,10},{9,7},{10,... | collective-permute-start | bytes 294920 | tf_op jit(solution)/shard_map/ppermute | solution.py:303
  55.7 1.3 %collective-permute-start.16 = (f32[32,768]{1,0:T(8,128)S(1)}, f32[32,768]{1,0:T(8,128)S(1)}, u32[]{:S(2)}, u32[]{:S(2)}) collective-permute-start(f32[32,768]{1,0:T(8,128)S(1)} %shard_map.99.partial), channel_id=1, source_target_pairs={{0,1},{1,0},{2,3},{3,2},{4,5},{5,4},{6,7},{7,6},{8,9},{9,8},{10,11... | collective-permute-start | bytes 294920 | tf_op jit(solution)/shard_map/ppermute | solution.py:313
  57.0 6.5 %collective-permute-start.18 = (f32[32,768]{1,0:T(8,128)S(1)}, f32[32,768]{1,0:T(8,128)S(1)}, u32[]{:S(2)}, u32[]{:S(2)}) collective-permute-start(f32[32,768]{1,0:T(8,128)S(1)} %shard_map.100.vectors.current.previous), channel_id=1, source_target_pairs={{0,4},{1,13},{2,6},{3,15},{4,8},{5,1},{6,10},{7,3},{8,12},{9,5},{1... | collective-permute-start | bytes 294920 | tf_op jit(solution)/shard_map/ppermute | solution.py:304
  57.1 7.4 %collective-permute-start.17 = (f32[32,768]{1,0:T(8,128)S(1)}, f32[32,768]{1,0:T(8,128)S(1)}, u32[]{:S(2)}, u32[]{:S(2)}) collective-permute-start(f32[32,768]{1,0:T(8,128)S(1)} %shard_map.100.vectors.current.previous), channel_id=1, source_target_pairs={{0,2},{1,15},{2,4},{3,1},{4,6},{5,3},{6,8},{7,5},{8,10},{9,7},{10,... | collective-permute-start | bytes 294920 | tf_op jit(solution)/shard_map/ppermute | solution.py:303
  65.0 1.3 %collective-permute-start.19 = (f32[32,768]{1,0:T(8,128)S(1)}, f32[32,768]{1,0:T(8,128)S(1)}, u32[]{:S(2)}, u32[]{:S(2)}) collective-permute-start(f32[32,768]{1,0:T(8,128)S(1)} %shard_map.103.partial), channel_id=1, source_target_pairs={{0,1},{1,0},{2,3},{3,2},{4,5},{5,4},{6,7},{7,6},{8,9},{9,8},{10,11... | collective-permute-start | bytes 294920 | tf_op jit(solution)/shard_map/ppermute | solution.py:313
  66.3 6.5 %collective-permute-start.21 = (f32[32,768]{1,0:T(8,128)S(1)}, f32[32,768]{1,0:T(8,128)S(1)}, u32[]{:S(2)}, u32[]{:S(2)}) collective-permute-start(f32[32,768]{1,0:T(8,128)S(1)} %shard_map.104.vectors.current.previous), channel_id=1, source_target_pairs={{0,4},{1,13},{2,6},{3,15},{4,8},{5,1},{6,10},{7,3},{8,12},{9,5},{1... | collective-permute-start | bytes 294920 | tf_op jit(solution)/shard_map/ppermute | solution.py:304
  66.4 7.4 %collective-permute-start.20 = (f32[32,768]{1,0:T(8,128)S(1)}, f32[32,768]{1,0:T(8,128)S(1)}, u32[]{:S(2)}, u32[]{:S(2)}) collective-permute-start(f32[32,768]{1,0:T(8,128)S(1)} %shard_map.104.vectors.current.previous), channel_id=1, source_target_pairs={{0,2},{1,15},{2,4},{3,1},{4,6},{5,3},{6,8},{7,5},{8,10},{9,7},{10,... | collective-permute-start | bytes 294920 | tf_op jit(solution)/shard_map/ppermute | solution.py:303
  74.3 1.3 %collective-permute-start.22 = (f32[32,768]{1,0:T(8,128)S(1)}, f32[32,768]{1,0:T(8,128)S(1)}, u32[]{:S(2)}, u32[]{:S(2)}) collective-permute-start(f32[32,768]{1,0:T(8,128)S(1)} %shard_map.107.partial), channel_id=1, source_target_pairs={{0,1},{1,0},{2,3},{3,2},{4,5},{5,4},{6,7},{7,6},{8,9},{9,8},{10,11... | collective-permute-start | bytes 294920 | tf_op jit(solution)/shard_map/ppermute | solution.py:313
  75.6 6.5 %collective-permute-start.24 = (f32[32,768]{1,0:T(8,128)S(1)}, f32[32,768]{1,0:T(8,128)S(1)}, u32[]{:S(2)}, u32[]{:S(2)}) collective-permute-start(f32[32,768]{1,0:T(8,128)S(1)} %shard_map.108.vectors.current), channel_id=1, source_target_pairs={{0,4},{1,13},{2,6},{3,15},{4,8},{5,1},{6,10},{7,3},{8,12},{9,5},{1... | collective-permute-start | bytes 294920 | tf_op jit(solution)/shard_map/ppermute | solution.py:304
  75.7 7.4 %collective-permute-start.23 = (f32[32,768]{1,0:T(8,128)S(1)}, f32[32,768]{1,0:T(8,128)S(1)}, u32[]{:S(2)}, u32[]{:S(2)}) collective-permute-start(f32[32,768]{1,0:T(8,128)S(1)} %shard_map.108.vectors.current), channel_id=1, source_target_pairs={{0,2},{1,15},{2,4},{3,1},{4,6},{5,3},{6,8},{7,5},{8,10},{9,7},{10,... | collective-permute-start | bytes 294920 | tf_op jit(solution)/shard_map/ppermute | solution.py:303
  83.5 1.3 %collective-permute-start.25 = (f32[32,768]{1,0:T(8,128)S(1)}, f32[32,768]{1,0:T(8,128)S(1)}, u32[]{:S(2)}, u32[]{:S(2)}) collective-permute-start(f32[32,768]{1,0:T(8,128)S(1)} %shard_map.111.partial), channel_id=1, source_target_pairs={{0,1},{1,0},{2,3},{3,2},{4,5},{5,4},{6,7},{7,6},{8,9},{9,8},{10,11... | collective-permute-start | bytes 294920 | tf_op jit(solution)/shard_map/ppermute | solution.py:313
  84.9 6.5 %collective-permute-start.28 = (f32[32,768]{1,0:T(8,128)S(1)}, f32[32,768]{1,0:T(8,128)S(1)}, u32[]{:S(2)}, u32[]{:S(2)}) collective-permute-start(f32[32,768]{1,0:T(8,128)S(1)} %shard_map.112.vectors.pair), channel_id=1, source_target_pairs={{0,4},{1,13},{2,6},{3,15},{4,8},{5,1},{6,10},{7,3},{8,12},{9,5},{1... | collective-permute-start | bytes 294920 | tf_op jit(solution)/shard_map/ppermute | solution.py:304
  85.0 7.4 %collective-permute-start.27 = (f32[32,768]{1,0:T(8,128)S(1)}, f32[32,768]{1,0:T(8,128)S(1)}, u32[]{:S(2)}, u32[]{:S(2)}) collective-permute-start(f32[32,768]{1,0:T(8,128)S(1)} %shard_map.112.vectors.pair), channel_id=1, source_target_pairs={{0,2},{1,15},{2,4},{3,1},{4,6},{5,3},{6,8},{7,5},{8,10},{9,7},{10,... | collective-permute-start | bytes 294920 | tf_op jit(solution)/shard_map/ppermute | solution.py:303
  85.1 7.8 %collective-permute-start.26 = (f32[32,384]{1,0:T(8,128)S(1)}, f32[32,384]{1,0:T(8,128)S(1)}, u32[]{:S(2)}, u32[]{:S(2)}) collective-permute-start(f32[32,384]{1,0:T(8,128)S(1)} %slice.4.vectors), channel_id=1, source_target_pairs={{0,16},{16,0},{1,17},{17,1},{2,18},{18,2},{3,19},{19,3},{4,20},{20... | collective-permute-start | bytes 147464 | tf_op jit(solution)/shard_map/ppermute | solution.py:324
  91.9 1.0 copy-start.3

commit v3 on v2

--- a/solution.py
+++ b/solution.py
@@ -34,36 +34,40 @@
     return [s for s in range(5 * rows) if not pair <= s < pair + rows]
 
 
-def gather_kernel(where, pattern, tiles, sent, table, zeros, sems, *, rows, stored, total):
+def offset_in_span(block, start, total):
+    offset = block - start
+    offset = jnp.where(offset < 0, offset + total, offset)
+    return jnp.where(offset >= total, offset - total, offset)
+
+
+def gather_kernel(pattern, tiles, sent, blocks, places, count, sems, *, rows, stored, total):
     pair = 2 * rows
     span = 2 * REACH + pair
-    core = where[0] % 2
-    first = (where[0] // 2) * pair
-    zeros[...] = jnp.zeros_like(zeros)
-    slots = sent_slots(rows)
+    copy = pltpu.make_async_copy(pattern, blocks, sems.at[0])
+    copy.start()
+    me = lax.axis_index("row")
+    core = me % 2
+    start = (me // 2) * pair - REACH
+    for offset in range(span):
+        places[offset] = -1
+    for place, slot in enumerate(sent_slots(rows)):
+        column = jnp.where(core == 0, column_of(slot, 1, rows), column_of(slot, 0, rows))
+        places[column + REACH] = place
+    count[0] = 0
+    sent[...] = jnp.zeros_like(sent)
+    copy.wait()
     for row in range(rows):
-        for entry in range(span):
-            table[row * span + entry] = -1
         for k in range(stored):
-            column = pattern[row, k] - first
-            column = jnp.where(column >= total // 2, column - total, column)
-            column = jnp.where(column < -(total // 2), column + total, column)
-            table[row * span + column + REACH] = k
-        for place, slot in enumerate(slots):
-            column = jnp.where(core == 0, column_of(slot, 1, rows), column_of(slot, 0, rows))
-            k = table[row * span + column + REACH]
-
-            @pl.when(k >= 0)
+            place = places[offset_in_span(blocks[row, k], start, total)]
+
+            @pl.when(place >= 0)
             def _():
-                pltpu.make_async_copy(tiles.at[row, k], sent.at[place, row], sems.at[place, row]).start()
-
-            @pl.when(k < 0)
-            def _():
-                pltpu.make_async_copy(zeros, sent.at[place, row], sems.at[place, row]).start()
-
-    for row in range(rows):
-        for place in range(len(slots)):
-            pltpu.make_async_copy(zeros, sent.at[place, row], sems.at[place, row]).wait()
+                count[0] += 1
+                pltpu.make_async_copy(tiles.at[row, k], sent.at[place, row], sems.at[1]).start()
+
+    @pl.loop(0, count[0])
+    def _(_):
+        pltpu.make_async_copy(tiles.at[0, 0], sent.at[0, 0], sems.at[1]).wait()
 
 
 def place_of(slot, rows):
@@ -79,9 +83,20 @@
     low[place * width : (place + 1) * width, lane * width : (lane + 1) * width] = rest
 
 
-def own_weights_kernel(where, table, tiles, *weights, rows):
+def own_weights_kernel(pattern, tiles, *refs, rows, stored, total):
+    weights, (blocks, table, sem) = refs[:6], refs[6:]
+    copy = pltpu.make_async_copy(pattern, blocks, sem)
+    copy.start()
     span = 2 * REACH + 2 * rows
-    core = where[0] % 2
+    me = lax.axis_index("row")
+    core = me % 2
+    start = (me // 2) * 2 * rows - REACH
+    for entry in range(rows * span):
+        table[entry] = -1
+    copy.wait()
+    for row in range(rows):
+        for k in range(stored):
+            table[row * span + offset_in_span(blocks[row, k], start, total)] = k
     for slot in range(5 * rows):
         group, place = place_of(slot, rows)
         for row in range(rows):
@@ -128,14 +143,32 @@
     out[:, half:] = second[...]
 
 
-def step_kernel(factors, partial, other, current, previous, out, *, half, first):
-    image = partial[:, :half] + other[:, half:], partial[:, half:] + other[:, :half]
+def halves(partial, other, half):
+    yield slice(0, half), partial[:, :half] + other[:, half:]
+    yield slice(half, 2 * half), partial[:, half:] + other[:, :half]
+
+
+def image_kernel(partial, other, out, *, half):
+    for lanes, image in halves(partial, other, half):
+        out[:, lanes] = image
+
+
+def second_kernel(factors, partial, other, image, initial, first, second, *, half):
     scale = factors[0:1, 0:1]
     shift = factors[1:2, 0:1]
-    for number, part in enumerate(image):
-        lanes = slice(number * half, (number + 1) * half)
-        value = scale * part - shift * current[:, lanes]
-        out[:, lanes] = value if first else 2.0 * value - previous[:, lanes]
+    for lanes, twice in halves(partial, other, half):
+        once = image[:, lanes]
+        start = initial[:, lanes]
+        value = scale * once - shift * start
+        first[:, lanes] = value
+        second[:, lanes] = 2.0 * (scale * (scale * twice - shift * once) - shift * value) - start
+
+
+def step_kernel(factors, partial, other, current, previous, out, *, half):
+    scale = factors[0:1, 0:1]
+    shift = factors[1:2, 0:1]
+    for lanes, image in halves(partial, other, half):
+        out[:, lanes] = 2.0 * (scale * image - shift * current[:, lanes]) - previous[:, lanes]
 
 
 def dot(a, b, dims):
@@ -152,7 +185,7 @@
     return jnp.concatenate([rows[:, i : i + count] for i in range(0, 128, count)], axis=0)
 
 
-def gram_kernel(where, pairs, pair, lower, packed, chosen, *, half):
+def gram_kernel(pairs, pair, lower, packed, chosen, *, half):
     own = pair[:, :half]
     below = lower[...]
     squares = [dot(own, own, NT), dot(below, below, NT), dot(below, own, NT)]
@@ -162,13 +195,17 @@
     total = jnp.zeros(chosen.shape, F32)
     for p in range(pairs.shape[1]):
         total = total + ((row == pairs[1, p]) & (column == pairs[0, p])).astype(F32)
-    chosen[...] = jnp.where(where[1] == 0, 0.0, total)
+    chosen[...] = jnp.where(lax.axis_index("cuts") == 0, 0.0, total)
 
 
 def cross_kernel(pair, partial, packed, out):
-    every = jnp.concatenate([packed[...], pack(dot(pair[...], partial[...], NT))], axis=0)
-    for device in range(out.shape[0]):
-        out[device] = every
+    out[...] = jnp.concatenate([packed[...], pack(dot(pair[...], partial[...], NT))], axis=0)
+
+
+def spread_kernel(one, other, out):
+    both = one[...] + other[...]
+    for chip in range(out.shape[0]):
+        out[chip] = both
 
 
 def summed(parts):
@@ -243,9 +280,6 @@
     whole = 2 * half
     initial = start_vectors[0]
     count = initial.shape[0]
-    me = lax.axis_index("row")
-    where = jnp.stack([me, lax.axis_index("cuts")]).astype(jnp.int32)
-    factors = jnp.broadcast_to(jnp.concatenate([1.0 / halfwidths, centers / halfwidths])[:, None], (2, 128))
 
     swap = [(i, i ^ 1) for i in range(devices)]
     below = [(s, (s + 1) % cuts) for s in range(cuts)]
@@ -262,21 +296,32 @@
     vec = jax.ShapeDtypeStruct((count, whole), F32)
 
     beside = lax.ppermute(initial, "row", swap)
-    sent, table = call(
+    sent = call(
         functools.partial(gather_kernel, rows=rows, stored=stored, total=total),
-        (
-            jax.ShapeDtypeStruct((places, rows, width, width), F32),
-            jax.ShapeDtypeStruct((rows * span,), jnp.int32),
-        ),
-        [SMEM, SMEM, HBM],
-        (VMEM, SMEM),
-        scratch_shapes=[pltpu.VMEM((width, width), F32), pltpu.SemaphoreType.DMA((places, rows))],
-    )(where, tile_pattern, pltpu.with_memory_space_constraint(block_tiles, pltpu.HBM))
+        jax.ShapeDtypeStruct((places, rows, width, width), F32),
+        [HBM, HBM],
+        VMEM,
+        scratch_shapes=[
+            pltpu.SMEM((rows, stored), jnp.int32),
+            pltpu.SMEM((span,), jnp.int32),
+            pltpu.SMEM((1,), jnp.int32),
+            pltpu.SemaphoreType.DMA((2,)),
+        ],
+        cost_estimate=pl.CostEstimate(flops=0, bytes_accessed=8 * 10**6, transcendentals=0),
+    )(*(pltpu.with_memory_space_constraint(array, pltpu.HBM) for array in (tile_pattern, block_tiles)))
     sent, beside = lax.optimization_barrier((sent, beside))
     received = lax.ppermute(sent, "row", swap)
     weights = call(
-        functools.partial(own_weights_kernel, rows=rows), shapes, [SMEM, SMEM, VMEM], (VMEM,) * 6
-    )(where, table, block_tiles)
+        functools.partial(own_weights_kernel, rows=rows, stored=stored, total=total),
+        shapes,
+        [HBM, VMEM],
+        (VMEM,) * 6,
+        scratch_shapes=[
+            pltpu.SMEM((rows, stored), jnp.int32),
+            pltpu.SMEM((rows * span,), jnp.int32),
+            pltpu.SemaphoreType.DMA,
+        ],
+    )(pltpu.with_memory_space_constraint(tile_pattern, pltpu.HBM), block_tiles)
     weights = call(
         functools.partial(other_weights_kernel, rows=rows),
         shapes,
@@ -307,17 +352,19 @@
         return part(add_kernel, near_weights, near, partial)
 
     current = call(functools.partial(join_kernel, half=half), vec, [VMEM, VMEM], VMEM)(initial, beside)
-    previous = current
-    for degree in range(DEG):
-        partial = apply_part(current)
-        other = lax.ppermute(partial, "row", swap)
-        following = call(
-            functools.partial(step_kernel, half=half, first=degree == 0),
-            vec,
-            [VMEM] * 5,
-            VMEM,
-        )(factors, partial, other, current, previous)
-        previous, current = current, following
+    def images(vectors):
+        partial = apply_part(vectors)
+        return partial, lax.ppermute(partial, "row", swap)
+
+    def step(kernel, out_shape, *operands):
+        out_specs = VMEM if out_shape is vec else (VMEM,) * len(out_shape)
+        return call(functools.partial(kernel, half=half), out_shape, [VMEM] * len(operands), out_specs)(*operands)
+
+    factors = jnp.broadcast_to(jnp.concatenate([1.0 / halfwidths, centers / halfwidths])[:, None], (2, 128))
+    image = step(image_kernel, vec, *images(current))
+    previous, current = step(second_kernel, (vec, vec), factors, *images(image), image, current)
+    for _ in range(DEG - 2):
+        previous, current = current, step(step_kernel, vec, factors, *images(current), current, previous)
 
     own = current[:, :half]
     strip = count * count // 128
@@ -328,13 +375,15 @@
     packed, chosen = call(
         functools.partial(gram_kernel, half=half),
         (jax.ShapeDtypeStruct((3 * strip, 128), F32), small),
-        [SMEM, SMEM, VMEM, VMEM],
+        [SMEM, VMEM, VMEM],
         (VMEM, VMEM),
-    )(where, dup_pairs[0].T, current, lower)
-    products = call(
-        cross_kernel, jax.ShapeDtypeStruct((devices, 4 * strip, 128), F32), [VMEM, VMEM, VMEM], VMEM
-    )(current, partial, packed)
-    parts = lax.all_to_all(products, "row", 0, 0, tiled=True)
+    )(dup_pairs[0].T, current, lower)
+    sums = jax.ShapeDtypeStruct((4 * strip, 128), F32)
+    products = call(cross_kernel, sums, [VMEM, VMEM, VMEM], VMEM)(current, partial, packed)
+    beside = lax.ppermute(products, "row", swap)
+    spread = call(spread_kernel, jax.ShapeDtypeStruct((chips, *sums.shape), F32), [VMEM, VMEM], VMEM)(products, beside)
+    same_core = [[2 * chip + core for chip in range(chips)] for core in range(2)]
+    parts = lax.all_to_all(spread, "row", 0, 0, tiled=True, axis_index_groups=same_core)
     filtered, projected = call(
         functools.partial(finish_kernel, order=total * width),
         (jax.ShapeDtypeStruct((count, half), F32), small),

time: 110 us -> 105 us (0.955)
  blocking collectives: 13.2 us -> 10.4 us
  local copies, waits for them, and re-layouts: 1.56 us -> 0.09 us
    all_to_all x1, blocking collectives: 13.2 us -> 10.4 us  [local(): lax.all_to_all(spread, 'row', 0, 0, tiled=True, axis_index_groups=same_core)]
    unnamed x8 -> x6, local copies, waits for them, and re-layouts: 1.49 us -> 0.01 us
    ppermute x8 -> x9, waiting for transfers between devices: 10.3 us -> 11.5 us  [the longest x8 10.3 us: images(): return (partial, lax.ppermute(partial, 'row', swap))]
    pallas_call x10 -> x11, Pallas kernels: 2.14 us -> 2.5 us  [the longest x1 1.77 us: local(): call(functools.partial(own_weights_kernel, rows=rows, stored=stored, tota...]
  transfers between devices with their start and end apart: 29 -> 30, of which waited for: 26 -> 27; matrix products, arithmetic and copies ran while one was open for 0% -> 0% of each run, Pallas kernels for 12% -> 12%
where the time goes in v3:
time: 105 us
  waiting for transfers between devices  62.8 us (60%)
  Pallas kernels  20.9 us (20%)
  blocking collectives  10.4 us (10%)
  starting transfers between devices  8.62 us (8%)
  between operations  2.36 us (2%)
    ppermute x9, waiting for transfers between devices, apply_part(): far = lax.ppermute(vectors, 'row', farther)  46.5 us
    pallas_call x27, Pallas kernels, part(): call(kernel, vec, [VMEM] * (len(vectors) + 2), VMEM, cost_estimate=pl.Cos...  11.3 us
    all_to_all x1, blocking collectives, local(): lax.all_to_all(spread, 'row', 0, 0, tiled=True, axis_index_groups=same_core)  10.4 us
    ppermute x8, waiting for transfers between devices, images(): return (partial, lax.ppermute(partial, 'row', swap))  10.3 us
    ppermute x9, waiting for transfers between devices, apply_part(): near = lax.ppermute(vectors, 'row', nearer)  4.83 us
    ppermute x9, starting transfers between devices, apply_part(): far = lax.ppermute(vectors, 'row', farther)  3.92 us
    pallas_call x1, Pallas kernels, local(): call(functools.partial(gather_kernel, rows=rows, stored=stored, total=tot...  2.97 us
    pallas_call x1, Pallas kernels, local(): call(functools.partial(finish_kernel, order=total * width), (jax.ShapeDty...  2.51 us
  transfers between devices with their start and end apart: 30, of which 27 were waited for; matrix products, arithmetic and copies ran while one was open for 0% of the time, Pallas kernels for 12%

profile of v3, /device:TPU:0, one launch (start us, length us, event | category | flops | bytes accessed | tf_op | source)
XLA Modules:
  0.0 105.2 jit_solution(2999786037750582907)
XLA Ops:
  0.6 0.5 collective-permute-start
  1.2 3.0 %shard_map.77 = f32[12,3,128,128]{3,2,1,0:T(8,128)S(1)} custom-call(s32[3,24]{1,0:T(4,128)} %pattern.3, f32[3,24,128,128]{3,2,1,0:T(8,128)} %tiles.3), custom_call_target="tpu_custom_call" | custom-call | bytes 8000000 | tf_op jit(solution)/shard_map/pallas_call | solution.py:299
  4.3 3.1 %collective-permute-start.2 = (f32[32,768]{1,0:T(8,128)S(1)}, f32[32,768]{1,0:T(8,128)S(1)}, u32[]{:S(2)}, u32[]{:S(2)}) collective-permute-start(f32[32,768]{1,0:T(8,128)S(1)} %shard_map.78.vectors.initial), channel_id=1, source_target_pairs={{0,4},{1,13},{2,6},{3,15},{4,8},{5,1},{6,10},{7,3},{8,12},{9,5},{1... | collective-permute-start | bytes 294920 | tf_op jit(solution)/shard_map/ppermute | solution.py:349
  7.4 1.5 %collective-permute-start.1 = (f32[32,768]{1,0:T(8,128)S(1)}, f32[32,768]{1,0:T(8,128)S(1)}, u32[]{:S(2)}, u32[]{:S(2)}) collective-permute-start(f32[32,768]{1,0:T(8,128)S(1)} %shard_map.78.vectors.initial), channel_id=1, source_target_pairs={{0,2},{1,15},{2,4},{3,1},{4,6},{5,3},{6,8},{7,5},{8,10},{9,7},{10,... | collective-permute-start | bytes 294920 | tf_op jit(solution)/shard_map/ppermute | solution.py:348
  8.9 1.8 %shard_map.79 = (bf16[768,768]{1,0:T(8,128)(2,1)S(1)}, bf16[768,768]{1,0:T(8,128)(2,1)S(1)}, bf16[768,768]{1,0:T(8,128)(2,1)S(1)}, bf16[768,768]{1,0:T(8,128)(2,...) custom-call(s32[3,24]{1,0:T(4,128)} %pattern.3, f32[3,24,128,128]{3,2,1,0:T(8,128)S(1)} %copy-done), custom_call_target="tpu_custom_call" | custom-call | flops 1000000 | bytes 100000 | tf_op jit(solution)/shard_map/pallas_call | solution.py:314
  10.6 0.7 shard_map.80
  11.4 0.3 shard_map.81.before
  11.7 1.3 %collective-permute-done.2.vectors = f32[32,768]{1,0:T(8,128)S(1)} collective-permute-done((f32[32,768]{1,0:T(8,128)S(1)}, f32[32,768]{1,0:T(8,128)S(1)}, u32[]{:S(2)}, u32[]{:S(2)}) %collective-permute-start.2) | collective-permute-done | bytes 98336 | tf_op jit(solution)/shard_map/ppermute | solution.py:349
  13.0 0.5 shard_map.82.before
  13.4 1.2 %collective-permute-done.1.vectors = f32[32,768]{1,0:T(8,128)S(1)} collective-permute-done((f32[32,768]{1,0:T(8,128)S(1)}, f32[32,768]{1,0:T(8,128)S(1)}, u32[]{:S(2)}, u32[]{:S(2)}) %collective-permute-start.1) | collective-permute-done | bytes 98336 | tf_op jit(solution)/shard_map/ppermute | solution.py:348
  14.7 0.5 shard_map.83.partial
  15.2 1.3 %collective-permute-done.4.other = f32[32,768]{1,0:T(8,128)S(1)} collective-permute-done((f32[32,768]{1,0:T(8,128)S(1)}, f32[32,768]{1,0:T(8,128)S(1)}, u32[]{:S(2)}, u32[]{:S(2)}) %collective-permute-start.4) | collective-permute-done | bytes 98336 | tf_op jit(solution)/shard_map/ppermute | solution.py:357
  16.5 0.4 collective-permute-start.6
  18.6 0.3 shard_map.85.before
  18.9 4.4 %collective-permute-done.6.vectors = f32[32,768]{1,0:T(8,128)S(1)} collective-permute-done((f32[32,768]{1,0:T(8,128)S(1)}, f32[32,768]{1,0:T(8,128)S(1)}, u32[]{:S(2)}, u32[]{:S(2)}) %collective-permute-start.6) | collective-permute-done | bytes 98336 | tf_op jit(solution)/shard_map/ppermute | solution.py:349
  23.3 0.5 shard_map.86.before
  23.8 0.5 collective-permute-done.5.vectors
  24.2 0.5 shard_map.87.partial
  24.8 1.2 %collective-permute-done.7.other = f32[32,768]{1,0:T(8,128)S(1)} collective-permute-done((f32[32,768]{1,0:T(8,128)S(1)}, f32[32,768]{1,0:T(8,128)S(1)}, u32[]{:S(2)}, u32[]{:S(2)}) %collective-permute-start.7) | collective-permute-done | bytes 98336 | tf_op jit(solution)/shard_map/ppermute | solution.py:357
  26.7 6.1 %collective-permute-done.9.vectors = f32[32,768]{1,0:T(8,128)S(1)} collective-permute-done((f32[32,768]{1,0:T(8,128)S(1)}, f32[32,768]{1,0:T(8,128)S(1)}, u32[]{:S(2)}, u32[]{:S(2)}) %collective-permute-start.9) | collective-permute-done | bytes 98336 | tf_op jit(solution)/shard_map/ppermute | solution.py:349
  32.8 0.5 shard_map.90.before
  33.2 0.4 collective-permute-done.8.vectors
  33.6 0.5 shard_map.91.partial
  34.1 1.3 %collective-permute-done.10.other = f32[32,768]{1,0:T(8,128)S(1)} collective-permute-done((f32[32,768]{1,0:T(8,128)S(1)}, f32[32,768]{1,0:T(8,128)S(1)}, u32[]{:S(2)}, u32[]{:S(2)}) %collective-permute-start.10) | collective-permute-done | bytes 98336 | tf_op jit(solution)/shard_map/ppermute | solution.py:357
  35.7 0.3 shard_map.93.before
  36.0 6.0 %collective-permute-done.12.vectors = f32[32,768]{1,0:T(8,128)S(1)} collective-permute-done((f32[32,768]{1,0:T(8,128)S(1)}, f32[32,768]{1,0:T(8,128)S(1)}, u32[]{:S(2)}, u32[]{:S(2)}) %collective-permute-start.12) | collective-permute-done | bytes 98336 | tf_op jit(solution)/shard_map/ppermute | solution.py:349
  42.0 0.5 shard_map.94.before
  42.4 0.5 collective-permute-done.11.vectors
  42.9 0.5 shard_map.95.partial
  43.4 1.3 %collective-permute-done.13.other = f32[32,768]{1,0:T(8,128)S(1)} collective-permute-done((f32[32,768]{1,0:T(8,128)S(1)}, f32[32,768]{1,0:T(8,128)S(1)}, u32[]{:S(2)}, u32[]{:S(2)}) %collective-permute-start.13) | collective-permute-done | bytes 98336 | tf_op jit(solution)/shard_map/ppermute | solution.py:357
  44.9 0.3 shard_map.97.before
  45.2 6.1 %collective-permute-done.15.vectors = f32[32,768]{1,0:T(8,128)S(1)} collective-permute-done((f32[32,768]{1,0:T(8,128)S(1)}, f32[32,768]{1,0:T(8,128)S(1)}, u32[]{:S(2)}, u32[]{:S(2)}) %collective-permute-start.15) | collective-permute-done | bytes 98336 | tf_op jit(solution)/shard_map/ppermute | solution.py:349
  51.3 0.5 shard_map.98.before
  51.8 0.5 collective-permute-done.14.vectors
  52.2 0.5 shard_map.99.partial
  52.7 1.3 %collective-permute-done.16.other = f32[32,768]{1,0:T(8,128)S(1)} collective-permute-done((f32[32,768]{1,0:T(8,128)S(1)}, f32[32,768]{1,0:T(8,128)S(1)}, u32[]{:S(2)}, u32[]{:S(2)}) %collective-permute-start.16) | collective-permute-done | bytes 98336 | tf_op jit(solution)/shard_map/ppermute | solution.py:357
  54.2 0.3 shard_map.101.before
  54.5 6.1 %collective-permute-done.18.vectors = f32[32,768]{1,0:T(8,128)S(1)} collective-permute-done((f32[32,768]{1,0:T(8,128)S(1)}, f32[32,768]{1,0:T(8,128)S(1)}, u32[]{:S(2)}, u32[]{:S(2)}) %collective-permute-start.18) | collective-permute-done | bytes 98336 | tf_op jit(solution)/shard_map/ppermute | solution.py:349
  60.6 0.5 shard_map.102.before
  61.1 0.5 collective-permute-done.17.vectors
  61.5 0.5 shard_map.103.partial
  62.0 1.3 %collective-permute-done.19.other = f32[32,768]{1,0:T(8,128)S(1)} collective-permute-done((f32[32,768]{1,0:T(8,128)S(1)}, f32[32,768]{1,0:T(8,128)S(1)}, u32[]{:S(2)}, u32[]{:S(2)}) %collective-permute-start.19) | collective-permute-done | bytes 98336 | tf_op jit(solution)/shard_map/ppermute | solution.py:357
  63.5 0.3 shard_map.105.before
  63.8 6.1 %collective-permute-done.21.vectors = f32[32,768]{1,0:T(8,128)S(1)} collective-permute-done((f32[32,768]{1,0:T(8,128)S(1)}, f32[32,768]{1,0:T(8,128)S(1)}, u32[]{:S(2)}, u32[]{:S(2)}) %collective-permute-start.21) | collective-permute-done | bytes 98336 | tf_op jit(solution)/shard_map/ppermute | solution.py:349
  69.9 0.5 shard_map.106.before
  70.4 0.5 collective-permute-done.20.vectors
  70.8 0.5 shard_map.107.partial
  71.3 1.3 %collective-permute-done.22.other = f32[32,768]{1,0:T(8,128)S(1)} collective-permute-done((f32[32,768]{1,0:T(8,128)S(1)}, f32[32,768]{1,0:T(8,128)S(1)}, u32[]{:S(2)}, u32[]{:S(2)}) %collective-permute-start.22) | collective-permute-done | bytes 98336 | tf_op jit(solution)/shard_map/ppermute | solution.py:357
  72.8 0.3 shard_map.109.before
  73.1 6.1 %collective-permute-done.24.vectors = f32[32,768]{1,0:T(8,128)S(1)} collective-permute-done((f32[32,768]{1,0:T(8,128)S(1)}, f32[32,768]{1,0:T(8,128)S(1)}, u32[]{:S(2)}, u32[]{:S(2)}) %collective-permute-start.24) | collective-permute-done | bytes 98336 | tf_op jit(solution)/shard_map/ppermute | solution.py:349
  79.2 0.5 shard_map.110.before
  79.7 0.5 collective-permute-done.23.vectors
  80.1 0.5 shard_map.111.partial
  80.6 1.3 %collective-permute-done.25.other = f32[32,768]{1,0:T(8,128)S(1)} collective-permute-done((f32[32,768]{1,0:T(8,128)S(1)}, f32[32,768]{1,0:T(8,128)S(1)}, u32[]{:S(2)}, u32[]{:S(2)}) %collective-permute-start.25) | collective-permute-done | bytes 98336 | tf_op jit(solution)/shard_map/ppermute | solution.py:357
  82.1 1.6 %collective-permute-start.26 = (f32[32,384]{1,0:T(8,128)S(1)}, f32[32,384]{1,0:T(8,128)S(1)}, u32[]{:S(2)}, u32[]{:S(2)}) collective-permute-start(f32[32,384]{1,0:T(8,128)S(1)} %slice.4.vectors), channel_id=1, source_target_pairs={{0,16},{16,0},{1,17},{17,1},{2,18},{18,2},{3,19},{19,3},{4,20},{20... | collective-permute-start | bytes 147464 | tf_op jit(solution)/shard_map/ppermute | solution.py:371
  84.0 4.5 %collective-permute-done.28.vectors = f32[32,768]{1,0:T(8,128)S(1)} collective-permute-done((f32[32,768]{1,0:T(8,128)S(1)}, f32[32,768]{1,0:T(8,128)S(1)}, u32[]{:S(2)}, u32[]{:S(2)}) %collective-permute-start.28) | collective-permute-done | bytes 98336 | tf_op jit(solution)/shard_map/ppermute | solution.py:349
  88.5 0.5 shard_map.114.before
  89.0 0.4 collective-permute-done.27.vectors
  89.4 0.5 shard_map.115.partial
  89.9 0.9 shard_map.116
  90.8 0.3 shard_map.117.one
  91.1 1.2 %collective-permute-done.29.other = f32[32,128]{1,0:T(8,128)S(1)} collective-permute-done((f32[32,128]{1,0:T(8,128)S(1)}, f32[32,128]{1,0:T(8,128)S(1)}, u32[]{:S(2)}, u32[]{:S(2)}) %collective-permute-start.29) | collective-permute-done | bytes 16416 | tf_op jit(solution)/shard_map/ppermute | solution.py:383
  92.3 10.4 %all_to_all.5.parts = f32[8,32,128]{2,1,0:T(8,128)S(1)} all-to-all(f32[8,32,128]{2,1,0:T(8,128)S(1)} %shard_map.118), channel_id=1, replica_groups={{0,2,4,6,8,10,12,14},{1,3,5,7,9,11,13,15},{16,18,20,22,24,26,28,30},{17..., dimensions={0} | all-to-all | bytes 262144 | tf_op jit(solution)/shard_map/all_to_all | solution.py:386
  102.7 2.5 %shard_map.119 = (f32[32,384]{1,0:T(8,128)}, f32[32,32]{1,0:T(8,128)}) custom-call(f32[8,32,128]{2,1,0:T(8,128)S(1)} %all_to_all.5.parts, f32[32,32]{1,0:T(8,128)S(1)} %get-tuple-element.43.chosen, f32[32,384]{1,0:T(8,128)S(1)} %slice.4.vectors, f32[32,384]{1,0:T(8,128)S(1)} %collective-permute-done.26.lower), custom_call_target="tpu_custom_call" | custom-call | flops 1000000 | bytes 100000 | tf_op jit(solution)/shard_map/pallas_call | solution.py:387
  (49 shorter events, 2.7 us)
Async XLA Ops:
  0.6 3.6 %copy-start.1 = (f32[1,32,384]{2,1,0:T(8,128)S(1)}, f32[1,32,384]{2,1,0:T(8,128)}, u32[]{:S(2)}) copy-start(f32[1,32,384]{2,1,0:T(8,128)} %param.8) | copy-start | bytes 147460
  0.6 3.5 %collective-permute-start = (f32[32,384]{1,0:T(8,128)}, f32[32,384]{1,0:T(8,128)S(1)}, u32[]{:S(2)}, u32[]{:S(2)}) collective-permute-start(f32[32,384]{1,0:T(8,128)} %bitcast.6), channel_id=1, source_target_pairs={{0,1},{1,0},{2,3},{3,2},{4,5},{5,4},{6,7},{7,6},{8,9},{9,8},{10,11... | collective-permute-start | bytes 147464 | tf_op jit(solution)/shard_map/ppermute | solution.py:298
  1.2 7.7 %copy-start = (f32[3,24,128,128]{3,2,1,0:T(8,128)S(1)}, f32[3,24,128,128]{3,2,1,0:T(8,128)}, u32[]{:S(2)}) copy-start(f32[3,24,128,128]{3,2,1,0:T(8,128)} %tiles.3) | copy-start | bytes 14155780
  4.1 6.5 %collective-permute-start.3 = (f32[12,3,128,128]{3,2,1,0:T(8,128)S(1)}, f32[12,3,128,128]{3,2,1,0:T(8,128)S(1)}, u32[]{:S(2)}, u32[]{:S(2)}) collective-permute-start(f32[12,3,128,128]{3,2,1,0:T(8,128)S(1)} %shard_map.77), channel_id=1, source_target_pairs={{0,1},{1,0},{2,3},{3,2},{4,5},{5,4},{6,7},{7,6},{8,9},{9,8},{10,11... | collective-permute-start | bytes 7077896 | tf_op jit(solution)/shard_map/ppermute | solution.py:313
  4.3 8.7 %collective-permute-start.2 = (f32[32,768]{1,0:T(8,128)S(1)}, f32[32,768]{1,0:T(8,128)S(1)}, u32[]{:S(2)}, u32[]{:S(2)}) collective-permute-start(f32[32,768]{1,0:T(8,128)S(1)} %shard_map.78.vectors.initial), channel_id=1, source_target_pairs={{0,4},{1,13},{2,6},{3,15},{4,8},{5,1},{6,10},{7,3},{8,12},{9,5},{1... | collective-permute-start | bytes 294920 | tf_op jit(solution)/shard_map/ppermute | solution.py:349
  7.4 7.3 %collective-permute-start.1 = (f32[32,768]{1,0:T(8,128)S(1)}, f32[32,768]{1,0:T(8,128)S(1)}, u32[]{:S(2)}, u32[]{:S(2)}) collective-permute-start(f32[32,768]{1,0:T(8,128)S(1)} %shard_map.78.vectors.initial), channel_id=1, source_target_pairs={{0,2},{1,15},{2,4},{3,1},{4,6},{5,3},{6,8},{7,5},{8,10},{9,7},{10,... | collective-permute-start | bytes 294920 | tf_op jit(solution)/shard_map/ppermute | solution.py:348
  15.2 1.3 %collective-permute-start.4 = (f32[32,768]{1,0:T(8,128)S(1)}, f32[32,768]{1,0:T(8,128)S(1)}, u32[]{:S(2)}, u32[]{:S(2)}) collective-permute-start(f32[32,768]{1,0:T(8,128)S(1)} %shard_map.83.partial), channel_id=1, source_target_pairs={{0,1},{1,0},{2,3},{3,2},{4,5},{5,4},{6,7},{7,6},{8,9},{9,8},{10,11... | collective-permute-start | bytes 294920 | tf_op jit(solution)/shard_map/ppermute | solution.py:357
  16.5 6.8 %collective-permute-start.6 = (f32[32,768]{1,0:T(8,128)S(1)}, f32[32,768]{1,0:T(8,128)S(1)}, u32[]{:S(2)}, u32[]{:S(2)}) collective-permute-start(f32[32,768]{1,0:T(8,128)S(1)} %shard_map.84.vectors.image), channel_id=1, source_target_pairs={{0,4},{1,13},{2,6},{3,15},{4,8},{5,1},{6,10},{7,3},{8,12},{9,5},{1... | collective-permute-start | bytes 294920 | tf_op jit(solution)/shard_map/ppermute | solution.py:349
  16.9 7.3 %collective-permute-start.5 = (f32[32,768]{1,0:T(8,128)S(1)}, f32[32,768]{1,0:T(8,128)S(1)}, u32[]{:S(2)}, u32[]{:S(2)}) collective-permute-start(f32[32,768]{1,0:T(8,128)S(1)} %shard_map.84.vectors.image), channel_id=1, source_target_pairs={{0,2},{1,15},{2,4},{3,1},{4,6},{5,3},{6,8},{7,5},{8,10},{9,7},{10,... | collective-permute-start | bytes 294920 | tf_op jit(solution)/shard_map/ppermute | solution.py:348
  24.7 1.3 %collective-permute-start.7 = (f32[32,768]{1,0:T(8,128)S(1)}, f32[32,768]{1,0:T(8,128)S(1)}, u32[]{:S(2)}, u32[]{:S(2)}) collective-permute-start(f32[32,768]{1,0:T(8,128)S(1)} %shard_map.87.partial), channel_id=1, source_target_pairs={{0,1},{1,0},{2,3},{3,2},{4,5},{5,4},{6,7},{7,6},{8,9},{9,8},{10,11... | collective-permute-start | bytes 294920 | tf_op jit(solution)/shard_map/ppermute | solution.py:357
  26.2 6.6 %collective-permute-start.9 = (f32[32,768]{1,0:T(8,128)S(1)}, f32[32,768]{1,0:T(8,128)S(1)}, u32[]{:S(2)}, u32[]{:S(2)}) collective-permute-start(f32[32,768]{1,0:T(8,128)S(1)} %get-tuple-element.38.vectors.current.previous), channel_id=1, source_target_pairs={{0,4},{1,13},{2,6},{3,15},{4,8},{5,1},{6,10},{7,3},{8,12},{9,5},{1... | collective-permute-start | bytes 294920 | tf_op jit(solution)/shard_map/ppermute | solution.py:349
  26.3 7.4 %collective-permute-start.8 = (f32[32,768]{1,0:T(8,128)S(1)}, f32[32,768]{1,0:T(8,128)S(1)}, u32[]{:S(2)}, u32[]{:S(2)}) collective-permute-start(f32[32,768]{1,0:T(8,128)S(1)} %get-tuple-element.38.vectors.current.previous), channel_id=1, source_target_pairs={{0,2},{1,15},{2,4},{3,1},{4,6},{5,3},{6,8},{7,5},{8,10},{9,7},{10,... | collective-permute-start | bytes 294920 | tf_op jit(solution)/shard_map/ppermute | solution.py:348
  34.1 1.3 %collective-permute-start.10 = (f32[32,768]{1,0:T(8,128)S(1)}, f32[32,768]{1,0:T(8,128)S(1)}, u32[]{:S(2)}, u32[]{:S(2)}) collective-permute-start(f32[32,768]{1,0:T(8,128)S(1)} %shard_map.91.partial), channel_id=1, source_target_pairs={{0,1},{1,0},{2,3},{3,2},{4,5},{5,4},{6,7},{7,6},{8,9},{9,8},{10,11... | collective-permute-start | bytes 294920 | tf_op jit(solution)/shard_map/ppermute | solution.py:357
  35.5 6.5 %collective-permute-start.12 = (f32[32,768]{1,0:T(8,128)S(1)}, f32[32,768]{1,0:T(8,128)S(1)}, u32[]{:S(2)}, u32[]{:S(2)}) collective-permute-start(f32[32,768]{1,0:T(8,128)S(1)} %shard_map.92.vectors.current.previous), channel_id=1, source_target_pairs={{0,4},{1,13},{2,6},{3,15},{4,8},{5,1},{6,10},{7,3},{8,12},{9,5},{1... | collective-permute-start | bytes 294920 | tf_op jit(solution)/shard_map/ppermute | solution.py:349
  35.6 7.4 %collective-permute-start.11 = (f32[32,768]{1,0:T(8,128)S(1)}, f32[32,768]{1,0:T(8,128)S(1)}, u32[]{:S(2)}, u32[]{:S(2)}) collective-permute-start(f32[32,768]{1,0:T(8,128)S(1)} %shard_map.92.vectors.current.previous), channel_id=1, source_target_pairs={{0,2},{1,15},{2,4},{3,1},{4,6},{5,3},{6,8},{7,5},{8,10},{9,7},{10,... | collective-permute-start | bytes 294920 | tf_op jit(solution)/shard_map/ppermute | solution.py:348
  43.4 1.3 %collective-permute-start.13 = (f32[32,768]{1,0:T(8,128)S(1)}, f32[32,768]{1,0:T(8,128)S(1)}, u32[]{:S(2)}, u32[]{:S(2)}) collective-permute-start(f32[32,768]{1,0:T(8,128)S(1)} %shard_map.95.partial), channel_id=1, source_target_pairs={{0,1},{1,0},{2,3},{3,2},{4,5},{5,4},{6,7},{7,6},{8,9},{9,8},{10,11... | collective-permute-start | bytes 294920 | tf_op jit(solution)/shard_map/ppermute | solution.py:357
  44.8 6.5 %collective-permute-start.15 = (f32[32,768]{1,0:T(8,128)S(1)}, f32[32,768]{1,0:T(8,128)S(1)}, u32[]{:S(2)}, u32[]{:S(2)}) collective-permute-start(f32[32,768]{1,0:T(8,128)S(1)} %shard_map.96.vectors.current.previous), channel_id=1, source_target_pairs={{0,4},{1,13},{2,6},{3,15},{4,8},{5,1},{6,10},{7,3},{8,12},{9,5},{1... | collective-permute-start | bytes 294920 | tf_op jit(solution)/shard_map/ppermute | solution.py:349
  44.9 7.4 %collective-permute-start.14 = (f32[32,768]{1,0:T(8,128)S(1)}, f32[32,768]{1,0:T(8,128)S(1)}, u32[]{:S(2)}, u32[]{:S(2)}) collective-permute-start(f32[32,768]{1,0:T(8,128)S(1)} %shard_map.96.vectors.current.previous), channel_id=1, source_target_pairs={{0,2},{1,15},{2,4},{3,1},{4,6},{5,3},{6,8},{7,5},{8,10},{9,7},{10,... | collective-permute-start | bytes 294920 | tf_op jit(solution)/shard_map/ppermute | solution.py:348
  52.7 1.3 %collective-permute-start.16 = (f32[32,768]{1,0:T(8,128)S(1)}, f32[32,768]{1,0:T(8,128)S(1)}, u32[]{:S(2)}, u32[]{:S(2)}) collective-permute-start(f32[32,768]{1,0:T(8,128)S(1)} %shard_map.99.partial), channel_id=1, source_target_pairs={{0,1},{1,0},{2,3},{3,2},{4,5},{5,4},{6,7},{7,6},{8,9},{9,8},{10,11... | collective-permute-start | bytes 294920 | tf_op jit(solution)/shard_map/ppermute | solution.py:357
  54.1 6.5 %collective-permute-start.18 = (f32[32,768]{1,0:T(8,128)S(1)}, f32[32,768]{1,0:T(8,128)S(1)}, u32[]{:S(2)}, u32[]{:S(2)}) collective-permute-start(f32[32,768]{1,0:T(8,128)S(1)} %shard_map.100.vectors.current.previous), channel_id=1, source_target_pairs={{0,4},{1,13},{2,6},{3,15},{4,8},{5,1},{6,10},{7,3},{8,12},{9,5},{1... | collective-permute-start | bytes 294920 | tf_op jit(solution)/shard_map/ppermute | solution.py:349
  54.1 7.4 %collective-permute-start.17 = (f32[32,768]{1,0:T(8,128)S(1)}, f32[32,768]{1,0:T(8,128)S(1)}, u32[]{:S(2)}, u32[]{:S(2)}) collective-permute-start(f32[32,768]{1,0:T(8,128)S(1)} %shard_map.100.vectors.current.previous), channel_id=1, source_target_pairs={{0,2},{1,15},{2,4},{3,1},{4,6},{5,3},{6,8},{7,5},{8,10},{9,7},{10,... | collective-permute-start | bytes 294920 | tf_op jit(solution)/shard_map/ppermute | solution.py:348
  62.0 1.3 %collective-permute-start.19 = (f32[32,768]{1,0:T(8,128)S(1)}, f32[32,768]{1,0:T(8,128)S(1)}, u32[]{:S(2)}, u32[]{:S(2)}) collective-permute-start(f32[32,768]{1,0:T(8,128)S(1)} %shard_map.103.partial), channel_id=1, source_target_pairs={{0,1},{1,0},{2,3},{3,2},{4,5},{5,4},{6,7},{7,6},{8,9},{9,8},{10,11... | collective-permute-start | bytes 294920 | tf_op jit(solution)/shard_map/ppermute | solution.py:357
  63.4 6.5 %collective-permute-start.21 = (f32[32,768]{1,0:T(8,128)S(1)}, f32[32,768]{1,0:T(8,128)S(1)}, u32[]{:S(2)}, u32[]{:S(2)}) collective-permute-start(f32[32,768]{1,0:T(8,128)S(1)} %shard_map.104.vectors.current.previous), channel_id=1, source_target_pairs={{0,4},{1,13},{2,6},{3,15},{4,8},{5,1},{6,10},{7,3},{8,12},{9,5},{1... | collective-permute-start | bytes 294920 | tf_op jit(solution)/shard_map/ppermute | solution.py:349
  63.4 7.4 %collective-permute-start.20 = (f32[32,768]{1,0:T(8,128)S(1)}, f32[32,768]{1,0:T(8,128)S(1)}, u32[]{:S(2)}, u32[]{:S(2)}) collective-permute-start(f32[32,768]{1,0:T(8,128)S(1)} %shard_map.104.vectors.current.previous), channel_id=1, source_target_pairs={{0,2},{1,15},{2,4},{3,1},{4,6},{5,3},{6,8},{7,5},{8,10},{9,7},{10,... | collective-permute-start | bytes 294920 | tf_op jit(solution)/shard_map/ppermute | solution.py:348
  71.3 1.3 %collective-permute-start.22 = (f32[32,768]{1,0:T(8,128)S(1)}, f32[32,768]{1,0:T(8,128)S(1)}, u32[]{:S(2)}, u32[]{:S(2)}) collective-permute-start(f32[32,768]{1,0:T(8,128)S(1)} %shard_map.107.partial), channel_id=1, source_target_pairs={{0,1},{1,0},{2,3},{3,2},{4,5},{5,4},{6,7},{7,6},{8,9},{9,8},{10,11... | collective-permute-start | bytes 294920 | tf_op jit(solution)/shard_map/ppermute | solution.py:357
  72.7 6.5 %collective-permute-start.24 = (f32[32,768]{1,0:T(8,128)S(1)}, f32[32,768]{1,0:T(8,128)S(1)}, u32[]{:S(2)}, u32[]{:S(2)}) collective-permute-start(f32[32,768]{1,0:T(8,128)S(1)} %shard_map.108.vectors.current), channel_id=1, source_target_pairs={{0,4},{1,13},{2,6},{3,15},{4,8},{5,1},{6,10},{7,3},{8,12},{9,5},{1... | collective-permute-start | bytes 294920 | tf_op jit(solution)/shard_map/ppermute | solution.py:349
  72.7 7.4 %collective-permute-start.23 = (f32[32,768]{1,0:T(8,128)S(1)}, f32[32,768]{1,0:T(8,128)S(1)}, u32[]{:S(2)}, u32[]{:S(2)}) collective-permute-start(f32[32,768]{1,0:T(8,128)S(1)} %shard_map.108.vectors.current), channel_id=1, source_target_pairs={{0,2},{1,15},{2,4},{3,1},{4,6},{5,3},{6,8},{7,5},{8,10},{9,7},{10,... | collective-permute-start | bytes 294920 | tf_op jit(solution)/shard_map/ppermute | solution.py:348
  80.6 1.3 %collective-permute-start.25 = (f32[32,768]{1,0:T(8,128)S(1)}, f32[32,768]{1,0:T(8,128)S(1)}, u32[]{:S(2)}, u32[]{:S(2)}) collective-permute-start(f32[32,768]{1,0:T(8,128)S(1)} %shard_map.111.partial), channel_id=1, source_target_pairs={{0,1},{1,0},{2,3},{3,2},{4,5},{5,4},{6,7},{7,6},{8,9},{9,8},{10,11... | collective-permute-start | bytes 294920 | tf_op jit(solution)/shard_map/ppermute | solution.py:357
  82.0 6.5 %collective-permute-start.28 = (f32[32,768]{1,0:T(8,128)S(1)}, f32[32,768]{1,0:T(8,128)S(1)}, u32[]{:S(2)}, u32[]{:S(2)}) collective-permute-start(f32[32,768]{1,0:T(8,128)S(1)} %shard_map.112.vectors.pair), channel_id=1, source_target_pairs={{0,4},{1,13},{2,6},{3,15},{4,8},{5,1},{6,10},{7,3},{8,12},{9,5},{1... | collective-permute-start | bytes 294920 | tf_op jit(solution)/shard_map/ppermute | solution.py:349
  82.0 7.4 %collective-permute-start.27 = (f32[32,768]{1,0:T(8,128)S(1)}, f32[32,768]{1,0:T(8,128)S(1)}, u32[]{:S(2)}, u32[]{:S(2)}) collective-permute-start(f32[32,768]{1,0:T(8,128)S(1)} %shard_map.112.vectors.pair), channel_id=1, source_target_pairs={{0,2},{1,15},{2,4},{3,1},{4,6},{5,3},{6,8},{7,5},{8,10},{9,7},{10,... | collective-permute-start | bytes 294920 | tf_op jit(solution)/shard_map/ppermute | solution.py:348
  82.1 7.8 %collective-permute-start.26 = (f32[32,384]{1,0:T(8,128)S(1)}, f32[32,384]{1,0:T(8,128)S(1)}, u32[]{:S(2)}, u32[]{:S(2)}) collective-permute-start(f32[32,384]{1,0:T(8,128)S(1)} %slice.4.vectors), channel_id=1, source_target_pairs={{0,16},{16,0},{1,17},{17,1},{2,18},{18,2},{3,19},{19,3},{4,20},{20... | collective-permute-start | bytes 147464 | tf_op jit(solution)/shard_map/ppermute | solution.py:371
  89.0 1.0 copy-start.2
  91.1 1.2 %collective-permute-start.29 = (f32[32,128]{1,0:T(8,128)S(1)}, f32[32,128]{1,0:T(8,128)S(1)}, u32[]{:S(2)}, u32[]{:S(2)}) collective-permute-start(f32[32,128]{1,0:T(8,128)S(1)} %shard_map.117.one), channel_id=1, source_target_pairs={{0,1},{1,0},{2,3},{3,2},{4,5},{5,4},{6,7},{7,6},{8,9},{9,8},{10,11... | collective-permute-start | bytes 49160 | tf_op jit(solution)/shard_map/ppermute | solution.py:383

commit v4 on v3

--- a/solution.py
+++ b/solution.py
@@ -130,7 +130,7 @@
     return by_high[:count] + (by_high[count:] + by_low)
 
 
-def own_kernel(vectors, high, low, out):
+def own_kernel(vectors, _after, high, low, out):
     out[...] = multiply(vectors[:, : high.shape[0]], high, low)
 
 
@@ -175,31 +175,25 @@
     return lax.dot_general(a, b, dims, precision=lax.Precision.HIGHEST, preferred_element_type=F32)
 
 
-def pack(square):
-    count = square.shape[0]
-    strip = count * count // 128
-    return jnp.concatenate([square[i * strip : (i + 1) * strip] for i in range(count // strip)], axis=1)
-
-
-def unpack(rows, count):
-    return jnp.concatenate([rows[:, i : i + count] for i in range(0, 128, count)], axis=0)
-
-
-def gram_kernel(pairs, pair, lower, packed, chosen, *, half):
+def chosen_kernel(pairs, _after, out):
+    row = lax.broadcasted_iota(jnp.int32, out.shape, 0)
+    column = lax.broadcasted_iota(jnp.int32, out.shape, 1)
+    total = jnp.zeros(out.shape, F32)
+    for p in range(pairs.shape[1]):
+        total = total + ((row == pairs[0, p]) & (column == pairs[1, p])).astype(F32)
+    out[...] = jnp.where(lax.axis_index("cuts") == 0, 0.0, total)
+
+
+def gram_kernel(pair, lower, gram, below, mixed, *, half):
     own = pair[:, :half]
-    below = lower[...]
-    squares = [dot(own, own, NT), dot(below, below, NT), dot(below, own, NT)]
-    packed[...] = jnp.concatenate([pack(square) for square in squares], axis=0)
-    row = lax.broadcasted_iota(jnp.int32, chosen.shape, 0)
-    column = lax.broadcasted_iota(jnp.int32, chosen.shape, 1)
-    total = jnp.zeros(chosen.shape, F32)
-    for p in range(pairs.shape[1]):
-        total = total + ((row == pairs[1, p]) & (column == pairs[0, p])).astype(F32)
-    chosen[...] = jnp.where(lax.axis_index("cuts") == 0, 0.0, total)
-
-
-def cross_kernel(pair, partial, packed, out):
-    out[...] = jnp.concatenate([packed[...], pack(dot(pair[...], partial[...], NT))], axis=0)
+    gram[...] = dot(own, own, NT)
+    below[...] = dot(lower[...], lower[...], NT)
+    mixed[...] = dot(own, lower[...], NT)
+
+
+def cross_kernel(pair, partial, gram, below, mixed, out):
+    cross = dot(pair[...], partial[...], NT)
+    out[...] = jnp.concatenate([gram[...], mixed[...], below[...], cross], axis=1)
 
 
 def spread_kernel(one, other, out):
@@ -215,52 +209,43 @@
     return total
 
 
-def inverses(gram, gram_below):
-    count = gram.shape[0]
-    block = 8
-    row = lax.broadcasted_iota(jnp.int32, (count, count), 0)
-    column = lax.broadcasted_iota(jnp.int32, (count, count), 1)
-    eye = (row == column).astype(F32)
-    work = jnp.concatenate([gram, eye, gram_below, eye], axis=1)
-    sub = lax.broadcasted_iota(jnp.int32, work.shape, 0)
-    left = lax.broadcasted_iota(jnp.int32, work.shape, 1) < 2 * count
-
-    def spread(values, k):
-        return jnp.where(left[: values.shape[0]], values[:, k : k + 1], values[:, 2 * count + k : 2 * count + k + 1])
-
+def inverses(squares):
+    count = squares.shape[0]
+    block = 16
+    sub = lax.broadcasted_iota(jnp.int32, squares.shape, 0)
+    lane = lax.broadcasted_iota(jnp.int32, squares.shape, 1)
+    left = lane < 2 * count
+    place = jnp.where(left, lane, lane - 2 * count)
+    work = jnp.where(place < count, squares, (place == sub + count).astype(F32))
     for k in range(0, count, block):
-        rows = [work[k + i : k + i + 1, :] for i in range(block)]
-        corner = [[spread(r, k + j) for j in range(block)] for r in rows]
-        columns = [spread(work, k + j) for j in range(block)]
+        columns = [
+            jnp.where(left, work[:, m : m + 1], work[:, 2 * count + m : 2 * count + m + 1]) for m in range(k, k + block)
+        ]
         for i in range(block):
-            pivot = 1.0 / corner[i][i]
-            factor = jnp.where(sub > k + i, columns[i] * pivot, 0.0)
-            work = work - factor * rows[i]
+            here = slice(k + i, k + i + 1)
+            factor = jnp.where(sub > k + i, columns[i] * (1.0 / columns[i][here]), 0.0)
             for j in range(i + 1, block):
-                columns[j] = columns[j] - factor * corner[i][j]
-                ratio = corner[j][i] * pivot
-                rows[j] = rows[j] - ratio * rows[i]
-                for m in range(i + 1, block):
-                    corner[j][m] = corner[j][m] - ratio * corner[i][m]
-
-    def scaled(start):
-        pivots = jnp.sum(eye * work[:, start : start + count], axis=1, keepdims=True)
-        return work[:, start + count : start + 2 * count] * (1.0 / jnp.sqrt(pivots))
-
-    return scaled(0), scaled(2 * count)
+                columns[j] = columns[j] - factor * columns[j][here]
+            work = work - factor * work[here]
+    pivots = jnp.where(place == sub, work, 0.0)
+    for start in (0, 2 * count):
+        pivot = jnp.sum(pivots[:, start : start + count], axis=1, keepdims=True)
+        yield work[:, start + count : start + 2 * count] * (1.0 / jnp.sqrt(pivot))
 
 
 def finish_kernel(parts, chosen, vectors, lower, filtered, projected, *, order):
     count = vectors.shape[0]
     total = summed(parts)
-    strip = count * count // 128
-    gram, gram_below, mixed, cross = (unpack(total[i * strip : (i + 1) * strip], count) for i in range(4))
-    inverse, inverse_below = inverses(gram, gram_below)
-    correlation = dot(dot(inverse_below, mixed, NN), inverse, NT)
+    mixed, cross = total[:, count : 2 * count], total[:, 3 * count :]
+    inverse, inverse_below = inverses(total)
+    scale = math.sqrt(order)
+    basis = scale * dot(inverse, vectors[...], NN)
+    lower_basis = scale * dot(inverse_below, lower[...], NN)
+    correlation = dot(dot(inverse, mixed, NN), inverse_below, NT)
     projected[...] = dot(dot(inverse, cross, NN), inverse, NT)
     some = jnp.max(chosen[...]) > 0.0
-    removal = jnp.where(some, dot((chosen[...] * correlation).T, inverse_below, NN), 0.0)
-    filtered[...] = math.sqrt(order) * (dot(inverse, vectors[...], NN) - dot(removal, lower[...], NN))
+    removal = jnp.where(some, dot(chosen[...] * correlation, lower_basis, NN), 0.0)
+    filtered[...] = basis - removal
 
 
 def call(kernel, out_shape, in_specs, out_specs, **options):
@@ -344,16 +329,16 @@
             ),
         )(*vectors, high, low)
 
-    def apply_part(vectors):
+    def apply_part(vectors, after):
         near = lax.ppermute(vectors, "row", nearer)
         far = lax.ppermute(vectors, "row", farther)
-        partial = part(own_kernel, own_weights, vectors)
+        partial = part(own_kernel, own_weights, vectors, after)
         partial = part(add_kernel, far_weights, far, partial)
         return part(add_kernel, near_weights, near, partial)
 
     current = call(functools.partial(join_kernel, half=half), vec, [VMEM, VMEM], VMEM)(initial, beside)
-    def images(vectors):
-        partial = apply_part(vectors)
+    def images(vectors, after):
+        partial = apply_part(vectors, after)
         return partial, lax.ppermute(partial, "row", swap)
 
     def step(kernel, out_shape, *operands):
@@ -361,25 +346,20 @@
         return call(functools.partial(kernel, half=half), out_shape, [VMEM] * len(operands), out_specs)(*operands)
 
     factors = jnp.broadcast_to(jnp.concatenate([1.0 / halfwidths, centers / halfwidths])[:, None], (2, 128))
-    image = step(image_kernel, vec, *images(current))
-    previous, current = step(second_kernel, (vec, vec), factors, *images(image), image, current)
+    image = step(image_kernel, vec, *images(current, current))
+    previous, current = step(second_kernel, (vec, vec), factors, *images(image, image), image, current)
+    small = jax.ShapeDtypeStruct((count, count), F32)
+    chosen = call(chosen_kernel, small, [SMEM, VMEM], VMEM)(dup_pairs[0].T, image)
     for _ in range(DEG - 2):
-        previous, current = current, step(step_kernel, vec, factors, *images(current), current, previous)
+        previous, current = current, step(step_kernel, vec, factors, *images(current, chosen), current, previous)
 
     own = current[:, :half]
-    strip = count * count // 128
     lower = lax.ppermute(own, "cuts", below)
-    partial = apply_part(current)
-    small = jax.ShapeDtypeStruct((count, count), F32)
+    partial = apply_part(current, chosen)
     lower, partial = lax.optimization_barrier((lower, partial))
-    packed, chosen = call(
-        functools.partial(gram_kernel, half=half),
-        (jax.ShapeDtypeStruct((3 * strip, 128), F32), small),
-        [SMEM, VMEM, VMEM],
-        (VMEM, VMEM),
-    )(dup_pairs[0].T, current, lower)
-    sums = jax.ShapeDtypeStruct((4 * strip, 128), F32)
-    products = call(cross_kernel, sums, [VMEM, VMEM, VMEM], VMEM)(current, partial, packed)
+    squares = call(functools.partial(gram_kernel, half=half), (small,) * 3, [VMEM, VMEM], (VMEM,) * 3)(current, lower)
+    sums = jax.ShapeDtypeStruct((count, 4 * count), F32)
+    products = call(cross_kernel, sums, [VMEM] * 5, VMEM)(current, partial, *squares)
     beside = lax.ppermute(products, "row", swap)
     spread = call(spread_kernel, jax.ShapeDtypeStruct((chips, *sums.shape), F32), [VMEM, VMEM], VMEM)(products, beside)
     same_core = [[2 * chip + core for chip in range(chips)] for core in range(2)]

time: 105 us -> 104 us (level)
  transfers between devices with their start and end apart: 30 -> 30, of which waited for: 27 -> 27; matrix products, arithmetic and copies ran while one was open for 0% -> 0% of each run, Pallas kernels for 12% -> 13%
where the time goes in v4:
time: 104 us
  waiting for transfers between devices  62.2 us (60%)
  Pallas kernels  20.3 us (20%)
  blocking collectives  10.4 us (10%)
  starting transfers between devices  8.64 us (8%)
  between operations  2.36 us (2%)
    ppermute x9, waiting for transfers between devices, apply_part(): far = lax.ppermute(vectors, 'row', farther)  45.9 us
    pallas_call x27, Pallas kernels, part(): call(kernel, vec, [VMEM] * (len(vectors) + 2), VMEM, cost_estimate=pl.Cos...  11.3 us
    all_to_all x1, blocking collectives, local(): lax.all_to_all(spread, 'row', 0, 0, tiled=True, axis_index_groups=same_core)  10.4 us
    ppermute x8, waiting for transfers between devices, images(): return (partial, lax.ppermute(partial, 'row', swap))  10.3 us
    ppermute x9, waiting for transfers between devices, apply_part(): near = lax.ppermute(vectors, 'row', nearer)  4.82 us
    ppermute x9, starting transfers between devices, apply_part(): far = lax.ppermute(vectors, 'row', farther)  3.9 us
    pallas_call x1, Pallas kernels, local(): call(functools.partial(gather_kernel, rows=rows, stored=stored, total=tot...  2.95 us
    ppermute x9, starting transfers between devices, apply_part(): near = lax.ppermute(vectors, 'row', nearer)  2.34 us
  transfers between devices with their start and end apart: 30, of which 27 were waited for; matrix products, arithmetic and copies ran while one was open for 0% of the time, Pallas kernels for 13%

profile of v4, /device:TPU:0, one launch (start us, length us, event | category | flops | bytes accessed | tf_op | source)
XLA Modules:
  0.0 104.1 jit_solution(13638146389404406126)
XLA Ops:
  0.6 0.5 collective-permute-start
  1.2 2.9 %shard_map.77 = f32[12,3,128,128]{3,2,1,0:T(8,128)S(1)} custom-call(s32[3,24]{1,0:T(4,128)} %pattern.3, f32[3,24,128,128]{3,2,1,0:T(8,128)} %tiles.3), custom_call_target="tpu_custom_call" | custom-call | bytes 8000000 | tf_op jit(solution)/shard_map/pallas_call | solution.py:284
  4.3 3.1 %collective-permute-start.2 = (f32[32,768]{1,0:T(8,128)S(1)}, f32[32,768]{1,0:T(8,128)S(1)}, u32[]{:S(2)}, u32[]{:S(2)}) collective-permute-start(f32[32,768]{1,0:T(8,128)S(1)} %shard_map.78.vectors._after.initial), channel_id=1, source_target_pairs={{0,4},{1,13},{2,6},{3,15},{4,8},{5,1},{6,10},{7,3},{8,12},{9,5},{1... | collective-permute-start | bytes 294920 | tf_op jit(solution)/shard_map/ppermute | solution.py:334
  7.3 1.5 %collective-permute-start.1 = (f32[32,768]{1,0:T(8,128)S(1)}, f32[32,768]{1,0:T(8,128)S(1)}, u32[]{:S(2)}, u32[]{:S(2)}) collective-permute-start(f32[32,768]{1,0:T(8,128)S(1)} %shard_map.78.vectors._after.initial), channel_id=1, source_target_pairs={{0,2},{1,15},{2,4},{3,1},{4,6},{5,3},{6,8},{7,5},{8,10},{9,7},{10,... | collective-permute-start | bytes 294920 | tf_op jit(solution)/shard_map/ppermute | solution.py:333
  8.8 1.8 %shard_map.79 = (bf16[768,768]{1,0:T(8,128)(2,1)S(1)}, bf16[768,768]{1,0:T(8,128)(2,1)S(1)}, bf16[768,768]{1,0:T(8,128)(2,1)S(1)}, bf16[768,768]{1,0:T(8,128)(2,...) custom-call(s32[3,24]{1,0:T(4,128)} %pattern.3, f32[3,24,128,128]{3,2,1,0:T(8,128)S(1)} %copy-done), custom_call_target="tpu_custom_call" | custom-call | flops 1000000 | bytes 100000 | tf_op jit(solution)/shard_map/pallas_call | solution.py:299
  10.6 0.7 shard_map.80
  11.7 1.3 %collective-permute-done.2.vectors = f32[32,768]{1,0:T(8,128)S(1)} collective-permute-done((f32[32,768]{1,0:T(8,128)S(1)}, f32[32,768]{1,0:T(8,128)S(1)}, u32[]{:S(2)}, u32[]{:S(2)}) %collective-permute-start.2) | collective-permute-done | bytes 98336 | tf_op jit(solution)/shard_map/ppermute | solution.py:334
  13.0 0.5 shard_map.82.before
  13.5 1.2 %collective-permute-done.1.vectors = f32[32,768]{1,0:T(8,128)S(1)} collective-permute-done((f32[32,768]{1,0:T(8,128)S(1)}, f32[32,768]{1,0:T(8,128)S(1)}, u32[]{:S(2)}, u32[]{:S(2)}) %collective-permute-start.1) | collective-permute-done | bytes 98336 | tf_op jit(solution)/shard_map/ppermute | solution.py:333
  14.7 0.5 shard_map.83.partial
  15.2 1.3 %collective-permute-done.4.other = f32[32,768]{1,0:T(8,128)S(1)} collective-permute-done((f32[32,768]{1,0:T(8,128)S(1)}, f32[32,768]{1,0:T(8,128)S(1)}, u32[]{:S(2)}, u32[]{:S(2)}) %collective-permute-start.4) | collective-permute-done | bytes 98336 | tf_op jit(solution)/shard_map/ppermute | solution.py:342
  16.5 0.4 collective-permute-start.6
  16.9 0.3 collective-permute-start.5
  18.6 0.3 shard_map.85.before
  18.9 4.4 %collective-permute-done.6.vectors = f32[32,768]{1,0:T(8,128)S(1)} collective-permute-done((f32[32,768]{1,0:T(8,128)S(1)}, f32[32,768]{1,0:T(8,128)S(1)}, u32[]{:S(2)}, u32[]{:S(2)}) %collective-permute-start.6) | collective-permute-done | bytes 98336 | tf_op jit(solution)/shard_map/ppermute | solution.py:334
  23.3 0.5 shard_map.86.before
  23.8 0.5 collective-permute-done.5.vectors
  24.2 0.5 shard_map.87.partial
  24.8 1.2 %collective-permute-done.7.other = f32[32,768]{1,0:T(8,128)S(1)} collective-permute-done((f32[32,768]{1,0:T(8,128)S(1)}, f32[32,768]{1,0:T(8,128)S(1)}, u32[]{:S(2)}, u32[]{:S(2)}) %collective-permute-start.7) | collective-permute-done | bytes 98336 | tf_op jit(solution)/shard_map/ppermute | solution.py:342
  26.4 0.6 shard_map.89._after.chosen
  27.0 0.3 shard_map.90.before
  27.3 5.5 %collective-permute-done.9.vectors = f32[32,768]{1,0:T(8,128)S(1)} collective-permute-done((f32[32,768]{1,0:T(8,128)S(1)}, f32[32,768]{1,0:T(8,128)S(1)}, u32[]{:S(2)}, u32[]{:S(2)}) %collective-permute-start.9) | collective-permute-done | bytes 98336 | tf_op jit(solution)/shard_map/ppermute | solution.py:334
  32.8 0.5 shard_map.91.before
  33.2 0.4 collective-permute-done.8.vectors
  33.6 0.5 shard_map.92.partial
  34.1 1.3 %collective-permute-done.10.other = f32[32,768]{1,0:T(8,128)S(1)} collective-permute-done((f32[32,768]{1,0:T(8,128)S(1)}, f32[32,768]{1,0:T(8,128)S(1)}, u32[]{:S(2)}, u32[]{:S(2)}) %collective-permute-start.10) | collective-permute-done | bytes 98336 | tf_op jit(solution)/shard_map/ppermute | solution.py:342
  35.7 0.3 shard_map.94.before
  36.0 6.0 %collective-permute-done.12.vectors = f32[32,768]{1,0:T(8,128)S(1)} collective-permute-done((f32[32,768]{1,0:T(8,128)S(1)}, f32[32,768]{1,0:T(8,128)S(1)}, u32[]{:S(2)}, u32[]{:S(2)}) %collective-permute-start.12) | collective-permute-done | bytes 98336 | tf_op jit(solution)/shard_map/ppermute | solution.py:334
  41.9 0.5 shard_map.95.before
  42.4 0.5 collective-permute-done.11.vectors
  42.9 0.5 shard_map.96.partial
  43.4 1.3 %collective-permute-done.13.other = f32[32,768]{1,0:T(8,128)S(1)} collective-permute-done((f32[32,768]{1,0:T(8,128)S(1)}, f32[32,768]{1,0:T(8,128)S(1)}, u32[]{:S(2)}, u32[]{:S(2)}) %collective-permute-start.13) | collective-permute-done | bytes 98336 | tf_op jit(solution)/shard_map/ppermute | solution.py:342
  44.9 0.3 shard_map.98.before
  45.2 6.1 %collective-permute-done.15.vectors = f32[32,768]{1,0:T(8,128)S(1)} collective-permute-done((f32[32,768]{1,0:T(8,128)S(1)}, f32[32,768]{1,0:T(8,128)S(1)}, u32[]{:S(2)}, u32[]{:S(2)}) %collective-permute-start.15) | collective-permute-done | bytes 98336 | tf_op jit(solution)/shard_map/ppermute | solution.py:334
  51.3 0.5 shard_map.99.before
  51.7 0.5 collective-permute-done.14.vectors
  52.2 0.5 shard_map.100.partial
  52.7 1.3 %collective-permute-done.16.other = f32[32,768]{1,0:T(8,128)S(1)} collective-permute-done((f32[32,768]{1,0:T(8,128)S(1)}, f32[32,768]{1,0:T(8,128)S(1)}, u32[]{:S(2)}, u32[]{:S(2)}) %collective-permute-start.16) | collective-permute-done | bytes 98336 | tf_op jit(solution)/shard_map/ppermute | solution.py:342
  54.2 0.3 shard_map.102.before
  54.5 6.1 %collective-permute-done.18.vectors = f32[32,768]{1,0:T(8,128)S(1)} collective-permute-done((f32[32,768]{1,0:T(8,128)S(1)}, f32[32,768]{1,0:T(8,128)S(1)}, u32[]{:S(2)}, u32[]{:S(2)}) %collective-permute-start.18) | collective-permute-done | bytes 98336 | tf_op jit(solution)/shard_map/ppermute | solution.py:334
  60.6 0.5 shard_map.103.before
  61.0 0.5 collective-permute-done.17.vectors
  61.5 0.5 shard_map.104.partial
  62.0 1.3 %collective-permute-done.19.other = f32[32,768]{1,0:T(8,128)S(1)} collective-permute-done((f32[32,768]{1,0:T(8,128)S(1)}, f32[32,768]{1,0:T(8,128)S(1)}, u32[]{:S(2)}, u32[]{:S(2)}) %collective-permute-start.19) | collective-permute-done | bytes 98336 | tf_op jit(solution)/shard_map/ppermute | solution.py:342
  63.5 0.3 shard_map.106.before
  63.8 6.1 %collective-permute-done.21.vectors = f32[32,768]{1,0:T(8,128)S(1)} collective-permute-done((f32[32,768]{1,0:T(8,128)S(1)}, f32[32,768]{1,0:T(8,128)S(1)}, u32[]{:S(2)}, u32[]{:S(2)}) %collective-permute-start.21) | collective-permute-done | bytes 98336 | tf_op jit(solution)/shard_map/ppermute | solution.py:334
  69.9 0.5 shard_map.107.before
  70.3 0.5 collective-permute-done.20.vectors
  70.8 0.5 shard_map.108.partial
  71.3 1.3 %collective-permute-done.22.other = f32[32,768]{1,0:T(8,128)S(1)} collective-permute-done((f32[32,768]{1,0:T(8,128)S(1)}, f32[32,768]{1,0:T(8,128)S(1)}, u32[]{:S(2)}, u32[]{:S(2)}) %collective-permute-start.22) | collective-permute-done | bytes 98336 | tf_op jit(solution)/shard_map/ppermute | solution.py:342
  72.8 0.3 shard_map.110.before
  73.1 6.1 %collective-permute-done.24.vectors = f32[32,768]{1,0:T(8,128)S(1)} collective-permute-done((f32[32,768]{1,0:T(8,128)S(1)}, f32[32,768]{1,0:T(8,128)S(1)}, u32[]{:S(2)}, u32[]{:S(2)}) %collective-permute-start.24) | collective-permute-done | bytes 98336 | tf_op jit(solution)/shard_map/ppermute | solution.py:334
  79.2 0.5 shard_map.111.before
  79.6 0.5 collective-permute-done.23.vectors
  80.1 0.5 shard_map.112.partial
  80.6 1.3 %collective-permute-done.25.other = f32[32,768]{1,0:T(8,128)S(1)} collective-permute-done((f32[32,768]{1,0:T(8,128)S(1)}, f32[32,768]{1,0:T(8,128)S(1)}, u32[]{:S(2)}, u32[]{:S(2)}) %collective-permute-start.25) | collective-permute-done | bytes 98336 | tf_op jit(solution)/shard_map/ppermute | solution.py:342
  82.1 1.6 %collective-permute-start.26 = (f32[32,384]{1,0:T(8,128)S(1)}, f32[32,384]{1,0:T(8,128)S(1)}, u32[]{:S(2)}, u32[]{:S(2)}) collective-permute-start(f32[32,384]{1,0:T(8,128)S(1)} %slice.4.vectors), channel_id=1, source_target_pairs={{0,16},{16,0},{1,17},{17,1},{2,18},{18,2},{3,19},{19,3},{4,20},{20... | collective-permute-start | bytes 147464 | tf_op jit(solution)/shard_map/ppermute | solution.py:357
  84.0 4.5 %collective-permute-done.28.vectors = f32[32,768]{1,0:T(8,128)S(1)} collective-permute-done((f32[32,768]{1,0:T(8,128)S(1)}, f32[32,768]{1,0:T(8,128)S(1)}, u32[]{:S(2)}, u32[]{:S(2)}) %collective-permute-start.28) | collective-permute-done | bytes 98336 | tf_op jit(solution)/shard_map/ppermute | solution.py:334
  88.5 0.5 shard_map.115.before
  88.9 0.5 collective-permute-done.27.vectors
  89.4 0.5 shard_map.116.partial
  90.5 1.2 %collective-permute-done.29.other = f32[32,128]{1,0:T(8,128)S(1)} collective-permute-done((f32[32,128]{1,0:T(8,128)S(1)}, f32[32,128]{1,0:T(8,128)S(1)}, u32[]{:S(2)}, u32[]{:S(2)}) %collective-permute-start.29) | collective-permute-done | bytes 16416 | tf_op jit(solution)/shard_map/ppermute | solution.py:363
  91.7 10.4 %all_to_all.5.parts = f32[8,32,128]{2,1,0:T(8,128)S(1)} all-to-all(f32[8,32,128]{2,1,0:T(8,128)S(1)} %shard_map.119), channel_id=1, replica_groups={{0,2,4,6,8,10,12,14},{1,3,5,7,9,11,13,15},{16,18,20,22,24,26,28,30},{17..., dimensions={0} | all-to-all | bytes 262144 | tf_op jit(solution)/shard_map/all_to_all | solution.py:366
  102.1 2.0 %shard_map.120 = (f32[32,384]{1,0:T(8,128)}, f32[32,32]{1,0:T(8,128)}) custom-call(f32[8,32,128]{2,1,0:T(8,128)S(1)} %all_to_all.5.parts, f32[32,32]{1,0:T(8,128)S(1)} %shard_map.89._after.chosen, f32[32,384]{1,0:T(8,128)S(1)} %slice.4.vectors, f32[32,384]{1,0:T(8,128)S(1)} %collective-permute-done.26.lower), custom_call_target="tpu_custom_call" | custom-call | flops 1000000 | bytes 100000 | tf_op jit(solution)/shard_map/pallas_call | solution.py:367
  (50 shorter events, 3.0 us)
Async XLA Ops:
  0.6 3.6 %copy-start.1 = (f32[1,32,384]{2,1,0:T(8,128)S(1)}, f32[1,32,384]{2,1,0:T(8,128)}, u32[]{:S(2)}) copy-start(f32[1,32,384]{2,1,0:T(8,128)} %param.8) | copy-start | bytes 147460
  0.6 3.5 %collective-permute-start = (f32[32,384]{1,0:T(8,128)}, f32[32,384]{1,0:T(8,128)S(1)}, u32[]{:S(2)}, u32[]{:S(2)}) collective-permute-start(f32[32,384]{1,0:T(8,128)} %bitcast.6), channel_id=1, source_target_pairs={{0,1},{1,0},{2,3},{3,2},{4,5},{5,4},{6,7},{7,6},{8,9},{9,8},{10,11... | collective-permute-start | bytes 147464 | tf_op jit(solution)/shard_map/ppermute | solution.py:283
  1.2 7.7 %copy-start = (f32[3,24,128,128]{3,2,1,0:T(8,128)S(1)}, f32[3,24,128,128]{3,2,1,0:T(8,128)}, u32[]{:S(2)}) copy-start(f32[3,24,128,128]{3,2,1,0:T(8,128)} %tiles.3) | copy-start | bytes 14155780
  4.1 6.5 %collective-permute-start.3 = (f32[12,3,128,128]{3,2,1,0:T(8,128)S(1)}, f32[12,3,128,128]{3,2,1,0:T(8,128)S(1)}, u32[]{:S(2)}, u32[]{:S(2)}) collective-permute-start(f32[12,3,128,128]{3,2,1,0:T(8,128)S(1)} %shard_map.77), channel_id=1, source_target_pairs={{0,1},{1,0},{2,3},{3,2},{4,5},{5,4},{6,7},{7,6},{8,9},{9,8},{10,11... | collective-permute-start | bytes 7077896 | tf_op jit(solution)/shard_map/ppermute | solution.py:298
  4.3 8.7 %collective-permute-start.2 = (f32[32,768]{1,0:T(8,128)S(1)}, f32[32,768]{1,0:T(8,128)S(1)}, u32[]{:S(2)}, u32[]{:S(2)}) collective-permute-start(f32[32,768]{1,0:T(8,128)S(1)} %shard_map.78.vectors._after.initial), channel_id=1, source_target_pairs={{0,4},{1,13},{2,6},{3,15},{4,8},{5,1},{6,10},{7,3},{8,12},{9,5},{1... | collective-permute-start | bytes 294920 | tf_op jit(solution)/shard_map/ppermute | solution.py:334
  7.3 7.3 %collective-permute-start.1 = (f32[32,768]{1,0:T(8,128)S(1)}, f32[32,768]{1,0:T(8,128)S(1)}, u32[]{:S(2)}, u32[]{:S(2)}) collective-permute-start(f32[32,768]{1,0:T(8,128)S(1)} %shard_map.78.vectors._after.initial), channel_id=1, source_target_pairs={{0,2},{1,15},{2,4},{3,1},{4,6},{5,3},{6,8},{7,5},{8,10},{9,7},{10,... | collective-permute-start | bytes 294920 | tf_op jit(solution)/shard_map/ppermute | solution.py:333
  15.1 1.3 %collective-permute-start.4 = (f32[32,768]{1,0:T(8,128)S(1)}, f32[32,768]{1,0:T(8,128)S(1)}, u32[]{:S(2)}, u32[]{:S(2)}) collective-permute-start(f32[32,768]{1,0:T(8,128)S(1)} %shard_map.83.partial), channel_id=1, source_target_pairs={{0,1},{1,0},{2,3},{3,2},{4,5},{5,4},{6,7},{7,6},{8,9},{9,8},{10,11... | collective-permute-start | bytes 294920 | tf_op jit(solution)/shard_map/ppermute | solution.py:342
  16.5 6.8 %collective-permute-start.6 = (f32[32,768]{1,0:T(8,128)S(1)}, f32[32,768]{1,0:T(8,128)S(1)}, u32[]{:S(2)}, u32[]{:S(2)}) collective-permute-start(f32[32,768]{1,0:T(8,128)S(1)} %shard_map.84.vectors._after.image), channel_id=1, source_target_pairs={{0,4},{1,13},{2,6},{3,15},{4,8},{5,1},{6,10},{7,3},{8,12},{9,5},{1... | collective-permute-start | bytes 294920 | tf_op jit(solution)/shard_map/ppermute | solution.py:334
  16.9 7.3 %collective-permute-start.5 = (f32[32,768]{1,0:T(8,128)S(1)}, f32[32,768]{1,0:T(8,128)S(1)}, u32[]{:S(2)}, u32[]{:S(2)}) collective-permute-start(f32[32,768]{1,0:T(8,128)S(1)} %shard_map.84.vectors._after.image), channel_id=1, source_target_pairs={{0,2},{1,15},{2,4},{3,1},{4,6},{5,3},{6,8},{7,5},{8,10},{9,7},{10,... | collective-permute-start | bytes 294920 | tf_op jit(solution)/shard_map/ppermute | solution.py:333
  23.7 2.6 %copy-start.2 = (s32[1,8,2]{1,2,0:T(2,128)S(1)}, s32[1,8,2]{1,2,0:T(2,128)}, u32[]{:S(2)}) copy-start(s32[1,8,2]{1,2,0:T(2,128)} %param.11) | copy-start | bytes 196
  24.7 1.3 %collective-permute-start.7 = (f32[32,768]{1,0:T(8,128)S(1)}, f32[32,768]{1,0:T(8,128)S(1)}, u32[]{:S(2)}, u32[]{:S(2)}) collective-permute-start(f32[32,768]{1,0:T(8,128)S(1)} %shard_map.87.partial), channel_id=1, source_target_pairs={{0,1},{1,0},{2,3},{3,2},{4,5},{5,4},{6,7},{7,6},{8,9},{9,8},{10,11... | collective-permute-start | bytes 294920 | tf_op jit(solution)/shard_map/ppermute | solution.py:342
  26.2 6.6 %collective-permute-start.9 = (f32[32,768]{1,0:T(8,128)S(1)}, f32[32,768]{1,0:T(8,128)S(1)}, u32[]{:S(2)}, u32[]{:S(2)}) collective-permute-start(f32[32,768]{1,0:T(8,128)S(1)} %get-tuple-element.39.vectors.current.previous), channel_id=1, source_target_pairs={{0,4},{1,13},{2,6},{3,15},{4,8},{5,1},{6,10},{7,3},{8,12},{9,5},{1... | collective-permute-start | bytes 294920 | tf_op jit(solution)/shard_map/ppermute | solution.py:334
  26.2 7.4 %collective-permute-start.8 = (f32[32,768]{1,0:T(8,128)S(1)}, f32[32,768]{1,0:T(8,128)S(1)}, u32[]{:S(2)}, u32[]{:S(2)}) collective-permute-start(f32[32,768]{1,0:T(8,128)S(1)} %get-tuple-element.39.vectors.current.previous), channel_id=1, source_target_pairs={{0,2},{1,15},{2,4},{3,1},{4,6},{5,3},{6,8},{7,5},{8,10},{9,7},{10,... | collective-permute-start | bytes 294920 | tf_op jit(solution)/shard_map/ppermute | solution.py:333
  34.1 1.3 %collective-permute-start.10 = (f32[32,768]{1,0:T(8,128)S(1)}, f32[32,768]{1,0:T(8,128)S(1)}, u32[]{:S(2)}, u32[]{:S(2)}) collective-permute-start(f32[32,768]{1,0:T(8,128)S(1)} %shard_map.92.partial), channel_id=1, source_target_pairs={{0,1},{1,0},{2,3},{3,2},{4,5},{5,4},{6,7},{7,6},{8,9},{9,8},{10,11... | collective-permute-start | bytes 294920 | tf_op jit(solution)/shard_map/ppermute | solution.py:342
  35.5 6.5 %collective-permute-start.12 = (f32[32,768]{1,0:T(8,128)S(1)}, f32[32,768]{1,0:T(8,128)S(1)}, u32[]{:S(2)}, u32[]{:S(2)}) collective-permute-start(f32[32,768]{1,0:T(8,128)S(1)} %shard_map.93.vectors.current.previous), channel_id=1, source_target_pairs={{0,4},{1,13},{2,6},{3,15},{4,8},{5,1},{6,10},{7,3},{8,12},{9,5},{1... | collective-permute-start | bytes 294920 | tf_op jit(solution)/shard_map/ppermute | solution.py:334
  35.5 7.4 %collective-permute-start.11 = (f32[32,768]{1,0:T(8,128)S(1)}, f32[32,768]{1,0:T(8,128)S(1)}, u32[]{:S(2)}, u32[]{:S(2)}) collective-permute-start(f32[32,768]{1,0:T(8,128)S(1)} %shard_map.93.vectors.current.previous), channel_id=1, source_target_pairs={{0,2},{1,15},{2,4},{3,1},{4,6},{5,3},{6,8},{7,5},{8,10},{9,7},{10,... | collective-permute-start | bytes 294920 | tf_op jit(solution)/shard_map/ppermute | solution.py:333
  43.4 1.3 %collective-permute-start.13 = (f32[32,768]{1,0:T(8,128)S(1)}, f32[32,768]{1,0:T(8,128)S(1)}, u32[]{:S(2)}, u32[]{:S(2)}) collective-permute-start(f32[32,768]{1,0:T(8,128)S(1)} %shard_map.96.partial), channel_id=1, source_target_pairs={{0,1},{1,0},{2,3},{3,2},{4,5},{5,4},{6,7},{7,6},{8,9},{9,8},{10,11... | collective-permute-start | bytes 294920 | tf_op jit(solution)/shard_map/ppermute | solution.py:342
  44.8 6.5 %collective-permute-start.15 = (f32[32,768]{1,0:T(8,128)S(1)}, f32[32,768]{1,0:T(8,128)S(1)}, u32[]{:S(2)}, u32[]{:S(2)}) collective-permute-start(f32[32,768]{1,0:T(8,128)S(1)} %shard_map.97.vectors.current.previous), channel_id=1, source_target_pairs={{0,4},{1,13},{2,6},{3,15},{4,8},{5,1},{6,10},{7,3},{8,12},{9,5},{1... | collective-permute-start | bytes 294920 | tf_op jit(solution)/shard_map/ppermute | solution.py:334
  44.8 7.4 %collective-permute-start.14 = (f32[32,768]{1,0:T(8,128)S(1)}, f32[32,768]{1,0:T(8,128)S(1)}, u32[]{:S(2)}, u32[]{:S(2)}) collective-permute-start(f32[32,768]{1,0:T(8,128)S(1)} %shard_map.97.vectors.current.previous), channel_id=1, source_target_pairs={{0,2},{1,15},{2,4},{3,1},{4,6},{5,3},{6,8},{7,5},{8,10},{9,7},{10,... | collective-permute-start | bytes 294920 | tf_op jit(solution)/shard_map/ppermute | solution.py:333
  52.7 1.3 %collective-permute-start.16 = (f32[32,768]{1,0:T(8,128)S(1)}, f32[32,768]{1,0:T(8,128)S(1)}, u32[]{:S(2)}, u32[]{:S(2)}) collective-permute-start(f32[32,768]{1,0:T(8,128)S(1)} %shard_map.100.partial), channel_id=1, source_target_pairs={{0,1},{1,0},{2,3},{3,2},{4,5},{5,4},{6,7},{7,6},{8,9},{9,8},{10,11... | collective-permute-start | bytes 294920 | tf_op jit(solution)/shard_map/ppermute | solution.py:342
  54.1 6.5 %collective-permute-start.18 = (f32[32,768]{1,0:T(8,128)S(1)}, f32[32,768]{1,0:T(8,128)S(1)}, u32[]{:S(2)}, u32[]{:S(2)}) collective-permute-start(f32[32,768]{1,0:T(8,128)S(1)} %shard_map.101.vectors.current.previous), channel_id=1, source_target_pairs={{0,4},{1,13},{2,6},{3,15},{4,8},{5,1},{6,10},{7,3},{8,12},{9,5},{1... | collective-permute-start | bytes 294920 | tf_op jit(solution)/shard_map/ppermute | solution.py:334
  54.1 7.4 %collective-permute-start.17 = (f32[32,768]{1,0:T(8,128)S(1)}, f32[32,768]{1,0:T(8,128)S(1)}, u32[]{:S(2)}, u32[]{:S(2)}) collective-permute-start(f32[32,768]{1,0:T(8,128)S(1)} %shard_map.101.vectors.current.previous), channel_id=1, source_target_pairs={{0,2},{1,15},{2,4},{3,1},{4,6},{5,3},{6,8},{7,5},{8,10},{9,7},{10,... | collective-permute-start | bytes 294920 | tf_op jit(solution)/shard_map/ppermute | solution.py:333
  62.0 1.3 %collective-permute-start.19 = (f32[32,768]{1,0:T(8,128)S(1)}, f32[32,768]{1,0:T(8,128)S(1)}, u32[]{:S(2)}, u32[]{:S(2)}) collective-permute-start(f32[32,768]{1,0:T(8,128)S(1)} %shard_map.104.partial), channel_id=1, source_target_pairs={{0,1},{1,0},{2,3},{3,2},{4,5},{5,4},{6,7},{7,6},{8,9},{9,8},{10,11... | collective-permute-start | bytes 294920 | tf_op jit(solution)/shard_map/ppermute | solution.py:342
  63.4 6.5 %collective-permute-start.21 = (f32[32,768]{1,0:T(8,128)S(1)}, f32[32,768]{1,0:T(8,128)S(1)}, u32[]{:S(2)}, u32[]{:S(2)}) collective-permute-start(f32[32,768]{1,0:T(8,128)S(1)} %shard_map.105.vectors.current.previous), channel_id=1, source_target_pairs={{0,4},{1,13},{2,6},{3,15},{4,8},{5,1},{6,10},{7,3},{8,12},{9,5},{1... | collective-permute-start | bytes 294920 | tf_op jit(solution)/shard_map/ppermute | solution.py:334
  63.4 7.4 %collective-permute-start.20 = (f32[32,768]{1,0:T(8,128)S(1)}, f32[32,768]{1,0:T(8,128)S(1)}, u32[]{:S(2)}, u32[]{:S(2)}) collective-permute-start(f32[32,768]{1,0:T(8,128)S(1)} %shard_map.105.vectors.current.previous), channel_id=1, source_target_pairs={{0,2},{1,15},{2,4},{3,1},{4,6},{5,3},{6,8},{7,5},{8,10},{9,7},{10,... | collective-permute-start | bytes 294920 | tf_op jit(solution)/shard_map/ppermute | solution.py:333
  71.3 1.3 %collective-permute-start.22 = (f32[32,768]{1,0:T(8,128)S(1)}, f32[32,768]{1,0:T(8,128)S(1)}, u32[]{:S(2)}, u32[]{:S(2)}) collective-permute-start(f32[32,768]{1,0:T(8,128)S(1)} %shard_map.108.partial), channel_id=1, source_target_pairs={{0,1},{1,0},{2,3},{3,2},{4,5},{5,4},{6,7},{7,6},{8,9},{9,8},{10,11... | collective-permute-start | bytes 294920 | tf_op jit(solution)/shard_map/ppermute | solution.py:342
  72.7 6.5 %collective-permute-start.24 = (f32[32,768]{1,0:T(8,128)S(1)}, f32[32,768]{1,0:T(8,128)S(1)}, u32[]{:S(2)}, u32[]{:S(2)}) collective-permute-start(f32[32,768]{1,0:T(8,128)S(1)} %shard_map.109.vectors.current), channel_id=1, source_target_pairs={{0,4},{1,13},{2,6},{3,15},{4,8},{5,1},{6,10},{7,3},{8,12},{9,5},{1... | collective-permute-start | bytes 294920 | tf_op jit(solution)/shard_map/ppermute | solution.py:334
  72.7 7.4 %collective-permute-start.23 = (f32[32,768]{1,0:T(8,128)S(1)}, f32[32,768]{1,0:T(8,128)S(1)}, u32[]{:S(2)}, u32[]{:S(2)}) collective-permute-start(f32[32,768]{1,0:T(8,128)S(1)} %shard_map.109.vectors.current), channel_id=1, source_target_pairs={{0,2},{1,15},{2,4},{3,1},{4,6},{5,3},{6,8},{7,5},{8,10},{9,7},{10,... | collective-permute-start | bytes 294920 | tf_op jit(solution)/shard_map/ppermute | solution.py:333
  80.6 1.3 %collective-permute-start.25 = (f32[32,768]{1,0:T(8,128)S(1)}, f32[32,768]{1,0:T(8,128)S(1)}, u32[]{:S(2)}, u32[]{:S(2)}) collective-permute-start(f32[32,768]{1,0:T(8,128)S(1)} %shard_map.112.partial), channel_id=1, source_target_pairs={{0,1},{1,0},{2,3},{3,2},{4,5},{5,4},{6,7},{7,6},{8,9},{9,8},{10,11... | collective-permute-start | bytes 294920 | tf_op jit(solution)/shard_map/ppermute | solution.py:342
  82.0 6.5 %collective-permute-start.28 = (f32[32,768]{1,0:T(8,128)S(1)}, f32[32,768]{1,0:T(8,128)S(1)}, u32[]{:S(2)}, u32[]{:S(2)}) collective-permute-start(f32[32,768]{1,0:T(8,128)S(1)} %shard_map.113.vectors.pair), channel_id=1, source_target_pairs={{0,4},{1,13},{2,6},{3,15},{4,8},{5,1},{6,10},{7,3},{8,12},{9,5},{1... | collective-permute-start | bytes 294920 | tf_op jit(solution)/shard_map/ppermute | solution.py:334
  82.0 7.4 %collective-permute-start.27 = (f32[32,768]{1,0:T(8,128)S(1)}, f32[32,768]{1,0:T(8,128)S(1)}, u32[]{:S(2)}, u32[]{:S(2)}) collective-permute-start(f32[32,768]{1,0:T(8,128)S(1)} %shard_map.113.vectors.pair), channel_id=1, source_target_pairs={{0,2},{1,15},{2,4},{3,1},{4,6},{5,3},{6,8},{7,5},{8,10},{9,7},{10,... | collective-permute-start | bytes 294920 | tf_op jit(solution)/shard_map/ppermute | solution.py:333
  82.1 7.8 %collective-permute-start.26 = (f32[32,384]{1,0:T(8,128)S(1)}, f32[32,384]{1,0:T(8,128)S(1)}, u32[]{:S(2)}, u32[]{:S(2)}) collective-permute-start(f32[32,384]{1,0:T(8,128)S(1)} %slice.4.vectors), channel_id=1, source_target_pairs={{0,16},{16,0},{1,17},{17,1},{2,18},{18,2},{3,19},{19,3},{4,20},{20... | collective-permute-start | bytes 147464 | tf_op jit(solution)/shard_map/ppermute | solution.py:357
  90.5 1.2 %collective-permute-start.29 = (f32[32,128]{1,0:T(8,128)S(1)}, f32[32,128]{1,0:T(8,128)S(1)}, u32[]{:S(2)}, u32[]{:S(2)}) collective-permute-start(f32[32,128]{1,0:T(8,128)S(1)} %shard_map.118.one), channel_id=1, source_target_pairs={{0,1},{1,0},{2,3},{3,2},{4,5},{5,4},{6,7},{7,6},{8,9},{9,8},{10,11... | collective-permute-start | bytes 49160 | tf_op jit(solution)/shard_map/ppermute | solution.py:363

commit v5 on v4

--- a/solution.py
+++ b/solution.py
@@ -84,25 +84,28 @@
 
 
 def own_weights_kernel(pattern, tiles, *refs, rows, stored, total):
-    weights, (blocks, table, sem) = refs[:6], refs[6:]
-    copy = pltpu.make_async_copy(pattern, blocks, sem)
-    copy.start()
+    weights, (blocks, table, held, sems) = refs[:6], refs[6:]
+    copies = [pltpu.make_async_copy(tiles.at[row], held.at[row], sems.at[row]) for row in range(rows)]
+    copies.append(pltpu.make_async_copy(pattern, blocks, sems.at[rows]))
+    for copy in reversed(copies):
+        copy.start()
     span = 2 * REACH + 2 * rows
     me = lax.axis_index("row")
     core = me % 2
     start = (me // 2) * 2 * rows - REACH
     for entry in range(rows * span):
         table[entry] = -1
-    copy.wait()
+    copies[rows].wait()
     for row in range(rows):
         for k in range(stored):
             table[row * span + offset_in_span(blocks[row, k], start, total)] = k
-    for slot in range(5 * rows):
-        group, place = place_of(slot, rows)
-        for row in range(rows):
+    for row in reversed(range(rows)):
+        copies[row].wait()
+        for slot in range(5 * rows):
+            group, place = place_of(slot, rows)
             column = jnp.where(core == 0, column_of(slot, 0, rows), column_of(slot, 1, rows))
             k = table[row * span + column + REACH]
-            tile = tiles[row, jnp.maximum(k, 0)]
+            tile = held[row, jnp.maximum(k, 0)]
             store_tile(jnp.where(k >= 0, tile, 0.0), *weights[2 * group : 2 * group + 2], place, row)
 
 
@@ -184,16 +187,13 @@
     out[...] = jnp.where(lax.axis_index("cuts") == 0, 0.0, total)
 
 
-def gram_kernel(pair, lower, gram, below, mixed, *, half):
+def products_kernel(vectors, before, high, low, pair, lower, out, *, half):
     own = pair[:, :half]
-    gram[...] = dot(own, own, NT)
-    below[...] = dot(lower[...], lower[...], NT)
-    mixed[...] = dot(own, lower[...], NT)
-
-
-def cross_kernel(pair, partial, gram, below, mixed, out):
-    cross = dot(pair[...], partial[...], NT)
-    out[...] = jnp.concatenate([gram[...], mixed[...], below[...], cross], axis=1)
+    below = lower[...]
+    partial = before[...] + multiply(vectors[...], high, low)
+    out[...] = jnp.concatenate(
+        [dot(own, own, NT), dot(own, below, NT), dot(below, below, NT), dot(pair[...], partial, NT)], axis=1
+    )
 
 
 def spread_kernel(one, other, out):
@@ -280,6 +280,7 @@
     )
     vec = jax.ShapeDtypeStruct((count, whole), F32)
 
+    in_hbm = [pltpu.with_memory_space_constraint(array, pltpu.HBM) for array in (tile_pattern, block_tiles)]
     beside = lax.ppermute(initial, "row", swap)
     sent = call(
         functools.partial(gather_kernel, rows=rows, stored=stored, total=total),
@@ -293,20 +294,21 @@
             pltpu.SemaphoreType.DMA((2,)),
         ],
         cost_estimate=pl.CostEstimate(flops=0, bytes_accessed=8 * 10**6, transcendentals=0),
-    )(*(pltpu.with_memory_space_constraint(array, pltpu.HBM) for array in (tile_pattern, block_tiles)))
+    )(*in_hbm)
     sent, beside = lax.optimization_barrier((sent, beside))
     received = lax.ppermute(sent, "row", swap)
     weights = call(
         functools.partial(own_weights_kernel, rows=rows, stored=stored, total=total),
         shapes,
-        [HBM, VMEM],
+        [HBM, HBM],
         (VMEM,) * 6,
         scratch_shapes=[
             pltpu.SMEM((rows, stored), jnp.int32),
             pltpu.SMEM((rows * span,), jnp.int32),
-            pltpu.SemaphoreType.DMA,
+            pltpu.VMEM(block_tiles.shape, F32),
+            pltpu.SemaphoreType.DMA((rows + 1,)),
         ],
-    )(pltpu.with_memory_space_constraint(tile_pattern, pltpu.HBM), block_tiles)
+    )(*in_hbm)
     weights = call(
         functools.partial(other_weights_kernel, rows=rows),
         shapes,
@@ -329,16 +331,15 @@
             ),
         )(*vectors, high, low)
 
-    def apply_part(vectors, after):
+    def most_of_image(vectors, after):
         near = lax.ppermute(vectors, "row", nearer)
         far = lax.ppermute(vectors, "row", farther)
         partial = part(own_kernel, own_weights, vectors, after)
-        partial = part(add_kernel, far_weights, far, partial)
-        return part(add_kernel, near_weights, near, partial)
+        return near, part(add_kernel, far_weights, far, partial)
 
     current = call(functools.partial(join_kernel, half=half), vec, [VMEM, VMEM], VMEM)(initial, beside)
     def images(vectors, after):
-        partial = apply_part(vectors, after)
+        partial = part(add_kernel, near_weights, *most_of_image(vectors, after))
         return partial, lax.ppermute(partial, "row", swap)
 
     def step(kernel, out_shape, *operands):
@@ -355,11 +356,11 @@
 
     own = current[:, :half]
     lower = lax.ppermute(own, "cuts", below)
-    partial = apply_part(current, chosen)
-    lower, partial = lax.optimization_barrier((lower, partial))
-    squares = call(functools.partial(gram_kernel, half=half), (small,) * 3, [VMEM, VMEM], (VMEM,) * 3)(current, lower)
+    near, partial = most_of_image(current, chosen)
     sums = jax.ShapeDtypeStruct((count, 4 * count), F32)
-    products = call(cross_kernel, sums, [VMEM] * 5, VMEM)(current, partial, *squares)
+    products = call(functools.partial(products_kernel, half=half), sums, [VMEM] * 6, VMEM)(
+        near, partial, *near_weights, current, lower
+    )
     beside = lax.ppermute(products, "row", swap)
     spread = call(spread_kernel, jax.ShapeDtypeStruct((chips, *sums.shape), F32), [VMEM, VMEM], VMEM)(products, beside)
     same_core = [[2 * chip + core for chip in range(chips)] for core in range(2)]

time: 104 us -> 104 us (level)
  waiting for transfers between devices: 62.2 us -> 61.1 us
    ppermute x18, waiting for transfers between devices: 50.7 us -> 49.6 us  [the longest x9 44 us: most_of_image(): far = lax.ppermute(vectors, 'row', farther)]
    pallas_call x27 -> x26, Pallas kernels: 11.3 us -> 10.8 us  [part(): call(kernel, vec, [VMEM] * (len(vectors) + 2), VMEM, cost_estimate=pl.Cos...]
where the time goes in v5:
time: 104 us
  waiting for transfers between devices  61.1 us (59%)
  Pallas kernels  20.6 us (20%)
  blocking collectives  10.4 us (10%)
  starting transfers between devices  9.47 us (9%)
  between operations  2.38 us (2%)
    ppermute x9, waiting for transfers between devices, most_of_image(): far = lax.ppermute(vectors, 'row', farther)  44 us
    pallas_call x26, Pallas kernels, part(): call(kernel, vec, [VMEM] * (len(vectors) + 2), VMEM, cost_estimate=pl.Cos...  10.8 us
    all_to_all x1, blocking collectives, local(): lax.all_to_all(spread, 'row', 0, 0, tiled=True, axis_index_groups=same_core)  10.4 us
    ppermute x8, waiting for transfers between devices, images(): return (partial, lax.ppermute(partial, 'row', swap))  10.3 us
    ppermute x9, waiting for transfers between devices, most_of_image(): near = lax.ppermute(vectors, 'row', nearer)  5.64 us
    ppermute x9, starting transfers between devices, most_of_image(): far = lax.ppermute(vectors, 'row', farther)  4.63 us
    pallas_call x1, Pallas kernels, local(): call(functools.partial(own_weights_kernel, rows=rows, stored=stored, tota...  2.73 us
    pallas_call x1, Pallas kernels, local(): call(functools.partial(gather_kernel, rows=rows, stored=stored, total=tot...  2.51 us
  transfers between devices with their start and end apart: 30, of which 27 were waited for; matrix products, arithmetic and copies ran while one was open for 0% of the time, Pallas kernels for 13%

profile of v5, /device:TPU:0, one launch (start us, length us, event | category | flops | bytes accessed | tf_op | source)
XLA Modules:
  0.0 104.1 jit_solution(15828425246111102156)
XLA Ops:
  0.6 0.5 collective-permute-start
  1.2 2.5 %shard_map.77 = f32[12,3,128,128]{3,2,1,0:T(8,128)S(1)} custom-call(s32[3,24]{1,0:T(4,128)} %pattern.3, f32[3,24,128,128]{3,2,1,0:T(8,128)} %tiles.3), custom_call_target="tpu_custom_call" | custom-call | bytes 8000000 | tf_op jit(solution)/shard_map/pallas_call | solution.py:285
  3.9 3.1 %collective-permute-start.2 = (f32[32,768]{1,0:T(8,128)S(1)}, f32[32,768]{1,0:T(8,128)S(1)}, u32[]{:S(2)}, u32[]{:S(2)}) collective-permute-start(f32[32,768]{1,0:T(8,128)S(1)} %shard_map.78.vectors._after.initial), channel_id=1, source_target_pairs={{0,4},{1,13},{2,6},{3,15},{4,8},{5,1},{6,10},{7,3},{8,12},{9,5},{1... | collective-permute-start | bytes 294920 | tf_op jit(solution)/shard_map/ppermute | solution.py:336
  6.9 1.5 %collective-permute-start.1 = (f32[32,768]{1,0:T(8,128)S(1)}, f32[32,768]{1,0:T(8,128)S(1)}, u32[]{:S(2)}, u32[]{:S(2)}) collective-permute-start(f32[32,768]{1,0:T(8,128)S(1)} %shard_map.78.vectors._after.initial), channel_id=1, source_target_pairs={{0,2},{1,15},{2,4},{3,1},{4,6},{5,3},{6,8},{7,5},{8,10},{9,7},{10,... | collective-permute-start | bytes 294920 | tf_op jit(solution)/shard_map/ppermute | solution.py:335
  8.4 2.7 %shard_map.79 = (bf16[768,768]{1,0:T(8,128)(2,1)S(1)}, bf16[768,768]{1,0:T(8,128)(2,1)S(1)}, bf16[768,768]{1,0:T(8,128)(2,1)S(1)}, bf16[768,768]{1,0:T(8,128)(2,...) custom-call(s32[3,24]{1,0:T(4,128)} %pattern.3, f32[3,24,128,128]{3,2,1,0:T(8,128)} %tiles.3), custom_call_target="tpu_custom_call" | custom-call | flops 1000000 | bytes 100000 | tf_op jit(solution)/shard_map/pallas_call | solution.py:300
  11.2 0.7 shard_map.80
  11.9 0.3 shard_map.81.before
  12.2 0.3 collective-permute-done.2.vectors
  12.5 0.5 shard_map.82.before
  13.0 1.2 %collective-permute-done.1.vectors = f32[32,768]{1,0:T(8,128)S(1)} collective-permute-done((f32[32,768]{1,0:T(8,128)S(1)}, f32[32,768]{1,0:T(8,128)S(1)}, u32[]{:S(2)}, u32[]{:S(2)}) %collective-permute-start.1) | collective-permute-done | bytes 98336 | tf_op jit(solution)/shard_map/ppermute | solution.py:335
  14.2 0.5 shard_map.83.partial
  14.7 1.3 %collective-permute-done.4.other = f32[32,768]{1,0:T(8,128)S(1)} collective-permute-done((f32[32,768]{1,0:T(8,128)S(1)}, f32[32,768]{1,0:T(8,128)S(1)}, u32[]{:S(2)}, u32[]{:S(2)}) %collective-permute-start.4) | collective-permute-done | bytes 98336 | tf_op jit(solution)/shard_map/ppermute | solution.py:343
  16.1 1.1 %collective-permute-start.6 = (f32[32,768]{1,0:T(8,128)S(1)}, f32[32,768]{1,0:T(8,128)S(1)}, u32[]{:S(2)}, u32[]{:S(2)}) collective-permute-start(f32[32,768]{1,0:T(8,128)S(1)} %shard_map.84.vectors._after.image), channel_id=1, source_target_pairs={{0,4},{1,13},{2,6},{3,15},{4,8},{5,1},{6,10},{7,3},{8,12},{9,5},{1... | collective-permute-start | bytes 294920 | tf_op jit(solution)/shard_map/ppermute | solution.py:336
  17.2 0.5 collective-permute-start.5
  19.1 0.3 shard_map.85.before
  19.4 3.4 %collective-permute-done.6.vectors = f32[32,768]{1,0:T(8,128)S(1)} collective-permute-done((f32[32,768]{1,0:T(8,128)S(1)}, f32[32,768]{1,0:T(8,128)S(1)}, u32[]{:S(2)}, u32[]{:S(2)}) %collective-permute-start.6) | collective-permute-done | bytes 98336 | tf_op jit(solution)/shard_map/ppermute | solution.py:336
  22.8 0.5 shard_map.86.before
  23.3 1.2 %collective-permute-done.5.vectors = f32[32,768]{1,0:T(8,128)S(1)} collective-permute-done((f32[32,768]{1,0:T(8,128)S(1)}, f32[32,768]{1,0:T(8,128)S(1)}, u32[]{:S(2)}, u32[]{:S(2)}) %collective-permute-start.5) | collective-permute-done | bytes 98336 | tf_op jit(solution)/shard_map/ppermute | solution.py:335
  24.5 0.5 shard_map.87.partial
  25.1 1.2 %collective-permute-done.7.other = f32[32,768]{1,0:T(8,128)S(1)} collective-permute-done((f32[32,768]{1,0:T(8,128)S(1)}, f32[32,768]{1,0:T(8,128)S(1)}, u32[]{:S(2)}, u32[]{:S(2)}) %collective-permute-start.7) | collective-permute-done | bytes 98336 | tf_op jit(solution)/shard_map/ppermute | solution.py:343
  26.6 0.6 shard_map.89._after.chosen
  27.2 0.3 shard_map.90.before
  27.5 5.4 %collective-permute-done.9.vectors = f32[32,768]{1,0:T(8,128)S(1)} collective-permute-done((f32[32,768]{1,0:T(8,128)S(1)}, f32[32,768]{1,0:T(8,128)S(1)}, u32[]{:S(2)}, u32[]{:S(2)}) %collective-permute-start.9) | collective-permute-done | bytes 98336 | tf_op jit(solution)/shard_map/ppermute | solution.py:336
  32.9 0.5 shard_map.91.before
  33.4 0.5 collective-permute-done.8.vectors
  33.9 0.5 shard_map.92.partial
  34.4 1.3 %collective-permute-done.10.other = f32[32,768]{1,0:T(8,128)S(1)} collective-permute-done((f32[32,768]{1,0:T(8,128)S(1)}, f32[32,768]{1,0:T(8,128)S(1)}, u32[]{:S(2)}, u32[]{:S(2)}) %collective-permute-start.10) | collective-permute-done | bytes 98336 | tf_op jit(solution)/shard_map/ppermute | solution.py:343
  35.9 0.3 shard_map.94.before
  36.2 6.0 %collective-permute-done.12.vectors = f32[32,768]{1,0:T(8,128)S(1)} collective-permute-done((f32[32,768]{1,0:T(8,128)S(1)}, f32[32,768]{1,0:T(8,128)S(1)}, u32[]{:S(2)}, u32[]{:S(2)}) %collective-permute-start.12) | collective-permute-done | bytes 98336 | tf_op jit(solution)/shard_map/ppermute | solution.py:336
  42.2 0.5 shard_map.95.before
  42.7 0.5 collective-permute-done.11.vectors
  43.2 0.5 shard_map.96.partial
  43.7 1.3 %collective-permute-done.13.other = f32[32,768]{1,0:T(8,128)S(1)} collective-permute-done((f32[32,768]{1,0:T(8,128)S(1)}, f32[32,768]{1,0:T(8,128)S(1)}, u32[]{:S(2)}, u32[]{:S(2)}) %collective-permute-start.13) | collective-permute-done | bytes 98336 | tf_op jit(solution)/shard_map/ppermute | solution.py:343
  45.5 6.1 %collective-permute-done.15.vectors = f32[32,768]{1,0:T(8,128)S(1)} collective-permute-done((f32[32,768]{1,0:T(8,128)S(1)}, f32[32,768]{1,0:T(8,128)S(1)}, u32[]{:S(2)}, u32[]{:S(2)}) %collective-permute-start.15) | collective-permute-done | bytes 98336 | tf_op jit(solution)/shard_map/ppermute | solution.py:336
  51.6 0.5 shard_map.99.before
  52.0 0.5 collective-permute-done.14.vectors
  52.5 0.5 shard_map.100.partial
  53.0 1.3 %collective-permute-done.16.other = f32[32,768]{1,0:T(8,128)S(1)} collective-permute-done((f32[32,768]{1,0:T(8,128)S(1)}, f32[32,768]{1,0:T(8,128)S(1)}, u32[]{:S(2)}, u32[]{:S(2)}) %collective-permute-start.16) | collective-permute-done | bytes 98336 | tf_op jit(solution)/shard_map/ppermute | solution.py:343
  54.5 0.3 shard_map.102.before
  54.8 6.1 %collective-permute-done.18.vectors = f32[32,768]{1,0:T(8,128)S(1)} collective-permute-done((f32[32,768]{1,0:T(8,128)S(1)}, f32[32,768]{1,0:T(8,128)S(1)}, u32[]{:S(2)}, u32[]{:S(2)}) %collective-permute-start.18) | collective-permute-done | bytes 98336 | tf_op jit(solution)/shard_map/ppermute | solution.py:336
  60.9 0.5 shard_map.103.before
  61.3 0.5 collective-permute-done.17.vectors
  61.8 0.5 shard_map.104.partial
  62.3 1.3 %collective-permute-done.19.other = f32[32,768]{1,0:T(8,128)S(1)} collective-permute-done((f32[32,768]{1,0:T(8,128)S(1)}, f32[32,768]{1,0:T(8,128)S(1)}, u32[]{:S(2)}, u32[]{:S(2)}) %collective-permute-start.19) | collective-permute-done | bytes 98336 | tf_op jit(solution)/shard_map/ppermute | solution.py:343
  64.1 6.1 %collective-permute-done.21.vectors = f32[32,768]{1,0:T(8,128)S(1)} collective-permute-done((f32[32,768]{1,0:T(8,128)S(1)}, f32[32,768]{1,0:T(8,128)S(1)}, u32[]{:S(2)}, u32[]{:S(2)}) %collective-permute-start.21) | collective-permute-done | bytes 98336 | tf_op jit(solution)/shard_map/ppermute | solution.py:336
  70.2 0.5 shard_map.107.before
  70.6 0.5 collective-permute-done.20.vectors
  71.1 0.5 shard_map.108.partial
  71.6 1.3 %collective-permute-done.22.other = f32[32,768]{1,0:T(8,128)S(1)} collective-permute-done((f32[32,768]{1,0:T(8,128)S(1)}, f32[32,768]{1,0:T(8,128)S(1)}, u32[]{:S(2)}, u32[]{:S(2)}) %collective-permute-start.22) | collective-permute-done | bytes 98336 | tf_op jit(solution)/shard_map/ppermute | solution.py:343
  73.1 0.3 shard_map.110.before
  73.4 6.1 %collective-permute-done.24.vectors = f32[32,768]{1,0:T(8,128)S(1)} collective-permute-done((f32[32,768]{1,0:T(8,128)S(1)}, f32[32,768]{1,0:T(8,128)S(1)}, u32[]{:S(2)}, u32[]{:S(2)}) %collective-permute-start.24) | collective-permute-done | bytes 98336 | tf_op jit(solution)/shard_map/ppermute | solution.py:336
  79.5 0.5 shard_map.111.before
  79.9 0.5 collective-permute-done.23.vectors
  80.4 0.5 shard_map.112.partial
  80.9 1.3 %collective-permute-done.25.other = f32[32,768]{1,0:T(8,128)S(1)} collective-permute-done((f32[32,768]{1,0:T(8,128)S(1)}, f32[32,768]{1,0:T(8,128)S(1)}, u32[]{:S(2)}, u32[]{:S(2)}) %collective-permute-start.25) | collective-permute-done | bytes 98336 | tf_op jit(solution)/shard_map/ppermute | solution.py:343
  82.4 1.6 %collective-permute-start.28 = (f32[32,384]{1,0:T(8,128)S(1)}, f32[32,384]{1,0:T(8,128)S(1)}, u32[]{:S(2)}, u32[]{:S(2)}) collective-permute-start(f32[32,384]{1,0:T(8,128)S(1)} %slice.4.vectors), channel_id=1, source_target_pairs={{0,16},{16,0},{1,17},{17,1},{2,18},{18,2},{3,19},{19,3},{4,20},{20... | collective-permute-start | bytes 147464 | tf_op jit(solution)/shard_map/ppermute | solution.py:358
  84.0 0.3 shard_map.114.before
  84.3 4.5 %collective-permute-done.27.vectors = f32[32,768]{1,0:T(8,128)S(1)} collective-permute-done((f32[32,768]{1,0:T(8,128)S(1)}, f32[32,768]{1,0:T(8,128)S(1)}, u32[]{:S(2)}, u32[]{:S(2)}) %collective-permute-start.27) | collective-permute-done | bytes 98336 | tf_op jit(solution)/shard_map/ppermute | solution.py:336
  88.7 0.5 shard_map.115.before
  89.2 0.4 collective-permute-done.26.vectors
  89.7 0.8 shard_map.116.one
  90.5 1.2 %collective-permute-done.29.other = f32[32,128]{1,0:T(8,128)S(1)} collective-permute-done((f32[32,128]{1,0:T(8,128)S(1)}, f32[32,128]{1,0:T(8,128)S(1)}, u32[]{:S(2)}, u32[]{:S(2)}) %collective-permute-start.29) | collective-permute-done | bytes 16416 | tf_op jit(solution)/shard_map/ppermute | solution.py:364
  91.7 10.4 %all_to_all.5.parts = f32[8,32,128]{2,1,0:T(8,128)S(1)} all-to-all(f32[8,32,128]{2,1,0:T(8,128)S(1)} %shard_map.117), channel_id=1, replica_groups={{0,2,4,6,8,10,12,14},{1,3,5,7,9,11,13,15},{16,18,20,22,24,26,28,30},{17..., dimensions={0} | all-to-all | bytes 262144 | tf_op jit(solution)/shard_map/all_to_all | solution.py:367
  102.1 2.0 %shard_map.118 = (f32[32,384]{1,0:T(8,128)}, f32[32,32]{1,0:T(8,128)}) custom-call(f32[8,32,128]{2,1,0:T(8,128)S(1)} %all_to_all.5.parts, f32[32,32]{1,0:T(8,128)S(1)} %shard_map.89._after.chosen, f32[32,384]{1,0:T(8,128)S(1)} %slice.4.vectors, f32[32,384]{1,0:T(8,128)S(1)} %collective-permute-done.28.lower), custom_call_target="tpu_custom_call" | custom-call | flops 1000000 | bytes 100000 | tf_op jit(solution)/shard_map/pallas_call | solution.py:368
  (46 shorter events, 2.3 us)
Async XLA Ops:
  0.6 3.2 %copy-start = (f32[1,32,384]{2,1,0:T(8,128)S(1)}, f32[1,32,384]{2,1,0:T(8,128)}, u32[]{:S(2)}) copy-start(f32[1,32,384]{2,1,0:T(8,128)} %param.8) | copy-start | bytes 147460
  0.6 3.0 %collective-permute-start = (f32[32,384]{1,0:T(8,128)}, f32[32,384]{1,0:T(8,128)S(1)}, u32[]{:S(2)}, u32[]{:S(2)}) collective-permute-start(f32[32,384]{1,0:T(8,128)} %bitcast.6), channel_id=1, source_target_pairs={{0,1},{1,0},{2,3},{3,2},{4,5},{5,4},{6,7},{7,6},{8,9},{9,8},{10,11... | collective-permute-start | bytes 147464 | tf_op jit(solution)/shard_map/ppermute | solution.py:284
  3.7 7.5 %collective-permute-start.3 = (f32[12,3,128,128]{3,2,1,0:T(8,128)S(1)}, f32[12,3,128,128]{3,2,1,0:T(8,128)S(1)}, u32[]{:S(2)}, u32[]{:S(2)}) collective-permute-start(f32[12,3,128,128]{3,2,1,0:T(8,128)S(1)} %shard_map.77), channel_id=1, source_target_pairs={{0,1},{1,0},{2,3},{3,2},{4,5},{5,4},{6,7},{7,6},{8,9},{9,8},{10,11... | collective-permute-start | bytes 7077896 | tf_op jit(solution)/shard_map/ppermute | solution.py:299
  3.9 8.7 %collective-permute-start.2 = (f32[32,768]{1,0:T(8,128)S(1)}, f32[32,768]{1,0:T(8,128)S(1)}, u32[]{:S(2)}, u32[]{:S(2)}) collective-permute-start(f32[32,768]{1,0:T(8,128)S(1)} %shard_map.78.vectors._after.initial), channel_id=1, source_target_pairs={{0,4},{1,13},{2,6},{3,15},{4,8},{5,1},{6,10},{7,3},{8,12},{9,5},{1... | collective-permute-start | bytes 294920 | tf_op jit(solution)/shard_map/ppermute | solution.py:336
  6.9 7.3 %collective-permute-start.1 = (f32[32,768]{1,0:T(8,128)S(1)}, f32[32,768]{1,0:T(8,128)S(1)}, u32[]{:S(2)}, u32[]{:S(2)}) collective-permute-start(f32[32,768]{1,0:T(8,128)S(1)} %shard_map.78.vectors._after.initial), channel_id=1, source_target_pairs={{0,2},{1,15},{2,4},{3,1},{4,6},{5,3},{6,8},{7,5},{8,10},{9,7},{10,... | collective-permute-start | bytes 294920 | tf_op jit(solution)/shard_map/ppermute | solution.py:335
  14.7 1.3 %collective-permute-start.4 = (f32[32,768]{1,0:T(8,128)S(1)}, f32[32,768]{1,0:T(8,128)S(1)}, u32[]{:S(2)}, u32[]{:S(2)}) collective-permute-start(f32[32,768]{1,0:T(8,128)S(1)} %shard_map.83.partial), channel_id=1, source_target_pairs={{0,1},{1,0},{2,3},{3,2},{4,5},{5,4},{6,7},{7,6},{8,9},{9,8},{10,11... | collective-permute-start | bytes 294920 | tf_op jit(solution)/shard_map/ppermute | solution.py:343
  16.1 6.8 %collective-permute-start.6 = (f32[32,768]{1,0:T(8,128)S(1)}, f32[32,768]{1,0:T(8,128)S(1)}, u32[]{:S(2)}, u32[]{:S(2)}) collective-permute-start(f32[32,768]{1,0:T(8,128)S(1)} %shard_map.84.vectors._after.image), channel_id=1, source_target_pairs={{0,4},{1,13},{2,6},{3,15},{4,8},{5,1},{6,10},{7,3},{8,12},{9,5},{1... | collective-permute-start | bytes 294920 | tf_op jit(solution)/shard_map/ppermute | solution.py:336
  17.2 7.3 %collective-permute-start.5 = (f32[32,768]{1,0:T(8,128)S(1)}, f32[32,768]{1,0:T(8,128)S(1)}, u32[]{:S(2)}, u32[]{:S(2)}) collective-permute-start(f32[32,768]{1,0:T(8,128)S(1)} %shard_map.84.vectors._after.image), channel_id=1, source_target_pairs={{0,2},{1,15},{2,4},{3,1},{4,6},{5,3},{6,8},{7,5},{8,10},{9,7},{10,... | collective-permute-start | bytes 294920 | tf_op jit(solution)/shard_map/ppermute | solution.py:335
  23.3 3.3 %copy-start.1 = (s32[1,8,2]{1,2,0:T(2,128)S(1)}, s32[1,8,2]{1,2,0:T(2,128)}, u32[]{:S(2)}) copy-start(s32[1,8,2]{1,2,0:T(2,128)} %param.11) | copy-start | bytes 196
  25.0 1.3 %collective-permute-start.7 = (f32[32,768]{1,0:T(8,128)S(1)}, f32[32,768]{1,0:T(8,128)S(1)}, u32[]{:S(2)}, u32[]{:S(2)}) collective-permute-start(f32[32,768]{1,0:T(8,128)S(1)} %shard_map.87.partial), channel_id=1, source_target_pairs={{0,1},{1,0},{2,3},{3,2},{4,5},{5,4},{6,7},{7,6},{8,9},{9,8},{10,11... | collective-permute-start | bytes 294920 | tf_op jit(solution)/shard_map/ppermute | solution.py:343
  26.5 6.5 %collective-permute-start.9 = (f32[32,768]{1,0:T(8,128)S(1)}, f32[32,768]{1,0:T(8,128)S(1)}, u32[]{:S(2)}, u32[]{:S(2)}) collective-permute-start(f32[32,768]{1,0:T(8,128)S(1)} %get-tuple-element.34.vectors.current.previous), channel_id=1, source_target_pairs={{0,4},{1,13},{2,6},{3,15},{4,8},{5,1},{6,10},{7,3},{8,12},{9,5},{1... | collective-permute-start | bytes 294920 | tf_op jit(solution)/shard_map/ppermute | solution.py:336
  26.5 7.4 %collective-permute-start.8 = (f32[32,768]{1,0:T(8,128)S(1)}, f32[32,768]{1,0:T(8,128)S(1)}, u32[]{:S(2)}, u32[]{:S(2)}) collective-permute-start(f32[32,768]{1,0:T(8,128)S(1)} %get-tuple-element.34.vectors.current.previous), channel_id=1, source_target_pairs={{0,2},{1,15},{2,4},{3,1},{4,6},{5,3},{6,8},{7,5},{8,10},{9,7},{10,... | collective-permute-start | bytes 294920 | tf_op jit(solution)/shard_map/ppermute | solution.py:335
  34.4 1.3 %collective-permute-start.10 = (f32[32,768]{1,0:T(8,128)S(1)}, f32[32,768]{1,0:T(8,128)S(1)}, u32[]{:S(2)}, u32[]{:S(2)}) collective-permute-start(f32[32,768]{1,0:T(8,128)S(1)} %shard_map.92.partial), channel_id=1, source_target_pairs={{0,1},{1,0},{2,3},{3,2},{4,5},{5,4},{6,7},{7,6},{8,9},{9,8},{10,11... | collective-permute-start | bytes 294920 | tf_op jit(solution)/shard_map/ppermute | solution.py:343
  35.8 6.5 %collective-permute-start.12 = (f32[32,768]{1,0:T(8,128)S(1)}, f32[32,768]{1,0:T(8,128)S(1)}, u32[]{:S(2)}, u32[]{:S(2)}) collective-permute-start(f32[32,768]{1,0:T(8,128)S(1)} %shard_map.93.vectors.current.previous), channel_id=1, source_target_pairs={{0,4},{1,13},{2,6},{3,15},{4,8},{5,1},{6,10},{7,3},{8,12},{9,5},{1... | collective-permute-start | bytes 294920 | tf_op jit(solution)/shard_map/ppermute | solution.py:336
  35.8 7.4 %collective-permute-start.11 = (f32[32,768]{1,0:T(8,128)S(1)}, f32[32,768]{1,0:T(8,128)S(1)}, u32[]{:S(2)}, u32[]{:S(2)}) collective-permute-start(f32[32,768]{1,0:T(8,128)S(1)} %shard_map.93.vectors.current.previous), channel_id=1, source_target_pairs={{0,2},{1,15},{2,4},{3,1},{4,6},{5,3},{6,8},{7,5},{8,10},{9,7},{10,... | collective-permute-start | bytes 294920 | tf_op jit(solution)/shard_map/ppermute | solution.py:335
  43.7 1.3 %collective-permute-start.13 = (f32[32,768]{1,0:T(8,128)S(1)}, f32[32,768]{1,0:T(8,128)S(1)}, u32[]{:S(2)}, u32[]{:S(2)}) collective-permute-start(f32[32,768]{1,0:T(8,128)S(1)} %shard_map.96.partial), channel_id=1, source_target_pairs={{0,1},{1,0},{2,3},{3,2},{4,5},{5,4},{6,7},{7,6},{8,9},{9,8},{10,11... | collective-permute-start | bytes 294920 | tf_op jit(solution)/shard_map/ppermute | solution.py:343
  45.1 6.5 %collective-permute-start.15 = (f32[32,768]{1,0:T(8,128)S(1)}, f32[32,768]{1,0:T(8,128)S(1)}, u32[]{:S(2)}, u32[]{:S(2)}) collective-permute-start(f32[32,768]{1,0:T(8,128)S(1)} %shard_map.97.vectors.current.previous), channel_id=1, source_target_pairs={{0,4},{1,13},{2,6},{3,15},{4,8},{5,1},{6,10},{7,3},{8,12},{9,5},{1... | collective-permute-start | bytes 294920 | tf_op jit(solution)/shard_map/ppermute | solution.py:336
  45.1 7.4 %collective-permute-start.14 = (f32[32,768]{1,0:T(8,128)S(1)}, f32[32,768]{1,0:T(8,128)S(1)}, u32[]{:S(2)}, u32[]{:S(2)}) collective-permute-start(f32[32,768]{1,0:T(8,128)S(1)} %shard_map.97.vectors.current.previous), channel_id=1, source_target_pairs={{0,2},{1,15},{2,4},{3,1},{4,6},{5,3},{6,8},{7,5},{8,10},{9,7},{10,... | collective-permute-start | bytes 294920 | tf_op jit(solution)/shard_map/ppermute | solution.py:335
  53.0 1.3 %collective-permute-start.16 = (f32[32,768]{1,0:T(8,128)S(1)}, f32[32,768]{1,0:T(8,128)S(1)}, u32[]{:S(2)}, u32[]{:S(2)}) collective-permute-start(f32[32,768]{1,0:T(8,128)S(1)} %shard_map.100.partial), channel_id=1, source_target_pairs={{0,1},{1,0},{2,3},{3,2},{4,5},{5,4},{6,7},{7,6},{8,9},{9,8},{10,11... | collective-permute-start | bytes 294920 | tf_op jit(solution)/shard_map/ppermute | solution.py:343
  54.4 6.5 %collective-permute-start.18 = (f32[32,768]{1,0:T(8,128)S(1)}, f32[32,768]{1,0:T(8,128)S(1)}, u32[]{:S(2)}, u32[]{:S(2)}) collective-permute-start(f32[32,768]{1,0:T(8,128)S(1)} %shard_map.101.vectors.current.previous), channel_id=1, source_target_pairs={{0,4},{1,13},{2,6},{3,15},{4,8},{5,1},{6,10},{7,3},{8,12},{9,5},{1... | collective-permute-start | bytes 294920 | tf_op jit(solution)/shard_map/ppermute | solution.py:336
  54.4 7.4 %collective-permute-start.17 = (f32[32,768]{1,0:T(8,128)S(1)}, f32[32,768]{1,0:T(8,128)S(1)}, u32[]{:S(2)}, u32[]{:S(2)}) collective-permute-start(f32[32,768]{1,0:T(8,128)S(1)} %shard_map.101.vectors.current.previous), channel_id=1, source_target_pairs={{0,2},{1,15},{2,4},{3,1},{4,6},{5,3},{6,8},{7,5},{8,10},{9,7},{10,... | collective-permute-start | bytes 294920 | tf_op jit(solution)/shard_map/ppermute | solution.py:335
  62.3 1.3 %collective-permute-start.19 = (f32[32,768]{1,0:T(8,128)S(1)}, f32[32,768]{1,0:T(8,128)S(1)}, u32[]{:S(2)}, u32[]{:S(2)}) collective-permute-start(f32[32,768]{1,0:T(8,128)S(1)} %shard_map.104.partial), channel_id=1, source_target_pairs={{0,1},{1,0},{2,3},{3,2},{4,5},{5,4},{6,7},{7,6},{8,9},{9,8},{10,11... | collective-permute-start | bytes 294920 | tf_op jit(solution)/shard_map/ppermute | solution.py:343
  63.7 6.5 %collective-permute-start.21 = (f32[32,768]{1,0:T(8,128)S(1)}, f32[32,768]{1,0:T(8,128)S(1)}, u32[]{:S(2)}, u32[]{:S(2)}) collective-permute-start(f32[32,768]{1,0:T(8,128)S(1)} %shard_map.105.vectors.current.previous), channel_id=1, source_target_pairs={{0,4},{1,13},{2,6},{3,15},{4,8},{5,1},{6,10},{7,3},{8,12},{9,5},{1... | collective-permute-start | bytes 294920 | tf_op jit(solution)/shard_map/ppermute | solution.py:336
  63.7 7.4 %collective-permute-start.20 = (f32[32,768]{1,0:T(8,128)S(1)}, f32[32,768]{1,0:T(8,128)S(1)}, u32[]{:S(2)}, u32[]{:S(2)}) collective-permute-start(f32[32,768]{1,0:T(8,128)S(1)} %shard_map.105.vectors.current.previous), channel_id=1, source_target_pairs={{0,2},{1,15},{2,4},{3,1},{4,6},{5,3},{6,8},{7,5},{8,10},{9,7},{10,... | collective-permute-start | bytes 294920 | tf_op jit(solution)/shard_map/ppermute | solution.py:335
  71.6 1.3 %collective-permute-start.22 = (f32[32,768]{1,0:T(8,128)S(1)}, f32[32,768]{1,0:T(8,128)S(1)}, u32[]{:S(2)}, u32[]{:S(2)}) collective-permute-start(f32[32,768]{1,0:T(8,128)S(1)} %shard_map.108.partial), channel_id=1, source_target_pairs={{0,1},{1,0},{2,3},{3,2},{4,5},{5,4},{6,7},{7,6},{8,9},{9,8},{10,11... | collective-permute-start | bytes 294920 | tf_op jit(solution)/shard_map/ppermute | solution.py:343
  73.0 6.5 %collective-permute-start.24 = (f32[32,768]{1,0:T(8,128)S(1)}, f32[32,768]{1,0:T(8,128)S(1)}, u32[]{:S(2)}, u32[]{:S(2)}) collective-permute-start(f32[32,768]{1,0:T(8,128)S(1)} %shard_map.109.vectors.current), channel_id=1, source_target_pairs={{0,4},{1,13},{2,6},{3,15},{4,8},{5,1},{6,10},{7,3},{8,12},{9,5},{1... | collective-permute-start | bytes 294920 | tf_op jit(solution)/shard_map/ppermute | solution.py:336
  73.0 7.4 %collective-permute-start.23 = (f32[32,768]{1,0:T(8,128)S(1)}, f32[32,768]{1,0:T(8,128)S(1)}, u32[]{:S(2)}, u32[]{:S(2)}) collective-permute-start(f32[32,768]{1,0:T(8,128)S(1)} %shard_map.109.vectors.current), channel_id=1, source_target_pairs={{0,2},{1,15},{2,4},{3,1},{4,6},{5,3},{6,8},{7,5},{8,10},{9,7},{10,... | collective-permute-start | bytes 294920 | tf_op jit(solution)/shard_map/ppermute | solution.py:335
  80.9 1.3 %collective-permute-start.25 = (f32[32,768]{1,0:T(8,128)S(1)}, f32[32,768]{1,0:T(8,128)S(1)}, u32[]{:S(2)}, u32[]{:S(2)}) collective-permute-start(f32[32,768]{1,0:T(8,128)S(1)} %shard_map.112.partial), channel_id=1, source_target_pairs={{0,1},{1,0},{2,3},{3,2},{4,5},{5,4},{6,7},{7,6},{8,9},{9,8},{10,11... | collective-permute-start | bytes 294920 | tf_op jit(solution)/shard_map/ppermute | solution.py:343
  82.3 6.5 %collective-permute-start.27 = (f32[32,768]{1,0:T(8,128)S(1)}, f32[32,768]{1,0:T(8,128)S(1)}, u32[]{:S(2)}, u32[]{:S(2)}) collective-permute-start(f32[32,768]{1,0:T(8,128)S(1)} %shard_map.113.vectors.pair), channel_id=1, source_target_pairs={{0,4},{1,13},{2,6},{3,15},{4,8},{5,1},{6,10},{7,3},{8,12},{9,5},{1... | collective-permute-start | bytes 294920 | tf_op jit(solution)/shard_map/ppermute | solution.py:336
  82.3 7.4 %collective-permute-start.26 = (f32[32,768]{1,0:T(8,128)S(1)}, f32[32,768]{1,0:T(8,128)S(1)}, u32[]{:S(2)}, u32[]{:S(2)}) collective-permute-start(f32[32,768]{1,0:T(8,128)S(1)} %shard_map.113.vectors.pair), channel_id=1, source_target_pairs={{0,2},{1,15},{2,4},{3,1},{4,6},{5,3},{6,8},{7,5},{8,10},{9,7},{10,... | collective-permute-start | bytes 294920 | tf_op jit(solution)/shard_map/ppermute | solution.py:335
  82.4 6.8 %collective-permute-start.28 = (f32[32,384]{1,0:T(8,128)S(1)}, f32[32,384]{1,0:T(8,128)S(1)}, u32[]{:S(2)}, u32[]{:S(2)}) collective-permute-start(f32[32,384]{1,0:T(8,128)S(1)} %slice.4.vectors), channel_id=1, source_target_pairs={{0,16},{16,0},{1,17},{17,1},{2,18},{18,2},{3,19},{19,3},{4,20},{20... | collective-permute-start | bytes 147464 | tf_op jit(solution)/shard_map/ppermute | solution.py:358
  90.5 1.2 %collective-permute-start.29 = (f32[32,128]{1,0:T(8,128)S(1)}, f32[32,128]{1,0:T(8,128)S(1)}, u32[]{:S(2)}, u32[]{:S(2)}) collective-permute-start(f32[32,128]{1,0:T(8,128)S(1)} %shard_map.116.one), channel_id=1, source_target_pairs={{0,1},{1,0},{2,3},{3,2},{4,5},{5,4},{6,7},{7,6},{8,9},{9,8},{10,11... | collective-permute-start | bytes 49160 | tf_op jit(solution)/shard_map/ppermute | solution.py:364

commit v6 on v4

--- a/solution.py
+++ b/solution.py
@@ -184,16 +184,13 @@
     out[...] = jnp.where(lax.axis_index("cuts") == 0, 0.0, total)
 
 
-def gram_kernel(pair, lower, gram, below, mixed, *, half):
+def products_kernel(vectors, before, high, low, pair, lower, out, *, half):
     own = pair[:, :half]
-    gram[...] = dot(own, own, NT)
-    below[...] = dot(lower[...], lower[...], NT)
-    mixed[...] = dot(own, lower[...], NT)
-
-
-def cross_kernel(pair, partial, gram, below, mixed, out):
-    cross = dot(pair[...], partial[...], NT)
-    out[...] = jnp.concatenate([gram[...], mixed[...], below[...], cross], axis=1)
+    below = lower[...]
+    partial = before[...] + multiply(vectors[...], high, low)
+    out[...] = jnp.concatenate(
+        [dot(own, own, NT), dot(own, below, NT), dot(below, below, NT), dot(pair[...], partial, NT)], axis=1
+    )
 
 
 def spread_kernel(one, other, out):
@@ -209,7 +206,7 @@
     return total
 
 
-def inverses(squares):
+def eliminated(squares):
     count = squares.shape[0]
     block = 16
     sub = lax.broadcasted_iota(jnp.int32, squares.shape, 0)
@@ -217,6 +214,7 @@
     left = lane < 2 * count
     place = jnp.where(left, lane, lane - 2 * count)
     work = jnp.where(place < count, squares, (place == sub + count).astype(F32))
+    beside = jnp.where(lane < count, pltpu.roll(squares, 3 * count, 1), pltpu.roll(squares, 2 * count, 1))
     for k in range(0, count, block):
         columns = [
             jnp.where(left, work[:, m : m + 1], work[:, 2 * count + m : 2 * count + m + 1]) for m in range(k, k + block)
@@ -227,22 +225,22 @@
             for j in range(i + 1, block):
                 columns[j] = columns[j] - factor * columns[j][here]
             work = work - factor * work[here]
+            beside = beside - factor * beside[here]
     pivots = jnp.where(place == sub, work, 0.0)
-    for start in (0, 2 * count):
-        pivot = jnp.sum(pivots[:, start : start + count], axis=1, keepdims=True)
-        yield work[:, start + count : start + 2 * count] * (1.0 / jnp.sqrt(pivot))
+    first = 1.0 / jnp.sqrt(jnp.sum(pivots[:, :count], axis=1, keepdims=True))
+    third = 1.0 / jnp.sqrt(jnp.sum(pivots[:, 2 * count : 3 * count], axis=1, keepdims=True))
+    inverse = work[:, count : 2 * count] * first
+    inverse_below = work[:, 3 * count :] * third
+    return inverse, inverse_below, beside[:, :count] * first, beside[:, count : 2 * count] * first
 
 
 def finish_kernel(parts, chosen, vectors, lower, filtered, projected, *, order):
-    count = vectors.shape[0]
-    total = summed(parts)
-    mixed, cross = total[:, count : 2 * count], total[:, 3 * count :]
-    inverse, inverse_below = inverses(total)
+    inverse, inverse_below, mixed, cross = eliminated(summed(parts))
     scale = math.sqrt(order)
     basis = scale * dot(inverse, vectors[...], NN)
     lower_basis = scale * dot(inverse_below, lower[...], NN)
-    correlation = dot(dot(inverse, mixed, NN), inverse_below, NT)
-    projected[...] = dot(dot(inverse, cross, NN), inverse, NT)
+    correlation = dot(mixed, inverse_below, NT)
+    projected[...] = dot(cross, inverse, NT)
     some = jnp.max(chosen[...]) > 0.0
     removal = jnp.where(some, dot(chosen[...] * correlation, lower_basis, NN), 0.0)
     filtered[...] = basis - removal
@@ -329,16 +327,15 @@
             ),
         )(*vectors, high, low)
 
-    def apply_part(vectors, after):
+    def most_of_image(vectors, after):
         near = lax.ppermute(vectors, "row", nearer)
         far = lax.ppermute(vectors, "row", farther)
         partial = part(own_kernel, own_weights, vectors, after)
-        partial = part(add_kernel, far_weights, far, partial)
-        return part(add_kernel, near_weights, near, partial)
+        return near, part(add_kernel, far_weights, far, partial)
 
     current = call(functools.partial(join_kernel, half=half), vec, [VMEM, VMEM], VMEM)(initial, beside)
     def images(vectors, after):
-        partial = apply_part(vectors, after)
+        partial = part(add_kernel, near_weights, *most_of_image(vectors, after))
         return partial, lax.ppermute(partial, "row", swap)
 
     def step(kernel, out_shape, *operands):
@@ -355,11 +352,11 @@
 
     own = current[:, :half]
     lower = lax.ppermute(own, "cuts", below)
-    partial = apply_part(current, chosen)
-    lower, partial = lax.optimization_barrier((lower, partial))
-    squares = call(functools.partial(gram_kernel, half=half), (small,) * 3, [VMEM, VMEM], (VMEM,) * 3)(current, lower)
+    near, partial = most_of_image(current, chosen)
     sums = jax.ShapeDtypeStruct((count, 4 * count), F32)
-    products = call(cross_kernel, sums, [VMEM] * 5, VMEM)(current, partial, *squares)
+    products = call(functools.partial(products_kernel, half=half), sums, [VMEM] * 6, VMEM)(
+        near, partial, *near_weights, current, lower
+    )
     beside = lax.ppermute(products, "row", swap)
     spread = call(spread_kernel, jax.ShapeDtypeStruct((chips, *sums.shape), F32), [VMEM, VMEM], VMEM)(products, beside)
     same_core = [[2 * chip + core for chip in range(chips)] for core in range(2)]

time: 104 us -> 104 us (level)
    pallas_call x27 -> x26, Pallas kernels: 11.3 us -> 10.8 us  [part(): call(kernel, vec, [VMEM] * (len(vectors) + 2), VMEM, cost_estimate=pl.Cos...]
where the time goes in v6:
time: 104 us
  waiting for transfers between devices  62.2 us (60%)
  Pallas kernels  19.9 us (19%)
  blocking collectives  10.4 us (10%)
  starting transfers between devices  8.66 us (8%)
  between operations  2.36 us (2%)
    ppermute x9, waiting for transfers between devices, most_of_image(): far = lax.ppermute(vectors, 'row', farther)  45.9 us
    pallas_call x26, Pallas kernels, part(): call(kernel, vec, [VMEM] * (len(vectors) + 2), VMEM, cost_estimate=pl.Cos...  10.8 us
    all_to_all x1, blocking collectives, local(): lax.all_to_all(spread, 'row', 0, 0, tiled=True, axis_index_groups=same_core)  10.4 us
    ppermute x8, waiting for transfers between devices, images(): return (partial, lax.ppermute(partial, 'row', swap))  10.3 us
    ppermute x9, waiting for transfers between devices, most_of_image(): near = lax.ppermute(vectors, 'row', nearer)  4.82 us
    ppermute x9, starting transfers between devices, most_of_image(): far = lax.ppermute(vectors, 'row', farther)  3.93 us
    pallas_call x1, Pallas kernels, local(): call(functools.partial(gather_kernel, rows=rows, stored=stored, total=tot...  2.97 us
    ppermute x9, starting transfers between devices, most_of_image(): near = lax.ppermute(vectors, 'row', nearer)  2.38 us
  transfers between devices with their start and end apart: 30, of which 27 were waited for; matrix products, arithmetic and copies ran while one was open for 0% of the time, Pallas kernels for 13%

profile of v6, /device:TPU:0, one launch (start us, length us, event | category | flops | bytes accessed | tf_op | source)
XLA Modules:
  0.0 103.7 jit_solution(7834222830786448611)
XLA Ops:
  0.6 0.5 collective-permute-start
  1.2 3.0 %shard_map.77 = f32[12,3,128,128]{3,2,1,0:T(8,128)S(1)} custom-call(s32[3,24]{1,0:T(4,128)} %pattern.3, f32[3,24,128,128]{3,2,1,0:T(8,128)} %tiles.3), custom_call_target="tpu_custom_call" | custom-call | bytes 8000000 | tf_op jit(solution)/shard_map/pallas_call | solution.py:282
  4.3 3.1 %collective-permute-start.2 = (f32[32,768]{1,0:T(8,128)S(1)}, f32[32,768]{1,0:T(8,128)S(1)}, u32[]{:S(2)}, u32[]{:S(2)}) collective-permute-start(f32[32,768]{1,0:T(8,128)S(1)} %shard_map.78.vectors._after.initial), channel_id=1, source_target_pairs={{0,4},{1,13},{2,6},{3,15},{4,8},{5,1},{6,10},{7,3},{8,12},{9,5},{1... | collective-permute-start | bytes 294920 | tf_op jit(solution)/shard_map/ppermute | solution.py:332
  7.4 1.5 %collective-permute-start.1 = (f32[32,768]{1,0:T(8,128)S(1)}, f32[32,768]{1,0:T(8,128)S(1)}, u32[]{:S(2)}, u32[]{:S(2)}) collective-permute-start(f32[32,768]{1,0:T(8,128)S(1)} %shard_map.78.vectors._after.initial), channel_id=1, source_target_pairs={{0,2},{1,15},{2,4},{3,1},{4,6},{5,3},{6,8},{7,5},{8,10},{9,7},{10,... | collective-permute-start | bytes 294920 | tf_op jit(solution)/shard_map/ppermute | solution.py:331
  8.9 1.8 %shard_map.79 = (bf16[768,768]{1,0:T(8,128)(2,1)S(1)}, bf16[768,768]{1,0:T(8,128)(2,1)S(1)}, bf16[768,768]{1,0:T(8,128)(2,1)S(1)}, bf16[768,768]{1,0:T(8,128)(2,...) custom-call(s32[3,24]{1,0:T(4,128)} %pattern.3, f32[3,24,128,128]{3,2,1,0:T(8,128)S(1)} %copy-done), custom_call_target="tpu_custom_call" | custom-call | flops 1000000 | bytes 100000 | tf_op jit(solution)/shard_map/pallas_call | solution.py:297
  10.6 0.7 shard_map.80
  11.4 0.3 shard_map.81.before
  11.7 1.3 %collective-permute-done.2.vectors = f32[32,768]{1,0:T(8,128)S(1)} collective-permute-done((f32[32,768]{1,0:T(8,128)S(1)}, f32[32,768]{1,0:T(8,128)S(1)}, u32[]{:S(2)}, u32[]{:S(2)}) %collective-permute-start.2) | collective-permute-done | bytes 98336 | tf_op jit(solution)/shard_map/ppermute | solution.py:332
  13.0 0.5 shard_map.82.before
  13.5 1.2 %collective-permute-done.1.vectors = f32[32,768]{1,0:T(8,128)S(1)} collective-permute-done((f32[32,768]{1,0:T(8,128)S(1)}, f32[32,768]{1,0:T(8,128)S(1)}, u32[]{:S(2)}, u32[]{:S(2)}) %collective-permute-start.1) | collective-permute-done | bytes 98336 | tf_op jit(solution)/shard_map/ppermute | solution.py:331
  14.7 0.5 shard_map.83.partial
  15.2 1.3 %collective-permute-done.4.other = f32[32,768]{1,0:T(8,128)S(1)} collective-permute-done((f32[32,768]{1,0:T(8,128)S(1)}, f32[32,768]{1,0:T(8,128)S(1)}, u32[]{:S(2)}, u32[]{:S(2)}) %collective-permute-start.4) | collective-permute-done | bytes 98336 | tf_op jit(solution)/shard_map/ppermute | solution.py:339
  16.5 0.4 collective-permute-start.6
  16.9 0.3 collective-permute-start.5
  18.6 0.3 shard_map.85.before
  18.9 4.4 %collective-permute-done.6.vectors = f32[32,768]{1,0:T(8,128)S(1)} collective-permute-done((f32[32,768]{1,0:T(8,128)S(1)}, f32[32,768]{1,0:T(8,128)S(1)}, u32[]{:S(2)}, u32[]{:S(2)}) %collective-permute-start.6) | collective-permute-done | bytes 98336 | tf_op jit(solution)/shard_map/ppermute | solution.py:332
  23.3 0.5 shard_map.86.before
  23.7 0.5 collective-permute-done.5.vectors
  24.2 0.5 shard_map.87.partial
  24.8 1.2 %collective-permute-done.7.other = f32[32,768]{1,0:T(8,128)S(1)} collective-permute-done((f32[32,768]{1,0:T(8,128)S(1)}, f32[32,768]{1,0:T(8,128)S(1)}, u32[]{:S(2)}, u32[]{:S(2)}) %collective-permute-start.7) | collective-permute-done | bytes 98336 | tf_op jit(solution)/shard_map/ppermute | solution.py:339
  26.4 0.6 shard_map.89._after.chosen
  27.0 0.3 shard_map.90.before
  27.3 5.5 %collective-permute-done.9.vectors = f32[32,768]{1,0:T(8,128)S(1)} collective-permute-done((f32[32,768]{1,0:T(8,128)S(1)}, f32[32,768]{1,0:T(8,128)S(1)}, u32[]{:S(2)}, u32[]{:S(2)}) %collective-permute-start.9) | collective-permute-done | bytes 98336 | tf_op jit(solution)/shard_map/ppermute | solution.py:332
  32.7 0.5 shard_map.91.before
  33.2 0.4 collective-permute-done.8.vectors
  33.6 0.5 shard_map.92.partial
  34.1 1.3 %collective-permute-done.10.other = f32[32,768]{1,0:T(8,128)S(1)} collective-permute-done((f32[32,768]{1,0:T(8,128)S(1)}, f32[32,768]{1,0:T(8,128)S(1)}, u32[]{:S(2)}, u32[]{:S(2)}) %collective-permute-start.10) | collective-permute-done | bytes 98336 | tf_op jit(solution)/shard_map/ppermute | solution.py:339
  36.0 6.0 %collective-permute-done.12.vectors = f32[32,768]{1,0:T(8,128)S(1)} collective-permute-done((f32[32,768]{1,0:T(8,128)S(1)}, f32[32,768]{1,0:T(8,128)S(1)}, u32[]{:S(2)}, u32[]{:S(2)}) %collective-permute-start.12) | collective-permute-done | bytes 98336 | tf_op jit(solution)/shard_map/ppermute | solution.py:332
  41.9 0.5 shard_map.95.before
  42.4 0.5 collective-permute-done.11.vectors
  42.9 0.5 shard_map.96.partial
  43.4 1.3 %collective-permute-done.13.other = f32[32,768]{1,0:T(8,128)S(1)} collective-permute-done((f32[32,768]{1,0:T(8,128)S(1)}, f32[32,768]{1,0:T(8,128)S(1)}, u32[]{:S(2)}, u32[]{:S(2)}) %collective-permute-start.13) | collective-permute-done | bytes 98336 | tf_op jit(solution)/shard_map/ppermute | solution.py:339
  44.9 0.3 shard_map.98.before
  45.2 6.1 %collective-permute-done.15.vectors = f32[32,768]{1,0:T(8,128)S(1)} collective-permute-done((f32[32,768]{1,0:T(8,128)S(1)}, f32[32,768]{1,0:T(8,128)S(1)}, u32[]{:S(2)}, u32[]{:S(2)}) %collective-permute-start.15) | collective-permute-done | bytes 98336 | tf_op jit(solution)/shard_map/ppermute | solution.py:332
  51.3 0.5 shard_map.99.before
  51.7 0.5 collective-permute-done.14.vectors
  52.2 0.5 shard_map.100.partial
  52.7 1.3 %collective-permute-done.16.other = f32[32,768]{1,0:T(8,128)S(1)} collective-permute-done((f32[32,768]{1,0:T(8,128)S(1)}, f32[32,768]{1,0:T(8,128)S(1)}, u32[]{:S(2)}, u32[]{:S(2)}) %collective-permute-start.16) | collective-permute-done | bytes 98336 | tf_op jit(solution)/shard_map/ppermute | solution.py:339
  54.2 0.3 shard_map.102.before
  54.5 6.1 %collective-permute-done.18.vectors = f32[32,768]{1,0:T(8,128)S(1)} collective-permute-done((f32[32,768]{1,0:T(8,128)S(1)}, f32[32,768]{1,0:T(8,128)S(1)}, u32[]{:S(2)}, u32[]{:S(2)}) %collective-permute-start.18) | collective-permute-done | bytes 98336 | tf_op jit(solution)/shard_map/ppermute | solution.py:332
  60.6 0.5 shard_map.103.before
  61.0 0.5 collective-permute-done.17.vectors
  61.5 0.5 shard_map.104.partial
  62.0 1.3 %collective-permute-done.19.other = f32[32,768]{1,0:T(8,128)S(1)} collective-permute-done((f32[32,768]{1,0:T(8,128)S(1)}, f32[32,768]{1,0:T(8,128)S(1)}, u32[]{:S(2)}, u32[]{:S(2)}) %collective-permute-start.19) | collective-permute-done | bytes 98336 | tf_op jit(solution)/shard_map/ppermute | solution.py:339
  63.5 0.3 shard_map.106.before
  63.8 6.1 %collective-permute-done.21.vectors = f32[32,768]{1,0:T(8,128)S(1)} collective-permute-done((f32[32,768]{1,0:T(8,128)S(1)}, f32[32,768]{1,0:T(8,128)S(1)}, u32[]{:S(2)}, u32[]{:S(2)}) %collective-permute-start.21) | collective-permute-done | bytes 98336 | tf_op jit(solution)/shard_map/ppermute | solution.py:332
  69.9 0.5 shard_map.107.before
  70.3 0.5 collective-permute-done.20.vectors
  70.8 0.5 shard_map.108.partial
  71.3 1.3 %collective-permute-done.22.other = f32[32,768]{1,0:T(8,128)S(1)} collective-permute-done((f32[32,768]{1,0:T(8,128)S(1)}, f32[32,768]{1,0:T(8,128)S(1)}, u32[]{:S(2)}, u32[]{:S(2)}) %collective-permute-start.22) | collective-permute-done | bytes 98336 | tf_op jit(solution)/shard_map/ppermute | solution.py:339
  72.8 0.3 shard_map.110.before
  73.1 6.1 %collective-permute-done.24.vectors = f32[32,768]{1,0:T(8,128)S(1)} collective-permute-done((f32[32,768]{1,0:T(8,128)S(1)}, f32[32,768]{1,0:T(8,128)S(1)}, u32[]{:S(2)}, u32[]{:S(2)}) %collective-permute-start.24) | collective-permute-done | bytes 98336 | tf_op jit(solution)/shard_map/ppermute | solution.py:332
  79.2 0.5 shard_map.111.before
  79.6 0.5 collective-permute-done.23.vectors
  80.1 0.5 shard_map.112.partial
  80.6 1.3 %collective-permute-done.25.other = f32[32,768]{1,0:T(8,128)S(1)} collective-permute-done((f32[32,768]{1,0:T(8,128)S(1)}, f32[32,768]{1,0:T(8,128)S(1)}, u32[]{:S(2)}, u32[]{:S(2)}) %collective-permute-start.25) | collective-permute-done | bytes 98336 | tf_op jit(solution)/shard_map/ppermute | solution.py:339
  82.1 1.6 %collective-permute-start.28 = (f32[32,384]{1,0:T(8,128)S(1)}, f32[32,384]{1,0:T(8,128)S(1)}, u32[]{:S(2)}, u32[]{:S(2)}) collective-permute-start(f32[32,384]{1,0:T(8,128)S(1)} %slice.4.vectors), channel_id=1, source_target_pairs={{0,16},{16,0},{1,17},{17,1},{2,18},{18,2},{3,19},{19,3},{4,20},{20... | collective-permute-start | bytes 147464 | tf_op jit(solution)/shard_map/ppermute | solution.py:354
  84.0 4.5 %collective-permute-done.27.vectors = f32[32,768]{1,0:T(8,128)S(1)} collective-permute-done((f32[32,768]{1,0:T(8,128)S(1)}, f32[32,768]{1,0:T(8,128)S(1)}, u32[]{:S(2)}, u32[]{:S(2)}) %collective-permute-start.27) | collective-permute-done | bytes 98336 | tf_op jit(solution)/shard_map/ppermute | solution.py:332
  88.5 0.5 shard_map.115.before
  89.0 0.4 collective-permute-done.26.vectors
  89.4 0.8 shard_map.116.one
  90.2 1.2 %collective-permute-done.29.other = f32[32,128]{1,0:T(8,128)S(1)} collective-permute-done((f32[32,128]{1,0:T(8,128)S(1)}, f32[32,128]{1,0:T(8,128)S(1)}, u32[]{:S(2)}, u32[]{:S(2)}) %collective-permute-start.29) | collective-permute-done | bytes 16416 | tf_op jit(solution)/shard_map/ppermute | solution.py:360
  91.4 10.4 %all_to_all.5.parts = f32[8,32,128]{2,1,0:T(8,128)S(1)} all-to-all(f32[8,32,128]{2,1,0:T(8,128)S(1)} %shard_map.117), channel_id=1, replica_groups={{0,2,4,6,8,10,12,14},{1,3,5,7,9,11,13,15},{16,18,20,22,24,26,28,30},{17..., dimensions={0} | all-to-all | bytes 262144 | tf_op jit(solution)/shard_map/all_to_all | solution.py:363
  101.8 1.8 %shard_map.118 = (f32[32,384]{1,0:T(8,128)}, f32[32,32]{1,0:T(8,128)}) custom-call(f32[8,32,128]{2,1,0:T(8,128)S(1)} %all_to_all.5.parts, f32[32,32]{1,0:T(8,128)S(1)} %shard_map.89._after.chosen, f32[32,384]{1,0:T(8,128)S(1)} %slice.4.vectors, f32[32,384]{1,0:T(8,128)S(1)} %collective-permute-done.28.lower), custom_call_target="tpu_custom_call" | custom-call | flops 1000000 | bytes 100000 | tf_op jit(solution)/shard_map/pallas_call | solution.py:364
  (48 shorter events, 2.4 us)
Async XLA Ops:
  0.6 3.6 %copy-start.1 = (f32[1,32,384]{2,1,0:T(8,128)S(1)}, f32[1,32,384]{2,1,0:T(8,128)}, u32[]{:S(2)}) copy-start(f32[1,32,384]{2,1,0:T(8,128)} %param.8) | copy-start | bytes 147460
  0.6 3.5 %collective-permute-start = (f32[32,384]{1,0:T(8,128)}, f32[32,384]{1,0:T(8,128)S(1)}, u32[]{:S(2)}, u32[]{:S(2)}) collective-permute-start(f32[32,384]{1,0:T(8,128)} %bitcast.6), channel_id=1, source_target_pairs={{0,1},{1,0},{2,3},{3,2},{4,5},{5,4},{6,7},{7,6},{8,9},{9,8},{10,11... | collective-permute-start | bytes 147464 | tf_op jit(solution)/shard_map/ppermute | solution.py:281
  1.2 7.7 %copy-start = (f32[3,24,128,128]{3,2,1,0:T(8,128)S(1)}, f32[3,24,128,128]{3,2,1,0:T(8,128)}, u32[]{:S(2)}) copy-start(f32[3,24,128,128]{3,2,1,0:T(8,128)} %tiles.3) | copy-start | bytes 14155780
  4.1 6.5 %collective-permute-start.3 = (f32[12,3,128,128]{3,2,1,0:T(8,128)S(1)}, f32[12,3,128,128]{3,2,1,0:T(8,128)S(1)}, u32[]{:S(2)}, u32[]{:S(2)}) collective-permute-start(f32[12,3,128,128]{3,2,1,0:T(8,128)S(1)} %shard_map.77), channel_id=1, source_target_pairs={{0,1},{1,0},{2,3},{3,2},{4,5},{5,4},{6,7},{7,6},{8,9},{9,8},{10,11... | collective-permute-start | bytes 7077896 | tf_op jit(solution)/shard_map/ppermute | solution.py:296
  4.3 8.7 %collective-permute-start.2 = (f32[32,768]{1,0:T(8,128)S(1)}, f32[32,768]{1,0:T(8,128)S(1)}, u32[]{:S(2)}, u32[]{:S(2)}) collective-permute-start(f32[32,768]{1,0:T(8,128)S(1)} %shard_map.78.vectors._after.initial), channel_id=1, source_target_pairs={{0,4},{1,13},{2,6},{3,15},{4,8},{5,1},{6,10},{7,3},{8,12},{9,5},{1... | collective-permute-start | bytes 294920 | tf_op jit(solution)/shard_map/ppermute | solution.py:332
  7.4 7.3 %collective-permute-start.1 = (f32[32,768]{1,0:T(8,128)S(1)}, f32[32,768]{1,0:T(8,128)S(1)}, u32[]{:S(2)}, u32[]{:S(2)}) collective-permute-start(f32[32,768]{1,0:T(8,128)S(1)} %shard_map.78.vectors._after.initial), channel_id=1, source_target_pairs={{0,2},{1,15},{2,4},{3,1},{4,6},{5,3},{6,8},{7,5},{8,10},{9,7},{10,... | collective-permute-start | bytes 294920 | tf_op jit(solution)/shard_map/ppermute | solution.py:331
  15.2 1.3 %collective-permute-start.4 = (f32[32,768]{1,0:T(8,128)S(1)}, f32[32,768]{1,0:T(8,128)S(1)}, u32[]{:S(2)}, u32[]{:S(2)}) collective-permute-start(f32[32,768]{1,0:T(8,128)S(1)} %shard_map.83.partial), channel_id=1, source_target_pairs={{0,1},{1,0},{2,3},{3,2},{4,5},{5,4},{6,7},{7,6},{8,9},{9,8},{10,11... | collective-permute-start | bytes 294920 | tf_op jit(solution)/shard_map/ppermute | solution.py:339
  16.5 6.8 %collective-permute-start.6 = (f32[32,768]{1,0:T(8,128)S(1)}, f32[32,768]{1,0:T(8,128)S(1)}, u32[]{:S(2)}, u32[]{:S(2)}) collective-permute-start(f32[32,768]{1,0:T(8,128)S(1)} %shard_map.84.vectors._after.image), channel_id=1, source_target_pairs={{0,4},{1,13},{2,6},{3,15},{4,8},{5,1},{6,10},{7,3},{8,12},{9,5},{1... | collective-permute-start | bytes 294920 | tf_op jit(solution)/shard_map/ppermute | solution.py:332
  16.9 7.3 %collective-permute-start.5 = (f32[32,768]{1,0:T(8,128)S(1)}, f32[32,768]{1,0:T(8,128)S(1)}, u32[]{:S(2)}, u32[]{:S(2)}) collective-permute-start(f32[32,768]{1,0:T(8,128)S(1)} %shard_map.84.vectors._after.image), channel_id=1, source_target_pairs={{0,2},{1,15},{2,4},{3,1},{4,6},{5,3},{6,8},{7,5},{8,10},{9,7},{10,... | collective-permute-start | bytes 294920 | tf_op jit(solution)/shard_map/ppermute | solution.py:331
  23.7 2.7 %copy-start.2 = (s32[1,8,2]{1,2,0:T(2,128)S(1)}, s32[1,8,2]{1,2,0:T(2,128)}, u32[]{:S(2)}) copy-start(s32[1,8,2]{1,2,0:T(2,128)} %param.11) | copy-start | bytes 196
  24.7 1.3 %collective-permute-start.7 = (f32[32,768]{1,0:T(8,128)S(1)}, f32[32,768]{1,0:T(8,128)S(1)}, u32[]{:S(2)}, u32[]{:S(2)}) collective-permute-start(f32[32,768]{1,0:T(8,128)S(1)} %shard_map.87.partial), channel_id=1, source_target_pairs={{0,1},{1,0},{2,3},{3,2},{4,5},{5,4},{6,7},{7,6},{8,9},{9,8},{10,11... | collective-permute-start | bytes 294920 | tf_op jit(solution)/shard_map/ppermute | solution.py:339
  26.2 6.6 %collective-permute-start.9 = (f32[32,768]{1,0:T(8,128)S(1)}, f32[32,768]{1,0:T(8,128)S(1)}, u32[]{:S(2)}, u32[]{:S(2)}) collective-permute-start(f32[32,768]{1,0:T(8,128)S(1)} %get-tuple-element.34.vectors.current.previous), channel_id=1, source_target_pairs={{0,4},{1,13},{2,6},{3,15},{4,8},{5,1},{6,10},{7,3},{8,12},{9,5},{1... | collective-permute-start | bytes 294920 | tf_op jit(solution)/shard_map/ppermute | solution.py:332
  26.2 7.4 %collective-permute-start.8 = (f32[32,768]{1,0:T(8,128)S(1)}, f32[32,768]{1,0:T(8,128)S(1)}, u32[]{:S(2)}, u32[]{:S(2)}) collective-permute-start(f32[32,768]{1,0:T(8,128)S(1)} %get-tuple-element.34.vectors.current.previous), channel_id=1, source_target_pairs={{0,2},{1,15},{2,4},{3,1},{4,6},{5,3},{6,8},{7,5},{8,10},{9,7},{10,... | collective-permute-start | bytes 294920 | tf_op jit(solution)/shard_map/ppermute | solution.py:331
  34.1 1.3 %collective-permute-start.10 = (f32[32,768]{1,0:T(8,128)S(1)}, f32[32,768]{1,0:T(8,128)S(1)}, u32[]{:S(2)}, u32[]{:S(2)}) collective-permute-start(f32[32,768]{1,0:T(8,128)S(1)} %shard_map.92.partial), channel_id=1, source_target_pairs={{0,1},{1,0},{2,3},{3,2},{4,5},{5,4},{6,7},{7,6},{8,9},{9,8},{10,11... | collective-permute-start | bytes 294920 | tf_op jit(solution)/shard_map/ppermute | solution.py:339
  35.5 6.5 %collective-permute-start.12 = (f32[32,768]{1,0:T(8,128)S(1)}, f32[32,768]{1,0:T(8,128)S(1)}, u32[]{:S(2)}, u32[]{:S(2)}) collective-permute-start(f32[32,768]{1,0:T(8,128)S(1)} %shard_map.93.vectors.current.previous), channel_id=1, source_target_pairs={{0,4},{1,13},{2,6},{3,15},{4,8},{5,1},{6,10},{7,3},{8,12},{9,5},{1... | collective-permute-start | bytes 294920 | tf_op jit(solution)/shard_map/ppermute | solution.py:332
  35.5 7.4 %collective-permute-start.11 = (f32[32,768]{1,0:T(8,128)S(1)}, f32[32,768]{1,0:T(8,128)S(1)}, u32[]{:S(2)}, u32[]{:S(2)}) collective-permute-start(f32[32,768]{1,0:T(8,128)S(1)} %shard_map.93.vectors.current.previous), channel_id=1, source_target_pairs={{0,2},{1,15},{2,4},{3,1},{4,6},{5,3},{6,8},{7,5},{8,10},{9,7},{10,... | collective-permute-start | bytes 294920 | tf_op jit(solution)/shard_map/ppermute | solution.py:331
  43.4 1.3 %collective-permute-start.13 = (f32[32,768]{1,0:T(8,128)S(1)}, f32[32,768]{1,0:T(8,128)S(1)}, u32[]{:S(2)}, u32[]{:S(2)}) collective-permute-start(f32[32,768]{1,0:T(8,128)S(1)} %shard_map.96.partial), channel_id=1, source_target_pairs={{0,1},{1,0},{2,3},{3,2},{4,5},{5,4},{6,7},{7,6},{8,9},{9,8},{10,11... | collective-permute-start | bytes 294920 | tf_op jit(solution)/shard_map/ppermute | solution.py:339
  44.8 6.5 %collective-permute-start.15 = (f32[32,768]{1,0:T(8,128)S(1)}, f32[32,768]{1,0:T(8,128)S(1)}, u32[]{:S(2)}, u32[]{:S(2)}) collective-permute-start(f32[32,768]{1,0:T(8,128)S(1)} %shard_map.97.vectors.current.previous), channel_id=1, source_target_pairs={{0,4},{1,13},{2,6},{3,15},{4,8},{5,1},{6,10},{7,3},{8,12},{9,5},{1... | collective-permute-start | bytes 294920 | tf_op jit(solution)/shard_map/ppermute | solution.py:332
  44.8 7.4 %collective-permute-start.14 = (f32[32,768]{1,0:T(8,128)S(1)}, f32[32,768]{1,0:T(8,128)S(1)}, u32[]{:S(2)}, u32[]{:S(2)}) collective-permute-start(f32[32,768]{1,0:T(8,128)S(1)} %shard_map.97.vectors.current.previous), channel_id=1, source_target_pairs={{0,2},{1,15},{2,4},{3,1},{4,6},{5,3},{6,8},{7,5},{8,10},{9,7},{10,... | collective-permute-start | bytes 294920 | tf_op jit(solution)/shard_map/ppermute | solution.py:331
  52.7 1.3 %collective-permute-start.16 = (f32[32,768]{1,0:T(8,128)S(1)}, f32[32,768]{1,0:T(8,128)S(1)}, u32[]{:S(2)}, u32[]{:S(2)}) collective-permute-start(f32[32,768]{1,0:T(8,128)S(1)} %shard_map.100.partial), channel_id=1, source_target_pairs={{0,1},{1,0},{2,3},{3,2},{4,5},{5,4},{6,7},{7,6},{8,9},{9,8},{10,11... | collective-permute-start | bytes 294920 | tf_op jit(solution)/shard_map/ppermute | solution.py:339
  54.1 6.5 %collective-permute-start.18 = (f32[32,768]{1,0:T(8,128)S(1)}, f32[32,768]{1,0:T(8,128)S(1)}, u32[]{:S(2)}, u32[]{:S(2)}) collective-permute-start(f32[32,768]{1,0:T(8,128)S(1)} %shard_map.101.vectors.current.previous), channel_id=1, source_target_pairs={{0,4},{1,13},{2,6},{3,15},{4,8},{5,1},{6,10},{7,3},{8,12},{9,5},{1... | collective-permute-start | bytes 294920 | tf_op jit(solution)/shard_map/ppermute | solution.py:332
  54.1 7.4 %collective-permute-start.17 = (f32[32,768]{1,0:T(8,128)S(1)}, f32[32,768]{1,0:T(8,128)S(1)}, u32[]{:S(2)}, u32[]{:S(2)}) collective-permute-start(f32[32,768]{1,0:T(8,128)S(1)} %shard_map.101.vectors.current.previous), channel_id=1, source_target_pairs={{0,2},{1,15},{2,4},{3,1},{4,6},{5,3},{6,8},{7,5},{8,10},{9,7},{10,... | collective-permute-start | bytes 294920 | tf_op jit(solution)/shard_map/ppermute | solution.py:331
  62.0 1.3 %collective-permute-start.19 = (f32[32,768]{1,0:T(8,128)S(1)}, f32[32,768]{1,0:T(8,128)S(1)}, u32[]{:S(2)}, u32[]{:S(2)}) collective-permute-start(f32[32,768]{1,0:T(8,128)S(1)} %shard_map.104.partial), channel_id=1, source_target_pairs={{0,1},{1,0},{2,3},{3,2},{4,5},{5,4},{6,7},{7,6},{8,9},{9,8},{10,11... | collective-permute-start | bytes 294920 | tf_op jit(solution)/shard_map/ppermute | solution.py:339
  63.4 6.5 %collective-permute-start.21 = (f32[32,768]{1,0:T(8,128)S(1)}, f32[32,768]{1,0:T(8,128)S(1)}, u32[]{:S(2)}, u32[]{:S(2)}) collective-permute-start(f32[32,768]{1,0:T(8,128)S(1)} %shard_map.105.vectors.current.previous), channel_id=1, source_target_pairs={{0,4},{1,13},{2,6},{3,15},{4,8},{5,1},{6,10},{7,3},{8,12},{9,5},{1... | collective-permute-start | bytes 294920 | tf_op jit(solution)/shard_map/ppermute | solution.py:332
  63.4 7.4 %collective-permute-start.20 = (f32[32,768]{1,0:T(8,128)S(1)}, f32[32,768]{1,0:T(8,128)S(1)}, u32[]{:S(2)}, u32[]{:S(2)}) collective-permute-start(f32[32,768]{1,0:T(8,128)S(1)} %shard_map.105.vectors.current.previous), channel_id=1, source_target_pairs={{0,2},{1,15},{2,4},{3,1},{4,6},{5,3},{6,8},{7,5},{8,10},{9,7},{10,... | collective-permute-start | bytes 294920 | tf_op jit(solution)/shard_map/ppermute | solution.py:331
  71.3 1.3 %collective-permute-start.22 = (f32[32,768]{1,0:T(8,128)S(1)}, f32[32,768]{1,0:T(8,128)S(1)}, u32[]{:S(2)}, u32[]{:S(2)}) collective-permute-start(f32[32,768]{1,0:T(8,128)S(1)} %shard_map.108.partial), channel_id=1, source_target_pairs={{0,1},{1,0},{2,3},{3,2},{4,5},{5,4},{6,7},{7,6},{8,9},{9,8},{10,11... | collective-permute-start | bytes 294920 | tf_op jit(solution)/shard_map/ppermute | solution.py:339
  72.7 6.5 %collective-permute-start.24 = (f32[32,768]{1,0:T(8,128)S(1)}, f32[32,768]{1,0:T(8,128)S(1)}, u32[]{:S(2)}, u32[]{:S(2)}) collective-permute-start(f32[32,768]{1,0:T(8,128)S(1)} %shard_map.109.vectors.current), channel_id=1, source_target_pairs={{0,4},{1,13},{2,6},{3,15},{4,8},{5,1},{6,10},{7,3},{8,12},{9,5},{1... | collective-permute-start | bytes 294920 | tf_op jit(solution)/shard_map/ppermute | solution.py:332
  72.7 7.4 %collective-permute-start.23 = (f32[32,768]{1,0:T(8,128)S(1)}, f32[32,768]{1,0:T(8,128)S(1)}, u32[]{:S(2)}, u32[]{:S(2)}) collective-permute-start(f32[32,768]{1,0:T(8,128)S(1)} %shard_map.109.vectors.current), channel_id=1, source_target_pairs={{0,2},{1,15},{2,4},{3,1},{4,6},{5,3},{6,8},{7,5},{8,10},{9,7},{10,... | collective-permute-start | bytes 294920 | tf_op jit(solution)/shard_map/ppermute | solution.py:331
  80.6 1.3 %collective-permute-start.25 = (f32[32,768]{1,0:T(8,128)S(1)}, f32[32,768]{1,0:T(8,128)S(1)}, u32[]{:S(2)}, u32[]{:S(2)}) collective-permute-start(f32[32,768]{1,0:T(8,128)S(1)} %shard_map.112.partial), channel_id=1, source_target_pairs={{0,1},{1,0},{2,3},{3,2},{4,5},{5,4},{6,7},{7,6},{8,9},{9,8},{10,11... | collective-permute-start | bytes 294920 | tf_op jit(solution)/shard_map/ppermute | solution.py:339
  82.0 6.5 %collective-permute-start.27 = (f32[32,768]{1,0:T(8,128)S(1)}, f32[32,768]{1,0:T(8,128)S(1)}, u32[]{:S(2)}, u32[]{:S(2)}) collective-permute-start(f32[32,768]{1,0:T(8,128)S(1)} %shard_map.113.vectors.pair), channel_id=1, source_target_pairs={{0,4},{1,13},{2,6},{3,15},{4,8},{5,1},{6,10},{7,3},{8,12},{9,5},{1... | collective-permute-start | bytes 294920 | tf_op jit(solution)/shard_map/ppermute | solution.py:332
  82.0 7.4 %collective-permute-start.26 = (f32[32,768]{1,0:T(8,128)S(1)}, f32[32,768]{1,0:T(8,128)S(1)}, u32[]{:S(2)}, u32[]{:S(2)}) collective-permute-start(f32[32,768]{1,0:T(8,128)S(1)} %shard_map.113.vectors.pair), channel_id=1, source_target_pairs={{0,2},{1,15},{2,4},{3,1},{4,6},{5,3},{6,8},{7,5},{8,10},{9,7},{10,... | collective-permute-start | bytes 294920 | tf_op jit(solution)/shard_map/ppermute | solution.py:331
  82.1 6.8 %collective-permute-start.28 = (f32[32,384]{1,0:T(8,128)S(1)}, f32[32,384]{1,0:T(8,128)S(1)}, u32[]{:S(2)}, u32[]{:S(2)}) collective-permute-start(f32[32,384]{1,0:T(8,128)S(1)} %slice.4.vectors), channel_id=1, source_target_pairs={{0,16},{16,0},{1,17},{17,1},{2,18},{18,2},{3,19},{19,3},{4,20},{20... | collective-permute-start | bytes 147464 | tf_op jit(solution)/shard_map/ppermute | solution.py:354
  90.2 1.2 %collective-permute-start.29 = (f32[32,128]{1,0:T(8,128)S(1)}, f32[32,128]{1,0:T(8,128)S(1)}, u32[]{:S(2)}, u32[]{:S(2)}) collective-permute-start(f32[32,128]{1,0:T(8,128)S(1)} %shard_map.116.one), channel_id=1, source_target_pairs={{0,1},{1,0},{2,3},{3,2},{4,5},{5,4},{6,7},{7,6},{8,9},{9,8},{10,11... | collective-permute-start | bytes 49160 | tf_op jit(solution)/shard_map/ppermute | solution.py:360

commit v7 on v6

--- a/solution.py
+++ b/solution.py
@@ -128,6 +128,11 @@
     by_high = lax.dot_general(both, high[...], NN, preferred_element_type=F32)
     by_low = lax.dot_general(top, low[...], NN, preferred_element_type=F32)
     return by_high[:count] + (by_high[count:] + by_low)
+
+
+def split(values):
+    top = values.astype(BF16)
+    return top, (values - top.astype(F32)).astype(BF16)
 
 
 def own_kernel(vectors, _after, high, low, out):
@@ -237,12 +242,12 @@
 def finish_kernel(parts, chosen, vectors, lower, filtered, projected, *, order):
     inverse, inverse_below, mixed, cross = eliminated(summed(parts))
     scale = math.sqrt(order)
-    basis = scale * dot(inverse, vectors[...], NN)
-    lower_basis = scale * dot(inverse_below, lower[...], NN)
+    basis = multiply(scale * inverse, *split(vectors[...]))
+    lower_basis = multiply(scale * inverse_below, *split(lower[...]))
     correlation = dot(mixed, inverse_below, NT)
     projected[...] = dot(cross, inverse, NT)
     some = jnp.max(chosen[...]) > 0.0
-    removal = jnp.where(some, dot(chosen[...] * correlation, lower_basis, NN), 0.0)
+    removal = jnp.where(some, multiply(chosen[...] * correlation, *split(lower_basis)), 0.0)
     filtered[...] = basis - removal
 
 

time: 104 us -> 104 us (level)
  no operation moved by 1% of the time
where the time goes in v7:
time: 104 us
  waiting for transfers between devices  62.2 us (60%)
  Pallas kernels  19.8 us (19%)
  blocking collectives  10.4 us (10%)
  starting transfers between devices  8.63 us (8%)
  between operations  2.36 us (2%)
    ppermute x9, waiting for transfers between devices, most_of_image(): far = lax.ppermute(vectors, 'row', farther)  45.9 us
    pallas_call x26, Pallas kernels, part(): call(kernel, vec, [VMEM] * (len(vectors) + 2), VMEM, cost_estimate=pl.Cos...  10.8 us
    all_to_all x1, blocking collectives, local(): lax.all_to_all(spread, 'row', 0, 0, tiled=True, axis_index_groups=same_core)  10.4 us
    ppermute x8, waiting for transfers between devices, images(): return (partial, lax.ppermute(partial, 'row', swap))  10.3 us
    ppermute x9, waiting for transfers between devices, most_of_image(): near = lax.ppermute(vectors, 'row', nearer)  4.88 us
    ppermute x9, starting transfers between devices, most_of_image(): far = lax.ppermute(vectors, 'row', farther)  3.92 us
    pallas_call x1, Pallas kernels, local(): call(functools.partial(gather_kernel, rows=rows, stored=stored, total=tot...  2.95 us
    ppermute x9, starting transfers between devices, most_of_image(): near = lax.ppermute(vectors, 'row', nearer)  2.3 us
  transfers between devices with their start and end apart: 30, of which 27 were waited for; matrix products, arithmetic and copies ran while one was open for 0% of the time, Pallas kernels for 13%

profile of v7, /device:TPU:0, one launch (start us, length us, event | category | flops | bytes accessed | tf_op | source)
XLA Modules:
  0.0 103.6 jit_solution(5688298004573489188)
XLA Ops:
  0.6 0.5 collective-permute-start
  1.2 2.9 %shard_map.77 = f32[12,3,128,128]{3,2,1,0:T(8,128)S(1)} custom-call(s32[3,24]{1,0:T(4,128)} %pattern.3, f32[3,24,128,128]{3,2,1,0:T(8,128)} %tiles.3), custom_call_target="tpu_custom_call" | custom-call | bytes 8000000 | tf_op jit(solution)/shard_map/pallas_call | solution.py:287
  4.3 3.1 %collective-permute-start.2 = (f32[32,768]{1,0:T(8,128)S(1)}, f32[32,768]{1,0:T(8,128)S(1)}, u32[]{:S(2)}, u32[]{:S(2)}) collective-permute-start(f32[32,768]{1,0:T(8,128)S(1)} %shard_map.78.vectors._after.initial), channel_id=1, source_target_pairs={{0,4},{1,13},{2,6},{3,15},{4,8},{5,1},{6,10},{7,3},{8,12},{9,5},{1... | collective-permute-start | bytes 294920 | tf_op jit(solution)/shard_map/ppermute | solution.py:337
  7.3 1.5 %collective-permute-start.1 = (f32[32,768]{1,0:T(8,128)S(1)}, f32[32,768]{1,0:T(8,128)S(1)}, u32[]{:S(2)}, u32[]{:S(2)}) collective-permute-start(f32[32,768]{1,0:T(8,128)S(1)} %shard_map.78.vectors._after.initial), channel_id=1, source_target_pairs={{0,2},{1,15},{2,4},{3,1},{4,6},{5,3},{6,8},{7,5},{8,10},{9,7},{10,... | collective-permute-start | bytes 294920 | tf_op jit(solution)/shard_map/ppermute | solution.py:336
  8.9 1.8 %shard_map.79 = (bf16[768,768]{1,0:T(8,128)(2,1)S(1)}, bf16[768,768]{1,0:T(8,128)(2,1)S(1)}, bf16[768,768]{1,0:T(8,128)(2,1)S(1)}, bf16[768,768]{1,0:T(8,128)(2,...) custom-call(s32[3,24]{1,0:T(4,128)} %pattern.3, f32[3,24,128,128]{3,2,1,0:T(8,128)S(1)} %copy-done), custom_call_target="tpu_custom_call" | custom-call | flops 1000000 | bytes 100000 | tf_op jit(solution)/shard_map/pallas_call | solution.py:302
  10.6 0.7 shard_map.80
  11.4 0.3 shard_map.81.before
  11.7 1.3 %collective-permute-done.2.vectors = f32[32,768]{1,0:T(8,128)S(1)} collective-permute-done((f32[32,768]{1,0:T(8,128)S(1)}, f32[32,768]{1,0:T(8,128)S(1)}, u32[]{:S(2)}, u32[]{:S(2)}) %collective-permute-start.2) | collective-permute-done | bytes 98336 | tf_op jit(solution)/shard_map/ppermute | solution.py:337
  12.9 0.5 shard_map.82.before
  13.4 1.2 %collective-permute-done.1.vectors = f32[32,768]{1,0:T(8,128)S(1)} collective-permute-done((f32[32,768]{1,0:T(8,128)S(1)}, f32[32,768]{1,0:T(8,128)S(1)}, u32[]{:S(2)}, u32[]{:S(2)}) %collective-permute-start.1) | collective-permute-done | bytes 98336 | tf_op jit(solution)/shard_map/ppermute | solution.py:336
  14.7 0.5 shard_map.83.partial
  15.2 1.3 %collective-permute-done.4.other = f32[32,768]{1,0:T(8,128)S(1)} collective-permute-done((f32[32,768]{1,0:T(8,128)S(1)}, f32[32,768]{1,0:T(8,128)S(1)}, u32[]{:S(2)}, u32[]{:S(2)}) %collective-permute-start.4) | collective-permute-done | bytes 98336 | tf_op jit(solution)/shard_map/ppermute | solution.py:344
  16.5 0.5 collective-permute-start.6
  18.6 0.3 shard_map.85.before
  18.9 4.4 %collective-permute-done.6.vectors = f32[32,768]{1,0:T(8,128)S(1)} collective-permute-done((f32[32,768]{1,0:T(8,128)S(1)}, f32[32,768]{1,0:T(8,128)S(1)}, u32[]{:S(2)}, u32[]{:S(2)}) %collective-permute-start.6) | collective-permute-done | bytes 98336 | tf_op jit(solution)/shard_map/ppermute | solution.py:337
  23.2 0.5 shard_map.86.before
  23.7 0.5 collective-permute-done.5.vectors
  24.2 0.5 shard_map.87.partial
  24.8 1.2 %collective-permute-done.7.other = f32[32,768]{1,0:T(8,128)S(1)} collective-permute-done((f32[32,768]{1,0:T(8,128)S(1)}, f32[32,768]{1,0:T(8,128)S(1)}, u32[]{:S(2)}, u32[]{:S(2)}) %collective-permute-start.7) | collective-permute-done | bytes 98336 | tf_op jit(solution)/shard_map/ppermute | solution.py:344
  26.4 0.6 shard_map.89._after.chosen
  26.9 0.3 shard_map.90.before
  27.2 5.5 %collective-permute-done.9.vectors = f32[32,768]{1,0:T(8,128)S(1)} collective-permute-done((f32[32,768]{1,0:T(8,128)S(1)}, f32[32,768]{1,0:T(8,128)S(1)}, u32[]{:S(2)}, u32[]{:S(2)}) %collective-permute-start.9) | collective-permute-done | bytes 98336 | tf_op jit(solution)/shard_map/ppermute | solution.py:337
  32.8 0.5 shard_map.91.before
  33.2 0.4 collective-permute-done.8.vectors
  33.6 0.5 shard_map.92.partial
  34.1 1.3 %collective-permute-done.10.other = f32[32,768]{1,0:T(8,128)S(1)} collective-permute-done((f32[32,768]{1,0:T(8,128)S(1)}, f32[32,768]{1,0:T(8,128)S(1)}, u32[]{:S(2)}, u32[]{:S(2)}) %collective-permute-start.10) | collective-permute-done | bytes 98336 | tf_op jit(solution)/shard_map/ppermute | solution.py:344
  35.7 0.3 shard_map.94.before
  36.0 6.0 %collective-permute-done.12.vectors = f32[32,768]{1,0:T(8,128)S(1)} collective-permute-done((f32[32,768]{1,0:T(8,128)S(1)}, f32[32,768]{1,0:T(8,128)S(1)}, u32[]{:S(2)}, u32[]{:S(2)}) %collective-permute-start.12) | collective-permute-done | bytes 98336 | tf_op jit(solution)/shard_map/ppermute | solution.py:337
  42.0 0.5 shard_map.95.before
  42.4 0.5 collective-permute-done.11.vectors
  42.9 0.5 shard_map.96.partial
  43.4 1.3 %collective-permute-done.13.other = f32[32,768]{1,0:T(8,128)S(1)} collective-permute-done((f32[32,768]{1,0:T(8,128)S(1)}, f32[32,768]{1,0:T(8,128)S(1)}, u32[]{:S(2)}, u32[]{:S(2)}) %collective-permute-start.13) | collective-permute-done | bytes 98336 | tf_op jit(solution)/shard_map/ppermute | solution.py:344
  44.9 0.3 shard_map.98.before
  45.2 6.1 %collective-permute-done.15.vectors = f32[32,768]{1,0:T(8,128)S(1)} collective-permute-done((f32[32,768]{1,0:T(8,128)S(1)}, f32[32,768]{1,0:T(8,128)S(1)}, u32[]{:S(2)}, u32[]{:S(2)}) %collective-permute-start.15) | collective-permute-done | bytes 98336 | tf_op jit(solution)/shard_map/ppermute | solution.py:337
  51.3 0.5 shard_map.99.before
  51.8 0.5 collective-permute-done.14.vectors
  52.2 0.5 shard_map.100.partial
  52.7 1.3 %collective-permute-done.16.other = f32[32,768]{1,0:T(8,128)S(1)} collective-permute-done((f32[32,768]{1,0:T(8,128)S(1)}, f32[32,768]{1,0:T(8,128)S(1)}, u32[]{:S(2)}, u32[]{:S(2)}) %collective-permute-start.16) | collective-permute-done | bytes 98336 | tf_op jit(solution)/shard_map/ppermute | solution.py:344
  54.2 0.3 shard_map.102.before
  54.5 6.1 %collective-permute-done.18.vectors = f32[32,768]{1,0:T(8,128)S(1)} collective-permute-done((f32[32,768]{1,0:T(8,128)S(1)}, f32[32,768]{1,0:T(8,128)S(1)}, u32[]{:S(2)}, u32[]{:S(2)}) %collective-permute-start.18) | collective-permute-done | bytes 98336 | tf_op jit(solution)/shard_map/ppermute | solution.py:337
  60.6 0.5 shard_map.103.before
  61.1 0.5 collective-permute-done.17.vectors
  61.5 0.5 shard_map.104.partial
  62.0 1.3 %collective-permute-done.19.other = f32[32,768]{1,0:T(8,128)S(1)} collective-permute-done((f32[32,768]{1,0:T(8,128)S(1)}, f32[32,768]{1,0:T(8,128)S(1)}, u32[]{:S(2)}, u32[]{:S(2)}) %collective-permute-start.19) | collective-permute-done | bytes 98336 | tf_op jit(solution)/shard_map/ppermute | solution.py:344
  63.5 0.3 shard_map.106.before
  63.8 6.1 %collective-permute-done.21.vectors = f32[32,768]{1,0:T(8,128)S(1)} collective-permute-done((f32[32,768]{1,0:T(8,128)S(1)}, f32[32,768]{1,0:T(8,128)S(1)}, u32[]{:S(2)}, u32[]{:S(2)}) %collective-permute-start.21) | collective-permute-done | bytes 98336 | tf_op jit(solution)/shard_map/ppermute | solution.py:337
  69.9 0.5 shard_map.107.before
  70.4 0.5 collective-permute-done.20.vectors
  70.8 0.5 shard_map.108.partial
  71.3 1.3 %collective-permute-done.22.other = f32[32,768]{1,0:T(8,128)S(1)} collective-permute-done((f32[32,768]{1,0:T(8,128)S(1)}, f32[32,768]{1,0:T(8,128)S(1)}, u32[]{:S(2)}, u32[]{:S(2)}) %collective-permute-start.22) | collective-permute-done | bytes 98336 | tf_op jit(solution)/shard_map/ppermute | solution.py:344
  72.8 0.3 shard_map.110.before
  73.1 6.1 %collective-permute-done.24.vectors = f32[32,768]{1,0:T(8,128)S(1)} collective-permute-done((f32[32,768]{1,0:T(8,128)S(1)}, f32[32,768]{1,0:T(8,128)S(1)}, u32[]{:S(2)}, u32[]{:S(2)}) %collective-permute-start.24) | collective-permute-done | bytes 98336 | tf_op jit(solution)/shard_map/ppermute | solution.py:337
  79.2 0.5 shard_map.111.before
  79.7 0.5 collective-permute-done.23.vectors
  80.1 0.5 shard_map.112.partial
  80.6 1.3 %collective-permute-done.25.other = f32[32,768]{1,0:T(8,128)S(1)} collective-permute-done((f32[32,768]{1,0:T(8,128)S(1)}, f32[32,768]{1,0:T(8,128)S(1)}, u32[]{:S(2)}, u32[]{:S(2)}) %collective-permute-start.25) | collective-permute-done | bytes 98336 | tf_op jit(solution)/shard_map/ppermute | solution.py:344
  82.1 1.6 %collective-permute-start.28 = (f32[32,384]{1,0:T(8,128)S(1)}, f32[32,384]{1,0:T(8,128)S(1)}, u32[]{:S(2)}, u32[]{:S(2)}) collective-permute-start(f32[32,384]{1,0:T(8,128)S(1)} %slice.4.vectors), channel_id=1, source_target_pairs={{0,16},{16,0},{1,17},{17,1},{2,18},{18,2},{3,19},{19,3},{4,20},{20... | collective-permute-start | bytes 147464 | tf_op jit(solution)/shard_map/ppermute | solution.py:359
  84.0 4.5 %collective-permute-done.27.vectors = f32[32,768]{1,0:T(8,128)S(1)} collective-permute-done((f32[32,768]{1,0:T(8,128)S(1)}, f32[32,768]{1,0:T(8,128)S(1)}, u32[]{:S(2)}, u32[]{:S(2)}) %collective-permute-start.27) | collective-permute-done | bytes 98336 | tf_op jit(solution)/shard_map/ppermute | solution.py:337
  88.5 0.5 shard_map.115.before
  89.0 0.4 collective-permute-done.26.vectors
  89.4 0.8 shard_map.116.one
  90.2 1.2 %collective-permute-done.29.other = f32[32,128]{1,0:T(8,128)S(1)} collective-permute-done((f32[32,128]{1,0:T(8,128)S(1)}, f32[32,128]{1,0:T(8,128)S(1)}, u32[]{:S(2)}, u32[]{:S(2)}) %collective-permute-start.29) | collective-permute-done | bytes 16416 | tf_op jit(solution)/shard_map/ppermute | solution.py:365
  91.4 10.4 %all_to_all.5.parts = f32[8,32,128]{2,1,0:T(8,128)S(1)} all-to-all(f32[8,32,128]{2,1,0:T(8,128)S(1)} %shard_map.117), channel_id=1, replica_groups={{0,2,4,6,8,10,12,14},{1,3,5,7,9,11,13,15},{16,18,20,22,24,26,28,30},{17..., dimensions={0} | all-to-all | bytes 262144 | tf_op jit(solution)/shard_map/all_to_all | solution.py:368
  101.8 1.7 %shard_map.118 = (f32[32,384]{1,0:T(8,128)}, f32[32,32]{1,0:T(8,128)}) custom-call(f32[8,32,128]{2,1,0:T(8,128)S(1)} %all_to_all.5.parts, f32[32,32]{1,0:T(8,128)S(1)} %shard_map.89._after.chosen, f32[32,384]{1,0:T(8,128)S(1)} %slice.4.vectors, f32[32,384]{1,0:T(8,128)S(1)} %collective-permute-done.28.lower), custom_call_target="tpu_custom_call" | custom-call | flops 1000000 | bytes 100000 | tf_op jit(solution)/shard_map/pallas_call | solution.py:369
  (48 shorter events, 2.4 us)
Async XLA Ops:
  0.6 3.6 %copy-start.1 = (f32[1,32,384]{2,1,0:T(8,128)S(1)}, f32[1,32,384]{2,1,0:T(8,128)}, u32[]{:S(2)}) copy-start(f32[1,32,384]{2,1,0:T(8,128)} %param.8) | copy-start | bytes 147460
  0.6 3.5 %collective-permute-start = (f32[32,384]{1,0:T(8,128)}, f32[32,384]{1,0:T(8,128)S(1)}, u32[]{:S(2)}, u32[]{:S(2)}) collective-permute-start(f32[32,384]{1,0:T(8,128)} %bitcast.6), channel_id=1, source_target_pairs={{0,1},{1,0},{2,3},{3,2},{4,5},{5,4},{6,7},{7,6},{8,9},{9,8},{10,11... | collective-permute-start | bytes 147464 | tf_op jit(solution)/shard_map/ppermute | solution.py:286
  1.2 7.7 %copy-start = (f32[3,24,128,128]{3,2,1,0:T(8,128)S(1)}, f32[3,24,128,128]{3,2,1,0:T(8,128)}, u32[]{:S(2)}) copy-start(f32[3,24,128,128]{3,2,1,0:T(8,128)} %tiles.3) | copy-start | bytes 14155780
  4.1 6.5 %collective-permute-start.3 = (f32[12,3,128,128]{3,2,1,0:T(8,128)S(1)}, f32[12,3,128,128]{3,2,1,0:T(8,128)S(1)}, u32[]{:S(2)}, u32[]{:S(2)}) collective-permute-start(f32[12,3,128,128]{3,2,1,0:T(8,128)S(1)} %shard_map.77), channel_id=1, source_target_pairs={{0,1},{1,0},{2,3},{3,2},{4,5},{5,4},{6,7},{7,6},{8,9},{9,8},{10,11... | collective-permute-start | bytes 7077896 | tf_op jit(solution)/shard_map/ppermute | solution.py:301
  4.3 8.7 %collective-permute-start.2 = (f32[32,768]{1,0:T(8,128)S(1)}, f32[32,768]{1,0:T(8,128)S(1)}, u32[]{:S(2)}, u32[]{:S(2)}) collective-permute-start(f32[32,768]{1,0:T(8,128)S(1)} %shard_map.78.vectors._after.initial), channel_id=1, source_target_pairs={{0,4},{1,13},{2,6},{3,15},{4,8},{5,1},{6,10},{7,3},{8,12},{9,5},{1... | collective-permute-start | bytes 294920 | tf_op jit(solution)/shard_map/ppermute | solution.py:337
  7.3 7.3 %collective-permute-start.1 = (f32[32,768]{1,0:T(8,128)S(1)}, f32[32,768]{1,0:T(8,128)S(1)}, u32[]{:S(2)}, u32[]{:S(2)}) collective-permute-start(f32[32,768]{1,0:T(8,128)S(1)} %shard_map.78.vectors._after.initial), channel_id=1, source_target_pairs={{0,2},{1,15},{2,4},{3,1},{4,6},{5,3},{6,8},{7,5},{8,10},{9,7},{10,... | collective-permute-start | bytes 294920 | tf_op jit(solution)/shard_map/ppermute | solution.py:336
  15.1 1.3 %collective-permute-start.4 = (f32[32,768]{1,0:T(8,128)S(1)}, f32[32,768]{1,0:T(8,128)S(1)}, u32[]{:S(2)}, u32[]{:S(2)}) collective-permute-start(f32[32,768]{1,0:T(8,128)S(1)} %shard_map.83.partial), channel_id=1, source_target_pairs={{0,1},{1,0},{2,3},{3,2},{4,5},{5,4},{6,7},{7,6},{8,9},{9,8},{10,11... | collective-permute-start | bytes 294920 | tf_op jit(solution)/shard_map/ppermute | solution.py:344
  16.5 6.8 %collective-permute-start.6 = (f32[32,768]{1,0:T(8,128)S(1)}, f32[32,768]{1,0:T(8,128)S(1)}, u32[]{:S(2)}, u32[]{:S(2)}) collective-permute-start(f32[32,768]{1,0:T(8,128)S(1)} %shard_map.84.vectors._after.image), channel_id=1, source_target_pairs={{0,4},{1,13},{2,6},{3,15},{4,8},{5,1},{6,10},{7,3},{8,12},{9,5},{1... | collective-permute-start | bytes 294920 | tf_op jit(solution)/shard_map/ppermute | solution.py:337
  16.9 7.3 %collective-permute-start.5 = (f32[32,768]{1,0:T(8,128)S(1)}, f32[32,768]{1,0:T(8,128)S(1)}, u32[]{:S(2)}, u32[]{:S(2)}) collective-permute-start(f32[32,768]{1,0:T(8,128)S(1)} %shard_map.84.vectors._after.image), channel_id=1, source_target_pairs={{0,2},{1,15},{2,4},{3,1},{4,6},{5,3},{6,8},{7,5},{8,10},{9,7},{10,... | collective-permute-start | bytes 294920 | tf_op jit(solution)/shard_map/ppermute | solution.py:336
  23.7 2.6 %copy-start.2 = (s32[1,8,2]{1,2,0:T(2,128)S(1)}, s32[1,8,2]{1,2,0:T(2,128)}, u32[]{:S(2)}) copy-start(s32[1,8,2]{1,2,0:T(2,128)} %param.11) | copy-start | bytes 196
  24.7 1.3 %collective-permute-start.7 = (f32[32,768]{1,0:T(8,128)S(1)}, f32[32,768]{1,0:T(8,128)S(1)}, u32[]{:S(2)}, u32[]{:S(2)}) collective-permute-start(f32[32,768]{1,0:T(8,128)S(1)} %shard_map.87.partial), channel_id=1, source_target_pairs={{0,1},{1,0},{2,3},{3,2},{4,5},{5,4},{6,7},{7,6},{8,9},{9,8},{10,11... | collective-permute-start | bytes 294920 | tf_op jit(solution)/shard_map/ppermute | solution.py:344
  26.2 6.6 %collective-permute-start.9 = (f32[32,768]{1,0:T(8,128)S(1)}, f32[32,768]{1,0:T(8,128)S(1)}, u32[]{:S(2)}, u32[]{:S(2)}) collective-permute-start(f32[32,768]{1,0:T(8,128)S(1)} %get-tuple-element.34.vectors.current.previous), channel_id=1, source_target_pairs={{0,4},{1,13},{2,6},{3,15},{4,8},{5,1},{6,10},{7,3},{8,12},{9,5},{1... | collective-permute-start | bytes 294920 | tf_op jit(solution)/shard_map/ppermute | solution.py:337
  26.3 7.4 %collective-permute-start.8 = (f32[32,768]{1,0:T(8,128)S(1)}, f32[32,768]{1,0:T(8,128)S(1)}, u32[]{:S(2)}, u32[]{:S(2)}) collective-permute-start(f32[32,768]{1,0:T(8,128)S(1)} %get-tuple-element.34.vectors.current.previous), channel_id=1, source_target_pairs={{0,2},{1,15},{2,4},{3,1},{4,6},{5,3},{6,8},{7,5},{8,10},{9,7},{10,... | collective-permute-start | bytes 294920 | tf_op jit(solution)/shard_map/ppermute | solution.py:336
  34.1 1.3 %collective-permute-start.10 = (f32[32,768]{1,0:T(8,128)S(1)}, f32[32,768]{1,0:T(8,128)S(1)}, u32[]{:S(2)}, u32[]{:S(2)}) collective-permute-start(f32[32,768]{1,0:T(8,128)S(1)} %shard_map.92.partial), channel_id=1, source_target_pairs={{0,1},{1,0},{2,3},{3,2},{4,5},{5,4},{6,7},{7,6},{8,9},{9,8},{10,11... | collective-permute-start | bytes 294920 | tf_op jit(solution)/shard_map/ppermute | solution.py:344
  35.5 6.5 %collective-permute-start.12 = (f32[32,768]{1,0:T(8,128)S(1)}, f32[32,768]{1,0:T(8,128)S(1)}, u32[]{:S(2)}, u32[]{:S(2)}) collective-permute-start(f32[32,768]{1,0:T(8,128)S(1)} %shard_map.93.vectors.current.previous), channel_id=1, source_target_pairs={{0,4},{1,13},{2,6},{3,15},{4,8},{5,1},{6,10},{7,3},{8,12},{9,5},{1... | collective-permute-start | bytes 294920 | tf_op jit(solution)/shard_map/ppermute | solution.py:337
  35.6 7.4 %collective-permute-start.11 = (f32[32,768]{1,0:T(8,128)S(1)}, f32[32,768]{1,0:T(8,128)S(1)}, u32[]{:S(2)}, u32[]{:S(2)}) collective-permute-start(f32[32,768]{1,0:T(8,128)S(1)} %shard_map.93.vectors.current.previous), channel_id=1, source_target_pairs={{0,2},{1,15},{2,4},{3,1},{4,6},{5,3},{6,8},{7,5},{8,10},{9,7},{10,... | collective-permute-start | bytes 294920 | tf_op jit(solution)/shard_map/ppermute | solution.py:336
  43.4 1.3 %collective-permute-start.13 = (f32[32,768]{1,0:T(8,128)S(1)}, f32[32,768]{1,0:T(8,128)S(1)}, u32[]{:S(2)}, u32[]{:S(2)}) collective-permute-start(f32[32,768]{1,0:T(8,128)S(1)} %shard_map.96.partial), channel_id=1, source_target_pairs={{0,1},{1,0},{2,3},{3,2},{4,5},{5,4},{6,7},{7,6},{8,9},{9,8},{10,11... | collective-permute-start | bytes 294920 | tf_op jit(solution)/shard_map/ppermute | solution.py:344
  44.8 6.5 %collective-permute-start.15 = (f32[32,768]{1,0:T(8,128)S(1)}, f32[32,768]{1,0:T(8,128)S(1)}, u32[]{:S(2)}, u32[]{:S(2)}) collective-permute-start(f32[32,768]{1,0:T(8,128)S(1)} %shard_map.97.vectors.current.previous), channel_id=1, source_target_pairs={{0,4},{1,13},{2,6},{3,15},{4,8},{5,1},{6,10},{7,3},{8,12},{9,5},{1... | collective-permute-start | bytes 294920 | tf_op jit(solution)/shard_map/ppermute | solution.py:337
  44.9 7.4 %collective-permute-start.14 = (f32[32,768]{1,0:T(8,128)S(1)}, f32[32,768]{1,0:T(8,128)S(1)}, u32[]{:S(2)}, u32[]{:S(2)}) collective-permute-start(f32[32,768]{1,0:T(8,128)S(1)} %shard_map.97.vectors.current.previous), channel_id=1, source_target_pairs={{0,2},{1,15},{2,4},{3,1},{4,6},{5,3},{6,8},{7,5},{8,10},{9,7},{10,... | collective-permute-start | bytes 294920 | tf_op jit(solution)/shard_map/ppermute | solution.py:336
  52.7 1.3 %collective-permute-start.16 = (f32[32,768]{1,0:T(8,128)S(1)}, f32[32,768]{1,0:T(8,128)S(1)}, u32[]{:S(2)}, u32[]{:S(2)}) collective-permute-start(f32[32,768]{1,0:T(8,128)S(1)} %shard_map.100.partial), channel_id=1, source_target_pairs={{0,1},{1,0},{2,3},{3,2},{4,5},{5,4},{6,7},{7,6},{8,9},{9,8},{10,11... | collective-permute-start | bytes 294920 | tf_op jit(solution)/shard_map/ppermute | solution.py:344
  54.1 6.5 %collective-permute-start.18 = (f32[32,768]{1,0:T(8,128)S(1)}, f32[32,768]{1,0:T(8,128)S(1)}, u32[]{:S(2)}, u32[]{:S(2)}) collective-permute-start(f32[32,768]{1,0:T(8,128)S(1)} %shard_map.101.vectors.current.previous), channel_id=1, source_target_pairs={{0,4},{1,13},{2,6},{3,15},{4,8},{5,1},{6,10},{7,3},{8,12},{9,5},{1... | collective-permute-start | bytes 294920 | tf_op jit(solution)/shard_map/ppermute | solution.py:337
  54.2 7.4 %collective-permute-start.17 = (f32[32,768]{1,0:T(8,128)S(1)}, f32[32,768]{1,0:T(8,128)S(1)}, u32[]{:S(2)}, u32[]{:S(2)}) collective-permute-start(f32[32,768]{1,0:T(8,128)S(1)} %shard_map.101.vectors.current.previous), channel_id=1, source_target_pairs={{0,2},{1,15},{2,4},{3,1},{4,6},{5,3},{6,8},{7,5},{8,10},{9,7},{10,... | collective-permute-start | bytes 294920 | tf_op jit(solution)/shard_map/ppermute | solution.py:336
  62.0 1.3 %collective-permute-start.19 = (f32[32,768]{1,0:T(8,128)S(1)}, f32[32,768]{1,0:T(8,128)S(1)}, u32[]{:S(2)}, u32[]{:S(2)}) collective-permute-start(f32[32,768]{1,0:T(8,128)S(1)} %shard_map.104.partial), channel_id=1, source_target_pairs={{0,1},{1,0},{2,3},{3,2},{4,5},{5,4},{6,7},{7,6},{8,9},{9,8},{10,11... | collective-permute-start | bytes 294920 | tf_op jit(solution)/shard_map/ppermute | solution.py:344
  63.4 6.5 %collective-permute-start.21 = (f32[32,768]{1,0:T(8,128)S(1)}, f32[32,768]{1,0:T(8,128)S(1)}, u32[]{:S(2)}, u32[]{:S(2)}) collective-permute-start(f32[32,768]{1,0:T(8,128)S(1)} %shard_map.105.vectors.current.previous), channel_id=1, source_target_pairs={{0,4},{1,13},{2,6},{3,15},{4,8},{5,1},{6,10},{7,3},{8,12},{9,5},{1... | collective-permute-start | bytes 294920 | tf_op jit(solution)/shard_map/ppermute | solution.py:337
  63.4 7.4 %collective-permute-start.20 = (f32[32,768]{1,0:T(8,128)S(1)}, f32[32,768]{1,0:T(8,128)S(1)}, u32[]{:S(2)}, u32[]{:S(2)}) collective-permute-start(f32[32,768]{1,0:T(8,128)S(1)} %shard_map.105.vectors.current.previous), channel_id=1, source_target_pairs={{0,2},{1,15},{2,4},{3,1},{4,6},{5,3},{6,8},{7,5},{8,10},{9,7},{10,... | collective-permute-start | bytes 294920 | tf_op jit(solution)/shard_map/ppermute | solution.py:336
  71.3 1.3 %collective-permute-start.22 = (f32[32,768]{1,0:T(8,128)S(1)}, f32[32,768]{1,0:T(8,128)S(1)}, u32[]{:S(2)}, u32[]{:S(2)}) collective-permute-start(f32[32,768]{1,0:T(8,128)S(1)} %shard_map.108.partial), channel_id=1, source_target_pairs={{0,1},{1,0},{2,3},{3,2},{4,5},{5,4},{6,7},{7,6},{8,9},{9,8},{10,11... | collective-permute-start | bytes 294920 | tf_op jit(solution)/shard_map/ppermute | solution.py:344
  72.7 6.5 %collective-permute-start.24 = (f32[32,768]{1,0:T(8,128)S(1)}, f32[32,768]{1,0:T(8,128)S(1)}, u32[]{:S(2)}, u32[]{:S(2)}) collective-permute-start(f32[32,768]{1,0:T(8,128)S(1)} %shard_map.109.vectors.current), channel_id=1, source_target_pairs={{0,4},{1,13},{2,6},{3,15},{4,8},{5,1},{6,10},{7,3},{8,12},{9,5},{1... | collective-permute-start | bytes 294920 | tf_op jit(solution)/shard_map/ppermute | solution.py:337
  72.7 7.4 %collective-permute-start.23 = (f32[32,768]{1,0:T(8,128)S(1)}, f32[32,768]{1,0:T(8,128)S(1)}, u32[]{:S(2)}, u32[]{:S(2)}) collective-permute-start(f32[32,768]{1,0:T(8,128)S(1)} %shard_map.109.vectors.current), channel_id=1, source_target_pairs={{0,2},{1,15},{2,4},{3,1},{4,6},{5,3},{6,8},{7,5},{8,10},{9,7},{10,... | collective-permute-start | bytes 294920 | tf_op jit(solution)/shard_map/ppermute | solution.py:336
  80.6 1.3 %collective-permute-start.25 = (f32[32,768]{1,0:T(8,128)S(1)}, f32[32,768]{1,0:T(8,128)S(1)}, u32[]{:S(2)}, u32[]{:S(2)}) collective-permute-start(f32[32,768]{1,0:T(8,128)S(1)} %shard_map.112.partial), channel_id=1, source_target_pairs={{0,1},{1,0},{2,3},{3,2},{4,5},{5,4},{6,7},{7,6},{8,9},{9,8},{10,11... | collective-permute-start | bytes 294920 | tf_op jit(solution)/shard_map/ppermute | solution.py:344
  82.0 6.5 %collective-permute-start.27 = (f32[32,768]{1,0:T(8,128)S(1)}, f32[32,768]{1,0:T(8,128)S(1)}, u32[]{:S(2)}, u32[]{:S(2)}) collective-permute-start(f32[32,768]{1,0:T(8,128)S(1)} %shard_map.113.vectors.pair), channel_id=1, source_target_pairs={{0,4},{1,13},{2,6},{3,15},{4,8},{5,1},{6,10},{7,3},{8,12},{9,5},{1... | collective-permute-start | bytes 294920 | tf_op jit(solution)/shard_map/ppermute | solution.py:337
  82.0 7.4 %collective-permute-start.26 = (f32[32,768]{1,0:T(8,128)S(1)}, f32[32,768]{1,0:T(8,128)S(1)}, u32[]{:S(2)}, u32[]{:S(2)}) collective-permute-start(f32[32,768]{1,0:T(8,128)S(1)} %shard_map.113.vectors.pair), channel_id=1, source_target_pairs={{0,2},{1,15},{2,4},{3,1},{4,6},{5,3},{6,8},{7,5},{8,10},{9,7},{10,... | collective-permute-start | bytes 294920 | tf_op jit(solution)/shard_map/ppermute | solution.py:336
  82.1 6.8 %collective-permute-start.28 = (f32[32,384]{1,0:T(8,128)S(1)}, f32[32,384]{1,0:T(8,128)S(1)}, u32[]{:S(2)}, u32[]{:S(2)}) collective-permute-start(f32[32,384]{1,0:T(8,128)S(1)} %slice.4.vectors), channel_id=1, source_target_pairs={{0,16},{16,0},{1,17},{17,1},{2,18},{18,2},{3,19},{19,3},{4,20},{20... | collective-permute-start | bytes 147464 | tf_op jit(solution)/shard_map/ppermute | solution.py:359
  90.2 1.2 %collective-permute-start.29 = (f32[32,128]{1,0:T(8,128)S(1)}, f32[32,128]{1,0:T(8,128)S(1)}, u32[]{:S(2)}, u32[]{:S(2)}) collective-permute-start(f32[32,128]{1,0:T(8,128)S(1)} %shard_map.116.one), channel_id=1, source_target_pairs={{0,1},{1,0},{2,3},{3,2},{4,5},{5,4},{6,7},{7,6},{8,9},{9,8},{10,11... | collective-permute-start | bytes 49160 | tf_op jit(solution)/shard_map/ppermute | solution.py:365

commit v8 on v6

--- a/solution.py
+++ b/solution.py
@@ -241,7 +241,7 @@
     lower_basis = scale * dot(inverse_below, lower[...], NN)
     correlation = dot(mixed, inverse_below, NT)
     projected[...] = dot(cross, inverse, NT)
-    some = jnp.max(chosen[...]) > 0.0
+    some = lax.axis_index("cuts") > 0
     removal = jnp.where(some, dot(chosen[...] * correlation, lower_basis, NN), 0.0)
     filtered[...] = basis - removal
 

time: 104 us -> 104 us (level)
  no operation moved by 1% of the time
where the time goes in v8:
time: 104 us
  waiting for transfers between devices  62.2 us (60%)
  Pallas kernels  19.9 us (19%)
  blocking collectives  10.4 us (10%)
  starting transfers between devices  8.68 us (8%)
  between operations  2.36 us (2%)
    ppermute x9, waiting for transfers between devices, most_of_image(): far = lax.ppermute(vectors, 'row', farther)  45.9 us
    pallas_call x26, Pallas kernels, part(): call(kernel, vec, [VMEM] * (len(vectors) + 2), VMEM, cost_estimate=pl.Cos...  10.8 us
    all_to_all x1, blocking collectives, local(): lax.all_to_all(spread, 'row', 0, 0, tiled=True, axis_index_groups=same_core)  10.4 us
    ppermute x8, waiting for transfers between devices, images(): return (partial, lax.ppermute(partial, 'row', swap))  10.3 us
    ppermute x9, waiting for transfers between devices, most_of_image(): near = lax.ppermute(vectors, 'row', nearer)  4.81 us
    ppermute x9, starting transfers between devices, most_of_image(): far = lax.ppermute(vectors, 'row', farther)  3.9 us
    pallas_call x1, Pallas kernels, local(): call(functools.partial(gather_kernel, rows=rows, stored=stored, total=tot...  2.93 us
    ppermute x9, starting transfers between devices, most_of_image(): near = lax.ppermute(vectors, 'row', nearer)  2.36 us
  transfers between devices with their start and end apart: 30, of which 27 were waited for; matrix products, arithmetic and copies ran while one was open for 0% of the time, Pallas kernels for 13%

profile of v8, /device:TPU:0, one launch (start us, length us, event | category | flops | bytes accessed | tf_op | source)
XLA Modules:
  0.0 103.7 jit_solution(6899692169310717222)
XLA Ops:
  0.6 0.5 collective-permute-start
  1.2 2.9 %shard_map.77 = f32[12,3,128,128]{3,2,1,0:T(8,128)S(1)} custom-call(s32[3,24]{1,0:T(4,128)} %pattern.3, f32[3,24,128,128]{3,2,1,0:T(8,128)} %tiles.3), custom_call_target="tpu_custom_call" | custom-call | bytes 8000000 | tf_op jit(solution)/shard_map/pallas_call | solution.py:282
  4.3 3.1 %collective-permute-start.2 = (f32[32,768]{1,0:T(8,128)S(1)}, f32[32,768]{1,0:T(8,128)S(1)}, u32[]{:S(2)}, u32[]{:S(2)}) collective-permute-start(f32[32,768]{1,0:T(8,128)S(1)} %shard_map.78.vectors._after.initial), channel_id=1, source_target_pairs={{0,4},{1,13},{2,6},{3,15},{4,8},{5,1},{6,10},{7,3},{8,12},{9,5},{1... | collective-permute-start | bytes 294920 | tf_op jit(solution)/shard_map/ppermute | solution.py:332
  7.3 1.5 %collective-permute-start.1 = (f32[32,768]{1,0:T(8,128)S(1)}, f32[32,768]{1,0:T(8,128)S(1)}, u32[]{:S(2)}, u32[]{:S(2)}) collective-permute-start(f32[32,768]{1,0:T(8,128)S(1)} %shard_map.78.vectors._after.initial), channel_id=1, source_target_pairs={{0,2},{1,15},{2,4},{3,1},{4,6},{5,3},{6,8},{7,5},{8,10},{9,7},{10,... | collective-permute-start | bytes 294920 | tf_op jit(solution)/shard_map/ppermute | solution.py:331
  8.9 1.8 %shard_map.79 = (bf16[768,768]{1,0:T(8,128)(2,1)S(1)}, bf16[768,768]{1,0:T(8,128)(2,1)S(1)}, bf16[768,768]{1,0:T(8,128)(2,1)S(1)}, bf16[768,768]{1,0:T(8,128)(2,...) custom-call(s32[3,24]{1,0:T(4,128)} %pattern.3, f32[3,24,128,128]{3,2,1,0:T(8,128)S(1)} %copy-done), custom_call_target="tpu_custom_call" | custom-call | flops 1000000 | bytes 100000 | tf_op jit(solution)/shard_map/pallas_call | solution.py:297
  10.6 0.7 shard_map.80
  11.4 0.3 shard_map.81.before
  11.7 1.3 %collective-permute-done.2.vectors = f32[32,768]{1,0:T(8,128)S(1)} collective-permute-done((f32[32,768]{1,0:T(8,128)S(1)}, f32[32,768]{1,0:T(8,128)S(1)}, u32[]{:S(2)}, u32[]{:S(2)}) %collective-permute-start.2) | collective-permute-done | bytes 98336 | tf_op jit(solution)/shard_map/ppermute | solution.py:332
  13.0 0.5 shard_map.82.before
  13.4 1.2 %collective-permute-done.1.vectors = f32[32,768]{1,0:T(8,128)S(1)} collective-permute-done((f32[32,768]{1,0:T(8,128)S(1)}, f32[32,768]{1,0:T(8,128)S(1)}, u32[]{:S(2)}, u32[]{:S(2)}) %collective-permute-start.1) | collective-permute-done | bytes 98336 | tf_op jit(solution)/shard_map/ppermute | solution.py:331
  14.7 0.5 shard_map.83.partial
  15.2 1.3 %collective-permute-done.4.other = f32[32,768]{1,0:T(8,128)S(1)} collective-permute-done((f32[32,768]{1,0:T(8,128)S(1)}, f32[32,768]{1,0:T(8,128)S(1)}, u32[]{:S(2)}, u32[]{:S(2)}) %collective-permute-start.4) | collective-permute-done | bytes 98336 | tf_op jit(solution)/shard_map/ppermute | solution.py:339
  16.5 0.4 collective-permute-start.6
  18.6 0.3 shard_map.85.before
  18.9 4.4 %collective-permute-done.6.vectors = f32[32,768]{1,0:T(8,128)S(1)} collective-permute-done((f32[32,768]{1,0:T(8,128)S(1)}, f32[32,768]{1,0:T(8,128)S(1)}, u32[]{:S(2)}, u32[]{:S(2)}) %collective-permute-start.6) | collective-permute-done | bytes 98336 | tf_op jit(solution)/shard_map/ppermute | solution.py:332
  23.3 0.5 shard_map.86.before
  23.8 0.5 collective-permute-done.5.vectors
  24.2 0.5 shard_map.87.partial
  24.8 1.2 %collective-permute-done.7.other = f32[32,768]{1,0:T(8,128)S(1)} collective-permute-done((f32[32,768]{1,0:T(8,128)S(1)}, f32[32,768]{1,0:T(8,128)S(1)}, u32[]{:S(2)}, u32[]{:S(2)}) %collective-permute-start.7) | collective-permute-done | bytes 98336 | tf_op jit(solution)/shard_map/ppermute | solution.py:339
  26.4 0.6 shard_map.89._after.chosen
  27.0 0.3 shard_map.90.before
  27.3 5.5 %collective-permute-done.9.vectors = f32[32,768]{1,0:T(8,128)S(1)} collective-permute-done((f32[32,768]{1,0:T(8,128)S(1)}, f32[32,768]{1,0:T(8,128)S(1)}, u32[]{:S(2)}, u32[]{:S(2)}) %collective-permute-start.9) | collective-permute-done | bytes 98336 | tf_op jit(solution)/shard_map/ppermute | solution.py:332
  32.7 0.5 shard_map.91.before
  33.2 0.4 collective-permute-done.8.vectors
  33.6 0.5 shard_map.92.partial
  34.1 1.3 %collective-permute-done.10.other = f32[32,768]{1,0:T(8,128)S(1)} collective-permute-done((f32[32,768]{1,0:T(8,128)S(1)}, f32[32,768]{1,0:T(8,128)S(1)}, u32[]{:S(2)}, u32[]{:S(2)}) %collective-permute-start.10) | collective-permute-done | bytes 98336 | tf_op jit(solution)/shard_map/ppermute | solution.py:339
  35.7 0.3 shard_map.94.before
  36.0 6.0 %collective-permute-done.12.vectors = f32[32,768]{1,0:T(8,128)S(1)} collective-permute-done((f32[32,768]{1,0:T(8,128)S(1)}, f32[32,768]{1,0:T(8,128)S(1)}, u32[]{:S(2)}, u32[]{:S(2)}) %collective-permute-start.12) | collective-permute-done | bytes 98336 | tf_op jit(solution)/shard_map/ppermute | solution.py:332
  41.9 0.5 shard_map.95.before
  42.4 0.5 collective-permute-done.11.vectors
  42.9 0.5 shard_map.96.partial
  43.4 1.3 %collective-permute-done.13.other = f32[32,768]{1,0:T(8,128)S(1)} collective-permute-done((f32[32,768]{1,0:T(8,128)S(1)}, f32[32,768]{1,0:T(8,128)S(1)}, u32[]{:S(2)}, u32[]{:S(2)}) %collective-permute-start.13) | collective-permute-done | bytes 98336 | tf_op jit(solution)/shard_map/ppermute | solution.py:339
  44.9 0.3 shard_map.98.before
  45.2 6.1 %collective-permute-done.15.vectors = f32[32,768]{1,0:T(8,128)S(1)} collective-permute-done((f32[32,768]{1,0:T(8,128)S(1)}, f32[32,768]{1,0:T(8,128)S(1)}, u32[]{:S(2)}, u32[]{:S(2)}) %collective-permute-start.15) | collective-permute-done | bytes 98336 | tf_op jit(solution)/shard_map/ppermute | solution.py:332
  51.3 0.5 shard_map.99.before
  51.7 0.5 collective-permute-done.14.vectors
  52.2 0.5 shard_map.100.partial
  52.7 1.3 %collective-permute-done.16.other = f32[32,768]{1,0:T(8,128)S(1)} collective-permute-done((f32[32,768]{1,0:T(8,128)S(1)}, f32[32,768]{1,0:T(8,128)S(1)}, u32[]{:S(2)}, u32[]{:S(2)}) %collective-permute-start.16) | collective-permute-done | bytes 98336 | tf_op jit(solution)/shard_map/ppermute | solution.py:339
  54.2 0.3 shard_map.102.before
  54.5 6.1 %collective-permute-done.18.vectors = f32[32,768]{1,0:T(8,128)S(1)} collective-permute-done((f32[32,768]{1,0:T(8,128)S(1)}, f32[32,768]{1,0:T(8,128)S(1)}, u32[]{:S(2)}, u32[]{:S(2)}) %collective-permute-start.18) | collective-permute-done | bytes 98336 | tf_op jit(solution)/shard_map/ppermute | solution.py:332
  60.6 0.5 shard_map.103.before
  61.0 0.5 collective-permute-done.17.vectors
  61.5 0.5 shard_map.104.partial
  62.0 1.3 %collective-permute-done.19.other = f32[32,768]{1,0:T(8,128)S(1)} collective-permute-done((f32[32,768]{1,0:T(8,128)S(1)}, f32[32,768]{1,0:T(8,128)S(1)}, u32[]{:S(2)}, u32[]{:S(2)}) %collective-permute-start.19) | collective-permute-done | bytes 98336 | tf_op jit(solution)/shard_map/ppermute | solution.py:339
  63.5 0.3 shard_map.106.before
  63.8 6.1 %collective-permute-done.21.vectors = f32[32,768]{1,0:T(8,128)S(1)} collective-permute-done((f32[32,768]{1,0:T(8,128)S(1)}, f32[32,768]{1,0:T(8,128)S(1)}, u32[]{:S(2)}, u32[]{:S(2)}) %collective-permute-start.21) | collective-permute-done | bytes 98336 | tf_op jit(solution)/shard_map/ppermute | solution.py:332
  69.9 0.5 shard_map.107.before
  70.3 0.5 collective-permute-done.20.vectors
  70.8 0.5 shard_map.108.partial
  71.3 1.3 %collective-permute-done.22.other = f32[32,768]{1,0:T(8,128)S(1)} collective-permute-done((f32[32,768]{1,0:T(8,128)S(1)}, f32[32,768]{1,0:T(8,128)S(1)}, u32[]{:S(2)}, u32[]{:S(2)}) %collective-permute-start.22) | collective-permute-done | bytes 98336 | tf_op jit(solution)/shard_map/ppermute | solution.py:339
  72.8 0.3 shard_map.110.before
  73.1 6.1 %collective-permute-done.24.vectors = f32[32,768]{1,0:T(8,128)S(1)} collective-permute-done((f32[32,768]{1,0:T(8,128)S(1)}, f32[32,768]{1,0:T(8,128)S(1)}, u32[]{:S(2)}, u32[]{:S(2)}) %collective-permute-start.24) | collective-permute-done | bytes 98336 | tf_op jit(solution)/shard_map/ppermute | solution.py:332
  79.2 0.5 shard_map.111.before
  79.6 0.5 collective-permute-done.23.vectors
  80.1 0.5 shard_map.112.partial
  80.6 1.3 %collective-permute-done.25.other = f32[32,768]{1,0:T(8,128)S(1)} collective-permute-done((f32[32,768]{1,0:T(8,128)S(1)}, f32[32,768]{1,0:T(8,128)S(1)}, u32[]{:S(2)}, u32[]{:S(2)}) %collective-permute-start.25) | collective-permute-done | bytes 98336 | tf_op jit(solution)/shard_map/ppermute | solution.py:339
  82.1 1.6 %collective-permute-start.28 = (f32[32,384]{1,0:T(8,128)S(1)}, f32[32,384]{1,0:T(8,128)S(1)}, u32[]{:S(2)}, u32[]{:S(2)}) collective-permute-start(f32[32,384]{1,0:T(8,128)S(1)} %slice.4.vectors), channel_id=1, source_target_pairs={{0,16},{16,0},{1,17},{17,1},{2,18},{18,2},{3,19},{19,3},{4,20},{20... | collective-permute-start | bytes 147464 | tf_op jit(solution)/shard_map/ppermute | solution.py:354
  84.0 4.5 %collective-permute-done.27.vectors = f32[32,768]{1,0:T(8,128)S(1)} collective-permute-done((f32[32,768]{1,0:T(8,128)S(1)}, f32[32,768]{1,0:T(8,128)S(1)}, u32[]{:S(2)}, u32[]{:S(2)}) %collective-permute-start.27) | collective-permute-done | bytes 98336 | tf_op jit(solution)/shard_map/ppermute | solution.py:332
  88.5 0.5 shard_map.115.before
  89.0 0.4 collective-permute-done.26.vectors
  89.4 0.8 shard_map.116.one
  90.2 1.2 %collective-permute-done.29.other = f32[32,128]{1,0:T(8,128)S(1)} collective-permute-done((f32[32,128]{1,0:T(8,128)S(1)}, f32[32,128]{1,0:T(8,128)S(1)}, u32[]{:S(2)}, u32[]{:S(2)}) %collective-permute-start.29) | collective-permute-done | bytes 16416 | tf_op jit(solution)/shard_map/ppermute | solution.py:360
  91.4 10.4 %all_to_all.5.parts = f32[8,32,128]{2,1,0:T(8,128)S(1)} all-to-all(f32[8,32,128]{2,1,0:T(8,128)S(1)} %shard_map.117), channel_id=1, replica_groups={{0,2,4,6,8,10,12,14},{1,3,5,7,9,11,13,15},{16,18,20,22,24,26,28,30},{17..., dimensions={0} | all-to-all | bytes 262144 | tf_op jit(solution)/shard_map/all_to_all | solution.py:363
  101.8 1.8 %shard_map.118 = (f32[32,384]{1,0:T(8,128)}, f32[32,32]{1,0:T(8,128)}) custom-call(f32[8,32,128]{2,1,0:T(8,128)S(1)} %all_to_all.5.parts, f32[32,32]{1,0:T(8,128)S(1)} %shard_map.89._after.chosen, f32[32,384]{1,0:T(8,128)S(1)} %slice.4.vectors, f32[32,384]{1,0:T(8,128)S(1)} %collective-permute-done.28.lower), custom_call_target="tpu_custom_call" | custom-call | flops 1000000 | bytes 100000 | tf_op jit(solution)/shard_map/pallas_call | solution.py:364
  (48 shorter events, 2.5 us)
Async XLA Ops:
  0.6 3.6 %copy-start.1 = (f32[1,32,384]{2,1,0:T(8,128)S(1)}, f32[1,32,384]{2,1,0:T(8,128)}, u32[]{:S(2)}) copy-start(f32[1,32,384]{2,1,0:T(8,128)} %param.8) | copy-start | bytes 147460
  0.6 3.5 %collective-permute-start = (f32[32,384]{1,0:T(8,128)}, f32[32,384]{1,0:T(8,128)S(1)}, u32[]{:S(2)}, u32[]{:S(2)}) collective-permute-start(f32[32,384]{1,0:T(8,128)} %bitcast.6), channel_id=1, source_target_pairs={{0,1},{1,0},{2,3},{3,2},{4,5},{5,4},{6,7},{7,6},{8,9},{9,8},{10,11... | collective-permute-start | bytes 147464 | tf_op jit(solution)/shard_map/ppermute | solution.py:281
  1.2 7.7 %copy-start = (f32[3,24,128,128]{3,2,1,0:T(8,128)S(1)}, f32[3,24,128,128]{3,2,1,0:T(8,128)}, u32[]{:S(2)}) copy-start(f32[3,24,128,128]{3,2,1,0:T(8,128)} %tiles.3) | copy-start | bytes 14155780
  4.1 6.5 %collective-permute-start.3 = (f32[12,3,128,128]{3,2,1,0:T(8,128)S(1)}, f32[12,3,128,128]{3,2,1,0:T(8,128)S(1)}, u32[]{:S(2)}, u32[]{:S(2)}) collective-permute-start(f32[12,3,128,128]{3,2,1,0:T(8,128)S(1)} %shard_map.77), channel_id=1, source_target_pairs={{0,1},{1,0},{2,3},{3,2},{4,5},{5,4},{6,7},{7,6},{8,9},{9,8},{10,11... | collective-permute-start | bytes 7077896 | tf_op jit(solution)/shard_map/ppermute | solution.py:296
  4.3 8.7 %collective-permute-start.2 = (f32[32,768]{1,0:T(8,128)S(1)}, f32[32,768]{1,0:T(8,128)S(1)}, u32[]{:S(2)}, u32[]{:S(2)}) collective-permute-start(f32[32,768]{1,0:T(8,128)S(1)} %shard_map.78.vectors._after.initial), channel_id=1, source_target_pairs={{0,4},{1,13},{2,6},{3,15},{4,8},{5,1},{6,10},{7,3},{8,12},{9,5},{1... | collective-permute-start | bytes 294920 | tf_op jit(solution)/shard_map/ppermute | solution.py:332
  7.3 7.3 %collective-permute-start.1 = (f32[32,768]{1,0:T(8,128)S(1)}, f32[32,768]{1,0:T(8,128)S(1)}, u32[]{:S(2)}, u32[]{:S(2)}) collective-permute-start(f32[32,768]{1,0:T(8,128)S(1)} %shard_map.78.vectors._after.initial), channel_id=1, source_target_pairs={{0,2},{1,15},{2,4},{3,1},{4,6},{5,3},{6,8},{7,5},{8,10},{9,7},{10,... | collective-permute-start | bytes 294920 | tf_op jit(solution)/shard_map/ppermute | solution.py:331
  15.1 1.3 %collective-permute-start.4 = (f32[32,768]{1,0:T(8,128)S(1)}, f32[32,768]{1,0:T(8,128)S(1)}, u32[]{:S(2)}, u32[]{:S(2)}) collective-permute-start(f32[32,768]{1,0:T(8,128)S(1)} %shard_map.83.partial), channel_id=1, source_target_pairs={{0,1},{1,0},{2,3},{3,2},{4,5},{5,4},{6,7},{7,6},{8,9},{9,8},{10,11... | collective-permute-start | bytes 294920 | tf_op jit(solution)/shard_map/ppermute | solution.py:339
  16.5 6.8 %collective-permute-start.6 = (f32[32,768]{1,0:T(8,128)S(1)}, f32[32,768]{1,0:T(8,128)S(1)}, u32[]{:S(2)}, u32[]{:S(2)}) collective-permute-start(f32[32,768]{1,0:T(8,128)S(1)} %shard_map.84.vectors._after.image), channel_id=1, source_target_pairs={{0,4},{1,13},{2,6},{3,15},{4,8},{5,1},{6,10},{7,3},{8,12},{9,5},{1... | collective-permute-start | bytes 294920 | tf_op jit(solution)/shard_map/ppermute | solution.py:332
  16.9 7.3 %collective-permute-start.5 = (f32[32,768]{1,0:T(8,128)S(1)}, f32[32,768]{1,0:T(8,128)S(1)}, u32[]{:S(2)}, u32[]{:S(2)}) collective-permute-start(f32[32,768]{1,0:T(8,128)S(1)} %shard_map.84.vectors._after.image), channel_id=1, source_target_pairs={{0,2},{1,15},{2,4},{3,1},{4,6},{5,3},{6,8},{7,5},{8,10},{9,7},{10,... | collective-permute-start | bytes 294920 | tf_op jit(solution)/shard_map/ppermute | solution.py:331
  23.7 2.6 %copy-start.2 = (s32[1,8,2]{1,2,0:T(2,128)S(1)}, s32[1,8,2]{1,2,0:T(2,128)}, u32[]{:S(2)}) copy-start(s32[1,8,2]{1,2,0:T(2,128)} %param.11) | copy-start | bytes 196
  24.7 1.3 %collective-permute-start.7 = (f32[32,768]{1,0:T(8,128)S(1)}, f32[32,768]{1,0:T(8,128)S(1)}, u32[]{:S(2)}, u32[]{:S(2)}) collective-permute-start(f32[32,768]{1,0:T(8,128)S(1)} %shard_map.87.partial), channel_id=1, source_target_pairs={{0,1},{1,0},{2,3},{3,2},{4,5},{5,4},{6,7},{7,6},{8,9},{9,8},{10,11... | collective-permute-start | bytes 294920 | tf_op jit(solution)/shard_map/ppermute | solution.py:339
  26.2 6.6 %collective-permute-start.9 = (f32[32,768]{1,0:T(8,128)S(1)}, f32[32,768]{1,0:T(8,128)S(1)}, u32[]{:S(2)}, u32[]{:S(2)}) collective-permute-start(f32[32,768]{1,0:T(8,128)S(1)} %get-tuple-element.34.vectors.current.previous), channel_id=1, source_target_pairs={{0,4},{1,13},{2,6},{3,15},{4,8},{5,1},{6,10},{7,3},{8,12},{9,5},{1... | collective-permute-start | bytes 294920 | tf_op jit(solution)/shard_map/ppermute | solution.py:332
  26.2 7.4 %collective-permute-start.8 = (f32[32,768]{1,0:T(8,128)S(1)}, f32[32,768]{1,0:T(8,128)S(1)}, u32[]{:S(2)}, u32[]{:S(2)}) collective-permute-start(f32[32,768]{1,0:T(8,128)S(1)} %get-tuple-element.34.vectors.current.previous), channel_id=1, source_target_pairs={{0,2},{1,15},{2,4},{3,1},{4,6},{5,3},{6,8},{7,5},{8,10},{9,7},{10,... | collective-permute-start | bytes 294920 | tf_op jit(solution)/shard_map/ppermute | solution.py:331
  34.1 1.3 %collective-permute-start.10 = (f32[32,768]{1,0:T(8,128)S(1)}, f32[32,768]{1,0:T(8,128)S(1)}, u32[]{:S(2)}, u32[]{:S(2)}) collective-permute-start(f32[32,768]{1,0:T(8,128)S(1)} %shard_map.92.partial), channel_id=1, source_target_pairs={{0,1},{1,0},{2,3},{3,2},{4,5},{5,4},{6,7},{7,6},{8,9},{9,8},{10,11... | collective-permute-start | bytes 294920 | tf_op jit(solution)/shard_map/ppermute | solution.py:339
  35.5 6.5 %collective-permute-start.12 = (f32[32,768]{1,0:T(8,128)S(1)}, f32[32,768]{1,0:T(8,128)S(1)}, u32[]{:S(2)}, u32[]{:S(2)}) collective-permute-start(f32[32,768]{1,0:T(8,128)S(1)} %shard_map.93.vectors.current.previous), channel_id=1, source_target_pairs={{0,4},{1,13},{2,6},{3,15},{4,8},{5,1},{6,10},{7,3},{8,12},{9,5},{1... | collective-permute-start | bytes 294920 | tf_op jit(solution)/shard_map/ppermute | solution.py:332
  35.5 7.4 %collective-permute-start.11 = (f32[32,768]{1,0:T(8,128)S(1)}, f32[32,768]{1,0:T(8,128)S(1)}, u32[]{:S(2)}, u32[]{:S(2)}) collective-permute-start(f32[32,768]{1,0:T(8,128)S(1)} %shard_map.93.vectors.current.previous), channel_id=1, source_target_pairs={{0,2},{1,15},{2,4},{3,1},{4,6},{5,3},{6,8},{7,5},{8,10},{9,7},{10,... | collective-permute-start | bytes 294920 | tf_op jit(solution)/shard_map/ppermute | solution.py:331
  43.4 1.3 %collective-permute-start.13 = (f32[32,768]{1,0:T(8,128)S(1)}, f32[32,768]{1,0:T(8,128)S(1)}, u32[]{:S(2)}, u32[]{:S(2)}) collective-permute-start(f32[32,768]{1,0:T(8,128)S(1)} %shard_map.96.partial), channel_id=1, source_target_pairs={{0,1},{1,0},{2,3},{3,2},{4,5},{5,4},{6,7},{7,6},{8,9},{9,8},{10,11... | collective-permute-start | bytes 294920 | tf_op jit(solution)/shard_map/ppermute | solution.py:339
  44.8 6.5 %collective-permute-start.15 = (f32[32,768]{1,0:T(8,128)S(1)}, f32[32,768]{1,0:T(8,128)S(1)}, u32[]{:S(2)}, u32[]{:S(2)}) collective-permute-start(f32[32,768]{1,0:T(8,128)S(1)} %shard_map.97.vectors.current.previous), channel_id=1, source_target_pairs={{0,4},{1,13},{2,6},{3,15},{4,8},{5,1},{6,10},{7,3},{8,12},{9,5},{1... | collective-permute-start | bytes 294920 | tf_op jit(solution)/shard_map/ppermute | solution.py:332
  44.8 7.4 %collective-permute-start.14 = (f32[32,768]{1,0:T(8,128)S(1)}, f32[32,768]{1,0:T(8,128)S(1)}, u32[]{:S(2)}, u32[]{:S(2)}) collective-permute-start(f32[32,768]{1,0:T(8,128)S(1)} %shard_map.97.vectors.current.previous), channel_id=1, source_target_pairs={{0,2},{1,15},{2,4},{3,1},{4,6},{5,3},{6,8},{7,5},{8,10},{9,7},{10,... | collective-permute-start | bytes 294920 | tf_op jit(solution)/shard_map/ppermute | solution.py:331
  52.7 1.3 %collective-permute-start.16 = (f32[32,768]{1,0:T(8,128)S(1)}, f32[32,768]{1,0:T(8,128)S(1)}, u32[]{:S(2)}, u32[]{:S(2)}) collective-permute-start(f32[32,768]{1,0:T(8,128)S(1)} %shard_map.100.partial), channel_id=1, source_target_pairs={{0,1},{1,0},{2,3},{3,2},{4,5},{5,4},{6,7},{7,6},{8,9},{9,8},{10,11... | collective-permute-start | bytes 294920 | tf_op jit(solution)/shard_map/ppermute | solution.py:339
  54.1 6.5 %collective-permute-start.18 = (f32[32,768]{1,0:T(8,128)S(1)}, f32[32,768]{1,0:T(8,128)S(1)}, u32[]{:S(2)}, u32[]{:S(2)}) collective-permute-start(f32[32,768]{1,0:T(8,128)S(1)} %shard_map.101.vectors.current.previous), channel_id=1, source_target_pairs={{0,4},{1,13},{2,6},{3,15},{4,8},{5,1},{6,10},{7,3},{8,12},{9,5},{1... | collective-permute-start | bytes 294920 | tf_op jit(solution)/shard_map/ppermute | solution.py:332
  54.1 7.4 %collective-permute-start.17 = (f32[32,768]{1,0:T(8,128)S(1)}, f32[32,768]{1,0:T(8,128)S(1)}, u32[]{:S(2)}, u32[]{:S(2)}) collective-permute-start(f32[32,768]{1,0:T(8,128)S(1)} %shard_map.101.vectors.current.previous), channel_id=1, source_target_pairs={{0,2},{1,15},{2,4},{3,1},{4,6},{5,3},{6,8},{7,5},{8,10},{9,7},{10,... | collective-permute-start | bytes 294920 | tf_op jit(solution)/shard_map/ppermute | solution.py:331
  62.0 1.3 %collective-permute-start.19 = (f32[32,768]{1,0:T(8,128)S(1)}, f32[32,768]{1,0:T(8,128)S(1)}, u32[]{:S(2)}, u32[]{:S(2)}) collective-permute-start(f32[32,768]{1,0:T(8,128)S(1)} %shard_map.104.partial), channel_id=1, source_target_pairs={{0,1},{1,0},{2,3},{3,2},{4,5},{5,4},{6,7},{7,6},{8,9},{9,8},{10,11... | collective-permute-start | bytes 294920 | tf_op jit(solution)/shard_map/ppermute | solution.py:339
  63.4 6.5 %collective-permute-start.21 = (f32[32,768]{1,0:T(8,128)S(1)}, f32[32,768]{1,0:T(8,128)S(1)}, u32[]{:S(2)}, u32[]{:S(2)}) collective-permute-start(f32[32,768]{1,0:T(8,128)S(1)} %shard_map.105.vectors.current.previous), channel_id=1, source_target_pairs={{0,4},{1,13},{2,6},{3,15},{4,8},{5,1},{6,10},{7,3},{8,12},{9,5},{1... | collective-permute-start | bytes 294920 | tf_op jit(solution)/shard_map/ppermute | solution.py:332
  63.4 7.4 %collective-permute-start.20 = (f32[32,768]{1,0:T(8,128)S(1)}, f32[32,768]{1,0:T(8,128)S(1)}, u32[]{:S(2)}, u32[]{:S(2)}) collective-permute-start(f32[32,768]{1,0:T(8,128)S(1)} %shard_map.105.vectors.current.previous), channel_id=1, source_target_pairs={{0,2},{1,15},{2,4},{3,1},{4,6},{5,3},{6,8},{7,5},{8,10},{9,7},{10,... | collective-permute-start | bytes 294920 | tf_op jit(solution)/shard_map/ppermute | solution.py:331
  71.3 1.3 %collective-permute-start.22 = (f32[32,768]{1,0:T(8,128)S(1)}, f32[32,768]{1,0:T(8,128)S(1)}, u32[]{:S(2)}, u32[]{:S(2)}) collective-permute-start(f32[32,768]{1,0:T(8,128)S(1)} %shard_map.108.partial), channel_id=1, source_target_pairs={{0,1},{1,0},{2,3},{3,2},{4,5},{5,4},{6,7},{7,6},{8,9},{9,8},{10,11... | collective-permute-start | bytes 294920 | tf_op jit(solution)/shard_map/ppermute | solution.py:339
  72.7 6.5 %collective-permute-start.24 = (f32[32,768]{1,0:T(8,128)S(1)}, f32[32,768]{1,0:T(8,128)S(1)}, u32[]{:S(2)}, u32[]{:S(2)}) collective-permute-start(f32[32,768]{1,0:T(8,128)S(1)} %shard_map.109.vectors.current), channel_id=1, source_target_pairs={{0,4},{1,13},{2,6},{3,15},{4,8},{5,1},{6,10},{7,3},{8,12},{9,5},{1... | collective-permute-start | bytes 294920 | tf_op jit(solution)/shard_map/ppermute | solution.py:332
  72.7 7.4 %collective-permute-start.23 = (f32[32,768]{1,0:T(8,128)S(1)}, f32[32,768]{1,0:T(8,128)S(1)}, u32[]{:S(2)}, u32[]{:S(2)}) collective-permute-start(f32[32,768]{1,0:T(8,128)S(1)} %shard_map.109.vectors.current), channel_id=1, source_target_pairs={{0,2},{1,15},{2,4},{3,1},{4,6},{5,3},{6,8},{7,5},{8,10},{9,7},{10,... | collective-permute-start | bytes 294920 | tf_op jit(solution)/shard_map/ppermute | solution.py:331
  80.6 1.3 %collective-permute-start.25 = (f32[32,768]{1,0:T(8,128)S(1)}, f32[32,768]{1,0:T(8,128)S(1)}, u32[]{:S(2)}, u32[]{:S(2)}) collective-permute-start(f32[32,768]{1,0:T(8,128)S(1)} %shard_map.112.partial), channel_id=1, source_target_pairs={{0,1},{1,0},{2,3},{3,2},{4,5},{5,4},{6,7},{7,6},{8,9},{9,8},{10,11... | collective-permute-start | bytes 294920 | tf_op jit(solution)/shard_map/ppermute | solution.py:339
  82.0 6.5 %collective-permute-start.27 = (f32[32,768]{1,0:T(8,128)S(1)}, f32[32,768]{1,0:T(8,128)S(1)}, u32[]{:S(2)}, u32[]{:S(2)}) collective-permute-start(f32[32,768]{1,0:T(8,128)S(1)} %shard_map.113.vectors.pair), channel_id=1, source_target_pairs={{0,4},{1,13},{2,6},{3,15},{4,8},{5,1},{6,10},{7,3},{8,12},{9,5},{1... | collective-permute-start | bytes 294920 | tf_op jit(solution)/shard_map/ppermute | solution.py:332
  82.0 7.4 %collective-permute-start.26 = (f32[32,768]{1,0:T(8,128)S(1)}, f32[32,768]{1,0:T(8,128)S(1)}, u32[]{:S(2)}, u32[]{:S(2)}) collective-permute-start(f32[32,768]{1,0:T(8,128)S(1)} %shard_map.113.vectors.pair), channel_id=1, source_target_pairs={{0,2},{1,15},{2,4},{3,1},{4,6},{5,3},{6,8},{7,5},{8,10},{9,7},{10,... | collective-permute-start | bytes 294920 | tf_op jit(solution)/shard_map/ppermute | solution.py:331
  82.1 6.8 %collective-permute-start.28 = (f32[32,384]{1,0:T(8,128)S(1)}, f32[32,384]{1,0:T(8,128)S(1)}, u32[]{:S(2)}, u32[]{:S(2)}) collective-permute-start(f32[32,384]{1,0:T(8,128)S(1)} %slice.4.vectors), channel_id=1, source_target_pairs={{0,16},{16,0},{1,17},{17,1},{2,18},{18,2},{3,19},{19,3},{4,20},{20... | collective-permute-start | bytes 147464 | tf_op jit(solution)/shard_map/ppermute | solution.py:354
  90.2 1.2 %collective-permute-start.29 = (f32[32,128]{1,0:T(8,128)S(1)}, f32[32,128]{1,0:T(8,128)S(1)}, u32[]{:S(2)}, u32[]{:S(2)}) collective-permute-start(f32[32,128]{1,0:T(8,128)S(1)} %shard_map.116.one), channel_id=1, source_target_pairs={{0,1},{1,0},{2,3},{3,2},{4,5},{5,4},{6,7},{7,6},{8,9},{9,8},{10,11... | collective-permute-start | bytes 49160 | tf_op jit(solution)/shard_map/ppermute | solution.py:360
